TPU v7x, 32 devices: a whole 2x2x4 slice. The times are simulated.
32 devices in a mesh: group: 2 (over x), dp: 16 (over z, y, core).
Axes of the slice: x: 2, y: 2, z: 4, core: 2. Of those that a mesh axis runs over, the one named last changes fastest.
Arguments:
- queries: bfloat16 [256, 4096], P(('group', 'dp')), parts along dimension 0, may hold values from -80 to 80
- new_keys: bfloat16 [256, 1024], P(('group', 'dp')), parts along dimension 0, may hold values from -6 to 6
- new_values: bfloat16 [256, 1024], P(('group', 'dp')), parts along dimension 0, may hold values from -6 to 6
- cache_keys: bfloat16 [256, 32, 1024], P(('group', 'dp')), parts along dimension 0, may hold values from -4 to 4
- cache_values: bfloat16 [256, 32, 1024], P(('group', 'dp')), parts along dimension 0, may hold values from -6 to 6
- lengths: int32 [256], P(('group', 'dp')), parts along dimension 0, may hold values from 2 to 32, as said below
- residual: bfloat16 [256, 4096], P(('group', 'dp')), parts along dimension 0, may hold values from -6 to 6
- norm_gain: bfloat16 [4096], replicated, may hold values from 0.099609375 to 1.8984375
- router_weight: bfloat16 [4096, 4], replicated, may hold values from -0.09375 to 0.09375
- gate_weight: bfloat16 [4096, 28672], P(None, 'dp'), may hold values from -0.09375 to 0.09375
- up_weight: bfloat16 [4096, 28672], P(None, 'dp'), may hold values from -0.09375 to 0.09375
- down_weight: bfloat16 [28672, 4096], P('dp'), may hold values from -0.0625 to 0.0625
- routes: int32 [256, 2], P('group'), parts along dimension 0, may hold values from 0 to 3, all different within a row; in each aligned block of 8 rows (0 to 7, 8 to 15, ...) at most 6 rows name the same one
Outputs:
- attended: bfloat16 [256, 4096], P(('group', 'dp')), parts along dimension 0
- expert_out: bfloat16 [256, 4096], P(('group', 'dp')), parts along dimension 0
There are 2 independent parts, one for each index of `group`. A program takes and returns all parts, laid end to end along the dimension named above; an argument that names none is the same for every part. Nothing has to cross between parts.
Inputs may be any that keep to these rules, and one draw needn't show every extreme that they name: `routes`: each row names two different experts; among the rows of one device no expert is named by more than 6 rows, and some expert reaches 6. `lengths`: some row has exactly 32 valid positions.
All inputs are finite; a program needn't handle non-finite values.
Results may differ from a plain program's by a relative error of at most 0.0095.
Values may be sent and summed in bfloat16 or wider, within the bound.
No kernel may reach another device: no remote copies, remote signals or barrier semaphores. Data moves between devices by JAX's collectives and lax.ppermute only.
A program may use at most 128 MiB of HBM per device.

v0:
```python
import jax
import jax.numpy as jnp
from jax import lax
from jax.sharding import PartitionSpec as P

D = 4096
HEADS = 32
KV_HEADS = 8
HEAD_DIM = 128
EXPERTS = 4
FF = 7168


def attend(queries, new_keys, new_values, cache_keys, cache_values, lengths, residual, norm_gain):
    row_count = queries.shape[0]
    positions = cache_keys.shape[1]
    groups = HEADS // KV_HEADS
    score_scale = 1.0 / HEAD_DIM**0.5
    query_b = queries.reshape(row_count, KV_HEADS, groups, HEAD_DIM)
    keys_b = cache_keys.reshape(row_count, positions, KV_HEADS, HEAD_DIM)
    values_b = cache_values.reshape(row_count, positions, KV_HEADS, HEAD_DIM)
    newk_b = new_keys.reshape(row_count, KV_HEADS, HEAD_DIM)
    newv_f = new_values.astype(jnp.float32).reshape(row_count, KV_HEADS, HEAD_DIM)
    scores = (
        jnp.einsum("rgjd,rtgd->rgjt", query_b, keys_b, preferred_element_type=jnp.float32)
        * score_scale
    )
    in_cache = (jnp.arange(positions)[None, :] < lengths[:, None])[:, None, None, :]
    scores = jnp.where(in_cache, scores, -jnp.inf)
    new_score = (
        jnp.einsum("rgjd,rgd->rgj", query_b, newk_b, preferred_element_type=jnp.float32)
        * score_scale
    )
    peak = jnp.maximum(jnp.max(scores, axis=-1), new_score)
    weights = jnp.exp(scores - peak[..., None])
    new_weight = jnp.exp(new_score - peak)
    total = jnp.sum(weights, axis=-1) + new_weight
    probs = (weights / total[..., None]).astype(jnp.bfloat16)
    new_prob = (new_weight / total).astype(jnp.bfloat16)
    mixed = jnp.einsum("rgjt,rtgd->rgjd", probs, values_b, preferred_element_type=jnp.float32)
    mixed = mixed + new_prob.astype(jnp.float32)[..., None] * newv_f[:, :, None, :]
    attended = (residual.astype(jnp.float32) + mixed.reshape(row_count, D)).astype(jnp.bfloat16)
    states = attended.astype(jnp.float32)
    normed = states * lax.rsqrt(jnp.mean(states * states, axis=-1, keepdims=True) + 1e-05)
    normed = (normed * norm_gain.astype(jnp.float32)).astype(jnp.bfloat16)
    return (attended, normed)


def expert_rows(inputs, gate_weight, up_weight, down_weight):
    gate = jnp.dot(inputs, gate_weight, preferred_element_type=jnp.float32)
    upper = jnp.dot(inputs, up_weight, preferred_element_type=jnp.float32)
    hidden = (jax.nn.silu(gate) * upper).astype(jnp.bfloat16)
    return jnp.dot(hidden, down_weight, preferred_element_type=jnp.float32)


def own_share(logits, row_routes, expert):
    expert_ids = jnp.arange(EXPERTS, dtype=jnp.int32)
    first_logit = jnp.sum(jnp.where(row_routes[:, 0:1] == expert_ids[None, :], logits, 0.0), axis=1)
    second_logit = jnp.sum(
        jnp.where(row_routes[:, 1:2] == expert_ids[None, :], logits, 0.0), axis=1
    )
    first_share = jax.nn.sigmoid(first_logit - second_logit)
    second_share = jax.nn.sigmoid(second_logit - first_logit)
    return jnp.where(row_routes[:, 0] == expert, first_share, 0.0) + jnp.where(
        row_routes[:, 1] == expert, second_share, 0.0
    )


def mix_rows(
    normed, half_rows, rows_dev, router_weight, gate_weight, up_weight, down_weight, routes
):
    dev_count = lax.axis_size("dp")
    my_index = lax.axis_index("dp")
    columns = gate_weight.shape[1]
    expert = my_index * columns // FF
    source_routes = routes.reshape(dev_count, rows_dev, 2)
    gathered = lax.all_gather(normed, "dp", axis=0, tiled=True)
    logits = jnp.dot(gathered, router_weight, preferred_element_type=jnp.float32)
    weighting = own_share(logits, source_routes.reshape(dev_count * half_rows, 2), expert)
    return lax.psum_scatter(
        expert_rows(gathered, gate_weight, up_weight, down_weight) * weighting[:, None],
        "dp",
        scatter_dimension=0,
        tiled=True,
    )


def body(
    queries,
    new_keys,
    new_values,
    cache_keys,
    cache_values,
    lengths,
    residual,
    norm_gain,
    router_weight,
    gate_weight,
    up_weight,
    down_weight,
    routes,
):
    rows_dev = queries.shape[0]
    pieces = 1
    half_rows = rows_dev // pieces
    attended, normed = attend(
        queries, new_keys, new_values, cache_keys, cache_values, lengths, residual, norm_gain
    )
    mixed = mix_rows(
        normed, half_rows, rows_dev, router_weight, gate_weight, up_weight, down_weight, routes
    )
    expert_out = mixed.astype(jnp.bfloat16)
    return (attended, expert_out)


def solution(mesh):
    placed = (
        P(("group", "dp"), None),
        P(("group", "dp"), None),
        P(("group", "dp"), None),
        P(("group", "dp"), None, None),
        P(("group", "dp"), None, None),
        P(("group", "dp")),
        P(("group", "dp"), None),
        P(),
        P(),
        P(None, "dp"),
        P(None, "dp"),
        P("dp", None),
        P("group", None),
    )
    return jax.shard_map(
        body,
        mesh=mesh,
        in_specs=placed,
        out_specs=(P(("group", "dp"), None), P(("group", "dp"), None)),
        check_vma=False,
    )
```

profile of v0, /device:TPU:0, one launch (start us, length us, event | category | flops | bytes accessed | tf_op | source)
XLA Modules:
  0.0 149.5 jit_solution(429353802495533278)
XLA Ops:
  7.2 0.0 copy-start
  7.2 0.0 all-gather.2.cloned.1.call-start
  7.2 0.8 iota_compare_fusion
  8.0 0.7 convert_element_type.37
  8.7 0.7 bitcast_convert_fusion
  9.4 1.0 fusion.13
  10.5 1.6 %fusion.22 = (f32[8,8,4]{2,1,0:T(8,128)S(1)}, f32[8,8,4,32]{3,2,1,0:T(4,128)S(1)}) fusion(bf16[8,8,4,128]{3,0,2,1:T(8,128)(2,1)} %bitcast.49, pred[8,32]{1,0:T(8,128)(4,1)S(1)} %iota_compare_fusion, bf16[8,32,1024]{2,1,0:T(8,128)(2,1)} %param.16), kind=kOutput, calls=%fused_computation.45 | convolution fusion | flops 2121472 | bytes 623872 | tf_op jit(solution)/shard_map/rgjd,rtgd->rgjt/dot_general | solution.py:25
  12.0 0.3 fusion.10
  12.4 0.0 copy-done
  12.4 0.3 convolution_add_fusion
  12.7 0.1 reshape.107
  12.8 1.0 fusion.7
  13.7 0.0 copy-start.2
  13.8 0.7 fusion.9
  14.5 0.0 all-gather.2.cloned.1.call-update
  14.5 0.0 reduce-scatter.2.cloned.1.call-start
  14.6 0.8 slice_bitcast_fusion
  15.3 40.0 %all-gather.2.cloned.1.call-done = bf16[128,4096]{1,0:T(8,128)(2,1)} async-done(((bf16[8,4096]{1,0:T(8,128)(2,1)}), bf16[128,4096]{1,0:T(8,128)(2,1)}) %all-gather.2.cloned.1.call-update) | async-done | bytes 1048592 | tf_op jit(solution)/shard_map/all_gather | solution.py:77
  55.3 0.0 copy-start.1
  55.3 1.7 %select_reduce_fusion.1 = (f32[128]{0:T(128)S(1)}, f32[128]{0:T(128)S(1)}) fusion(s32[128]{0:T(128)S(1)} %get-tuple-element.9, s32[128]{0:T(128)S(1)} %get-tuple-element.8, bf16[128,4096]{1,0:T(8,128)(2,1)} %all-gather.2.cloned.1.call-done, bf16[4096,4]{0,1:T(4,128)(2,1)} %param.21), kind=kOutput, calls=%fused_computation.35 | convolution fusion | flops 4197120 | bytes 1083392 | tf_op jit(solution)/shard_map/dot_general | solution.py:78
  57.0 0.8 fusion.20
  57.8 7.6 %fusion.23 = f32[128,1792]{1,0:T(8,128)S(1)} fusion(bf16[128,4096]{1,0:T(8,128)(2,1)} %all-gather.2.cloned.1.call-done, bf16[4096,1792]{1,0:T(8,128)(2,1)} %param.22), kind=kOutput, calls=%fused_computation.46 | convolution fusion | flops 1879048192 | bytes 16646144 | tf_op jit(solution)/shard_map/dot_general | solution.py:50
  65.4 0.0 copy-done.1
  65.4 15.1 %convolution_multiply_fusion = f32[128,4096]{1,0:T(8,128)} fusion(bf16[1792,4096]{1,0:T(8,128)(2,1)} %param.24, f32[128]{0:T(128)S(1)} %fusion.20, bf16[128,4096]{1,0:T(8,128)(2,1)S(1)} %copy-done.1, bf16[4096,1792]{1,0:T(8,128)(2,1)} %param.23, f32[128,1792]{1,0:T(8,128)S(1)} %fusion.23), kind=kOutput, calls=%fused_computation | convolution fusion | flops 3759996928 | bytes 33423872 | tf_op jit(solution)/shard_map/dot_general | solution.py:53
  80.5 0.0 copy-done.2
  80.5 0.0 reduce-scatter.2.cloned.1.call-update
  80.5 60.6 %reduce-scatter.2.cloned.1.call-done = f32[8,4096]{1,0:T(8,128)} async-done(((f32[128,4096]{1,0:T(8,128)}), f32[8,4096]{1,0:T(8,128)}) %reduce-scatter.2.cloned.1.call-update) | async-done | bytes 131088 | tf_op jit(solution)/shard_map/reduce_scatter | solution.py:80
  141.1 1.5 %convert_element_type.40 = bf16[8,4096]{1,0:T(8,128)(2,1)} convert(f32[8,4096]{1,0:T(8,128)} %reduce-scatter.2.cloned.1.call-done) | non-fusion elementwise | flops 32768 | bytes 196608 | tf_op jit(solution)/shard_map/convert_element_type | solution.py:112
  (4 shorter events, 0.0 us)
Async XLA Ops:
  7.2 5.2 %copy-start = (bf16[8,32,1024]{2,1,0:T(8,128)(2,1)S(1)}, bf16[8,32,1024]{2,1,0:T(8,128)(2,1)}, u32[]{:S(2)}) copy-start(bf16[8,32,1024]{2,1,0:T(8,128)(2,1)} %param.17) | copy-start | bytes 1572868
  7.2 48.1 %all-gather.2.cloned.1.call-start = ((), (), s32[]{:S(2)}) async-start(), calls=%async_computation.1 | async-start | bytes 1114112 | tf_op jit(solution)/shard_map/all_gather | solution.py:77
  13.7 66.8 %copy-start.2 = (bf16[8,4096]{1,0:T(8,128)(2,1)}, bf16[8,4096]{1,0:T(8,128)(2,1)S(1)}, u32[]{:S(2)}) copy-start(bf16[8,4096]{1,0:T(8,128)(2,1)S(1)} %get-tuple-element.5) | copy-start | bytes 196612
  14.5 126.6 %reduce-scatter.2.cloned.1.call-start = ((), (), s32[]{:S(2)}) async-start(), calls=%async_computation.2 | async-start | bytes 2228224 | tf_op jit(solution)/shard_map/reduce_scatter | solution.py:80
  55.3 10.1 %copy-start.1 = (bf16[128,4096]{1,0:T(8,128)(2,1)S(1)}, bf16[128,4096]{1,0:T(8,128)(2,1)}, u32[]{:S(2)}) copy-start(bf16[128,4096]{1,0:T(8,128)(2,1)} %all-gather.2.cloned.1.call-done) | copy-start | bytes 3145732
Sparse Core Ops, SparseCore 0:
  14.6 40.6 all-gather.1
  80.6 60.4 reduce-scatter.1
where the time goes:
time: 150 us; the launch traced here: 149 us
  waiting for transfers between devices  101 us (67%)
  matrix products  27.3 us (18%)
  between operations  14.2 us (9%)
  other arithmetic  6.52 us (4%)
    reduce_scatter x1, waiting for transfers between devices, mix_rows(): lax.psum_scatter(expert_rows(gathered, gate_weight, up_weight, down_weigh...  60.6 us
    all_gather x1, waiting for transfers between devices, mix_rows(): gathered = lax.all_gather(normed, 'dp', axis=0, tiled=True)  40 us
    dot_general x1, matrix products, expert_rows(): return jnp.dot(hidden, down_weight, preferred_element_type=jnp.float32)  15.1 us
    dot_general x1, matrix products, expert_rows(): gate = jnp.dot(inputs, gate_weight, preferred_element_type=jnp.float32)  7.58 us
  transfers between devices with their start and end apart: 2, of which 2 were waited for; matrix products, arithmetic and copies ran while one was open for 1% of the time, Pallas kernels for 0%

commit v1 on v0

--- a/solution.py
+++ b/solution.py
@@ -53,36 +53,29 @@
     return jnp.dot(hidden, down_weight, preferred_element_type=jnp.float32)
 
 
-def own_share(logits, row_routes, expert):
+def row_shares(normed, router_weight, routes):
+    logits = jnp.dot(normed, router_weight, preferred_element_type=jnp.float32)
     expert_ids = jnp.arange(EXPERTS, dtype=jnp.int32)
-    first_logit = jnp.sum(jnp.where(row_routes[:, 0:1] == expert_ids[None, :], logits, 0.0), axis=1)
-    second_logit = jnp.sum(
-        jnp.where(row_routes[:, 1:2] == expert_ids[None, :], logits, 0.0), axis=1
-    )
+    first_hot = routes[:, 0:1] == expert_ids[None, :]
+    second_hot = routes[:, 1:2] == expert_ids[None, :]
+    first_logit = jnp.sum(jnp.where(first_hot, logits, 0.0), axis=1)
+    second_logit = jnp.sum(jnp.where(second_hot, logits, 0.0), axis=1)
     first_share = jax.nn.sigmoid(first_logit - second_logit)
     second_share = jax.nn.sigmoid(second_logit - first_logit)
-    return jnp.where(row_routes[:, 0] == expert, first_share, 0.0) + jnp.where(
-        row_routes[:, 1] == expert, second_share, 0.0
+    return jnp.where(first_hot, first_share[:, None], 0.0) + jnp.where(
+        second_hot, second_share[:, None], 0.0
     )
 
 
-def mix_rows(
-    normed, half_rows, rows_dev, router_weight, gate_weight, up_weight, down_weight, routes
-):
-    dev_count = lax.axis_size("dp")
-    my_index = lax.axis_index("dp")
-    columns = gate_weight.shape[1]
-    expert = my_index * columns // FF
-    source_routes = routes.reshape(dev_count, rows_dev, 2)
-    gathered = lax.all_gather(normed, "dp", axis=0, tiled=True)
-    logits = jnp.dot(gathered, router_weight, preferred_element_type=jnp.float32)
-    weighting = own_share(logits, source_routes.reshape(dev_count * half_rows, 2), expert)
-    return lax.psum_scatter(
-        expert_rows(gathered, gate_weight, up_weight, down_weight) * weighting[:, None],
-        "dp",
-        scatter_dimension=0,
-        tiled=True,
+def plane_shift(value, count, offset):
+    plane = count // EXPERTS
+    return lax.ppermute(
+        value, "dp", [(i, (i + offset * plane) % count) for i in range(count)]
     )
+
+
+def swap(value, count, bit):
+    return lax.ppermute(value, "dp", [(i, i ^ bit) for i in range(count)])
 
 
 def body(
@@ -100,17 +93,37 @@
     down_weight,
     routes,
 ):
-    rows_dev = queries.shape[0]
-    pieces = 1
-    half_rows = rows_dev // pieces
+    rows = queries.shape[0]
+    count = lax.axis_size("dp")
+    index = lax.axis_index("dp")
+    plane = count // EXPERTS
+    bits = [1 << k for k in reversed(range(plane.bit_length() - 1))]
     attended, normed = attend(
         queries, new_keys, new_values, cache_keys, cache_values, lengths, residual, norm_gain
     )
-    mixed = mix_rows(
-        normed, half_rows, rows_dev, router_weight, gate_weight, up_weight, down_weight, routes
+    own_routes = lax.dynamic_slice_in_dim(routes, index * rows, rows, 0)
+    share = row_shares(normed, router_weight, own_routes)
+
+    gathered = jnp.concatenate(
+        [normed] + [plane_shift(normed, count, k) for k in range(1, EXPERTS)], axis=0
     )
-    expert_out = mixed.astype(jnp.bfloat16)
-    return (attended, expert_out)
+    for bit in bits:
+        gathered = jnp.concatenate([gathered, swap(gathered, count, bit)], axis=0)
+
+    terms = expert_rows(gathered, gate_weight, up_weight, down_weight)
+    for bit in reversed(bits):
+        half = terms.shape[0] // 2
+        other = swap(terms[half:].astype(jnp.bfloat16), count, bit)
+        terms = terms[:half] + other.astype(jnp.float32)
+    terms = terms.astype(jnp.bfloat16).reshape(EXPERTS, rows, D)
+
+    expert = index // plane
+    total = jnp.zeros((rows, D), jnp.float32)
+    for k in range(EXPERTS):
+        result = terms[k] if k == 0 else plane_shift(terms[k], count, -k)
+        column = lax.dynamic_slice_in_dim(share, (expert + k) % EXPERTS, 1, 1)
+        total = total + column * result.astype(jnp.float32)
+    return (attended, total.astype(jnp.bfloat16))
 
 
 def solution(mesh):

time: 150 us -> 74.2 us (0.49)
  waiting for transfers between devices: 101 us -> 26 us
  between operations: 14.2 us -> 0.93 us
  starting transfers between devices: 0.08 us -> 13 us
  local copies, waits for them, and re-layouts: 0.84 us -> 3.13 us
  matrix products: 27.3 us -> 25.2 us
    reduce_scatter x1 -> x0, waiting for transfers between devices: 60.6 us -> none  [mix_rows(): lax.psum_scatter(expert_rows(gathered, gate_weight, up_weight, down_weigh...]
    all_gather x1 -> x0, waiting for transfers between devices: 40 us -> none  [mix_rows(): gathered = lax.all_gather(normed, 'dp', axis=0, tiled=True)]
    ppermute x0 -> x10, waiting for transfers between devices: none -> 26 us  [the longest x4 16 us: swap(): return lax.ppermute(value, 'dp', [(i, i ^ bit) for i in range(count)])]
    ppermute x0 -> x10, starting transfers between devices: none -> 13 us  [the longest x6 9.6 us: plane_shift(): lax.ppermute(value, 'dp', [(i, (i + offset * plane) % count) for i in ran...]
    unnamed x6 -> x16, local copies, waits for them, and re-layouts: 0.02 us -> 2.01 us
  transfers between devices with their start and end apart: 2 -> 10, of which waited for: 2 -> 9; matrix products, arithmetic and copies ran while one was open for 1% -> 2% of each run, Pallas kernels for 0% -> 0%
where the time goes in v1:
time: 74.2 us; the launch traced here: 73.8 us
  waiting for transfers between devices  26 us (35%)
  matrix products  25.2 us (34%)
  starting transfers between devices  13 us (18%)
  other arithmetic  5.54 us (7%)
  local copies, waits for them, and re-layouts  3.13 us (4%)
  between operations  0.93 us (1%)
    ppermute x4, waiting for transfers between devices, swap(): return lax.ppermute(value, 'dp', [(i, i ^ bit) for i in range(count)])  16 us
    dot_general x1, matrix products, expert_rows(): return jnp.dot(hidden, down_weight, preferred_element_type=jnp.float32)  14.1 us
    ppermute x6, waiting for transfers between devices, plane_shift(): lax.ppermute(value, 'dp', [(i, (i + offset * plane) % count) for i in ran...  10 us
    ppermute x6, starting transfers between devices, plane_shift(): lax.ppermute(value, 'dp', [(i, (i + offset * plane) % count) for i in ran...  9.6 us
    dot_general x1, matrix products, expert_rows(): gate = jnp.dot(inputs, gate_weight, preferred_element_type=jnp.float32)  7.25 us
    ppermute x4, starting transfers between devices, swap(): return lax.ppermute(value, 'dp', [(i, i ^ bit) for i in range(count)])  3.39 us
    unnamed x16, local copies, waits for them, and re-layouts  2.01 us
    dot_general x1, matrix products, attend(): jnp.einsum('rgjd,rtgd->rgjt', query_b, keys_b, preferred_element_type=jnp...  1.55 us
  transfers between devices with their start and end apart: 10, of which 9 were waited for; matrix products, arithmetic and copies ran while one was open for 2% of the time, Pallas kernels for 0%

profile of v1, /device:TPU:0, one launch (start us, length us, event | category | flops | bytes accessed | tf_op | source)
XLA Modules:
  0.0 73.8 jit_solution(9560888585028985673)
XLA Ops:
  0.6 0.8 %iota_compare_fusion = pred[8,32]{1,0:T(8,128)(4,1)S(1)} fusion(s32[8]{0:T(128)} %param.18), kind=kLoop, calls=%fused_computation.49 | loop fusion | flops 256 | bytes 288 | tf_op jit(solution)/shard_map/lt | solution.py:28
  1.4 0.7 convert_element_type.60
  2.1 0.7 bitcast_convert_fusion
  2.9 1.0 %fusion.14 = f32[8,8,1,4]{3,2,1,0:T(1,128)S(1)} fusion(bf16[8,8,4,128]{3,0,2,1:T(8,128)(2,1)} %bitcast.46, bf16[8,8,128,1]{2,0,1,3:T(8,128)(2,1)} %bitcast.48), kind=kOutput, calls=%fused_computation.28 | convolution fusion | flops 65536 | bytes 82944 | tf_op jit(solution)/shard_map/rgjd,rgd->rgj/dot_general | solution.py:31
  3.9 1.6 %fusion.27 = (f32[8,8,4]{2,1,0:T(8,128)S(1)}, f32[8,8,4,32]{3,2,1,0:T(4,128)S(1)}) fusion(bf16[8,8,4,128]{3,0,2,1:T(8,128)(2,1)} %bitcast.47, pred[8,32]{1,0:T(8,128)(4,1)S(1)} %iota_compare_fusion, bf16[8,32,1024]{2,1,0:T(8,128)(2,1)} %param.16), kind=kOutput, calls=%fused_computation.71 | convolution fusion | flops 2121472 | bytes 623872 | tf_op jit(solution)/shard_map/rgjd,rtgd->rgjt/dot_general | solution.py:25
  5.5 0.3 fusion.11
  5.8 0.3 convolution_add_fusion
  6.2 1.0 %fusion.8 = (f32[8]{0:T(128)S(1)}, bf16[8,4096]{1,0:T(8,128)(2,1)S(1)}) fusion(f32[8,4096]{1,0:T(8,128)S(1)} %reshape.80, bf16[8,4096]{1,0:T(8,128)(2,1)} %param.19), kind=kLoop, calls=%fused_computation.18 | loop fusion | flops 196600 | bytes 262176 | tf_op jit(solution)/shard_map/reduce_sum | solution.py:44
  7.3 5.1 %collective-permute-start.2 = (bf16[8,4096]{1,0:T(8,128)(2,1)S(1)}, bf16[8,4096]{1,0:T(8,128)(2,1)S(1)}, u32[]{:S(2)}, u32[]{:S(2)}) collective-permute-start(bf16[8,4096]{1,0:T(8,128)(2,1)S(1)} %get-tuple-element.5), channel_id=1, source_target_pairs={{0,12},{1,13},{2,14},{3,15},{4,0},{5,1},{6,2},{7,3},{8,4},{9,5},{1... | collective-permute-start | bytes 196616 | tf_op jit(solution)/shard_map/ppermute | solution.py:72
  12.4 1.0 %collective-permute-start = (bf16[8,4096]{1,0:T(8,128)(2,1)S(1)}, bf16[8,4096]{1,0:T(8,128)(2,1)S(1)}, u32[]{:S(2)}, u32[]{:S(2)}) collective-permute-start(bf16[8,4096]{1,0:T(8,128)(2,1)S(1)} %get-tuple-element.5), channel_id=1, source_target_pairs={{0,4},{1,5},{2,6},{3,7},{4,8},{5,9},{6,10},{7,11},{8,12},{9,13},{1... | collective-permute-start | bytes 196616 | tf_op jit(solution)/shard_map/ppermute | solution.py:72
  13.4 1.5 %collective-permute-done.2 = bf16[8,4096]{1,0:T(8,128)(2,1)S(1)} collective-permute-done((bf16[8,4096]{1,0:T(8,128)(2,1)S(1)}, bf16[8,4096]{1,0:T(8,128)(2,1)S(1)}, u32[]{:S(2)}, u32[]{:S(2)}) %collective-permute-start.2) | collective-permute-done | bytes 65568 | tf_op jit(solution)/shard_map/ppermute | solution.py:72
  14.9 4.0 %collective-permute-done.1 = bf16[8,4096]{1,0:T(8,128)(2,1)S(1)} collective-permute-done((bf16[8,4096]{1,0:T(8,128)(2,1)S(1)}, bf16[8,4096]{1,0:T(8,128)(2,1)S(1)}, u32[]{:S(2)}, u32[]{:S(2)}) %collective-permute-start.1) | collective-permute-done | bytes 65568 | tf_op jit(solution)/shard_map/ppermute | solution.py:72
  18.9 1.6 %collective-permute-start.3 = (bf16[32,4096]{1,0:T(8,128)(2,1)S(1)}, bf16[32,4096]{1,0:T(8,128)(2,1)S(1)}, u32[]{:S(2)}, u32[]{:S(2)}) collective-permute-start(bf16[32,4096]{1,0:T(8,128)(2,1)S(1)} %pad_maximum_fusion), channel_id=1, source_target_pairs={{0,2},{1,3},{2,0},{3,1},{4,6},{5,7},{6,4},{7,5},{8,10},{9,11},{10,... | collective-permute-start | bytes 786440 | tf_op jit(solution)/shard_map/ppermute | solution.py:78
  20.5 6.5 %collective-permute-done.3 = bf16[32,4096]{1,0:T(8,128)(2,1)S(1)} collective-permute-done((bf16[32,4096]{1,0:T(8,128)(2,1)S(1)}, bf16[32,4096]{1,0:T(8,128)(2,1)S(1)}, u32[]{:S(2)}, u32[]{:S(2)}) %collective-permute-start.3) | collective-permute-done | bytes 262176 | tf_op jit(solution)/shard_map/ppermute | solution.py:78
  27.1 1.9 %collective-permute-done.4 = bf16[64,4096]{1,0:T(8,128)(2,1)S(1)} collective-permute-done((bf16[64,4096]{1,0:T(8,128)(2,1)S(1)}, bf16[64,4096]{1,0:T(8,128)(2,1)S(1)}, u32[]{:S(2)}, u32[]{:S(2)}) %collective-permute-start.4) | collective-permute-done | bytes 524320 | tf_op jit(solution)/shard_map/ppermute | solution.py:78
  29.1 1.0 %copy-done.1 = bf16[128,4096]{1,0:T(8,128)(2,1)} copy-done((bf16[128,4096]{1,0:T(8,128)(2,1)}, bf16[128,4096]{1,0:T(8,128)(2,1)S(1)}, u32[]{:S(2)}) %copy-start.1) | copy-done | bytes 1048600
  30.0 7.3 %fusion.30 = f32[128,1792]{1,0:T(8,128)S(1)} fusion(bf16[128,4096]{1,0:T(8,128)(2,1)S(1)} %constant_dynamic-update-slice_fusion.5, bf16[4096,1792]{1,0:T(8,128)(2,1)} %param.22), kind=kOutput, calls=%fused_computation.73 | convolution fusion | flops 1879048192 | bytes 16646144 | tf_op jit(solution)/shard_map/dot_general | solution.py:50
  37.3 14.1 %fusion.6 = f32[128,4096]{1,0:T(8,128)S(1)} fusion(bf16[1792,4096]{1,0:T(8,128)(2,1)} %param.24, f32[128,1792]{1,0:T(8,128)S(1)} %fusion.30, bf16[128,4096]{1,0:T(8,128)(2,1)} %copy-done.1, bf16[4096,1792]{1,0:T(8,128)(2,1)} %param.23), kind=kOutput, calls=%fused_computation.13 | convolution fusion | flops 3759472640 | bytes 33423360 | tf_op jit(solution)/shard_map/dot_general | solution.py:53
  51.4 0.8 %slice.63 = bf16[64,4096]{1,0:T(8,128)(2,1)} slice(f32[128,4096]{1,0:T(8,128)S(1)} %fusion.6), slice={[64:128], [0:4096]} | slice | bytes 1048576 | tf_op jit(solution)/shard_map/slice | solution.py:116
  52.4 1.0 %select_reduce_fusion.1 = (f32[8]{0:T(128)S(1)}, f32[8]{0:T(128)S(1)}) fusion(s32[8]{0:T(128)S(1)} %get-tuple-element.28, s32[8]{0:T(128)S(1)} %get-tuple-element.27, bf16[8,4096]{1,0:T(8,128)(2,1)} %copy-done.3, bf16[4096,4]{0,1:T(4,128)(2,1)} %param.21), kind=kOutput, calls=%fused_computation.53 | convolution fusion | flops 262320 | bytes 98432 | tf_op jit(solution)/shard_map/dot_general | solution.py:57
  53.4 0.9 %collective-permute-done.5 = bf16[64,4096]{1,0:T(8,128)(2,1)S(1)} collective-permute-done((bf16[64,4096]{1,0:T(8,128)(2,1)}, bf16[64,4096]{1,0:T(8,128)(2,1)S(1)}, u32[]{:S(2)}, u32[]{:S(2)}) %collective-permute-start.5) | collective-permute-done | bytes 524320 | tf_op jit(solution)/shard_map/ppermute | solution.py:78
  54.4 1.0 %copy-done.2 = f32[64,4096]{1,0:T(8,128)} copy-done((f32[64,4096]{1,0:T(8,128)}, f32[64,4096]{1,0:T(8,128)S(1)}, u32[]{:S(2)}) %copy-start.2) | copy-done | bytes 1048600
  55.4 1.6 %collective-permute-start.6 = (bf16[32,4096]{1,0:T(8,128)(2,1)S(1)}, bf16[32,4096]{1,0:T(8,128)(2,1)S(1)}, u32[]{:S(2)}, u32[]{:S(2)}) collective-permute-start(bf16[32,4096]{1,0:T(8,128)(2,1)S(1)} %slice.64), channel_id=1, source_target_pairs={{0,2},{1,3},{2,0},{3,1},{4,6},{5,7},{6,4},{7,5},{8,10},{9,11},{10,... | collective-permute-start | bytes 786440 | tf_op jit(solution)/shard_map/ppermute | solution.py:78
  57.1 6.7 %collective-permute-done.6 = bf16[32,4096]{1,0:T(8,128)(2,1)S(1)} collective-permute-done((bf16[32,4096]{1,0:T(8,128)(2,1)S(1)}, bf16[32,4096]{1,0:T(8,128)(2,1)S(1)}, u32[]{:S(2)}, u32[]{:S(2)}) %collective-permute-start.6) | collective-permute-done | bytes 262176 | tf_op jit(solution)/shard_map/ppermute | solution.py:78
  63.9 1.1 %fusion.5 = bf16[32,4096]{1,0:T(8,128)(2,1)S(1)} fusion(f32[64,4096]{1,0:T(8,128)} %copy-done.2, bf16[32,4096]{1,0:T(8,128)(2,1)S(1)} %collective-permute-done.6), kind=kLoop, calls=%fused_computation.12 | loop fusion | flops 393216 | bytes 1048576 | tf_op jit(solution)/shard_map/convert_element_type | solution.py:118
  65.0 0.3 collective-permute-start.7
  65.3 1.8 %collective-permute-start.9 = (bf16[8,4096]{1,0:T(8,128)(2,1)S(1)}, bf16[8,4096]{1,0:T(8,128)(2,1)S(1)}, u32[]{:S(2)}, u32[]{:S(2)}) collective-permute-start(bf16[8,4096]{1,0:T(8,128)(2,1)S(1)} %get-tuple-element.9), channel_id=1, source_target_pairs={{0,4},{1,5},{2,6},{3,7},{4,8},{5,9},{6,10},{7,11},{8,12},{9,13},{1... | collective-permute-start | bytes 196616 | tf_op jit(solution)/shard_map/ppermute | solution.py:72
  67.1 1.4 %collective-permute-start.8 = (bf16[8,4096]{1,0:T(8,128)(2,1)S(1)}, bf16[8,4096]{1,0:T(8,128)(2,1)S(1)}, u32[]{:S(2)}, u32[]{:S(2)}) collective-permute-start(bf16[8,4096]{1,0:T(8,128)(2,1)S(1)} %get-tuple-element.10), channel_id=1, source_target_pairs={{0,8},{1,9},{2,10},{3,11},{4,12},{5,13},{6,14},{7,15},{8,0},{9,1},... | collective-permute-start | bytes 196616 | tf_op jit(solution)/shard_map/ppermute | solution.py:72
  68.5 2.1 %collective-permute-done.7 = bf16[8,4096]{1,0:T(8,128)(2,1)S(1)} collective-permute-done((bf16[8,4096]{1,0:T(8,128)(2,1)S(1)}, bf16[8,4096]{1,0:T(8,128)(2,1)S(1)}, u32[]{:S(2)}, u32[]{:S(2)}) %collective-permute-start.7) | collective-permute-done | bytes 65568 | tf_op jit(solution)/shard_map/ppermute | solution.py:72
  70.6 1.0 %collective-permute-done.9 = bf16[8,4096]{1,0:T(8,128)(2,1)S(1)} collective-permute-done((bf16[8,4096]{1,0:T(8,128)(2,1)S(1)}, bf16[8,4096]{1,0:T(8,128)(2,1)S(1)}, u32[]{:S(2)}, u32[]{:S(2)}) %collective-permute-start.9) | collective-permute-done | bytes 65568 | tf_op jit(solution)/shard_map/ppermute | solution.py:72
  71.6 1.4 %collective-permute-done.8 = bf16[8,4096]{1,0:T(8,128)(2,1)S(1)} collective-permute-done((bf16[8,4096]{1,0:T(8,128)(2,1)S(1)}, bf16[8,4096]{1,0:T(8,128)(2,1)S(1)}, u32[]{:S(2)}, u32[]{:S(2)}) %collective-permute-start.8) | collective-permute-done | bytes 65568 | tf_op jit(solution)/shard_map/ppermute | solution.py:72
  73.0 0.7 %add_convert_fusion = bf16[8,4096]{1,0:T(8,128)(2,1)} fusion(bf16[8,4096]{1,0:T(8,128)(2,1)S(1)} %collective-permute-done.9, bf16[8,4096]{1,0:T(8,128)(2,1)S(1)} %collective-permute-done.8, bf16[8,4096]{1,0:T(8,128)(2,1)S(1)} %collective-permute-done.7, bf16[32,4096]{1,0:T(8,128)(2,1)S(1)} %fusion.5, f32[8]{0:T(128)S(1)} %get-tuple-element.22, ...), kind=kLoop, calls=%fused_computation.21 | loop fusion | flops 393216 | bytes 327808 | tf_op jit(solution)/shard_map/convert_element_type | solution.py:126
  (35 shorter events, 0.8 us)
Async XLA Ops:
  0.6 5.2 %copy-start = (bf16[8,32,1024]{2,1,0:T(8,128)(2,1)S(1)}, bf16[8,32,1024]{2,1,0:T(8,128)(2,1)}, u32[]{:S(2)}) copy-start(bf16[8,32,1024]{2,1,0:T(8,128)(2,1)} %param.17) | copy-start | bytes 1572868
  7.2 11.7 %copy-start.4 = (bf16[8,4096]{1,0:T(8,128)(2,1)}, bf16[8,4096]{1,0:T(8,128)(2,1)S(1)}, u32[]{:S(2)}) copy-start(bf16[8,4096]{1,0:T(8,128)(2,1)S(1)} %get-tuple-element.7) | copy-start | bytes 196612
  7.3 19.7 %copy-start.3 = (bf16[8,4096]{1,0:T(8,128)(2,1)}, bf16[8,4096]{1,0:T(8,128)(2,1)S(1)}, u32[]{:S(2)}) copy-start(bf16[8,4096]{1,0:T(8,128)(2,1)S(1)} %get-tuple-element.5) | copy-start | bytes 196612
  7.3 7.6 %collective-permute-start.2 = (bf16[8,4096]{1,0:T(8,128)(2,1)S(1)}, bf16[8,4096]{1,0:T(8,128)(2,1)S(1)}, u32[]{:S(2)}, u32[]{:S(2)}) collective-permute-start(bf16[8,4096]{1,0:T(8,128)(2,1)S(1)} %get-tuple-element.5), channel_id=1, source_target_pairs={{0,12},{1,13},{2,14},{3,15},{4,0},{5,1},{6,2},{7,3},{8,4},{9,5},{1... | collective-permute-start | bytes 196616 | tf_op jit(solution)/shard_map/ppermute | solution.py:72
  12.4 6.5 %collective-permute-start.1 = (bf16[8,4096]{1,0:T(8,128)(2,1)S(1)}, bf16[8,4096]{1,0:T(8,128)(2,1)S(1)}, u32[]{:S(2)}, u32[]{:S(2)}) collective-permute-start(bf16[8,4096]{1,0:T(8,128)(2,1)S(1)} %get-tuple-element.5), channel_id=1, source_target_pairs={{0,8},{1,9},{2,10},{3,11},{4,12},{5,13},{6,14},{7,15},{8,0},{9,1},... | collective-permute-start | bytes 196616 | tf_op jit(solution)/shard_map/ppermute | solution.py:72
  12.4 6.5 %collective-permute-start = (bf16[8,4096]{1,0:T(8,128)(2,1)S(1)}, bf16[8,4096]{1,0:T(8,128)(2,1)S(1)}, u32[]{:S(2)}, u32[]{:S(2)}) collective-permute-start(bf16[8,4096]{1,0:T(8,128)(2,1)S(1)} %get-tuple-element.5), channel_id=1, source_target_pairs={{0,4},{1,5},{2,6},{3,7},{4,8},{5,9},{6,10},{7,11},{8,12},{9,13},{1... | collective-permute-start | bytes 196616 | tf_op jit(solution)/shard_map/ppermute | solution.py:72
  18.9 8.1 %collective-permute-start.3 = (bf16[32,4096]{1,0:T(8,128)(2,1)S(1)}, bf16[32,4096]{1,0:T(8,128)(2,1)S(1)}, u32[]{:S(2)}, u32[]{:S(2)}) collective-permute-start(bf16[32,4096]{1,0:T(8,128)(2,1)S(1)} %pad_maximum_fusion), channel_id=1, source_target_pairs={{0,2},{1,3},{2,0},{3,1},{4,6},{5,7},{6,4},{7,5},{8,10},{9,11},{10,... | collective-permute-start | bytes 786440 | tf_op jit(solution)/shard_map/ppermute | solution.py:78
  27.0 2.0 %collective-permute-start.4 = (bf16[64,4096]{1,0:T(8,128)(2,1)S(1)}, bf16[64,4096]{1,0:T(8,128)(2,1)S(1)}, u32[]{:S(2)}, u32[]{:S(2)}) collective-permute-start(bf16[64,4096]{1,0:T(8,128)(2,1)S(1)} %get-tuple-element.11), channel_id=1, source_target_pairs={{0,1},{1,0},{2,3},{3,2},{4,5},{5,4},{6,7},{7,6},{8,9},{9,8},{10,11... | collective-permute-start | bytes 1572872 | tf_op jit(solution)/shard_map/ppermute | solution.py:78
  29.0 1.0 %copy-start.1 = (bf16[128,4096]{1,0:T(8,128)(2,1)}, bf16[128,4096]{1,0:T(8,128)(2,1)S(1)}, u32[]{:S(2)}) copy-start(bf16[128,4096]{1,0:T(8,128)(2,1)S(1)} %constant_dynamic-update-slice_fusion.5) | copy-start | bytes 3145732
  37.3 15.1 %copy-start.5 = (s32[128,2]{0,1:T(2,128)S(1)}, s32[128,2]{0,1:T(2,128)}, u32[]{:S(2)}) copy-start(s32[128,2]{0,1:T(2,128)} %param.25) | copy-start | bytes 3076
  52.2 2.1 %collective-permute-start.5 = (bf16[64,4096]{1,0:T(8,128)(2,1)}, bf16[64,4096]{1,0:T(8,128)(2,1)S(1)}, u32[]{:S(2)}, u32[]{:S(2)}) collective-permute-start(bf16[64,4096]{1,0:T(8,128)(2,1)} %slice.63), channel_id=1, source_target_pairs={{0,1},{1,0},{2,3},{3,2},{4,5},{5,4},{6,7},{7,6},{8,9},{9,8},{10,11... | collective-permute-start | bytes 1572872 | tf_op jit(solution)/shard_map/ppermute | solution.py:78
  54.4 1.0 %copy-start.2 = (f32[64,4096]{1,0:T(8,128)}, f32[64,4096]{1,0:T(8,128)S(1)}, u32[]{:S(2)}) copy-start(f32[64,4096]{1,0:T(8,128)S(1)} %slice_add_fusion) | copy-start | bytes 3145732
  55.4 8.4 %collective-permute-start.6 = (bf16[32,4096]{1,0:T(8,128)(2,1)S(1)}, bf16[32,4096]{1,0:T(8,128)(2,1)S(1)}, u32[]{:S(2)}, u32[]{:S(2)}) collective-permute-start(bf16[32,4096]{1,0:T(8,128)(2,1)S(1)} %slice.64), channel_id=1, source_target_pairs={{0,2},{1,3},{2,0},{3,1},{4,6},{5,7},{6,4},{7,5},{8,10},{9,11},{10,... | collective-permute-start | bytes 786440 | tf_op jit(solution)/shard_map/ppermute | solution.py:78
  65.0 5.6 %collective-permute-start.7 = (bf16[8,4096]{1,0:T(8,128)(2,1)S(1)}, bf16[8,4096]{1,0:T(8,128)(2,1)S(1)}, u32[]{:S(2)}, u32[]{:S(2)}) collective-permute-start(bf16[8,4096]{1,0:T(8,128)(2,1)S(1)} %get-tuple-element.8), channel_id=1, source_target_pairs={{0,12},{1,13},{2,14},{3,15},{4,0},{5,1},{6,2},{7,3},{8,4},{9,5},{1... | collective-permute-start | bytes 196616 | tf_op jit(solution)/shard_map/ppermute | solution.py:72
  65.3 6.4 %collective-permute-start.9 = (bf16[8,4096]{1,0:T(8,128)(2,1)S(1)}, bf16[8,4096]{1,0:T(8,128)(2,1)S(1)}, u32[]{:S(2)}, u32[]{:S(2)}) collective-permute-start(bf16[8,4096]{1,0:T(8,128)(2,1)S(1)} %get-tuple-element.9), channel_id=1, source_target_pairs={{0,4},{1,5},{2,6},{3,7},{4,8},{5,9},{6,10},{7,11},{8,12},{9,13},{1... | collective-permute-start | bytes 196616 | tf_op jit(solution)/shard_map/ppermute | solution.py:72
  67.1 6.0 %collective-permute-start.8 = (bf16[8,4096]{1,0:T(8,128)(2,1)S(1)}, bf16[8,4096]{1,0:T(8,128)(2,1)S(1)}, u32[]{:S(2)}, u32[]{:S(2)}) collective-permute-start(bf16[8,4096]{1,0:T(8,128)(2,1)S(1)} %get-tuple-element.10), channel_id=1, source_target_pairs={{0,8},{1,9},{2,10},{3,11},{4,12},{5,13},{6,14},{7,15},{8,0},{9,1},... | collective-permute-start | bytes 196616 | tf_op jit(solution)/shard_map/ppermute | solution.py:72

commit v2 on v1

v2 whole, which is shorter than its diff:
```python
import functools

import jax
import jax.numpy as jnp
from jax import lax
from jax.experimental import pallas as pl
from jax.experimental.pallas import tpu as pltpu
from jax.sharding import PartitionSpec as P

HEADS = 32
KV_HEADS = 8
HEAD_DIM = 128
EXPERTS = 4
MIB = 1 << 20
F32 = jnp.float32
BF16 = jnp.bfloat16
VMEM = pl.BlockSpec(memory_space=pltpu.VMEM)
ANY = pl.BlockSpec(memory_space=pl.ANY)


def dot(a, b, contract_last=False):
    dims = (((1,), (1 if contract_last else 0,)), ((), ()))
    return lax.dot_general(a, b, dims, preferred_element_type=F32)


def attend_kernel(plane, *refs):
    sources, (attended, normed, share), held, semaphores = (
        refs[:10], refs[10:13], refs[13:23], refs[23]
    )
    copies = [
        pltpu.make_async_copy(source, target, semaphores.at[i])
        for i, (source, target) in enumerate(zip(sources, held))
    ]
    for copy in copies:
        copy.start()
    (queries, cache_keys, new_keys, lengths, cache_values, new_values, residual, gain, router,
     routes) = held
    for copy in copies:
        copy.wait()
    rows, width = queries.shape
    positions = cache_keys.shape[1]
    groups = HEADS // KV_HEADS
    scale = 1.0 / HEAD_DIM**0.5
    every = rows * positions
    block = groups * rows

    query = queries[...].astype(F32)
    stacked = jnp.concatenate(
        [query[:, h * HEAD_DIM : (h + 1) * HEAD_DIM] for h in range(HEADS)], axis=0
    )
    stacked_b = stacked.astype(BF16)
    keys = cache_keys[...].reshape(every, KV_HEADS * HEAD_DIM)
    values = cache_values[...].reshape(every, KV_HEADS * HEAD_DIM)
    newk = new_keys[...].astype(F32)
    newv = new_values[...].astype(F32)

    row_of = lax.broadcasted_iota(jnp.int32, (block, every), 0) % rows
    column = lax.broadcasted_iota(jnp.int32, (block, every), 1)
    position = column % positions
    column_row = column // positions
    limit = jnp.zeros((block, every), jnp.int32)
    for r in range(rows):
        limit = jnp.where(column_row == r, lengths[r], limit)
    valid = (row_of == column_row) & (position < limit)

    pieces = []
    for g in range(KV_HEADS):
        lanes = slice(g * HEAD_DIM, (g + 1) * HEAD_DIM)
        mine = slice(g * block, (g + 1) * block)
        scores = dot(stacked_b[mine], keys[:, lanes], contract_last=True) * scale
        scores = jnp.where(valid, scores, -jnp.inf)
        own_key = jnp.concatenate([newk[:, lanes]] * groups, axis=0)
        new_score = jnp.sum(stacked[mine] * own_key, axis=1, keepdims=True) * scale
        peak = jnp.maximum(jnp.max(scores, axis=1, keepdims=True), new_score)
        weights = jnp.exp(scores - peak)
        new_weight = jnp.exp(new_score - peak)
        total = jnp.sum(weights, axis=1, keepdims=True) + new_weight
        probs = (weights / total).astype(BF16)
        new_prob = (new_weight / total).astype(BF16).astype(F32)
        own_value = jnp.concatenate([newv[:, lanes]] * groups, axis=0)
        mixed = dot(probs, values[:, lanes]) + new_prob * own_value
        pieces += [mixed[j * rows : (j + 1) * rows] for j in range(groups)]

    states = (residual[...].astype(F32) + jnp.concatenate(pieces, axis=1)).astype(BF16)
    attended[...] = states
    states = states.astype(F32)
    norm = lax.rsqrt(jnp.mean(states * states, axis=1, keepdims=True) + 1e-05)
    gains = gain[...].astype(F32)
    logits = [jnp.zeros((rows, 128), F32) for _ in range(EXPERTS)]
    for c in range(width // 128):
        lanes = slice(c * 128, (c + 1) * 128)
        part = (states[:, lanes] * norm * gains[c : c + 1]).astype(BF16)
        normed[:, lanes] = part
        part = part.astype(F32)
        for e in range(EXPERTS):
            logits[e] += part * router[e : e + 1, lanes].astype(F32)
    logits = [jnp.sum(value, axis=1, keepdims=True) for value in logits]

    index = lax.axis_index("dp")
    base = index * rows
    row = lax.broadcasted_iota(jnp.int32, (rows, 1), 0)
    first = jnp.zeros((rows, 1), jnp.int32)
    second = jnp.zeros((rows, 1), jnp.int32)
    for r in range(rows):
        first = jnp.where(row == r, routes[0, base + r], first)
        second = jnp.where(row == r, routes[1, base + r], second)
    first_logit = jnp.zeros((rows, 1), F32)
    second_logit = jnp.zeros((rows, 1), F32)
    for e in range(EXPERTS):
        first_logit = jnp.where(first == e, logits[e], first_logit)
        second_logit = jnp.where(second == e, logits[e], second_logit)
    first_share = 1.0 / (1.0 + jnp.exp(second_logit - first_logit))
    second_share = 1.0 / (1.0 + jnp.exp(first_logit - second_logit))
    lane = lax.broadcasted_iota(jnp.int32, (rows, 128), 1)
    expert = (index // plane + lane) % EXPERTS
    expert = jnp.where(lane < EXPERTS, expert, -1)
    share[...] = jnp.where(first == expert, first_share, 0.0) + jnp.where(
        second == expert, second_share, 0.0
    )


def attend(plane, queries, new_keys, new_values, cache_keys, cache_values, lengths, residual,
           norm_gain, router_weight, routes):
    rows, width = queries.shape
    operands = (
        queries,
        cache_keys,
        new_keys,
        lengths,
        cache_values,
        new_values,
        residual,
        norm_gain.reshape(-1, 128),
        router_weight.T,
        routes.T,
    )
    in_smem = (3, 9)
    return pl.pallas_call(
        functools.partial(attend_kernel, plane),
        out_shape=(
            jax.ShapeDtypeStruct((rows, width), BF16),
            jax.ShapeDtypeStruct((rows, width), BF16),
            jax.ShapeDtypeStruct((rows, 128), F32),
        ),
        in_specs=[ANY] * len(operands),
        out_specs=(VMEM, VMEM, VMEM),
        scratch_shapes=[
            (pltpu.SMEM if i in in_smem else pltpu.VMEM)(operand.shape, operand.dtype)
            for i, operand in enumerate(operands)
        ]
        + [pltpu.SemaphoreType.DMA((len(operands),))],
        compiler_params=pltpu.CompilerParams(vmem_limit_bytes=5 * MIB),
        name="attend",
    )(*[pltpu.with_memory_space_constraint(operand, pltpu.HBM) for operand in operands])


def expert_kernel(inputs, gate_weight, up_weight, down_weight, keep, send, hidden):
    columns = gate_weight.shape[1]
    width = down_weight.shape[1]
    half = keep.shape[0]
    step = 256 if columns % 256 == 0 else columns
    x = inputs[...]
    for f in range(0, columns, step):
        gate = dot(x, gate_weight[:, f : f + step])
        upper = dot(x, up_weight[:, f : f + step])
        hidden[:, f : f + step] = (gate / (1.0 + jnp.exp(-gate)) * upper).astype(BF16)
    h = hidden[...]
    for n in range(0, width, 512):
        terms = dot(h, down_weight[:, n : n + 512])
        keep[:, n : n + 512] = terms[:half]
        send[:, n : n + 512] = terms[half:].astype(BF16)


def expert_rows(inputs, gate_weight, up_weight, down_weight):
    rows, width = inputs.shape
    columns = gate_weight.shape[1]
    half = rows // 2
    return pl.pallas_call(
        expert_kernel,
        out_shape=(
            jax.ShapeDtypeStruct((half, width), F32),
            jax.ShapeDtypeStruct((half, width), BF16),
        ),
        in_specs=[VMEM] * 4,
        out_specs=(VMEM, VMEM),
        scratch_shapes=[pltpu.VMEM((rows, columns), BF16)],
        compiler_params=pltpu.CompilerParams(vmem_limit_bytes=4 * MIB * max(1, rows // 128)),
        cost_estimate=pl.CostEstimate(
            flops=6 * rows * width * columns, bytes_accessed=0, transcendentals=rows * columns
        ),
        name="experts",
    )(inputs, gate_weight, up_weight, down_weight)


def load_kernel(source, after, target, token, semaphore):
    copy = pltpu.make_async_copy(source, target, semaphore)
    copy.start()
    token[...] = jnp.zeros(token.shape, token.dtype)
    copy.wait()


def load(source, after):
    return pl.pallas_call(
        load_kernel,
        out_shape=(
            pltpu.VMEM(source.shape, source.dtype),
            jax.ShapeDtypeStruct((8, 128), F32),
        ),
        in_specs=[ANY, ANY],
        out_specs=(VMEM, VMEM),
        scratch_shapes=[pltpu.SemaphoreType.DMA],
        compiler_params=pltpu.CompilerParams(vmem_limit_bytes=MIB),
        cost_estimate=pl.CostEstimate(
            flops=0, bytes_accessed=2 * source.size, transcendentals=0
        ),
        name="load",
    )(pltpu.with_memory_space_constraint(source, pltpu.HBM), after)


def join_kernel(*refs):
    out, row = refs[-1], 0
    for piece in refs[1:-1]:
        out[row : row + piece.shape[0]] = piece[...]
        row += piece.shape[0]


def join(after, *pieces):
    rows = sum(piece.shape[0] for piece in pieces)
    return pl.pallas_call(
        join_kernel,
        out_shape=jax.ShapeDtypeStruct((rows, pieces[0].shape[1]), BF16),
        in_specs=[ANY] + [VMEM] * len(pieces),
        out_specs=VMEM,
        compiler_params=pltpu.CompilerParams(vmem_limit_bytes=1 * MIB),
        name="join",
    )(after, *pieces)


def fold_kernel(held, arrived, keep, send):
    half = keep.shape[0]
    keep[...] = held[:half] + arrived[:half].astype(F32)
    send[...] = (held[half:] + arrived[half:].astype(F32)).astype(BF16)


def fold(held, arrived):
    half, width = held.shape[0] // 2, held.shape[1]
    return pl.pallas_call(
        fold_kernel,
        out_shape=(
            jax.ShapeDtypeStruct((half, width), F32),
            jax.ShapeDtypeStruct((half, width), BF16),
        ),
        in_specs=[VMEM] * 2,
        out_specs=(VMEM, VMEM),
        compiler_params=pltpu.CompilerParams(vmem_limit_bytes=4 * MIB * max(1, half // 32)),
        name="fold",
    )(held, arrived)


def last_fold_kernel(held, arrived, *outs):
    rows = outs[0].shape[0]
    for k, out in enumerate(outs):
        block = slice(k * rows, (k + 1) * rows)
        out[...] = (held[block] + arrived[block].astype(F32)).astype(BF16)


def last_fold(held, arrived):
    rows, width = held.shape[0] // EXPERTS, held.shape[1]
    return pl.pallas_call(
        last_fold_kernel,
        out_shape=(jax.ShapeDtypeStruct((rows, width), BF16),) * EXPERTS,
        in_specs=[VMEM] * 2,
        out_specs=(VMEM,) * EXPERTS,
        compiler_params=pltpu.CompilerParams(vmem_limit_bytes=4 * MIB),
        name="last_fold",
    )(held, arrived)


def combine_kernel(share, *refs):
    results, out = refs[:-1], refs[-1]
    total = jnp.zeros(out.shape, F32)
    for k, result in enumerate(results):
        total = total + share[:, k : k + 1] * result[...].astype(F32)
    out[...] = total.astype(BF16)


def combine(share, results):
    return pl.pallas_call(
        combine_kernel,
        out_shape=jax.ShapeDtypeStruct(results[0].shape, BF16),
        in_specs=[VMEM] * (1 + EXPERTS),
        out_specs=VMEM,
        compiler_params=pltpu.CompilerParams(vmem_limit_bytes=4 * MIB),
        name="combine",
    )(share, *results)


def plane_shift(value, count, offset):
    plane = count // EXPERTS
    return lax.ppermute(
        value, "dp", [(i, (i + offset * plane) % count) for i in range(count)]
    )


def swap(value, count, bit):
    return lax.ppermute(value, "dp", [(i, i ^ bit) for i in range(count)])


def body(
    queries,
    new_keys,
    new_values,
    cache_keys,
    cache_values,
    lengths,
    residual,
    norm_gain,
    router_weight,
    gate_weight,
    up_weight,
    down_weight,
    routes,
):
    count = lax.axis_size("dp")
    plane = count // EXPERTS
    bits = [1 << k for k in reversed(range(plane.bit_length() - 1))]
    attended, normed, share = attend(
        plane, queries, new_keys, new_values, cache_keys, cache_values, lengths, residual,
        norm_gain, router_weight, routes,
    )

    gate, token = load(gate_weight, normed)
    gathered = join(token, normed, *[plane_shift(normed, count, k) for k in range(1, EXPERTS)])
    up, token = load(up_weight, gathered)
    gathered = join(token, gathered, swap(gathered, count, bits[0]))
    down, token = load(down_weight, gathered)
    for bit in bits[1:]:
        gathered = join(token, gathered, swap(gathered, count, bit))

    held, send = expert_rows(gathered, gate, up, down)
    for bit in bits[:0:-1]:
        held, send = fold(held, swap(send, count, bit))
    terms = last_fold(held, swap(send, count, bits[0]))
    results = [terms[0]] + [plane_shift(terms[k], count, -k) for k in range(1, EXPERTS)]
    return (attended, combine(share, results))


def solution(mesh):
    placed = (
        P(("group", "dp"), None),
        P(("group", "dp"), None),
        P(("group", "dp"), None),
        P(("group", "dp"), None, None),
        P(("group", "dp"), None, None),
        P(("group", "dp")),
        P(("group", "dp"), None),
        P(),
        P(),
        P(None, "dp"),
        P(None, "dp"),
        P("dp", None),
        P("group", None),
    )
    return jax.shard_map(
        body,
        mesh=mesh,
        in_specs=placed,
        out_specs=(P(("group", "dp"), None), P(("group", "dp"), None)),
        check_vma=False,
    )
```

time: 74.2 us -> 57.5 us (0.77)
  Pallas kernels: 0 us -> 27.3 us
  matrix products: 25.2 us -> 0 us
  waiting for transfers between devices: 26 us -> 15.9 us
  other arithmetic: 5.54 us -> 0 us
  local copies, waits for them, and re-layouts: 3.13 us -> 0 us
    pallas_call x0 -> x11, Pallas kernels: none -> 27.3 us  [the longest x3 15.5 us: load(): pl.pallas_call(load_kernel, out_shape=(pltpu.VMEM(source.shape, source.dt...]
    dot_general x6 -> x0, matrix products: 25.2 us -> none  [the longest x1 14.1 us: expert_rows(): return jnp.dot(hidden, down_weight, preferred_element_type=jnp.float32)]
    ppermute x4, waiting for transfers between devices: 16 us -> 9.92 us  [swap(): return lax.ppermute(value, 'dp', [(i, i ^ bit) for i in range(count)])]
    ppermute x6, waiting for transfers between devices: 10 us -> 5.96 us  [plane_shift(): lax.ppermute(value, 'dp', [(i, (i + offset * plane) % count) for i in ran...]
    convert_element_type x3 -> x0, other arithmetic: 2.53 us -> none  [the longest x1 1.09 us: body(): terms = terms.astype(jnp.bfloat16).reshape(EXPERTS, rows, D)]
    unnamed x16 -> x0, local copies, waits for them, and re-layouts: 2.01 us -> none
    reduce_sum x2 -> x0, other arithmetic: 1.26 us -> none  [the longest x1 0.99 us: attend(): jnp.mean(states * states, axis=-1, keepdims=True) + 1e-05]
    slice x3 -> x0, local copies, waits for them, and re-layouts: 0.89 us -> none  [the longest x2 0.87 us: body(): other = swap(terms[half:].astype(jnp.bfloat16), count, bit)]
  transfers between devices with their start and end apart: 10 -> 10, of which waited for: 9 -> 6; matrix products, arithmetic and copies ran while one was open for 2% -> 0% of each run, Pallas kernels for 0% -> 27%
where the time goes in v2:
time: 57.5 us; the launch traced here: 57.3 us
  Pallas kernels  27.3 us (47%)
  waiting for transfers between devices  15.9 us (28%)
  starting transfers between devices  13.4 us (23%)
  between operations  0.73 us (1%)
    pallas_call x3, Pallas kernels, load(): pl.pallas_call(load_kernel, out_shape=(pltpu.VMEM(source.shape, source.dt...  15.5 us
    ppermute x4, waiting for transfers between devices, swap(): return lax.ppermute(value, 'dp', [(i, i ^ bit) for i in range(count)])  9.92 us
    ppermute x6, starting transfers between devices, plane_shift(): lax.ppermute(value, 'dp', [(i, (i + offset * plane) % count) for i in ran...  9.62 us
    pallas_call x1, Pallas kernels, expert_rows(): pl.pallas_call(expert_kernel, out_shape=(jax.ShapeDtypeStruct((half, widt...  6.03 us
    ppermute x6, waiting for transfers between devices, plane_shift(): lax.ppermute(value, 'dp', [(i, (i + offset * plane) % count) for i in ran...  5.96 us
    pallas_call x1, Pallas kernels, attend(): pl.pallas_call(functools.partial(attend_kernel, plane), out_shape=(jax.Sh...  4.68 us
    ppermute x4, starting transfers between devices, swap(): return lax.ppermute(value, 'dp', [(i, i ^ bit) for i in range(count)])  3.82 us
  transfers between devices with their start and end apart: 10, of which 6 were waited for; matrix products, arithmetic and copies ran while one was open for 0% of the time, Pallas kernels for 27%

profile of v2, /device:TPU:0, one launch (start us, length us, event | category | flops | bytes accessed | tf_op | source)
XLA Modules:
  0.0 57.3 jit_solution(3804161231337478064)
XLA Ops:
  0.6 4.7 %attend.1 = (bf16[8,4096]{1,0:T(8,128)(2,1)}, bf16[8,4096]{1,0:T(8,128)(2,1)S(1)}, f32[8,128]{1,0:T(8,128)S(1)}) custom-call(bf16[8,4096]{1,0:T(8,128)(2,1)} %refs_0_.1, bf16[8,32,1024]{2,1,0:T(8,128)(2,1)} %refs_1_.1, bf16[8,1024]{1,0:T(8,128)(2,1)} %refs_2_.1, s32[8]{0:T(128)} %refs_3_.1, bf16[8,32,1024]{2,1,0:T(8,128)(2,1)} %refs_4_.1, ...), custom_call_target="tpu_custom_call" | custom-call | tf_op jit(solution)/shard_map/attend/pallas_call | solution.py:138
  5.3 5.1 %collective-permute-start.2 = (bf16[8,4096]{1,0:T(8,128)(2,1)S(1)}, bf16[8,4096]{1,0:T(8,128)(2,1)S(1)}, u32[]{:S(2)}, u32[]{:S(2)}) collective-permute-start(bf16[8,4096]{1,0:T(8,128)(2,1)S(1)} %get-tuple-element.21.after.refs_1_), channel_id=1, source_target_pairs={{0,12},{1,13},{2,14},{3,15},{4,0},{5,1},{6,2},{7,3},{8,4},{9,5},{1... | collective-permute-start | bytes 196616 | tf_op jit(solution)/shard_map/ppermute | solution.py:300
  10.4 0.0 collective-permute-start.1
  10.4 1.0 %collective-permute-start = (bf16[8,4096]{1,0:T(8,128)(2,1)S(1)}, bf16[8,4096]{1,0:T(8,128)(2,1)S(1)}, u32[]{:S(2)}, u32[]{:S(2)}) collective-permute-start(bf16[8,4096]{1,0:T(8,128)(2,1)S(1)} %get-tuple-element.21.after.refs_1_), channel_id=1, source_target_pairs={{0,4},{1,5},{2,6},{3,7},{4,8},{5,9},{6,10},{7,11},{8,12},{9,13},{1... | collective-permute-start | bytes 196616 | tf_op jit(solution)/shard_map/ppermute | solution.py:300
  11.4 5.2 %load.3 = (bf16[4096,1792]{1,0:T(8,128)(2,1)S(1)}, f32[8,128]{1,0:T(8,128)S(1)}) custom-call(bf16[4096,1792]{1,0:T(8,128)(2,1)} %source.3, bf16[8,4096]{1,0:T(8,128)(2,1)S(1)} %get-tuple-element.21.after.refs_1_), custom_call_target="tpu_custom_call" | custom-call | bytes 14680064 | tf_op jit(solution)/shard_map/load/pallas_call | solution.py:203
  16.6 0.0 collective-permute-done.2.refs_4_
  16.6 0.3 collective-permute-done.1.refs_3_
  16.9 0.0 collective-permute-done.refs_2_
  16.9 1.6 %collective-permute-start.3 = (bf16[32,4096]{1,0:T(8,128)(2,1)S(1)}, bf16[32,4096]{1,0:T(8,128)(2,1)S(1)}, u32[]{:S(2)}, u32[]{:S(2)}) collective-permute-start(bf16[32,4096]{1,0:T(8,128)(2,1)S(1)} %join.3.after.refs_1_), channel_id=1, source_target_pairs={{0,2},{1,3},{2,0},{3,1},{4,6},{5,7},{6,4},{7,5},{8,10},{9,11},{10,... | collective-permute-start | bytes 786440 | tf_op jit(solution)/shard_map/ppermute | solution.py:306
  18.5 5.2 %load.4 = (bf16[4096,1792]{1,0:T(8,128)(2,1)S(1)}, f32[8,128]{1,0:T(8,128)S(1)}) custom-call(bf16[4096,1792]{1,0:T(8,128)(2,1)} %source.4, bf16[32,4096]{1,0:T(8,128)(2,1)S(1)} %join.3.after.refs_1_), custom_call_target="tpu_custom_call" | custom-call | bytes 14680064 | tf_op jit(solution)/shard_map/load/pallas_call | solution.py:203
  23.7 1.3 %collective-permute-done.3.refs_2_ = bf16[32,4096]{1,0:T(8,128)(2,1)S(1)} collective-permute-done((bf16[32,4096]{1,0:T(8,128)(2,1)S(1)}, bf16[32,4096]{1,0:T(8,128)(2,1)S(1)}, u32[]{:S(2)}, u32[]{:S(2)}) %collective-permute-start.3) | collective-permute-done | bytes 262176 | tf_op jit(solution)/shard_map/ppermute | solution.py:306
  25.1 0.1 collective-permute-start.4
  25.1 5.2 %load.5 = (bf16[1792,4096]{1,0:T(8,128)(2,1)S(1)}, f32[8,128]{1,0:T(8,128)S(1)}) custom-call(bf16[1792,4096]{1,0:T(8,128)(2,1)} %source.5, bf16[64,4096]{1,0:T(8,128)(2,1)S(1)} %join.4.after.refs_1_), custom_call_target="tpu_custom_call" | custom-call | bytes 14680064 | tf_op jit(solution)/shard_map/load/pallas_call | solution.py:203
  30.3 0.0 collective-permute-done.4.refs_2_
  30.3 0.1 join.5.inputs
  30.4 6.0 %experts.1 = (f32[64,4096]{1,0:T(8,128)S(1)}, bf16[64,4096]{1,0:T(8,128)(2,1)S(1)}) custom-call(bf16[128,4096]{1,0:T(8,128)(2,1)S(1)} %join.5.inputs, bf16[4096,1792]{1,0:T(8,128)(2,1)S(1)} %get-tuple-element.25.gate_weight, bf16[4096,1792]{1,0:T(8,128)(2,1)S(1)} %get-tuple-element.26.up_weight, bf16[1792,4096]{1,0:T(8,128)(2,1)S(1)} %get-tuple-element.27.down_weight), custom_call_target="tpu_custom_call" | custom-call | flops 5637144576 | tf_op jit(solution)/shard_map/experts/pallas_call | solution.py:178
  36.5 0.6 collective-permute-start.5
  37.0 1.5 %collective-permute-done.5.arrived = bf16[64,4096]{1,0:T(8,128)(2,1)S(1)} collective-permute-done((bf16[64,4096]{1,0:T(8,128)(2,1)S(1)}, bf16[64,4096]{1,0:T(8,128)(2,1)S(1)}, u32[]{:S(2)}, u32[]{:S(2)}) %collective-permute-start.5) | collective-permute-done | bytes 524320 | tf_op jit(solution)/shard_map/ppermute | solution.py:306
  38.6 0.1 fold.1
  38.6 1.6 %collective-permute-start.6 = (bf16[32,4096]{1,0:T(8,128)(2,1)S(1)}, bf16[32,4096]{1,0:T(8,128)(2,1)S(1)}, u32[]{:S(2)}, u32[]{:S(2)}) collective-permute-start(bf16[32,4096]{1,0:T(8,128)(2,1)S(1)} %get-tuple-element.31), channel_id=1, source_target_pairs={{0,2},{1,3},{2,0},{3,1},{4,6},{5,7},{6,4},{7,5},{8,10},{9,11},{10,... | collective-permute-start | bytes 786440 | tf_op jit(solution)/shard_map/ppermute | solution.py:306
  40.2 7.0 %collective-permute-done.6.arrived = bf16[32,4096]{1,0:T(8,128)(2,1)S(1)} collective-permute-done((bf16[32,4096]{1,0:T(8,128)(2,1)S(1)}, bf16[32,4096]{1,0:T(8,128)(2,1)S(1)}, u32[]{:S(2)}, u32[]{:S(2)}) %collective-permute-start.6) | collective-permute-done | bytes 262176 | tf_op jit(solution)/shard_map/ppermute | solution.py:306
  47.3 2.1 %collective-permute-start.7 = (bf16[8,4096]{1,0:T(8,128)(2,1)S(1)}, bf16[8,4096]{1,0:T(8,128)(2,1)S(1)}, u32[]{:S(2)}, u32[]{:S(2)}) collective-permute-start(bf16[8,4096]{1,0:T(8,128)(2,1)S(1)} %get-tuple-element.33), channel_id=1, source_target_pairs={{0,12},{1,13},{2,14},{3,15},{4,0},{5,1},{6,2},{7,3},{8,4},{9,5},{1... | collective-permute-start | bytes 196616 | tf_op jit(solution)/shard_map/ppermute | solution.py:300
  49.4 0.8 %collective-permute-start.8 = (bf16[8,4096]{1,0:T(8,128)(2,1)S(1)}, bf16[8,4096]{1,0:T(8,128)(2,1)S(1)}, u32[]{:S(2)}, u32[]{:S(2)}) collective-permute-start(bf16[8,4096]{1,0:T(8,128)(2,1)S(1)} %get-tuple-element.34), channel_id=1, source_target_pairs={{0,8},{1,9},{2,10},{3,11},{4,12},{5,13},{6,14},{7,15},{8,0},{9,1},... | collective-permute-start | bytes 196616 | tf_op jit(solution)/shard_map/ppermute | solution.py:300
  50.3 0.6 %collective-permute-start.9 = (bf16[8,4096]{1,0:T(8,128)(2,1)S(1)}, bf16[8,4096]{1,0:T(8,128)(2,1)S(1)}, u32[]{:S(2)}, u32[]{:S(2)}) collective-permute-start(bf16[8,4096]{1,0:T(8,128)(2,1)S(1)} %get-tuple-element.35), channel_id=1, source_target_pairs={{0,4},{1,5},{2,6},{3,7},{4,8},{5,9},{6,10},{7,11},{8,12},{9,13},{1... | collective-permute-start | bytes 196616 | tf_op jit(solution)/shard_map/ppermute | solution.py:300
  50.9 1.1 %collective-permute-done.7.refs_1_ = bf16[8,4096]{1,0:T(8,128)(2,1)S(1)} collective-permute-done((bf16[8,4096]{1,0:T(8,128)(2,1)S(1)}, bf16[8,4096]{1,0:T(8,128)(2,1)S(1)}, u32[]{:S(2)}, u32[]{:S(2)}) %collective-permute-start.7) | collective-permute-done | bytes 65568 | tf_op jit(solution)/shard_map/ppermute | solution.py:300
  52.0 4.6 %collective-permute-done.8.refs_2_ = bf16[8,4096]{1,0:T(8,128)(2,1)S(1)} collective-permute-done((bf16[8,4096]{1,0:T(8,128)(2,1)S(1)}, bf16[8,4096]{1,0:T(8,128)(2,1)S(1)}, u32[]{:S(2)}, u32[]{:S(2)}) %collective-permute-start.8) | collective-permute-done | bytes 65568 | tf_op jit(solution)/shard_map/ppermute | solution.py:300
  56.5 0.0 collective-permute-done.9.refs_3_
  56.5 0.7 %combine.1 = bf16[8,4096]{1,0:T(8,128)(2,1)} custom-call(f32[8,128]{1,0:T(8,128)S(1)} %get-tuple-element.20.share, bf16[8,4096]{1,0:T(8,128)(2,1)S(1)} %get-tuple-element.32.refs_0_, bf16[8,4096]{1,0:T(8,128)(2,1)S(1)} %collective-permute-done.7.refs_1_, bf16[8,4096]{1,0:T(8,128)(2,1)S(1)} %collective-permute-done.8.refs_2_, ...), custom_call_target="tpu_custom_call" | custom-call | tf_op jit(solution)/shard_map/combine/pallas_call | solution.py:288
  (3 shorter events, 0.1 us)
Async XLA Ops:
  5.3 11.3 %collective-permute-start.2 = (bf16[8,4096]{1,0:T(8,128)(2,1)S(1)}, bf16[8,4096]{1,0:T(8,128)(2,1)S(1)}, u32[]{:S(2)}, u32[]{:S(2)}) collective-permute-start(bf16[8,4096]{1,0:T(8,128)(2,1)S(1)} %get-tuple-element.21.after.refs_1_), channel_id=1, source_target_pairs={{0,12},{1,13},{2,14},{3,15},{4,0},{5,1},{6,2},{7,3},{8,4},{9,5},{1... | collective-permute-start | bytes 196616 | tf_op jit(solution)/shard_map/ppermute | solution.py:300
  10.4 6.5 %collective-permute-start.1 = (bf16[8,4096]{1,0:T(8,128)(2,1)S(1)}, bf16[8,4096]{1,0:T(8,128)(2,1)S(1)}, u32[]{:S(2)}, u32[]{:S(2)}) collective-permute-start(bf16[8,4096]{1,0:T(8,128)(2,1)S(1)} %get-tuple-element.21.after.refs_1_), channel_id=1, source_target_pairs={{0,8},{1,9},{2,10},{3,11},{4,12},{5,13},{6,14},{7,15},{8,0},{9,1},... | collective-permute-start | bytes 196616 | tf_op jit(solution)/shard_map/ppermute | solution.py:300
  10.4 6.5 %collective-permute-start = (bf16[8,4096]{1,0:T(8,128)(2,1)S(1)}, bf16[8,4096]{1,0:T(8,128)(2,1)S(1)}, u32[]{:S(2)}, u32[]{:S(2)}) collective-permute-start(bf16[8,4096]{1,0:T(8,128)(2,1)S(1)} %get-tuple-element.21.after.refs_1_), channel_id=1, source_target_pairs={{0,4},{1,5},{2,6},{3,7},{4,8},{5,9},{6,10},{7,11},{8,12},{9,13},{1... | collective-permute-start | bytes 196616 | tf_op jit(solution)/shard_map/ppermute | solution.py:300
  16.9 8.1 %collective-permute-start.3 = (bf16[32,4096]{1,0:T(8,128)(2,1)S(1)}, bf16[32,4096]{1,0:T(8,128)(2,1)S(1)}, u32[]{:S(2)}, u32[]{:S(2)}) collective-permute-start(bf16[32,4096]{1,0:T(8,128)(2,1)S(1)} %join.3.after.refs_1_), channel_id=1, source_target_pairs={{0,2},{1,3},{2,0},{3,1},{4,6},{5,7},{6,4},{7,5},{8,10},{9,11},{10,... | collective-permute-start | bytes 786440 | tf_op jit(solution)/shard_map/ppermute | solution.py:306
  25.1 5.3 %collective-permute-start.4 = (bf16[64,4096]{1,0:T(8,128)(2,1)S(1)}, bf16[64,4096]{1,0:T(8,128)(2,1)S(1)}, u32[]{:S(2)}, u32[]{:S(2)}) collective-permute-start(bf16[64,4096]{1,0:T(8,128)(2,1)S(1)} %join.4.after.refs_1_), channel_id=1, source_target_pairs={{0,1},{1,0},{2,3},{3,2},{4,5},{5,4},{6,7},{7,6},{8,9},{9,8},{10,11... | collective-permute-start | bytes 1572872 | tf_op jit(solution)/shard_map/ppermute | solution.py:306
  36.5 2.1 %collective-permute-start.5 = (bf16[64,4096]{1,0:T(8,128)(2,1)S(1)}, bf16[64,4096]{1,0:T(8,128)(2,1)S(1)}, u32[]{:S(2)}, u32[]{:S(2)}) collective-permute-start(bf16[64,4096]{1,0:T(8,128)(2,1)S(1)} %get-tuple-element.29), channel_id=1, source_target_pairs={{0,1},{1,0},{2,3},{3,2},{4,5},{5,4},{6,7},{7,6},{8,9},{9,8},{10,11... | collective-permute-start | bytes 1572872 | tf_op jit(solution)/shard_map/ppermute | solution.py:306
  38.6 8.7 %collective-permute-start.6 = (bf16[32,4096]{1,0:T(8,128)(2,1)S(1)}, bf16[32,4096]{1,0:T(8,128)(2,1)S(1)}, u32[]{:S(2)}, u32[]{:S(2)}) collective-permute-start(bf16[32,4096]{1,0:T(8,128)(2,1)S(1)} %get-tuple-element.31), channel_id=1, source_target_pairs={{0,2},{1,3},{2,0},{3,1},{4,6},{5,7},{6,4},{7,5},{8,10},{9,11},{10,... | collective-permute-start | bytes 786440 | tf_op jit(solution)/shard_map/ppermute | solution.py:306
  47.3 4.6 %collective-permute-start.7 = (bf16[8,4096]{1,0:T(8,128)(2,1)S(1)}, bf16[8,4096]{1,0:T(8,128)(2,1)S(1)}, u32[]{:S(2)}, u32[]{:S(2)}) collective-permute-start(bf16[8,4096]{1,0:T(8,128)(2,1)S(1)} %get-tuple-element.33), channel_id=1, source_target_pairs={{0,12},{1,13},{2,14},{3,15},{4,0},{5,1},{6,2},{7,3},{8,4},{9,5},{1... | collective-permute-start | bytes 196616 | tf_op jit(solution)/shard_map/ppermute | solution.py:300
  49.4 7.1 %collective-permute-start.8 = (bf16[8,4096]{1,0:T(8,128)(2,1)S(1)}, bf16[8,4096]{1,0:T(8,128)(2,1)S(1)}, u32[]{:S(2)}, u32[]{:S(2)}) collective-permute-start(bf16[8,4096]{1,0:T(8,128)(2,1)S(1)} %get-tuple-element.34), channel_id=1, source_target_pairs={{0,8},{1,9},{2,10},{3,11},{4,12},{5,13},{6,14},{7,15},{8,0},{9,1},... | collective-permute-start | bytes 196616 | tf_op jit(solution)/shard_map/ppermute | solution.py:300
  50.3 6.3 %collective-permute-start.9 = (bf16[8,4096]{1,0:T(8,128)(2,1)S(1)}, bf16[8,4096]{1,0:T(8,128)(2,1)S(1)}, u32[]{:S(2)}, u32[]{:S(2)}) collective-permute-start(bf16[8,4096]{1,0:T(8,128)(2,1)S(1)} %get-tuple-element.35), channel_id=1, source_target_pairs={{0,4},{1,5},{2,6},{3,7},{4,8},{5,9},{6,10},{7,11},{8,12},{9,13},{1... | collective-permute-start | bytes 196616 | tf_op jit(solution)/shard_map/ppermute | solution.py:300

commit v3 on v2

--- a/solution.py
+++ b/solution.py
@@ -12,6 +12,8 @@
 HEAD_DIM = 128
 EXPERTS = 4
 MIB = 1 << 20
+WAYS = 4
+PARTS = 2
 F32 = jnp.float32
 BF16 = jnp.bfloat16
 VMEM = pl.BlockSpec(memory_space=pltpu.VMEM)
@@ -23,15 +25,26 @@
     return lax.dot_general(a, b, dims, preferred_element_type=F32)
 
 
+def weight_copies(source, target, semaphores):
+    step = source.shape[0] // WAYS
+    return [
+        pltpu.make_async_copy(
+            source.at[pl.ds(i * step, step)], target.at[pl.ds(i * step, step)], semaphores.at[i]
+        )
+        for i in range(WAYS)
+    ]
+
+
 def attend_kernel(plane, *refs):
     sources, (attended, normed, share), held, semaphores = (
-        refs[:10], refs[10:13], refs[13:23], refs[23]
-    )
+        refs[:10], refs[11:14], refs[15:25], refs[25]
+    )
+    weight = weight_copies(refs[10], refs[14], refs[26])
     copies = [
         pltpu.make_async_copy(source, target, semaphores.at[i])
         for i, (source, target) in enumerate(zip(sources, held))
     ]
-    for copy in copies:
+    for copy in copies + weight:
         copy.start()
     (queries, cache_keys, new_keys, lengths, cache_values, new_values, residual, gain, router,
      routes) = held
@@ -117,10 +130,12 @@
     share[...] = jnp.where(first == expert, first_share, 0.0) + jnp.where(
         second == expert, second_share, 0.0
     )
+    for copy in weight:
+        copy.wait()
 
 
 def attend(plane, queries, new_keys, new_values, cache_keys, cache_values, lengths, residual,
-           norm_gain, router_weight, routes):
+           norm_gain, router_weight, routes, weight):
     rows, width = queries.shape
     operands = (
         queries,
@@ -141,62 +156,81 @@
             jax.ShapeDtypeStruct((rows, width), BF16),
             jax.ShapeDtypeStruct((rows, width), BF16),
             jax.ShapeDtypeStruct((rows, 128), F32),
-        ),
-        in_specs=[ANY] * len(operands),
-        out_specs=(VMEM, VMEM, VMEM),
+            pltpu.VMEM(weight.shape, weight.dtype),
+        ),
+        in_specs=[ANY] * (len(operands) + 1),
+        out_specs=(VMEM,) * 4,
         scratch_shapes=[
             (pltpu.SMEM if i in in_smem else pltpu.VMEM)(operand.shape, operand.dtype)
             for i, operand in enumerate(operands)
         ]
-        + [pltpu.SemaphoreType.DMA((len(operands),))],
+        + [pltpu.SemaphoreType.DMA((len(operands),)), pltpu.SemaphoreType.DMA((WAYS,))],
         compiler_params=pltpu.CompilerParams(vmem_limit_bytes=5 * MIB),
         name="attend",
-    )(*[pltpu.with_memory_space_constraint(operand, pltpu.HBM) for operand in operands])
-
-
-def expert_kernel(inputs, gate_weight, up_weight, down_weight, keep, send, hidden):
+    )(*[pltpu.with_memory_space_constraint(x, pltpu.HBM) for x in (*operands, weight)])
+
+
+def hidden_kernel(inputs, gate_weight, up_weight, hidden):
     columns = gate_weight.shape[1]
-    width = down_weight.shape[1]
-    half = keep.shape[0]
     step = 256 if columns % 256 == 0 else columns
     x = inputs[...]
     for f in range(0, columns, step):
         gate = dot(x, gate_weight[:, f : f + step])
         upper = dot(x, up_weight[:, f : f + step])
         hidden[:, f : f + step] = (gate / (1.0 + jnp.exp(-gate)) * upper).astype(BF16)
+
+
+def hidden_rows(inputs, gate_weight, up_weight):
+    rows, width = inputs.shape
+    columns = gate_weight.shape[1]
+    return pl.pallas_call(
+        hidden_kernel,
+        out_shape=jax.ShapeDtypeStruct((rows, columns), BF16),
+        in_specs=[VMEM] * 3,
+        out_specs=VMEM,
+        compiler_params=pltpu.CompilerParams(vmem_limit_bytes=4 * MIB * max(1, rows // 128)),
+        cost_estimate=pl.CostEstimate(
+            flops=4 * rows * width * columns, bytes_accessed=0, transcendentals=rows * columns
+        ),
+        name="hidden",
+    )(inputs, gate_weight, up_weight)
+
+
+def down_kernel(first, hidden, down_weight, keep, send):
+    half, width = keep.shape
     h = hidden[...]
     for n in range(0, width, 512):
-        terms = dot(h, down_weight[:, n : n + 512])
+        terms = dot(h, down_weight[:, first + n : first + n + 512])
         keep[:, n : n + 512] = terms[:half]
         send[:, n : n + 512] = terms[half:].astype(BF16)
 
 
-def expert_rows(inputs, gate_weight, up_weight, down_weight):
-    rows, width = inputs.shape
-    columns = gate_weight.shape[1]
-    half = rows // 2
-    return pl.pallas_call(
-        expert_kernel,
+def down_rows(hidden, down_weight, part):
+    rows, columns = hidden.shape
+    half, width = rows // 2, down_weight.shape[1] // PARTS
+    return pl.pallas_call(
+        functools.partial(down_kernel, part * width),
         out_shape=(
             jax.ShapeDtypeStruct((half, width), F32),
             jax.ShapeDtypeStruct((half, width), BF16),
         ),
-        in_specs=[VMEM] * 4,
+        in_specs=[VMEM] * 2,
         out_specs=(VMEM, VMEM),
-        scratch_shapes=[pltpu.VMEM((rows, columns), BF16)],
         compiler_params=pltpu.CompilerParams(vmem_limit_bytes=4 * MIB * max(1, rows // 128)),
         cost_estimate=pl.CostEstimate(
-            flops=6 * rows * width * columns, bytes_accessed=0, transcendentals=rows * columns
-        ),
-        name="experts",
-    )(inputs, gate_weight, up_weight, down_weight)
-
-
-def load_kernel(source, after, target, token, semaphore):
-    copy = pltpu.make_async_copy(source, target, semaphore)
-    copy.start()
+            flops=2 * rows * width * columns, bytes_accessed=0, transcendentals=0
+        ),
+        name="down",
+    )(hidden, down_weight)
+
+
+def load_kernel(source, after, target, token, semaphores):
+    copies = weight_copies(source, target, semaphores)
+    for copy in copies:
+        copy.start()
     token[...] = jnp.zeros(token.shape, token.dtype)
-    copy.wait()
+    for copy in copies:
+        copy.wait()
 
 
 def load(source, after):
@@ -208,7 +242,7 @@
         ),
         in_specs=[ANY, ANY],
         out_specs=(VMEM, VMEM),
-        scratch_shapes=[pltpu.SemaphoreType.DMA],
+        scratch_shapes=[pltpu.SemaphoreType.DMA((WAYS,))],
         compiler_params=pltpu.CompilerParams(vmem_limit_bytes=MIB),
         cost_estimate=pl.CostEstimate(
             flops=0, bytes_accessed=2 * source.size, transcendentals=0
@@ -278,17 +312,20 @@
 
 def combine_kernel(share, *refs):
     results, out = refs[:-1], refs[-1]
-    total = jnp.zeros(out.shape, F32)
-    for k, result in enumerate(results):
-        total = total + share[:, k : k + 1] * result[...].astype(F32)
-    out[...] = total.astype(BF16)
+    width = results[0].shape[1]
+    for part in range(PARTS):
+        total = jnp.zeros(results[0].shape, F32)
+        for k in range(EXPERTS):
+            total = total + share[:, k : k + 1] * results[part * EXPERTS + k][...].astype(F32)
+        out[:, part * width : (part + 1) * width] = total.astype(BF16)
 
 
 def combine(share, results):
+    rows, width = results[0].shape
     return pl.pallas_call(
         combine_kernel,
-        out_shape=jax.ShapeDtypeStruct(results[0].shape, BF16),
-        in_specs=[VMEM] * (1 + EXPERTS),
+        out_shape=jax.ShapeDtypeStruct((rows, width * PARTS), BF16),
+        in_specs=[VMEM] * (1 + len(results)),
         out_specs=VMEM,
         compiler_params=pltpu.CompilerParams(vmem_limit_bytes=4 * MIB),
         name="combine",
@@ -324,24 +361,26 @@
     count = lax.axis_size("dp")
     plane = count // EXPERTS
     bits = [1 << k for k in reversed(range(plane.bit_length() - 1))]
-    attended, normed, share = attend(
+    attended, normed, share, down = attend(
         plane, queries, new_keys, new_values, cache_keys, cache_values, lengths, residual,
-        norm_gain, router_weight, routes,
+        norm_gain, router_weight, routes, down_weight,
     )
 
     gate, token = load(gate_weight, normed)
     gathered = join(token, normed, *[plane_shift(normed, count, k) for k in range(1, EXPERTS)])
     up, token = load(up_weight, gathered)
-    gathered = join(token, gathered, swap(gathered, count, bits[0]))
-    down, token = load(down_weight, gathered)
-    for bit in bits[1:]:
+    for bit in bits:
         gathered = join(token, gathered, swap(gathered, count, bit))
 
-    held, send = expert_rows(gathered, gate, up, down)
-    for bit in bits[:0:-1]:
-        held, send = fold(held, swap(send, count, bit))
-    terms = last_fold(held, swap(send, count, bits[0]))
-    results = [terms[0]] + [plane_shift(terms[k], count, -k) for k in range(1, EXPERTS)]
+    hidden = hidden_rows(gathered, gate, up)
+    results = []
+    for part in range(PARTS):
+        held, send = down_rows(hidden, down, part)
+        for bit in bits[:0:-1]:
+            held, send = fold(held, swap(send, count, bit))
+        terms = last_fold(held, swap(send, count, bits[0]))
+        results += [terms[0]]
+        results += [plane_shift(terms[k], count, -k) for k in range(1, EXPERTS)]
     return (attended, combine(share, results))
 
 

time: 57.5 us -> 56.9 us (0.990)
  starting transfers between devices: 13.4 us -> 18.7 us
  waiting for transfers between devices: 15.9 us -> 12.3 us
  Pallas kernels: 27.3 us -> 25 us
    pallas_call x3 -> x2, Pallas kernels: 15.5 us -> 10.6 us  [load(): pl.pallas_call(load_kernel, out_shape=(pltpu.VMEM(source.shape, source.dt...]
    ppermute x6 -> x9, starting transfers between devices: 9.62 us -> 13.7 us  [plane_shift(): lax.ppermute(value, 'dp', [(i, (i + offset * plane) % count) for i in ran...]
    ppermute x4 -> x6, waiting for transfers between devices: 9.92 us -> 6.77 us  [swap(): return lax.ppermute(value, 'dp', [(i, i ^ bit) for i in range(count)])]
    pallas_call x1, Pallas kernels: 4.68 us -> 7.03 us  [attend(): pl.pallas_call(functools.partial(attend_kernel, plane), out_shape=(jax.Sh...]
    ppermute x4 -> x6, starting transfers between devices: 3.82 us -> 5 us  [swap(): return lax.ppermute(value, 'dp', [(i, i ^ bit) for i in range(count)])]
    ppermute x6 -> x9, waiting for transfers between devices: 5.96 us -> 5.54 us  [plane_shift(): lax.ppermute(value, 'dp', [(i, (i + offset * plane) % count) for i in ran...]
    pallas_call x2 -> x4, Pallas kernels: 6.78 us -> 7.12 us  [the longest x1 4.05 us: hidden_rows(): pl.pallas_call(hidden_kernel, out_shape=jax.ShapeDtypeStruct((rows, colum...]
  transfers between devices with their start and end apart: 10 -> 15, of which waited for: 6 -> 7; matrix products, arithmetic and copies ran while one was open for 0% -> 0% of each run, Pallas kernels for 27% -> 21%
where the time goes in v3:
time: 56.9 us; the launch traced here: 56.7 us
  Pallas kernels  25 us (44%)
  starting transfers between devices  18.7 us (33%)
  waiting for transfers between devices  12.3 us (22%)
  between operations  0.74 us (1%)
    ppermute x9, starting transfers between devices, plane_shift(): lax.ppermute(value, 'dp', [(i, (i + offset * plane) % count) for i in ran...  13.7 us
    pallas_call x2, Pallas kernels, load(): pl.pallas_call(load_kernel, out_shape=(pltpu.VMEM(source.shape, source.dt...  10.6 us
    pallas_call x1, Pallas kernels, attend(): pl.pallas_call(functools.partial(attend_kernel, plane), out_shape=(jax.Sh...  7.03 us
    ppermute x6, waiting for transfers between devices, swap(): return lax.ppermute(value, 'dp', [(i, i ^ bit) for i in range(count)])  6.77 us
    ppermute x9, waiting for transfers between devices, plane_shift(): lax.ppermute(value, 'dp', [(i, (i + offset * plane) % count) for i in ran...  5.54 us
    ppermute x6, starting transfers between devices, swap(): return lax.ppermute(value, 'dp', [(i, i ^ bit) for i in range(count)])  5 us
    pallas_call x1, Pallas kernels, hidden_rows(): pl.pallas_call(hidden_kernel, out_shape=jax.ShapeDtypeStruct((rows, colum...  4.05 us
    pallas_call x2, Pallas kernels, down_rows(): pl.pallas_call(functools.partial(down_kernel, part * width), out_shape=(j...  2.32 us
  transfers between devices with their start and end apart: 15, of which 7 were waited for; matrix products, arithmetic and copies ran while one was open for 0% of the time, Pallas kernels for 21%

profile of v3, /device:TPU:0, one launch (start us, length us, event | category | flops | bytes accessed | tf_op | source)
XLA Modules:
  0.0 56.7 jit_solution(1461440275998484733)
XLA Ops:
  0.6 7.0 %attend.1 = (bf16[8,4096]{1,0:T(8,128)(2,1)}, bf16[8,4096]{1,0:T(8,128)(2,1)S(1)}, f32[8,128]{1,0:T(8,128)S(1)}, bf16[1792,4096]{1,0:T(8,128)(2,1)S(1)}) custom-call(bf16[8,4096]{1,0:T(8,128)(2,1)} %refs_0_.1, bf16[8,32,1024]{2,1,0:T(8,128)(2,1)} %refs_1_.1, bf16[8,1024]{1,0:T(8,128)(2,1)} %refs_2_.1, s32[8]{0:T(128)} %refs_3_.1, ...), custom_call_target="tpu_custom_call" | custom-call | tf_op jit(solution)/shard_map/attend/pallas_call | solution.py:153
  7.7 5.1 %collective-permute-start.2 = (bf16[8,4096]{1,0:T(8,128)(2,1)S(1)}, bf16[8,4096]{1,0:T(8,128)(2,1)S(1)}, u32[]{:S(2)}, u32[]{:S(2)}) collective-permute-start(bf16[8,4096]{1,0:T(8,128)(2,1)S(1)} %get-tuple-element.28.after.refs_1_), channel_id=1, source_target_pairs={{0,12},{1,13},{2,14},{3,15},{4,0},{5,1},{6,2},{7,3},{8,4},{9,5},{1... | collective-permute-start | bytes 196616 | tf_op jit(solution)/shard_map/ppermute | solution.py:337
  12.8 0.0 collective-permute-start.1
  12.8 1.0 %collective-permute-start = (bf16[8,4096]{1,0:T(8,128)(2,1)S(1)}, bf16[8,4096]{1,0:T(8,128)(2,1)S(1)}, u32[]{:S(2)}, u32[]{:S(2)}) collective-permute-start(bf16[8,4096]{1,0:T(8,128)(2,1)S(1)} %get-tuple-element.28.after.refs_1_), channel_id=1, source_target_pairs={{0,4},{1,5},{2,6},{3,7},{4,8},{5,9},{6,10},{7,11},{8,12},{9,13},{1... | collective-permute-start | bytes 196616 | tf_op jit(solution)/shard_map/ppermute | solution.py:337
  13.8 5.3 %load.2 = (bf16[4096,1792]{1,0:T(8,128)(2,1)S(1)}, f32[8,128]{1,0:T(8,128)S(1)}) custom-call(bf16[4096,1792]{1,0:T(8,128)(2,1)} %source.2, bf16[8,4096]{1,0:T(8,128)(2,1)S(1)} %get-tuple-element.28.after.refs_1_), custom_call_target="tpu_custom_call" | custom-call | bytes 14680064 | tf_op jit(solution)/shard_map/load/pallas_call | solution.py:237
  19.1 0.2 collective-permute-done.1.refs_3_
  19.3 1.6 %collective-permute-start.3 = (bf16[32,4096]{1,0:T(8,128)(2,1)S(1)}, bf16[32,4096]{1,0:T(8,128)(2,1)S(1)}, u32[]{:S(2)}, u32[]{:S(2)}) collective-permute-start(bf16[32,4096]{1,0:T(8,128)(2,1)S(1)} %join.3.after.refs_1_), channel_id=1, source_target_pairs={{0,2},{1,3},{2,0},{3,1},{4,6},{5,7},{6,4},{7,5},{8,10},{9,11},{10,... | collective-permute-start | bytes 786440 | tf_op jit(solution)/shard_map/ppermute | solution.py:343
  20.9 5.3 %load.3 = (bf16[4096,1792]{1,0:T(8,128)(2,1)S(1)}, f32[8,128]{1,0:T(8,128)S(1)}) custom-call(bf16[4096,1792]{1,0:T(8,128)(2,1)} %source.3, bf16[32,4096]{1,0:T(8,128)(2,1)S(1)} %join.3.after.refs_1_), custom_call_target="tpu_custom_call" | custom-call | bytes 14680064 | tf_op jit(solution)/shard_map/load/pallas_call | solution.py:237
  26.1 1.2 %collective-permute-done.3.refs_2_ = bf16[32,4096]{1,0:T(8,128)(2,1)S(1)} collective-permute-done((bf16[32,4096]{1,0:T(8,128)(2,1)S(1)}, bf16[32,4096]{1,0:T(8,128)(2,1)S(1)}, u32[]{:S(2)}, u32[]{:S(2)}) %collective-permute-start.3) | collective-permute-done | bytes 262176 | tf_op jit(solution)/shard_map/ppermute | solution.py:343
  27.4 0.1 collective-permute-start.4
  27.5 1.9 %collective-permute-done.4.refs_2_ = bf16[64,4096]{1,0:T(8,128)(2,1)S(1)} collective-permute-done((bf16[64,4096]{1,0:T(8,128)(2,1)S(1)}, bf16[64,4096]{1,0:T(8,128)(2,1)S(1)}, u32[]{:S(2)}, u32[]{:S(2)}) %collective-permute-start.4) | collective-permute-done | bytes 524320 | tf_op jit(solution)/shard_map/ppermute | solution.py:343
  29.4 0.1 join.5.inputs
  29.5 4.0 %hidden.1 = bf16[128,1792]{1,0:T(8,128)(2,1)S(1)} custom-call(bf16[128,4096]{1,0:T(8,128)(2,1)S(1)} %join.5.inputs, bf16[4096,1792]{1,0:T(8,128)(2,1)S(1)} %get-tuple-element.31.gate_weight, bf16[4096,1792]{1,0:T(8,128)(2,1)S(1)} %get-tuple-element.32.up_weight), custom_call_target="tpu_custom_call" | custom-call | flops 3758096384 | tf_op jit(solution)/shard_map/hidden/pallas_call | solution.py:186
  33.5 1.2 %down.3 = (f32[64,2048]{1,0:T(8,128)S(1)}, bf16[64,2048]{1,0:T(8,128)(2,1)S(1)}) custom-call(bf16[128,1792]{1,0:T(8,128)(2,1)S(1)} %hidden.1, bf16[1792,4096]{1,0:T(8,128)(2,1)S(1)} %get-tuple-element.33.down_weight), custom_call_target="tpu_custom_call" | custom-call | flops 939524096 | tf_op jit(solution)/shard_map/down/pallas_call | solution.py:211
  34.7 0.2 collective-permute-start.10
  34.9 1.2 %down.2 = (f32[64,2048]{1,0:T(8,128)S(1)}, bf16[64,2048]{1,0:T(8,128)(2,1)S(1)}) custom-call(bf16[128,1792]{1,0:T(8,128)(2,1)S(1)} %hidden.1, bf16[1792,4096]{1,0:T(8,128)(2,1)S(1)} %get-tuple-element.33.down_weight), custom_call_target="tpu_custom_call" | custom-call | flops 939524096 | tf_op jit(solution)/shard_map/down/pallas_call | solution.py:211
  36.0 0.5 collective-permute-start.5
  36.5 0.1 fold.3
  36.6 1.6 %collective-permute-start.11 = (bf16[32,2048]{1,0:T(8,128)(2,1)S(1)}, bf16[32,2048]{1,0:T(8,128)(2,1)S(1)}, u32[]{:S(2)}, u32[]{:S(2)}) collective-permute-start(bf16[32,2048]{1,0:T(8,128)(2,1)S(1)} %get-tuple-element.45), channel_id=1, source_target_pairs={{0,2},{1,3},{2,0},{3,1},{4,6},{5,7},{6,4},{7,5},{8,10},{9,11},{10,... | collective-permute-start | bytes 393224 | tf_op jit(solution)/shard_map/ppermute | solution.py:343
  38.1 0.1 fold.2
  38.2 1.1 %collective-permute-start.6 = (bf16[32,2048]{1,0:T(8,128)(2,1)S(1)}, bf16[32,2048]{1,0:T(8,128)(2,1)S(1)}, u32[]{:S(2)}, u32[]{:S(2)}) collective-permute-start(bf16[32,2048]{1,0:T(8,128)(2,1)S(1)} %get-tuple-element.37), channel_id=1, source_target_pairs={{0,2},{1,3},{2,0},{3,1},{4,6},{5,7},{6,4},{7,5},{8,10},{9,11},{10,... | collective-permute-start | bytes 393224 | tf_op jit(solution)/shard_map/ppermute | solution.py:343
  39.3 3.6 %collective-permute-done.11.arrived = bf16[32,2048]{1,0:T(8,128)(2,1)S(1)} collective-permute-done((bf16[32,2048]{1,0:T(8,128)(2,1)S(1)}, bf16[32,2048]{1,0:T(8,128)(2,1)S(1)}, u32[]{:S(2)}, u32[]{:S(2)}) %collective-permute-start.11) | collective-permute-done | bytes 131104 | tf_op jit(solution)/shard_map/ppermute | solution.py:343
  43.0 2.2 %collective-permute-start.12 = (bf16[8,2048]{1,0:T(8,128)(2,1)S(1)}, bf16[8,2048]{1,0:T(8,128)(2,1)S(1)}, u32[]{:S(2)}, u32[]{:S(2)}) collective-permute-start(bf16[8,2048]{1,0:T(8,128)(2,1)S(1)} %get-tuple-element.47), channel_id=1, source_target_pairs={{0,12},{1,13},{2,14},{3,15},{4,0},{5,1},{6,2},{7,3},{8,4},{9,5},{1... | collective-permute-start | bytes 98312 | tf_op jit(solution)/shard_map/ppermute | solution.py:337
  45.2 0.8 %collective-permute-start.13 = (bf16[8,2048]{1,0:T(8,128)(2,1)S(1)}, bf16[8,2048]{1,0:T(8,128)(2,1)S(1)}, u32[]{:S(2)}, u32[]{:S(2)}) collective-permute-start(bf16[8,2048]{1,0:T(8,128)(2,1)S(1)} %get-tuple-element.48), channel_id=1, source_target_pairs={{0,8},{1,9},{2,10},{3,11},{4,12},{5,13},{6,14},{7,15},{8,0},{9,1},... | collective-permute-start | bytes 98312 | tf_op jit(solution)/shard_map/ppermute | solution.py:337
  46.0 0.5 collective-permute-start.14
  46.5 3.4 %collective-permute-start.7 = (bf16[8,2048]{1,0:T(8,128)(2,1)S(1)}, bf16[8,2048]{1,0:T(8,128)(2,1)S(1)}, u32[]{:S(2)}, u32[]{:S(2)}) collective-permute-start(bf16[8,2048]{1,0:T(8,128)(2,1)S(1)} %get-tuple-element.39), channel_id=1, source_target_pairs={{0,12},{1,13},{2,14},{3,15},{4,0},{5,1},{6,2},{7,3},{8,4},{9,5},{1... | collective-permute-start | bytes 98312 | tf_op jit(solution)/shard_map/ppermute | solution.py:337
  49.9 0.3 collective-permute-start.8
  50.2 0.3 collective-permute-start.9
  50.6 1.2 %collective-permute-done.14.refs_7_ = bf16[8,2048]{1,0:T(8,128)(2,1)S(1)} collective-permute-done((bf16[8,2048]{1,0:T(8,128)(2,1)S(1)}, bf16[8,2048]{1,0:T(8,128)(2,1)S(1)}, u32[]{:S(2)}, u32[]{:S(2)}) %collective-permute-start.14) | collective-permute-done | bytes 32800 | tf_op jit(solution)/shard_map/ppermute | solution.py:337
  51.7 3.0 %collective-permute-done.8.refs_2_ = bf16[8,2048]{1,0:T(8,128)(2,1)S(1)} collective-permute-done((bf16[8,2048]{1,0:T(8,128)(2,1)S(1)}, bf16[8,2048]{1,0:T(8,128)(2,1)S(1)}, u32[]{:S(2)}, u32[]{:S(2)}) %collective-permute-start.8) | collective-permute-done | bytes 32800 | tf_op jit(solution)/shard_map/ppermute | solution.py:337
  54.7 1.2 %collective-permute-done.9.refs_3_ = bf16[8,2048]{1,0:T(8,128)(2,1)S(1)} collective-permute-done((bf16[8,2048]{1,0:T(8,128)(2,1)S(1)}, bf16[8,2048]{1,0:T(8,128)(2,1)S(1)}, u32[]{:S(2)}, u32[]{:S(2)}) %collective-permute-start.9) | collective-permute-done | bytes 32800 | tf_op jit(solution)/shard_map/ppermute | solution.py:337
  56.0 0.7 %combine.1 = bf16[8,4096]{1,0:T(8,128)(2,1)} custom-call(f32[8,128]{1,0:T(8,128)S(1)} %get-tuple-element.27.share, bf16[8,2048]{1,0:T(8,128)(2,1)S(1)} %get-tuple-element.38.refs_0_, bf16[8,2048]{1,0:T(8,128)(2,1)S(1)} %collective-permute-done.7.refs_1_, bf16[8,2048]{1,0:T(8,128)(2,1)S(1)} %collective-permute-done.8.refs_2_, ...), custom_call_target="tpu_custom_call" | custom-call | tf_op jit(solution)/shard_map/combine/pallas_call | solution.py:325
  (12 shorter events, 0.1 us)
Async XLA Ops:
  7.7 11.4 %collective-permute-start.2 = (bf16[8,4096]{1,0:T(8,128)(2,1)S(1)}, bf16[8,4096]{1,0:T(8,128)(2,1)S(1)}, u32[]{:S(2)}, u32[]{:S(2)}) collective-permute-start(bf16[8,4096]{1,0:T(8,128)(2,1)S(1)} %get-tuple-element.28.after.refs_1_), channel_id=1, source_target_pairs={{0,12},{1,13},{2,14},{3,15},{4,0},{5,1},{6,2},{7,3},{8,4},{9,5},{1... | collective-permute-start | bytes 196616 | tf_op jit(solution)/shard_map/ppermute | solution.py:337
  12.8 6.5 %collective-permute-start.1 = (bf16[8,4096]{1,0:T(8,128)(2,1)S(1)}, bf16[8,4096]{1,0:T(8,128)(2,1)S(1)}, u32[]{:S(2)}, u32[]{:S(2)}) collective-permute-start(bf16[8,4096]{1,0:T(8,128)(2,1)S(1)} %get-tuple-element.28.after.refs_1_), channel_id=1, source_target_pairs={{0,8},{1,9},{2,10},{3,11},{4,12},{5,13},{6,14},{7,15},{8,0},{9,1},... | collective-permute-start | bytes 196616 | tf_op jit(solution)/shard_map/ppermute | solution.py:337
  12.8 6.5 %collective-permute-start = (bf16[8,4096]{1,0:T(8,128)(2,1)S(1)}, bf16[8,4096]{1,0:T(8,128)(2,1)S(1)}, u32[]{:S(2)}, u32[]{:S(2)}) collective-permute-start(bf16[8,4096]{1,0:T(8,128)(2,1)S(1)} %get-tuple-element.28.after.refs_1_), channel_id=1, source_target_pairs={{0,4},{1,5},{2,6},{3,7},{4,8},{5,9},{6,10},{7,11},{8,12},{9,13},{1... | collective-permute-start | bytes 196616 | tf_op jit(solution)/shard_map/ppermute | solution.py:337
  19.3 8.1 %collective-permute-start.3 = (bf16[32,4096]{1,0:T(8,128)(2,1)S(1)}, bf16[32,4096]{1,0:T(8,128)(2,1)S(1)}, u32[]{:S(2)}, u32[]{:S(2)}) collective-permute-start(bf16[32,4096]{1,0:T(8,128)(2,1)S(1)} %join.3.after.refs_1_), channel_id=1, source_target_pairs={{0,2},{1,3},{2,0},{3,1},{4,6},{5,7},{6,4},{7,5},{8,10},{9,11},{10,... | collective-permute-start | bytes 786440 | tf_op jit(solution)/shard_map/ppermute | solution.py:343
  27.4 2.0 %collective-permute-start.4 = (bf16[64,4096]{1,0:T(8,128)(2,1)S(1)}, bf16[64,4096]{1,0:T(8,128)(2,1)S(1)}, u32[]{:S(2)}, u32[]{:S(2)}) collective-permute-start(bf16[64,4096]{1,0:T(8,128)(2,1)S(1)} %join.4.refs_1_), channel_id=1, source_target_pairs={{0,1},{1,0},{2,3},{3,2},{4,5},{5,4},{6,7},{7,6},{8,9},{9,8},{10,11... | collective-permute-start | bytes 1572872 | tf_op jit(solution)/shard_map/ppermute | solution.py:343
  34.7 1.8 %collective-permute-start.10 = (bf16[64,2048]{1,0:T(8,128)(2,1)S(1)}, bf16[64,2048]{1,0:T(8,128)(2,1)S(1)}, u32[]{:S(2)}, u32[]{:S(2)}) collective-permute-start(bf16[64,2048]{1,0:T(8,128)(2,1)S(1)} %get-tuple-element.43), channel_id=1, source_target_pairs={{0,1},{1,0},{2,3},{3,2},{4,5},{5,4},{6,7},{7,6},{8,9},{9,8},{10,11... | collective-permute-start | bytes 786440 | tf_op jit(solution)/shard_map/ppermute | solution.py:343
  36.0 2.1 %collective-permute-start.5 = (bf16[64,2048]{1,0:T(8,128)(2,1)S(1)}, bf16[64,2048]{1,0:T(8,128)(2,1)S(1)}, u32[]{:S(2)}, u32[]{:S(2)}) collective-permute-start(bf16[64,2048]{1,0:T(8,128)(2,1)S(1)} %get-tuple-element.35), channel_id=1, source_target_pairs={{0,1},{1,0},{2,3},{3,2},{4,5},{5,4},{6,7},{7,6},{8,9},{9,8},{10,11... | collective-permute-start | bytes 786440 | tf_op jit(solution)/shard_map/ppermute | solution.py:343
  36.6 6.4 %collective-permute-start.11 = (bf16[32,2048]{1,0:T(8,128)(2,1)S(1)}, bf16[32,2048]{1,0:T(8,128)(2,1)S(1)}, u32[]{:S(2)}, u32[]{:S(2)}) collective-permute-start(bf16[32,2048]{1,0:T(8,128)(2,1)S(1)} %get-tuple-element.45), channel_id=1, source_target_pairs={{0,2},{1,3},{2,0},{3,1},{4,6},{5,7},{6,4},{7,5},{8,10},{9,11},{10,... | collective-permute-start | bytes 393224 | tf_op jit(solution)/shard_map/ppermute | solution.py:343
  38.2 8.3 %collective-permute-start.6 = (bf16[32,2048]{1,0:T(8,128)(2,1)S(1)}, bf16[32,2048]{1,0:T(8,128)(2,1)S(1)}, u32[]{:S(2)}, u32[]{:S(2)}) collective-permute-start(bf16[32,2048]{1,0:T(8,128)(2,1)S(1)} %get-tuple-element.37), channel_id=1, source_target_pairs={{0,2},{1,3},{2,0},{3,1},{4,6},{5,7},{6,4},{7,5},{8,10},{9,11},{10,... | collective-permute-start | bytes 393224 | tf_op jit(solution)/shard_map/ppermute | solution.py:343
  43.0 7.2 %collective-permute-start.12 = (bf16[8,2048]{1,0:T(8,128)(2,1)S(1)}, bf16[8,2048]{1,0:T(8,128)(2,1)S(1)}, u32[]{:S(2)}, u32[]{:S(2)}) collective-permute-start(bf16[8,2048]{1,0:T(8,128)(2,1)S(1)} %get-tuple-element.47), channel_id=1, source_target_pairs={{0,12},{1,13},{2,14},{3,15},{4,0},{5,1},{6,2},{7,3},{8,4},{9,5},{1... | collective-permute-start | bytes 98312 | tf_op jit(solution)/shard_map/ppermute | solution.py:337
  45.2 5.4 %collective-permute-start.13 = (bf16[8,2048]{1,0:T(8,128)(2,1)S(1)}, bf16[8,2048]{1,0:T(8,128)(2,1)S(1)}, u32[]{:S(2)}, u32[]{:S(2)}) collective-permute-start(bf16[8,2048]{1,0:T(8,128)(2,1)S(1)} %get-tuple-element.48), channel_id=1, source_target_pairs={{0,8},{1,9},{2,10},{3,11},{4,12},{5,13},{6,14},{7,15},{8,0},{9,1},... | collective-permute-start | bytes 98312 | tf_op jit(solution)/shard_map/ppermute | solution.py:337
  46.0 5.7 %collective-permute-start.14 = (bf16[8,2048]{1,0:T(8,128)(2,1)S(1)}, bf16[8,2048]{1,0:T(8,128)(2,1)S(1)}, u32[]{:S(2)}, u32[]{:S(2)}) collective-permute-start(bf16[8,2048]{1,0:T(8,128)(2,1)S(1)} %get-tuple-element.49), channel_id=1, source_target_pairs={{0,4},{1,5},{2,6},{3,7},{4,8},{5,9},{6,10},{7,11},{8,12},{9,13},{1... | collective-permute-start | bytes 98312 | tf_op jit(solution)/shard_map/ppermute | solution.py:337
  46.5 5.2 %collective-permute-start.7 = (bf16[8,2048]{1,0:T(8,128)(2,1)S(1)}, bf16[8,2048]{1,0:T(8,128)(2,1)S(1)}, u32[]{:S(2)}, u32[]{:S(2)}) collective-permute-start(bf16[8,2048]{1,0:T(8,128)(2,1)S(1)} %get-tuple-element.39), channel_id=1, source_target_pairs={{0,12},{1,13},{2,14},{3,15},{4,0},{5,1},{6,2},{7,3},{8,4},{9,5},{1... | collective-permute-start | bytes 98312 | tf_op jit(solution)/shard_map/ppermute | solution.py:337
  49.9 4.8 %collective-permute-start.8 = (bf16[8,2048]{1,0:T(8,128)(2,1)S(1)}, bf16[8,2048]{1,0:T(8,128)(2,1)S(1)}, u32[]{:S(2)}, u32[]{:S(2)}) collective-permute-start(bf16[8,2048]{1,0:T(8,128)(2,1)S(1)} %get-tuple-element.40), channel_id=1, source_target_pairs={{0,8},{1,9},{2,10},{3,11},{4,12},{5,13},{6,14},{7,15},{8,0},{9,1},... | collective-permute-start | bytes 98312 | tf_op jit(solution)/shard_map/ppermute | solution.py:337
  50.2 5.7 %collective-permute-start.9 = (bf16[8,2048]{1,0:T(8,128)(2,1)S(1)}, bf16[8,2048]{1,0:T(8,128)(2,1)S(1)}, u32[]{:S(2)}, u32[]{:S(2)}) collective-permute-start(bf16[8,2048]{1,0:T(8,128)(2,1)S(1)} %get-tuple-element.41), channel_id=1, source_target_pairs={{0,4},{1,5},{2,6},{3,7},{4,8},{5,9},{6,10},{7,11},{8,12},{9,13},{1... | collective-permute-start | bytes 98312 | tf_op jit(solution)/shard_map/ppermute | solution.py:337

commit v4 on v3

--- a/solution.py
+++ b/solution.py
@@ -14,6 +14,7 @@
 MIB = 1 << 20
 WAYS = 4
 PARTS = 2
+MOST = 6
 F32 = jnp.float32
 BF16 = jnp.bfloat16
 VMEM = pl.BlockSpec(memory_space=pltpu.VMEM)
@@ -25,21 +26,46 @@
     return lax.dot_general(a, b, dims, preferred_element_type=F32)
 
 
-def weight_copies(source, target, semaphores):
-    step = source.shape[0] // WAYS
+def weight_copies(source, target, semaphores, first=0):
+    step, columns = source.shape[0] // WAYS, target.shape[1]
     return [
         pltpu.make_async_copy(
-            source.at[pl.ds(i * step, step)], target.at[pl.ds(i * step, step)], semaphores.at[i]
+            source.at[pl.ds(i * step, step), pl.ds(first, columns)],
+            target.at[pl.ds(i * step, step)],
+            semaphores.at[i],
         )
         for i in range(WAYS)
     ]
 
 
-def attend_kernel(plane, *refs):
-    sources, (attended, normed, share), held, semaphores = (
-        refs[:10], refs[11:14], refs[15:25], refs[25]
-    )
-    weight = weight_copies(refs[10], refs[14], refs[26])
+def one_hot(mask):
+    return mask.astype(F32).astype(BF16)
+
+
+def grid(shape):
+    return [lax.broadcasted_iota(jnp.int32, shape, axis) for axis in (0, 1)]
+
+
+def pack(picks, block):
+    quarter = block.shape[1] // 4
+    parts = [block[:, m * quarter : (m + 1) * quarter] for m in range(4)]
+    return [
+        (dot(picks[0], parts[m]) + dot(picks[1 + m], parts[3])).astype(BF16) for m in range(3)
+    ]
+
+
+def unpack(picks, block):
+    quarter = block.shape[1] // 3
+    parts = [block[:, m * quarter : (m + 1) * quarter] for m in range(3)]
+    tail = dot(picks[1], parts[0]) + dot(picks[2], parts[1]) + dot(picks[3], parts[2])
+    return [dot(picks[0], part) for part in parts] + [tail]
+
+
+def attend_kernel(*refs):
+    sources, (attended, packed, share, take), held, semaphores = (
+        refs[:10], refs[11:15], refs[16:26], refs[26]
+    )
+    weight = weight_copies(refs[10], refs[15], refs[27])
     copies = [
         pltpu.make_async_copy(source, target, semaphores.at[i])
         for i, (source, target) in enumerate(zip(sources, held))
@@ -100,41 +126,65 @@
     norm = lax.rsqrt(jnp.mean(states * states, axis=1, keepdims=True) + 1e-05)
     gains = gain[...].astype(F32)
     logits = [jnp.zeros((rows, 128), F32) for _ in range(EXPERTS)]
+    parts = []
     for c in range(width // 128):
         lanes = slice(c * 128, (c + 1) * 128)
-        part = (states[:, lanes] * norm * gains[c : c + 1]).astype(BF16)
-        normed[:, lanes] = part
-        part = part.astype(F32)
+        part = (states[:, lanes] * norm * gains[c : c + 1]).astype(BF16).astype(F32)
+        parts.append(part)
         for e in range(EXPERTS):
             logits[e] += part * router[e : e + 1, lanes].astype(F32)
     logits = [jnp.sum(value, axis=1, keepdims=True) for value in logits]
 
-    index = lax.axis_index("dp")
-    base = index * rows
-    row = lax.broadcasted_iota(jnp.int32, (rows, 1), 0)
-    first = jnp.zeros((rows, 1), jnp.int32)
-    second = jnp.zeros((rows, 1), jnp.int32)
+    base = lax.axis_index("dp") * rows
+    sub, lane = grid((2 * rows, 128))
+    expert_down = jnp.zeros((2 * rows, 128), jnp.int32)
+    slot_down = jnp.zeros((2 * rows, 128), jnp.int32)
+    across = lax.broadcasted_iota(jnp.int32, (8, 128), 1)
+    expert_across = jnp.zeros((8, 128), jnp.int32)
+    slot_across = jnp.zeros((8, 128), jnp.int32)
+    counts = [jnp.int32(0)] * EXPERTS
     for r in range(rows):
-        first = jnp.where(row == r, routes[0, base + r], first)
-        second = jnp.where(row == r, routes[1, base + r], second)
-    first_logit = jnp.zeros((rows, 1), F32)
-    second_logit = jnp.zeros((rows, 1), F32)
+        names = [routes[0, base + r], routes[1, base + r]]
+        for choice, name in ((r, names[0]), (rows + r, names[1])):
+            slot = jnp.int32(0)
+            for e in range(EXPERTS):
+                slot = jnp.where(name == e, counts[e], slot)
+            expert_down = jnp.where(sub == choice, name, expert_down)
+            slot_down = jnp.where(sub == choice, slot, slot_down)
+            expert_across = jnp.where(across == choice, name, expert_across)
+            slot_across = jnp.where(across == choice, slot, slot_across)
+        for e in range(EXPERTS):
+            named = (names[0] == e) | (names[1] == e)
+            counts[e] = counts[e] + jnp.where(named, 1, 0)
+
+    late = jnp.where(slot_down >= 3, 1, 0)
+    take[0] = one_hot(lane == expert_down * 8 + slot_down)
+    for m in range(3):
+        take[1 + m] = one_hot((lane == expert_down * 8 + 6 + late) & (slot_down - 3 * late == m))
+    place, choice = grid((8 * EXPERTS, 128))
+    expert, slot = expert_across[0:1], slot_across[0:1]
+    late = jnp.where(slot >= 3, 1, 0)
+    chosen = choice < 2 * rows
+    picks = [one_hot((place == expert * 8 + slot) & chosen)]
+    for m in range(3):
+        picks.append(one_hot((place == expert * 8 + 6 + late) & (slot - 3 * late == m) & chosen))
+    normed = jnp.concatenate(parts, axis=1)
+    normed = jnp.concatenate([normed, normed], axis=0).astype(BF16)
+    quarter = width // 4
+    for m, value in enumerate(pack([pick[:, : 2 * rows] for pick in picks], normed)):
+        packed[:, m * quarter : (m + 1) * quarter] = value
+
+    chosen_logits = jnp.zeros((2 * rows, 1), F32)
     for e in range(EXPERTS):
-        first_logit = jnp.where(first == e, logits[e], first_logit)
-        second_logit = jnp.where(second == e, logits[e], second_logit)
-    first_share = 1.0 / (1.0 + jnp.exp(second_logit - first_logit))
-    second_share = 1.0 / (1.0 + jnp.exp(first_logit - second_logit))
-    lane = lax.broadcasted_iota(jnp.int32, (rows, 128), 1)
-    expert = (index // plane + lane) % EXPERTS
-    expert = jnp.where(lane < EXPERTS, expert, -1)
-    share[...] = jnp.where(first == expert, first_share, 0.0) + jnp.where(
-        second == expert, second_share, 0.0
-    )
+        both = jnp.concatenate([logits[e], logits[e]], axis=0)
+        chosen_logits = jnp.where(expert_down[:, :1] == e, both, chosen_logits)
+    other = jnp.concatenate([chosen_logits[rows:], chosen_logits[:rows]], axis=0)
+    share[...] = jnp.broadcast_to(1.0 / (1.0 + jnp.exp(other - chosen_logits)), share.shape)
     for copy in weight:
         copy.wait()
 
 
-def attend(plane, queries, new_keys, new_values, cache_keys, cache_values, lengths, residual,
+def attend(queries, new_keys, new_values, cache_keys, cache_values, lengths, residual,
            norm_gain, router_weight, routes, weight):
     rows, width = queries.shape
     operands = (
@@ -151,15 +201,16 @@
     )
     in_smem = (3, 9)
     return pl.pallas_call(
-        functools.partial(attend_kernel, plane),
+        attend_kernel,
         out_shape=(
             jax.ShapeDtypeStruct((rows, width), BF16),
-            jax.ShapeDtypeStruct((rows, width), BF16),
-            jax.ShapeDtypeStruct((rows, 128), F32),
-            pltpu.VMEM(weight.shape, weight.dtype),
+            jax.ShapeDtypeStruct((8 * EXPERTS, width * 3 // 4), BF16),
+            jax.ShapeDtypeStruct((2 * rows, 128), F32),
+            jax.ShapeDtypeStruct((4, 2 * rows, 128), BF16),
+            pltpu.VMEM((weight.shape[0], weight.shape[1] // PARTS), weight.dtype),
         ),
         in_specs=[ANY] * (len(operands) + 1),
-        out_specs=(VMEM,) * 4,
+        out_specs=(VMEM,) * 5,
         scratch_shapes=[
             (pltpu.SMEM if i in in_smem else pltpu.VMEM)(operand.shape, operand.dtype)
             for i, operand in enumerate(operands)
@@ -196,20 +247,20 @@
     )(inputs, gate_weight, up_weight)
 
 
-def down_kernel(first, hidden, down_weight, keep, send):
+def down_kernel(hidden, down_weight, keep, send):
     half, width = keep.shape
     h = hidden[...]
     for n in range(0, width, 512):
-        terms = dot(h, down_weight[:, first + n : first + n + 512])
+        terms = dot(h, down_weight[:, n : n + 512])
         keep[:, n : n + 512] = terms[:half]
         send[:, n : n + 512] = terms[half:].astype(BF16)
 
 
-def down_rows(hidden, down_weight, part):
+def down_rows(hidden, down_weight):
     rows, columns = hidden.shape
-    half, width = rows // 2, down_weight.shape[1] // PARTS
-    return pl.pallas_call(
-        functools.partial(down_kernel, part * width),
+    half, width = rows // 2, down_weight.shape[1]
+    return pl.pallas_call(
+        down_kernel,
         out_shape=(
             jax.ShapeDtypeStruct((half, width), F32),
             jax.ShapeDtypeStruct((half, width), BF16),
@@ -224,8 +275,8 @@
     )(hidden, down_weight)
 
 
-def load_kernel(source, after, target, token, semaphores):
-    copies = weight_copies(source, target, semaphores)
+def load_kernel(first, source, after, target, token, semaphores):
+    copies = weight_copies(source, target, semaphores, first)
     for copy in copies:
         copy.start()
     token[...] = jnp.zeros(token.shape, token.dtype)
@@ -233,11 +284,12 @@
         copy.wait()
 
 
-def load(source, after):
-    return pl.pallas_call(
-        load_kernel,
+def load(source, after, first=0):
+    shape = (source.shape[0], source.shape[1] - first)
+    return pl.pallas_call(
+        functools.partial(load_kernel, first),
         out_shape=(
-            pltpu.VMEM(source.shape, source.dtype),
+            pltpu.VMEM(shape, source.dtype),
             jax.ShapeDtypeStruct((8, 128), F32),
         ),
         in_specs=[ANY, ANY],
@@ -245,10 +297,34 @@
         scratch_shapes=[pltpu.SemaphoreType.DMA((WAYS,))],
         compiler_params=pltpu.CompilerParams(vmem_limit_bytes=MIB),
         cost_estimate=pl.CostEstimate(
-            flops=0, bytes_accessed=2 * source.size, transcendentals=0
+            flops=0, bytes_accessed=2 * shape[0] * shape[1], transcendentals=0
         ),
         name="load",
     )(pltpu.with_memory_space_constraint(source, pltpu.HBM), after)
+
+
+def collect_kernel(arrived, token, gathered):
+    row, lane = grid((MOST * EXPERTS, 8 * EXPERTS))
+    plane = sum([jnp.where(row >= MOST * e, 1, 0) for e in range(1, EXPERTS)])
+    slot = row - MOST * plane
+    late = jnp.where(slot >= 3, 1, 0)
+    picks = [one_hot(lane == plane * 8 + slot)]
+    for m in range(3):
+        picks.append(one_hot((lane == plane * 8 + 6 + late) & (slot - 3 * late == m)))
+    quarter = gathered.shape[1] // 4
+    for m, value in enumerate(unpack(picks, arrived[...])):
+        gathered[:, m * quarter : (m + 1) * quarter] = value.astype(BF16)
+
+
+def collect(arrived, token):
+    return pl.pallas_call(
+        collect_kernel,
+        out_shape=jax.ShapeDtypeStruct((MOST * EXPERTS, arrived.shape[1] // 3 * 4), BF16),
+        in_specs=[VMEM, ANY],
+        out_specs=VMEM,
+        compiler_params=pltpu.CompilerParams(vmem_limit_bytes=2 * MIB),
+        name="collect",
+    )(arrived, token)
 
 
 def join_kernel(*refs):
@@ -291,51 +367,59 @@
     )(held, arrived)
 
 
-def last_fold_kernel(held, arrived, *outs):
-    rows = outs[0].shape[0]
-    for k, out in enumerate(outs):
-        block = slice(k * rows, (k + 1) * rows)
-        out[...] = (held[block] + arrived[block].astype(F32)).astype(BF16)
+def last_fold_kernel(held, arrived, packed):
+    block = (held[...] + arrived[...].astype(F32)).astype(BF16)
+    place, row = grid((8 * EXPERTS, MOST * EXPERTS))
+    plane, slot = place // 8, place % 8
+    picks = [one_hot((row == plane * MOST + slot) & (slot < MOST))]
+    for m in range(3):
+        picks.append(one_hot((row == plane * MOST + 3 * (slot - 6) + m) & (slot >= MOST)))
+    quarter = block.shape[1] // 4
+    for m, value in enumerate(pack(picks, block)):
+        packed[:, m * quarter : (m + 1) * quarter] = value
 
 
 def last_fold(held, arrived):
-    rows, width = held.shape[0] // EXPERTS, held.shape[1]
     return pl.pallas_call(
         last_fold_kernel,
-        out_shape=(jax.ShapeDtypeStruct((rows, width), BF16),) * EXPERTS,
+        out_shape=jax.ShapeDtypeStruct((8 * EXPERTS, held.shape[1] // 4 * 3), BF16),
         in_specs=[VMEM] * 2,
-        out_specs=(VMEM,) * EXPERTS,
-        compiler_params=pltpu.CompilerParams(vmem_limit_bytes=4 * MIB),
+        out_specs=VMEM,
+        compiler_params=pltpu.CompilerParams(vmem_limit_bytes=2 * MIB),
         name="last_fold",
     )(held, arrived)
 
 
-def combine_kernel(share, *refs):
+def combine_kernel(share, take, *refs):
     results, out = refs[:-1], refs[-1]
-    width = results[0].shape[1]
-    for part in range(PARTS):
-        total = jnp.zeros(results[0].shape, F32)
-        for k in range(EXPERTS):
-            total = total + share[:, k : k + 1] * results[part * EXPERTS + k][...].astype(F32)
-        out[:, part * width : (part + 1) * width] = total.astype(BF16)
-
-
-def combine(share, results):
-    rows, width = results[0].shape
+    rows = out.shape[0]
+    quarter = results[0].shape[1] // 3
+    picks = [take[i][:, : 8 * EXPERTS] for i in range(4)]
+    shares = share[:, :1]
+    for part, result in enumerate(results):
+        for m, value in enumerate(unpack(picks, result[...])):
+            value = value * shares
+            first = (part * 4 + m) * quarter
+            out[:, first : first + quarter] = (value[:rows] + value[rows:]).astype(BF16)
+
+
+def combine(share, take, results):
+    width = results[0].shape[1] // 3 * 4
     return pl.pallas_call(
         combine_kernel,
-        out_shape=jax.ShapeDtypeStruct((rows, width * PARTS), BF16),
-        in_specs=[VMEM] * (1 + len(results)),
+        out_shape=jax.ShapeDtypeStruct((share.shape[0] // 2, width * PARTS), BF16),
+        in_specs=[VMEM] * (2 + len(results)),
         out_specs=VMEM,
-        compiler_params=pltpu.CompilerParams(vmem_limit_bytes=4 * MIB),
+        compiler_params=pltpu.CompilerParams(vmem_limit_bytes=2 * MIB),
         name="combine",
-    )(share, *results)
-
-
-def plane_shift(value, count, offset):
+    )(share, take, *results)
+
+
+def between_planes(value, count):
     plane = count // EXPERTS
-    return lax.ppermute(
-        value, "dp", [(i, (i + offset * plane) % count) for i in range(count)]
+    groups = [[e * plane + p for e in range(EXPERTS)] for p in range(plane)]
+    return lax.all_to_all(
+        value, "dp", split_axis=0, concat_axis=0, axis_index_groups=groups, tiled=True
     )
 
 
@@ -361,27 +445,27 @@
     count = lax.axis_size("dp")
     plane = count // EXPERTS
     bits = [1 << k for k in reversed(range(plane.bit_length() - 1))]
-    attended, normed, share, down = attend(
-        plane, queries, new_keys, new_values, cache_keys, cache_values, lengths, residual,
-        norm_gain, router_weight, routes, down_weight,
-    )
-
-    gate, token = load(gate_weight, normed)
-    gathered = join(token, normed, *[plane_shift(normed, count, k) for k in range(1, EXPERTS)])
+    attended, packed, share, take, down = attend(
+        queries, new_keys, new_values, cache_keys, cache_values, lengths, residual, norm_gain,
+        router_weight, routes, down_weight,
+    )
+
+    gate, token = load(gate_weight, packed)
+    gathered = collect(between_planes(packed, count), token)
     up, token = load(up_weight, gathered)
-    for bit in bits:
+    gathered = join(token, gathered, swap(gathered, count, bits[0]))
+    down_rest, token = load(down_weight, gathered, down.shape[1])
+    for bit in bits[1:]:
         gathered = join(token, gathered, swap(gathered, count, bit))
 
     hidden = hidden_rows(gathered, gate, up)
     results = []
-    for part in range(PARTS):
-        held, send = down_rows(hidden, down, part)
+    for weight in (down, down_rest):
+        held, send = down_rows(hidden, weight)
         for bit in bits[:0:-1]:
             held, send = fold(held, swap(send, count, bit))
-        terms = last_fold(held, swap(send, count, bits[0]))
-        results += [terms[0]]
-        results += [plane_shift(terms[k], count, -k) for k in range(1, EXPERTS)]
-    return (attended, combine(share, results))
+        results.append(between_planes(last_fold(held, swap(send, count, bits[0])), count))
+    return (attended, combine(share, take, results))
 
 
 def solution(mesh):

time: 56.9 us -> 75.3 us (1.32)
  blocking collectives: 0 us -> 9.81 us
  local copies, waits for them, and re-layouts: 0 us -> 9.56 us
  Pallas kernels: 25 us -> 30.6 us
  waiting for transfers between devices: 12.3 us -> 8.72 us
  starting transfers between devices: 18.7 us -> 15.4 us
    ppermute x9 -> x0, starting transfers between devices: 13.7 us -> none  [plane_shift(): lax.ppermute(value, 'dp', [(i, (i + offset * plane) % count) for i in ran...]
    all_to_all x0 -> x2, starting transfers between devices: none -> 11.4 us  [between_planes(): lax.all_to_all(value, 'dp', split_axis=0, concat_axis=0, axis_index_group...]
    all_to_all x0 -> x1, blocking collectives: none -> 9.81 us  [between_planes(): lax.all_to_all(value, 'dp', split_axis=0, concat_axis=0, axis_index_group...]
    unnamed x0 -> x16, local copies, waits for them, and re-layouts: none -> 9.56 us
    ppermute x9 -> x0, waiting for transfers between devices: 5.54 us -> none  [plane_shift(): lax.ppermute(value, 'dp', [(i, (i + offset * plane) % count) for i in ran...]
    pallas_call x8 -> x10, Pallas kernels: 20.7 us -> 25.6 us  [the longest x3 14.6 us: load(): pl.pallas_call(functools.partial(load_kernel, first), out_shape=(pltpu.VM...]
    ppermute x6, starting transfers between devices: 5 us -> 3.97 us  [swap(): return lax.ppermute(value, 'dp', [(i, i ^ bit) for i in range(count)])]
    ppermute x6, waiting for transfers between devices: 6.77 us -> 7.8 us  [swap(): return lax.ppermute(value, 'dp', [(i, i ^ bit) for i in range(count)])]
  transfers between devices with their start and end apart: 15 -> 8, of which waited for: 7 -> 3; matrix products, arithmetic and copies ran while one was open for 0% -> 0% of each run, Pallas kernels for 21% -> 23%
where the time goes in v4:
time: 75.3 us; the launch traced here: 75 us
  Pallas kernels  30.6 us (41%)
  starting transfers between devices  15.4 us (20%)
  blocking collectives  9.81 us (13%)
  local copies, waits for them, and re-layouts  9.56 us (13%)
  waiting for transfers between devices  8.72 us (12%)
  between operations  0.85 us (1%)
    pallas_call x3, Pallas kernels, load(): pl.pallas_call(functools.partial(load_kernel, first), out_shape=(pltpu.VM...  14.6 us
    all_to_all x2, starting transfers between devices, between_planes(): lax.all_to_all(value, 'dp', split_axis=0, concat_axis=0, axis_index_group...  11.4 us
    all_to_all x1, blocking collectives, between_planes(): lax.all_to_all(value, 'dp', split_axis=0, concat_axis=0, axis_index_group...  9.81 us
    unnamed x16, local copies, waits for them, and re-layouts  9.56 us
    ppermute x6, waiting for transfers between devices, swap(): return lax.ppermute(value, 'dp', [(i, i ^ bit) for i in range(count)])  7.8 us
    pallas_call x1, Pallas kernels, attend(): pl.pallas_call(attend_kernel, out_shape=(jax.ShapeDtypeStruct((rows, widt...  6.24 us
    pallas_call x1, Pallas kernels, hidden_rows(): pl.pallas_call(hidden_kernel, out_shape=jax.ShapeDtypeStruct((rows, colum...  4.86 us
    ppermute x6, starting transfers between devices, swap(): return lax.ppermute(value, 'dp', [(i, i ^ bit) for i in range(count)])  3.97 us
  transfers between devices with their start and end apart: 8, of which 3 were waited for; matrix products, arithmetic and copies ran while one was open for 0% of the time, Pallas kernels for 23%

profile of v4, /device:TPU:0, one launch (start us, length us, event | category | flops | bytes accessed | tf_op | source)
XLA Modules:
  0.0 75.0 jit_solution(8530424419222501347)
XLA Ops:
  0.6 6.2 %attend.1 = (bf16[8,4096]{1,0:T(8,128)(2,1)}, bf16[32,3072]{1,0:T(8,128)(2,1)}, f32[16,128]{1,0:T(8,128)S(1)}, bf16[4,16,128]{2,1,0:T(8,128)(2,1)S(1)}, bf16[1792,2048]{1,0:T(8,128)(2,1)S(1)}) custom-call(bf16[8,4096]{1,0:T(8,128)(2,1)} %refs_0_.1, bf16[8,32,1024]{2,1,0:T(8,128)(2,1)} %refs_1_.1, bf16[8,1024]{1,0:T(8,128)(2,1)} %refs_2_.1, s32[8]{0:T(128)} %refs_3_.1, ...), custom_call_target="tpu_custom_call" | custom-call | tf_op jit(solution)/shard_map/attend/pallas_call | solution.py:203
  6.9 2.9 %copy-done.1 = bf16[1792,2048]{1,0:T(8,128)(2,1)} copy-done((bf16[1792,2048]{1,0:T(8,128)(2,1)}, bf16[1792,2048]{1,0:T(8,128)(2,1)S(1)}, u32[]{:S(2)}) %copy-start.1) | copy-done | bytes 7340056
  9.8 6.3 %all-to-all-start = ((bf16[4,8,3072]{2,1,0:T(8,128)(2,1)}), bf16[4,8,3072]{2,1,0:T(8,128)(2,1)S(1)}, u32[]{:S(2)}, u32[]{:S(2)}) async-start(bf16[4,8,3072]{2,1,0:T(8,128)(2,1)} %bitcast.3), calls=%async_computation | async-start | bytes 393216 | tf_op jit(solution)/shard_map/all_to_all | solution.py:421
  16.1 5.3 %load.3 = (bf16[4096,1792]{1,0:T(8,128)(2,1)S(1)}, f32[8,128]{1,0:T(8,128)S(1)}) custom-call(bf16[4096,1792]{1,0:T(8,128)(2,1)} %source.3, bf16[32,3072]{1,0:T(8,128)(2,1)} %get-tuple-element.24.after), custom_call_target="tpu_custom_call" | custom-call | bytes 14680064 | tf_op jit(solution)/shard_map/load/pallas_call | solution.py:289
  21.4 5.2 %copy-done = bf16[4096,1792]{1,0:T(8,128)(2,1)} copy-done((bf16[4096,1792]{1,0:T(8,128)(2,1)}, bf16[4096,1792]{1,0:T(8,128)(2,1)S(1)}, u32[]{:S(2)}) %copy-start) | copy-done | bytes 14680088
  26.6 0.0 all-to-all-done
  26.6 0.2 collect.1.after.refs_1_
  26.9 0.0 slice-start
  26.9 1.6 %collective-permute-start = (bf16[24,4096]{1,0:T(8,128)(2,1)S(1)}, bf16[24,4096]{1,0:T(8,128)(2,1)S(1)}, u32[]{:S(2)}, u32[]{:S(2)}) collective-permute-start(bf16[24,4096]{1,0:T(8,128)(2,1)S(1)} %collect.1.after.refs_1_), channel_id=1, source_target_pairs={{0,2},{1,3},{2,0},{3,1},{4,6},{5,7},{6,4},{7,5},{8,10},{9,11},{10,... | collective-permute-start | bytes 589832 | tf_op jit(solution)/shard_map/ppermute | solution.py:427
  28.5 6.0 %load.4 = (bf16[4096,1792]{1,0:T(8,128)(2,1)S(1)}, f32[8,128]{1,0:T(8,128)S(1)}) custom-call(bf16[4096,1792]{1,0:T(8,128)(2,1)} %source.4, bf16[24,4096]{1,0:T(8,128)(2,1)S(1)} %collect.1.after.refs_1_), custom_call_target="tpu_custom_call" | custom-call | bytes 14680064 | tf_op jit(solution)/shard_map/load/pallas_call | solution.py:289
  34.5 0.0 collective-permute-done.refs_2_
  34.5 0.0 slice-start.2
  34.6 0.1 collective-permute-start.1
  34.6 3.3 %load.5 = (bf16[1792,2048]{1,0:T(8,128)(2,1)S(1)}, f32[8,128]{1,0:T(8,128)S(1)}) custom-call(bf16[1792,4096]{1,0:T(8,128)(2,1)} %source.5, bf16[48,4096]{1,0:T(8,128)(2,1)S(1)} %join.2.after.refs_1_), custom_call_target="tpu_custom_call" | custom-call | bytes 7340032 | tf_op jit(solution)/shard_map/load/pallas_call | solution.py:289
  38.0 0.1 join.3.inputs
  38.1 0.8 %slice-done.2 = s8[4194304]{0:T(1024)(128)(4,1)S(1)} async-done(((s8[14680064]{0:T(1024)(128)(4,1)}), s8[4194304]{0:T(1024)(128)(4,1)S(1)}, s32[]{:S(2)}) %slice-start.2) | async-done | bytes 4194328
  38.9 0.6 slice-done.3
  39.5 4.9 %hidden.1 = bf16[96,1792]{1,0:T(8,128)(2,1)S(1)} custom-call(bf16[96,4096]{1,0:T(8,128)(2,1)S(1)} %join.3.inputs, bf16[4096,1792]{1,0:T(8,128)(2,1)S(1)} %bitcast.10, bf16[4096,1792]{1,0:T(8,128)(2,1)S(1)} %get-tuple-element.29.up_weight), custom_call_target="tpu_custom_call" | custom-call | flops 2818572288 | tf_op jit(solution)/shard_map/hidden/pallas_call | solution.py:237
  44.4 1.4 %down.3 = (f32[48,2048]{1,0:T(8,128)S(1)}, bf16[48,2048]{1,0:T(8,128)(2,1)S(1)}) custom-call(bf16[96,1792]{1,0:T(8,128)(2,1)S(1)} %hidden.1, bf16[1792,2048]{1,0:T(8,128)(2,1)S(1)} %get-tuple-element.35.down_weight), custom_call_target="tpu_custom_call" | custom-call | flops 704643072 | tf_op jit(solution)/shard_map/down/pallas_call | solution.py:262
  45.7 0.1 collective-permute-start.4
  45.8 1.4 %down.2 = (f32[48,2048]{1,0:T(8,128)S(1)}, bf16[48,2048]{1,0:T(8,128)(2,1)S(1)}) custom-call(bf16[96,1792]{1,0:T(8,128)(2,1)S(1)} %hidden.1, bf16[1792,2048]{1,0:T(8,128)(2,1)S(1)} %bitcast.12), custom_call_target="tpu_custom_call" | custom-call | flops 704643072 | tf_op jit(solution)/shard_map/down/pallas_call | solution.py:262
  47.2 0.5 collective-permute-start.2
  47.8 0.9 %collective-permute-start.5 = (bf16[24,2048]{1,0:T(8,128)(2,1)S(1)}, bf16[24,2048]{1,0:T(8,128)(2,1)S(1)}, u32[]{:S(2)}, u32[]{:S(2)}) collective-permute-start(bf16[24,2048]{1,0:T(8,128)(2,1)S(1)} %get-tuple-element.39), channel_id=1, source_target_pairs={{0,2},{1,3},{2,0},{3,1},{4,6},{5,7},{6,4},{7,5},{8,10},{9,11},{10,... | collective-permute-start | bytes 294920 | tf_op jit(solution)/shard_map/ppermute | solution.py:427
  48.6 3.9 %collective-permute-done.5.arrived = bf16[24,2048]{1,0:T(8,128)(2,1)S(1)} collective-permute-done((bf16[24,2048]{1,0:T(8,128)(2,1)S(1)}, bf16[24,2048]{1,0:T(8,128)(2,1)S(1)}, u32[]{:S(2)}, u32[]{:S(2)}) %collective-permute-start.5) | collective-permute-done | bytes 98336 | tf_op jit(solution)/shard_map/ppermute | solution.py:427
  52.6 0.8 %last_fold.3 = bf16[32,1536]{1,0:T(8,128)(2,1)} custom-call(f32[24,2048]{1,0:T(8,128)S(1)} %get-tuple-element.38.held, bf16[24,2048]{1,0:T(8,128)(2,1)S(1)} %collective-permute-done.5.arrived), custom_call_target="tpu_custom_call" | custom-call | tf_op jit(solution)/shard_map/last_fold/pallas_call | solution.py:383
  53.4 5.1 %all-to-all-start.2 = ((bf16[4,8,1536]{2,1,0:T(8,128)(2,1)}), bf16[4,8,1536]{2,1,0:T(8,128)(2,1)S(1)}, u32[]{:S(2)}, u32[]{:S(2)}) async-start(bf16[4,8,1536]{2,1,0:T(8,128)(2,1)} %bitcast.7), calls=%async_computation.2 | async-start | bytes 196608 | tf_op jit(solution)/shard_map/all_to_all | solution.py:421
  58.5 0.8 %collective-permute-start.3 = (bf16[24,2048]{1,0:T(8,128)(2,1)S(1)}, bf16[24,2048]{1,0:T(8,128)(2,1)S(1)}, u32[]{:S(2)}, u32[]{:S(2)}) collective-permute-start(bf16[24,2048]{1,0:T(8,128)(2,1)S(1)} %get-tuple-element.34), channel_id=1, source_target_pairs={{0,2},{1,3},{2,0},{3,1},{4,6},{5,7},{6,4},{7,5},{8,10},{9,11},{10,... | collective-permute-start | bytes 294920 | tf_op jit(solution)/shard_map/ppermute | solution.py:427
  59.4 3.8 %collective-permute-done.3.arrived = bf16[24,2048]{1,0:T(8,128)(2,1)S(1)} collective-permute-done((bf16[24,2048]{1,0:T(8,128)(2,1)S(1)}, bf16[24,2048]{1,0:T(8,128)(2,1)S(1)}, u32[]{:S(2)}, u32[]{:S(2)}) %collective-permute-start.3) | collective-permute-done | bytes 98336 | tf_op jit(solution)/shard_map/ppermute | solution.py:427
  63.2 0.2 last_fold.2
  63.4 0.9 %all-to-all-done.2 = bf16[4,8,1536]{2,1,0:T(8,128)(2,1)S(1)} async-done(((bf16[4,8,1536]{2,1,0:T(8,128)(2,1)}), bf16[4,8,1536]{2,1,0:T(8,128)(2,1)S(1)}, u32[]{:S(2)}, u32[]{:S(2)}) %all-to-all-start.2) | async-done | bytes 98336 | tf_op jit(solution)/shard_map/all_to_all | solution.py:421
  64.3 9.8 %all_to_all.33 = bf16[4,8,1536]{2,1,0:T(8,128)(2,1)S(1)} all-to-all(bf16[4,8,1536]{2,1,0:T(8,128)(2,1)S(1)} %bitcast.16), channel_id=1, replica_groups={{0,4,8,12},{1,5,9,13},{2,6,10,14},{3,7,11,15},{16,20,24,28},{17,21,25,2..., dimensions={0} | all-to-all | bytes 196608 | tf_op jit(solution)/shard_map/all_to_all | solution.py:421
  74.1 0.8 %combine.1 = bf16[8,4096]{1,0:T(8,128)(2,1)} custom-call(f32[16,128]{1,0:T(8,128)S(1)} %get-tuple-element.22.share, bf16[4,16,128]{2,1,0:T(8,128)(2,1)S(1)} %get-tuple-element.23.take, bf16[32,1536]{1,0:T(8,128)(2,1)S(1)} %bitcast.15, bf16[32,1536]{1,0:T(8,128)(2,1)S(1)} %bitcast.14), custom_call_target="tpu_custom_call" | custom-call | tf_op jit(solution)/shard_map/combine/pallas_call | solution.py:408
  (18 shorter events, 0.1 us)
Async XLA Ops:
  6.9 2.9 %copy-start.1 = (bf16[1792,2048]{1,0:T(8,128)(2,1)}, bf16[1792,2048]{1,0:T(8,128)(2,1)S(1)}, u32[]{:S(2)}) copy-start(bf16[1792,2048]{1,0:T(8,128)(2,1)S(1)} %get-tuple-element.30.down_weight) | copy-start | bytes 22020100
  9.8 16.8 %all-to-all-start = ((bf16[4,8,3072]{2,1,0:T(8,128)(2,1)}), bf16[4,8,3072]{2,1,0:T(8,128)(2,1)S(1)}, u32[]{:S(2)}, u32[]{:S(2)}) async-start(bf16[4,8,3072]{2,1,0:T(8,128)(2,1)} %bitcast.3), calls=%async_computation | async-start | bytes 393216 | tf_op jit(solution)/shard_map/all_to_all | solution.py:421
  21.4 5.2 %copy-start = (bf16[4096,1792]{1,0:T(8,128)(2,1)}, bf16[4096,1792]{1,0:T(8,128)(2,1)S(1)}, u32[]{:S(2)}) copy-start(bf16[4096,1792]{1,0:T(8,128)(2,1)S(1)} %get-tuple-element.28.gate_weight) | copy-start | bytes 44040196
  26.9 11.2 %slice-start = ((s8[14680064]{0:T(1024)(128)(4,1)}), s8[4194304]{0:T(1024)(128)(4,1)S(1)}, s32[]{:S(2)}) async-start(s8[14680064]{0:T(1024)(128)(4,1)} %bitcast.9), calls=%async_computation.3 | async-start | bytes 8388608
  26.9 11.2 %slice-start.1 = ((s8[14680064]{0:T(1024)(128)(4,1)}), s8[4194304]{0:T(1024)(128)(4,1)S(1)}, s32[]{:S(2)}) async-start(s8[14680064]{0:T(1024)(128)(4,1)} %bitcast.9), calls=%async_computation.4 | async-start | bytes 8388608
  26.9 7.6 %collective-permute-start = (bf16[24,4096]{1,0:T(8,128)(2,1)S(1)}, bf16[24,4096]{1,0:T(8,128)(2,1)S(1)}, u32[]{:S(2)}, u32[]{:S(2)}) collective-permute-start(bf16[24,4096]{1,0:T(8,128)(2,1)S(1)} %collect.1.after.refs_1_), channel_id=1, source_target_pairs={{0,2},{1,3},{2,0},{3,1},{4,6},{5,7},{6,4},{7,5},{8,10},{9,11},{10,... | collective-permute-start | bytes 589832 | tf_op jit(solution)/shard_map/ppermute | solution.py:427
  34.5 4.4 %slice-start.2 = ((s8[14680064]{0:T(1024)(128)(4,1)}), s8[4194304]{0:T(1024)(128)(4,1)S(1)}, s32[]{:S(2)}) async-start(s8[14680064]{0:T(1024)(128)(4,1)} %bitcast.9), calls=%async_computation.5 | async-start | bytes 8388608
  34.5 4.9 %slice-start.3 = ((s8[14680064]{0:T(1024)(128)(4,1)}), s8[2097152]{0:T(1024)(128)(4,1)S(1)}, s32[]{:S(2)}) async-start(s8[14680064]{0:T(1024)(128)(4,1)} %bitcast.9), calls=%async_computation.6 | async-start | bytes 4194304
  34.6 3.4 %collective-permute-start.1 = (bf16[48,4096]{1,0:T(8,128)(2,1)S(1)}, bf16[48,4096]{1,0:T(8,128)(2,1)S(1)}, u32[]{:S(2)}, u32[]{:S(2)}) collective-permute-start(bf16[48,4096]{1,0:T(8,128)(2,1)S(1)} %join.2.after.refs_1_), channel_id=1, source_target_pairs={{0,1},{1,0},{2,3},{3,2},{4,5},{5,4},{6,7},{7,6},{8,9},{9,8},{10,11... | collective-permute-start | bytes 1179656 | tf_op jit(solution)/shard_map/ppermute | solution.py:427
  38.0 7.8 %slice-start.4 = ((s8[7340032]{0:T(1024)(128)(4,1)}), s8[4194304]{0:T(1024)(128)(4,1)S(1)}, s32[]{:S(2)}) async-start(s8[7340032]{0:T(1024)(128)(4,1)} %bitcast.11), calls=%async_computation.7 | async-start | bytes 8388608
  39.5 6.3 %slice-start.5 = ((s8[7340032]{0:T(1024)(128)(4,1)}), s8[3145728]{0:T(1024)(128)(4,1)S(1)}, s32[]{:S(2)}) async-start(s8[7340032]{0:T(1024)(128)(4,1)} %bitcast.11), calls=%async_computation.8 | async-start | bytes 6291456
  45.7 2.0 %collective-permute-start.4 = (bf16[48,2048]{1,0:T(8,128)(2,1)S(1)}, bf16[48,2048]{1,0:T(8,128)(2,1)S(1)}, u32[]{:S(2)}, u32[]{:S(2)}) collective-permute-start(bf16[48,2048]{1,0:T(8,128)(2,1)S(1)} %get-tuple-element.37), channel_id=1, source_target_pairs={{0,1},{1,0},{2,3},{3,2},{4,5},{5,4},{6,7},{7,6},{8,9},{9,8},{10,11... | collective-permute-start | bytes 589832 | tf_op jit(solution)/shard_map/ppermute | solution.py:427
  47.2 11.3 %collective-permute-start.2 = (bf16[48,2048]{1,0:T(8,128)(2,1)S(1)}, bf16[48,2048]{1,0:T(8,128)(2,1)S(1)}, u32[]{:S(2)}, u32[]{:S(2)}) collective-permute-start(bf16[48,2048]{1,0:T(8,128)(2,1)S(1)} %get-tuple-element.32), channel_id=1, source_target_pairs={{0,1},{1,0},{2,3},{3,2},{4,5},{5,4},{6,7},{7,6},{8,9},{9,8},{10,11... | collective-permute-start | bytes 589832 | tf_op jit(solution)/shard_map/ppermute | solution.py:427
  47.8 4.8 %collective-permute-start.5 = (bf16[24,2048]{1,0:T(8,128)(2,1)S(1)}, bf16[24,2048]{1,0:T(8,128)(2,1)S(1)}, u32[]{:S(2)}, u32[]{:S(2)}) collective-permute-start(bf16[24,2048]{1,0:T(8,128)(2,1)S(1)} %get-tuple-element.39), channel_id=1, source_target_pairs={{0,2},{1,3},{2,0},{3,1},{4,6},{5,7},{6,4},{7,5},{8,10},{9,11},{10,... | collective-permute-start | bytes 294920 | tf_op jit(solution)/shard_map/ppermute | solution.py:427
  53.4 10.9 %all-to-all-start.2 = ((bf16[4,8,1536]{2,1,0:T(8,128)(2,1)}), bf16[4,8,1536]{2,1,0:T(8,128)(2,1)S(1)}, u32[]{:S(2)}, u32[]{:S(2)}) async-start(bf16[4,8,1536]{2,1,0:T(8,128)(2,1)} %bitcast.7), calls=%async_computation.2 | async-start | bytes 196608 | tf_op jit(solution)/shard_map/all_to_all | solution.py:421
  58.5 4.7 %collective-permute-start.3 = (bf16[24,2048]{1,0:T(8,128)(2,1)S(1)}, bf16[24,2048]{1,0:T(8,128)(2,1)S(1)}, u32[]{:S(2)}, u32[]{:S(2)}) collective-permute-start(bf16[24,2048]{1,0:T(8,128)(2,1)S(1)} %get-tuple-element.34), channel_id=1, source_target_pairs={{0,2},{1,3},{2,0},{3,1},{4,6},{5,7},{6,4},{7,5},{8,10},{9,11},{10,... | collective-permute-start | bytes 294920 | tf_op jit(solution)/shard_map/ppermute | solution.py:427

commit v5 on v4

--- a/solution.py
+++ b/solution.py
@@ -61,11 +61,11 @@
     return [dot(picks[0], part) for part in parts] + [tail]
 
 
-def attend_kernel(*refs):
-    sources, (attended, packed, share, take), held, semaphores = (
-        refs[:10], refs[11:15], refs[16:26], refs[26]
+def attend_kernel(plane, *refs):
+    sources, attended, packed, (share, take), held, semaphores = (
+        refs[:10], refs[11], refs[12:16], refs[16:18], refs[19:29], refs[29]
     )
-    weight = weight_copies(refs[10], refs[15], refs[27])
+    weight = weight_copies(refs[10], refs[18], refs[30])
     copies = [
         pltpu.make_async_copy(source, target, semaphores.at[i])
         for i, (source, target) in enumerate(zip(sources, held))
@@ -74,7 +74,7 @@
         copy.start()
     (queries, cache_keys, new_keys, lengths, cache_values, new_values, residual, gain, router,
      routes) = held
-    for copy in copies:
+    for copy in copies[:4] + copies[9:]:
         copy.wait()
     rows, width = queries.shape
     positions = cache_keys.shape[1]
@@ -89,9 +89,7 @@
     )
     stacked_b = stacked.astype(BF16)
     keys = cache_keys[...].reshape(every, KV_HEADS * HEAD_DIM)
-    values = cache_values[...].reshape(every, KV_HEADS * HEAD_DIM)
     newk = new_keys[...].astype(F32)
-    newv = new_values[...].astype(F32)
 
     row_of = lax.broadcasted_iota(jnp.int32, (block, every), 0) % rows
     column = lax.broadcasted_iota(jnp.int32, (block, every), 1)
@@ -102,23 +100,39 @@
         limit = jnp.where(column_row == r, lengths[r], limit)
     valid = (row_of == column_row) & (position < limit)
 
-    pieces = []
-    for g in range(KV_HEADS):
-        lanes = slice(g * HEAD_DIM, (g + 1) * HEAD_DIM)
-        mine = slice(g * block, (g + 1) * block)
-        scores = dot(stacked_b[mine], keys[:, lanes], contract_last=True) * scale
-        scores = jnp.where(valid, scores, -jnp.inf)
-        own_key = jnp.concatenate([newk[:, lanes]] * groups, axis=0)
-        new_score = jnp.sum(stacked[mine] * own_key, axis=1, keepdims=True) * scale
-        peak = jnp.maximum(jnp.max(scores, axis=1, keepdims=True), new_score)
-        weights = jnp.exp(scores - peak)
-        new_weight = jnp.exp(new_score - peak)
-        total = jnp.sum(weights, axis=1, keepdims=True) + new_weight
-        probs = (weights / total).astype(BF16)
-        new_prob = (new_weight / total).astype(BF16).astype(F32)
-        own_value = jnp.concatenate([newv[:, lanes]] * groups, axis=0)
-        mixed = dot(probs, values[:, lanes]) + new_prob * own_value
-        pieces += [mixed[j * rows : (j + 1) * rows] for j in range(groups)]
+    heads = range(KV_HEADS)
+    lanes = [slice(g * HEAD_DIM, (g + 1) * HEAD_DIM) for g in heads]
+    mine = [slice(g * block, (g + 1) * block) for g in heads]
+    scores = [dot(stacked_b[mine[g]], keys[:, lanes[g]], contract_last=True) for g in heads]
+    scores = [jnp.where(valid, score * scale, -jnp.inf) for score in scores]
+    own_keys = [jnp.concatenate([newk[:, lanes[g]]] * groups, axis=0) for g in heads]
+    new_scores = [
+        jnp.sum(stacked[mine[g]] * own_keys[g], axis=1, keepdims=True) * scale for g in heads
+    ]
+    peaks = [
+        jnp.maximum(jnp.max(score, axis=1, keepdims=True), new)
+        for score, new in zip(scores, new_scores)
+    ]
+    weights = [jnp.exp(score - peak) for score, peak in zip(scores, peaks)]
+    new_weights = [jnp.exp(new - peak) for new, peak in zip(new_scores, peaks)]
+    totals = [
+        jnp.sum(weight, axis=1, keepdims=True) + new
+        for weight, new in zip(weights, new_weights)
+    ]
+    probs = [(weight / total).astype(BF16) for weight, total in zip(weights, totals)]
+    new_probs = [
+        (new / total).astype(BF16).astype(F32) for new, total in zip(new_weights, totals)
+    ]
+    for copy in copies[4:9]:
+        copy.wait()
+    values = cache_values[...].reshape(every, KV_HEADS * HEAD_DIM)
+    newv = new_values[...].astype(F32)
+    mixed = [
+        dot(probs[g], values[:, lanes[g]])
+        + new_probs[g] * jnp.concatenate([newv[:, lanes[g]]] * groups, axis=0)
+        for g in heads
+    ]
+    pieces = [value[j * rows : (j + 1) * rows] for value in mixed for j in range(groups)]
 
     states = (residual[...].astype(F32) + jnp.concatenate(pieces, axis=1)).astype(BF16)
     attended[...] = states
@@ -135,7 +149,9 @@
             logits[e] += part * router[e : e + 1, lanes].astype(F32)
     logits = [jnp.sum(value, axis=1, keepdims=True) for value in logits]
 
-    base = lax.axis_index("dp") * rows
+    index = lax.axis_index("dp")
+    base = index * rows
+    own = index // plane
     sub, lane = grid((2 * rows, 128))
     expert_down = jnp.zeros((2 * rows, 128), jnp.int32)
     slot_down = jnp.zeros((2 * rows, 128), jnp.int32)
@@ -144,7 +160,7 @@
     slot_across = jnp.zeros((8, 128), jnp.int32)
     counts = [jnp.int32(0)] * EXPERTS
     for r in range(rows):
-        names = [routes[0, base + r], routes[1, base + r]]
+        names = [(routes[c, base + r] + EXPERTS - own) % EXPERTS for c in range(2)]
         for choice, name in ((r, names[0]), (rows + r, names[1])):
             slot = jnp.int32(0)
             for e in range(EXPERTS):
@@ -172,19 +188,21 @@
     normed = jnp.concatenate([normed, normed], axis=0).astype(BF16)
     quarter = width // 4
     for m, value in enumerate(pack([pick[:, : 2 * rows] for pick in picks], normed)):
-        packed[:, m * quarter : (m + 1) * quarter] = value
+        for k, target in enumerate(packed):
+            target[:, m * quarter : (m + 1) * quarter] = value[8 * k : 8 * k + 8]
 
     chosen_logits = jnp.zeros((2 * rows, 1), F32)
     for e in range(EXPERTS):
         both = jnp.concatenate([logits[e], logits[e]], axis=0)
-        chosen_logits = jnp.where(expert_down[:, :1] == e, both, chosen_logits)
+        relative = (e + EXPERTS - own) % EXPERTS
+        chosen_logits = jnp.where(expert_down[:, :1] == relative, both, chosen_logits)
     other = jnp.concatenate([chosen_logits[rows:], chosen_logits[:rows]], axis=0)
     share[...] = jnp.broadcast_to(1.0 / (1.0 + jnp.exp(other - chosen_logits)), share.shape)
     for copy in weight:
         copy.wait()
 
 
-def attend(queries, new_keys, new_values, cache_keys, cache_values, lengths, residual,
+def attend(plane, queries, new_keys, new_values, cache_keys, cache_values, lengths, residual,
            norm_gain, router_weight, routes, weight):
     rows, width = queries.shape
     operands = (
@@ -201,16 +219,16 @@
     )
     in_smem = (3, 9)
     return pl.pallas_call(
-        attend_kernel,
+        functools.partial(attend_kernel, plane),
         out_shape=(
             jax.ShapeDtypeStruct((rows, width), BF16),
-            jax.ShapeDtypeStruct((8 * EXPERTS, width * 3 // 4), BF16),
+            *[jax.ShapeDtypeStruct((8, width * 3 // 4), BF16)] * EXPERTS,
             jax.ShapeDtypeStruct((2 * rows, 128), F32),
             jax.ShapeDtypeStruct((4, 2 * rows, 128), BF16),
             pltpu.VMEM((weight.shape[0], weight.shape[1] // PARTS), weight.dtype),
         ),
         in_specs=[ANY] * (len(operands) + 1),
-        out_specs=(VMEM,) * 5,
+        out_specs=(VMEM,) * (4 + EXPERTS),
         scratch_shapes=[
             (pltpu.SMEM if i in in_smem else pltpu.VMEM)(operand.shape, operand.dtype)
             for i, operand in enumerate(operands)
@@ -224,19 +242,26 @@
 def hidden_kernel(inputs, gate_weight, up_weight, hidden):
     columns = gate_weight.shape[1]
     step = 256 if columns % 256 == 0 else columns
-    x = inputs[...]
+    x = padded(inputs[...])
     for f in range(0, columns, step):
         gate = dot(x, gate_weight[:, f : f + step])
         upper = dot(x, up_weight[:, f : f + step])
         hidden[:, f : f + step] = (gate / (1.0 + jnp.exp(-gate)) * upper).astype(BF16)
 
 
+def padded(x):
+    extra = -x.shape[0] % 128
+    if extra == 0:
+        return x
+    return jnp.concatenate([x, jnp.zeros((extra, x.shape[1]), x.dtype)], axis=0)
+
+
 def hidden_rows(inputs, gate_weight, up_weight):
     rows, width = inputs.shape
     columns = gate_weight.shape[1]
     return pl.pallas_call(
         hidden_kernel,
-        out_shape=jax.ShapeDtypeStruct((rows, columns), BF16),
+        out_shape=jax.ShapeDtypeStruct((rows + -rows % 128, columns), BF16),
         in_specs=[VMEM] * 3,
         out_specs=VMEM,
         compiler_params=pltpu.CompilerParams(vmem_limit_bytes=4 * MIB * max(1, rows // 128)),
@@ -253,11 +278,11 @@
     for n in range(0, width, 512):
         terms = dot(h, down_weight[:, n : n + 512])
         keep[:, n : n + 512] = terms[:half]
-        send[:, n : n + 512] = terms[half:].astype(BF16)
-
-
-def down_rows(hidden, down_weight):
-    rows, columns = hidden.shape
+        send[:, n : n + 512] = terms[half : 2 * half].astype(BF16)
+
+
+def down_rows(hidden, down_weight, rows):
+    columns = hidden.shape[1]
     half, width = rows // 2, down_weight.shape[1]
     return pl.pallas_call(
         down_kernel,
@@ -303,7 +328,8 @@
     )(pltpu.with_memory_space_constraint(source, pltpu.HBM), after)
 
 
-def collect_kernel(arrived, token, gathered):
+def collect_kernel(token, *refs):
+    arrived, gathered = refs[:-1], refs[-1]
     row, lane = grid((MOST * EXPERTS, 8 * EXPERTS))
     plane = sum([jnp.where(row >= MOST * e, 1, 0) for e in range(1, EXPERTS)])
     slot = row - MOST * plane
@@ -312,19 +338,19 @@
     for m in range(3):
         picks.append(one_hot((lane == plane * 8 + 6 + late) & (slot - 3 * late == m)))
     quarter = gathered.shape[1] // 4
-    for m, value in enumerate(unpack(picks, arrived[...])):
+    for m, value in enumerate(unpack(picks, jnp.concatenate([x[...] for x in arrived], axis=0))):
         gathered[:, m * quarter : (m + 1) * quarter] = value.astype(BF16)
 
 
-def collect(arrived, token):
+def collect(token, arrived):
     return pl.pallas_call(
         collect_kernel,
-        out_shape=jax.ShapeDtypeStruct((MOST * EXPERTS, arrived.shape[1] // 3 * 4), BF16),
-        in_specs=[VMEM, ANY],
+        out_shape=jax.ShapeDtypeStruct((MOST * EXPERTS, arrived[0].shape[1] // 3 * 4), BF16),
+        in_specs=[ANY] + [VMEM] * EXPERTS,
         out_specs=VMEM,
         compiler_params=pltpu.CompilerParams(vmem_limit_bytes=2 * MIB),
         name="collect",
-    )(arrived, token)
+    )(token, *arrived)
 
 
 def join_kernel(*refs):
@@ -367,7 +393,7 @@
     )(held, arrived)
 
 
-def last_fold_kernel(held, arrived, packed):
+def last_fold_kernel(held, arrived, *packed):
     block = (held[...] + arrived[...].astype(F32)).astype(BF16)
     place, row = grid((8 * EXPERTS, MOST * EXPERTS))
     plane, slot = place // 8, place % 8
@@ -376,28 +402,30 @@
         picks.append(one_hot((row == plane * MOST + 3 * (slot - 6) + m) & (slot >= MOST)))
     quarter = block.shape[1] // 4
     for m, value in enumerate(pack(picks, block)):
-        packed[:, m * quarter : (m + 1) * quarter] = value
+        for k, target in enumerate(packed):
+            target[:, m * quarter : (m + 1) * quarter] = value[8 * k : 8 * k + 8]
 
 
 def last_fold(held, arrived):
     return pl.pallas_call(
         last_fold_kernel,
-        out_shape=jax.ShapeDtypeStruct((8 * EXPERTS, held.shape[1] // 4 * 3), BF16),
+        out_shape=[jax.ShapeDtypeStruct((8, held.shape[1] // 4 * 3), BF16)] * EXPERTS,
         in_specs=[VMEM] * 2,
-        out_specs=VMEM,
+        out_specs=[VMEM] * EXPERTS,
         compiler_params=pltpu.CompilerParams(vmem_limit_bytes=2 * MIB),
         name="last_fold",
     )(held, arrived)
 
 
 def combine_kernel(share, take, *refs):
-    results, out = refs[:-1], refs[-1]
+    out = refs[-1]
+    results = [refs[p * EXPERTS : (p + 1) * EXPERTS] for p in range(PARTS)]
     rows = out.shape[0]
-    quarter = results[0].shape[1] // 3
+    quarter = refs[0].shape[1] // 3
     picks = [take[i][:, : 8 * EXPERTS] for i in range(4)]
     shares = share[:, :1]
     for part, result in enumerate(results):
-        for m, value in enumerate(unpack(picks, result[...])):
+        for m, value in enumerate(unpack(picks, jnp.concatenate([x[...] for x in result], axis=0))):
             value = value * shares
             first = (part * 4 + m) * quarter
             out[:, first : first + quarter] = (value[:rows] + value[rows:]).astype(BF16)
@@ -415,12 +443,14 @@
     )(share, take, *results)
 
 
-def between_planes(value, count):
+def between_planes(blocks, count, direction):
     plane = count // EXPERTS
-    groups = [[e * plane + p for e in range(EXPERTS)] for p in range(plane)]
-    return lax.all_to_all(
-        value, "dp", split_axis=0, concat_axis=0, axis_index_groups=groups, tiled=True
-    )
+    return [blocks[0]] + [
+        lax.ppermute(
+            blocks[k], "dp", [(i, (i + direction * k * plane) % count) for i in range(count)]
+        )
+        for k in range(1, EXPERTS)
+    ]
 
 
 def swap(value, count, bit):
@@ -445,13 +475,13 @@
     count = lax.axis_size("dp")
     plane = count // EXPERTS
     bits = [1 << k for k in reversed(range(plane.bit_length() - 1))]
-    attended, packed, share, take, down = attend(
-        queries, new_keys, new_values, cache_keys, cache_values, lengths, residual, norm_gain,
+    attended, *packed, share, take, down = attend(
+        plane, queries, new_keys, new_values, cache_keys, cache_values, lengths, residual, norm_gain,
         router_weight, routes, down_weight,
     )
 
-    gate, token = load(gate_weight, packed)
-    gathered = collect(between_planes(packed, count), token)
+    gate, token = load(gate_weight, packed[0])
+    gathered = collect(token, between_planes(packed, count, 1))
     up, token = load(up_weight, gathered)
     gathered = join(token, gathered, swap(gathered, count, bits[0]))
     down_rest, token = load(down_weight, gathered, down.shape[1])
@@ -461,10 +491,11 @@
     hidden = hidden_rows(gathered, gate, up)
     results = []
     for weight in (down, down_rest):
-        held, send = down_rows(hidden, weight)
+        held, send = down_rows(hidden, weight, gathered.shape[0])
         for bit in bits[:0:-1]:
             held, send = fold(held, swap(send, count, bit))
-        results.append(between_planes(last_fold(held, swap(send, count, bits[0])), count))
+        blocks = last_fold(held, swap(send, count, bits[0]))
+        results += between_planes(blocks, count, -1)
     return (attended, combine(share, take, results))
 
 

time: 75.3 us -> 53.5 us (0.71)
  blocking collectives: 9.81 us -> 0 us
  local copies, waits for them, and re-layouts: 9.56 us -> 0 us
  Pallas kernels: 30.6 us -> 25.9 us
  starting transfers between devices: 15.4 us -> 17.8 us
    ppermute x0 -> x9, starting transfers between devices: none -> 14.1 us  [between_planes(): lax.ppermute(blocks[k], 'dp', [(i, (i + direction * k * plane) % count) f...]
    all_to_all x2 -> x0, starting transfers between devices: 11.4 us -> none  [between_planes(): lax.all_to_all(value, 'dp', split_axis=0, concat_axis=0, axis_index_group...]
    all_to_all x1 -> x0, blocking collectives: 9.81 us -> none  [between_planes(): lax.all_to_all(value, 'dp', split_axis=0, concat_axis=0, axis_index_group...]
    unnamed x16 -> x0, local copies, waits for them, and re-layouts: 9.56 us -> none
    ppermute x0 -> x9, waiting for transfers between devices: none -> 4.62 us  [between_planes(): lax.ppermute(blocks[k], 'dp', [(i, (i + direction * k * plane) % count) f...]
    ppermute x6, waiting for transfers between devices: 7.8 us -> 4.27 us  [swap(): return lax.ppermute(value, 'dp', [(i, i ^ bit) for i in range(count)])]
    pallas_call x4, Pallas kernels: 12.1 us -> 8.73 us  [the longest x1 4.33 us: attend(): pl.pallas_call(functools.partial(attend_kernel, plane), out_shape=(jax.Sh...]
    all_to_all x2 -> x0, waiting for transfers between devices: 0.92 us -> none  [between_planes(): lax.all_to_all(value, 'dp', split_axis=0, concat_axis=0, axis_index_group...]
  transfers between devices with their start and end apart: 8 -> 15, of which waited for: 3 -> 5; matrix products, arithmetic and copies ran while one was open for 0% -> 0% of each run, Pallas kernels for 23% -> 29%
where the time goes in v5:
time: 53.5 us; the launch traced here: 53.4 us
  Pallas kernels  25.9 us (48%)
  starting transfers between devices  17.8 us (33%)
  waiting for transfers between devices  8.89 us (17%)
  between operations  0.8 us (1%)
    ppermute x9, starting transfers between devices, between_planes(): lax.ppermute(blocks[k], 'dp', [(i, (i + direction * k * plane) % count) f...  14.1 us
    pallas_call x3, Pallas kernels, load(): pl.pallas_call(functools.partial(load_kernel, first), out_shape=(pltpu.VM...  13.8 us
    ppermute x9, waiting for transfers between devices, between_planes(): lax.ppermute(blocks[k], 'dp', [(i, (i + direction * k * plane) % count) f...  4.62 us
    pallas_call x1, Pallas kernels, attend(): pl.pallas_call(functools.partial(attend_kernel, plane), out_shape=(jax.Sh...  4.33 us
    ppermute x6, waiting for transfers between devices, swap(): return lax.ppermute(value, 'dp', [(i, i ^ bit) for i in range(count)])  4.27 us
    pallas_call x1, Pallas kernels, hidden_rows(): pl.pallas_call(hidden_kernel, out_shape=jax.ShapeDtypeStruct((rows + -row...  4.04 us
    ppermute x6, starting transfers between devices, swap(): return lax.ppermute(value, 'dp', [(i, i ^ bit) for i in range(count)])  3.66 us
    pallas_call x2, Pallas kernels, down_rows(): pl.pallas_call(down_kernel, out_shape=(jax.ShapeDtypeStruct((half, width)...  2.25 us
  transfers between devices with their start and end apart: 15, of which 5 were waited for; matrix products, arithmetic and copies ran while one was open for 0% of the time, Pallas kernels for 29%

profile of v5, /device:TPU:0, one launch (start us, length us, event | category | flops | bytes accessed | tf_op | source)
XLA Modules:
  0.0 53.4 jit_solution(12946785337948246249)
XLA Ops:
  0.6 4.3 %attend.1 = (bf16[8,4096]{1,0:T(8,128)(2,1)}, bf16[8,3072]{1,0:T(8,128)(2,1)S(1)}, bf16[8,3072]{1,0:T(8,128)(2,1)S(1)}, bf16[8,3072]{1,0:T(8,128)(2,1)S(1)}, bf1...) custom-call(bf16[8,4096]{1,0:T(8,128)(2,1)} %refs_0_.1, ...), custom_call_target="tpu_custom_call" | custom-call | tf_op jit(solution)/shard_map/attend/pallas_call | solution.py:221
  5.0 3.1 %collective-permute-start = (bf16[8,3072]{1,0:T(8,128)(2,1)S(1)}, bf16[8,3072]{1,0:T(8,128)(2,1)S(1)}, u32[]{:S(2)}, u32[]{:S(2)}) collective-permute-start(bf16[8,3072]{1,0:T(8,128)(2,1)S(1)} %get-tuple-element.37), channel_id=1, source_target_pairs={{0,4},{1,5},{2,6},{3,7},{4,8},{5,9},{6,10},{7,11},{8,12},{9,13},{1... | collective-permute-start | bytes 147464 | tf_op jit(solution)/shard_map/ppermute | solution.py:449
  8.1 2.6 %collective-permute-start.1 = (bf16[8,3072]{1,0:T(8,128)(2,1)S(1)}, bf16[8,3072]{1,0:T(8,128)(2,1)S(1)}, u32[]{:S(2)}, u32[]{:S(2)}) collective-permute-start(bf16[8,3072]{1,0:T(8,128)(2,1)S(1)} %get-tuple-element.38), channel_id=1, source_target_pairs={{0,8},{1,9},{2,10},{3,11},{4,12},{5,13},{6,14},{7,15},{8,0},{9,1},... | collective-permute-start | bytes 147464 | tf_op jit(solution)/shard_map/ppermute | solution.py:449
  10.6 1.3 %collective-permute-start.2 = (bf16[8,3072]{1,0:T(8,128)(2,1)S(1)}, bf16[8,3072]{1,0:T(8,128)(2,1)S(1)}, u32[]{:S(2)}, u32[]{:S(2)}) collective-permute-start(bf16[8,3072]{1,0:T(8,128)(2,1)S(1)} %get-tuple-element.39), channel_id=1, source_target_pairs={{0,12},{1,13},{2,14},{3,15},{4,0},{5,1},{6,2},{7,3},{8,4},{9,5},{1... | collective-permute-start | bytes 147464 | tf_op jit(solution)/shard_map/ppermute | solution.py:449
  12.0 5.3 %load.3 = (bf16[4096,1792]{1,0:T(8,128)(2,1)S(1)}, f32[8,128]{1,0:T(8,128)S(1)}) custom-call(bf16[4096,1792]{1,0:T(8,128)(2,1)} %source.3, bf16[8,3072]{1,0:T(8,128)(2,1)S(1)} %get-tuple-element.35.after.refs_0_), custom_call_target="tpu_custom_call" | custom-call | bytes 14680064 | tf_op jit(solution)/shard_map/load/pallas_call | solution.py:314
  17.3 0.0 collective-permute-done.1.refs_2_
  17.3 0.2 collect.1.after.refs_1_
  17.6 1.6 %collective-permute-start.3 = (bf16[24,4096]{1,0:T(8,128)(2,1)S(1)}, bf16[24,4096]{1,0:T(8,128)(2,1)S(1)}, u32[]{:S(2)}, u32[]{:S(2)}) collective-permute-start(bf16[24,4096]{1,0:T(8,128)(2,1)S(1)} %collect.1.after.refs_1_), channel_id=1, source_target_pairs={{0,2},{1,3},{2,0},{3,1},{4,6},{5,7},{6,4},{7,5},{8,10},{9,11},{10,... | collective-permute-start | bytes 589832 | tf_op jit(solution)/shard_map/ppermute | solution.py:457
  19.2 5.3 %load.4 = (bf16[4096,1792]{1,0:T(8,128)(2,1)S(1)}, f32[8,128]{1,0:T(8,128)S(1)}) custom-call(bf16[4096,1792]{1,0:T(8,128)(2,1)} %source.4, bf16[24,4096]{1,0:T(8,128)(2,1)S(1)} %collect.1.after.refs_1_), custom_call_target="tpu_custom_call" | custom-call | bytes 14680064 | tf_op jit(solution)/shard_map/load/pallas_call | solution.py:314
  24.5 0.1 collective-permute-start.4
  24.6 3.2 %load.5 = (bf16[1792,2048]{1,0:T(8,128)(2,1)S(1)}, f32[8,128]{1,0:T(8,128)S(1)}) custom-call(bf16[1792,4096]{1,0:T(8,128)(2,1)} %source.5, bf16[48,4096]{1,0:T(8,128)(2,1)S(1)} %join.2.after.refs_1_), custom_call_target="tpu_custom_call" | custom-call | bytes 7340032 | tf_op jit(solution)/shard_map/load/pallas_call | solution.py:314
  27.8 0.1 join.3.inputs
  27.8 4.0 %hidden.1 = bf16[128,1792]{1,0:T(8,128)(2,1)S(1)} custom-call(bf16[96,4096]{1,0:T(8,128)(2,1)S(1)} %join.3.inputs, bf16[4096,1792]{1,0:T(8,128)(2,1)S(1)} %get-tuple-element.42.gate_weight, bf16[4096,1792]{1,0:T(8,128)(2,1)S(1)} %get-tuple-element.43.up_weight), custom_call_target="tpu_custom_call" | custom-call | flops 2818572288 | tf_op jit(solution)/shard_map/hidden/pallas_call | solution.py:262
  31.9 1.1 %down.3 = (f32[48,2048]{1,0:T(8,128)S(1)}, bf16[48,2048]{1,0:T(8,128)(2,1)S(1)}) custom-call(bf16[128,1792]{1,0:T(8,128)(2,1)S(1)} %hidden.1, bf16[1792,2048]{1,0:T(8,128)(2,1)S(1)} %get-tuple-element.53.down_weight), custom_call_target="tpu_custom_call" | custom-call | flops 704643072 | tf_op jit(solution)/shard_map/down/pallas_call | solution.py:287
  33.0 0.6 %collective-permute-start.10 = (bf16[48,2048]{1,0:T(8,128)(2,1)S(1)}, bf16[48,2048]{1,0:T(8,128)(2,1)S(1)}, u32[]{:S(2)}, u32[]{:S(2)}) collective-permute-start(bf16[48,2048]{1,0:T(8,128)(2,1)S(1)} %get-tuple-element.55), channel_id=1, source_target_pairs={{0,1},{1,0},{2,3},{3,2},{4,5},{5,4},{6,7},{7,6},{8,9},{9,8},{10,11... | collective-permute-start | bytes 589832 | tf_op jit(solution)/shard_map/ppermute | solution.py:457
  33.6 1.1 %down.2 = (f32[48,2048]{1,0:T(8,128)S(1)}, bf16[48,2048]{1,0:T(8,128)(2,1)S(1)}) custom-call(bf16[128,1792]{1,0:T(8,128)(2,1)S(1)} %hidden.1, bf16[1792,2048]{1,0:T(8,128)(2,1)S(1)} %get-tuple-element.44.down_weight), custom_call_target="tpu_custom_call" | custom-call | flops 704643072 | tf_op jit(solution)/shard_map/down/pallas_call | solution.py:287
  34.7 0.1 collective-permute-start.5
  34.8 0.6 %collective-permute-start.11 = (bf16[24,2048]{1,0:T(8,128)(2,1)S(1)}, bf16[24,2048]{1,0:T(8,128)(2,1)S(1)}, u32[]{:S(2)}, u32[]{:S(2)}) collective-permute-start(bf16[24,2048]{1,0:T(8,128)(2,1)S(1)} %get-tuple-element.57), channel_id=1, source_target_pairs={{0,2},{1,3},{2,0},{3,1},{4,6},{5,7},{6,4},{7,5},{8,10},{9,11},{10,... | collective-permute-start | bytes 294920 | tf_op jit(solution)/shard_map/ppermute | solution.py:457
  35.4 0.8 %collective-permute-done.5.arrived = bf16[48,2048]{1,0:T(8,128)(2,1)S(1)} collective-permute-done((bf16[48,2048]{1,0:T(8,128)(2,1)S(1)}, bf16[48,2048]{1,0:T(8,128)(2,1)S(1)}, u32[]{:S(2)}, u32[]{:S(2)}) %collective-permute-start.5) | collective-permute-done | bytes 196640 | tf_op jit(solution)/shard_map/ppermute | solution.py:457
  36.3 0.8 %collective-permute-start.6 = (bf16[24,2048]{1,0:T(8,128)(2,1)S(1)}, bf16[24,2048]{1,0:T(8,128)(2,1)S(1)}, u32[]{:S(2)}, u32[]{:S(2)}) collective-permute-start(bf16[24,2048]{1,0:T(8,128)(2,1)S(1)} %get-tuple-element.48), channel_id=1, source_target_pairs={{0,2},{1,3},{2,0},{3,1},{4,6},{5,7},{6,4},{7,5},{8,10},{9,11},{10,... | collective-permute-start | bytes 294920 | tf_op jit(solution)/shard_map/ppermute | solution.py:457
  37.0 3.5 %collective-permute-done.11.arrived = bf16[24,2048]{1,0:T(8,128)(2,1)S(1)} collective-permute-done((bf16[24,2048]{1,0:T(8,128)(2,1)S(1)}, bf16[24,2048]{1,0:T(8,128)(2,1)S(1)}, u32[]{:S(2)}, u32[]{:S(2)}) %collective-permute-start.11) | collective-permute-done | bytes 98336 | tf_op jit(solution)/shard_map/ppermute | solution.py:457
  40.5 0.2 last_fold.3
  40.7 0.6 %collective-permute-start.12 = (bf16[8,1536]{1,0:T(8,128)(2,1)S(1)}, bf16[8,1536]{1,0:T(8,128)(2,1)S(1)}, u32[]{:S(2)}, u32[]{:S(2)}) collective-permute-start(bf16[8,1536]{1,0:T(8,128)(2,1)S(1)} %get-tuple-element.59), channel_id=1, source_target_pairs={{0,12},{1,13},{2,14},{3,15},{4,0},{5,1},{6,2},{7,3},{8,4},{9,5},{1... | collective-permute-start | bytes 73736 | tf_op jit(solution)/shard_map/ppermute | solution.py:449
  41.3 1.6 %collective-permute-start.13 = (bf16[8,1536]{1,0:T(8,128)(2,1)S(1)}, bf16[8,1536]{1,0:T(8,128)(2,1)S(1)}, u32[]{:S(2)}, u32[]{:S(2)}) collective-permute-start(bf16[8,1536]{1,0:T(8,128)(2,1)S(1)} %get-tuple-element.60), channel_id=1, source_target_pairs={{0,8},{1,9},{2,10},{3,11},{4,12},{5,13},{6,14},{7,15},{8,0},{9,1},... | collective-permute-start | bytes 73736 | tf_op jit(solution)/shard_map/ppermute | solution.py:449
  42.9 0.2 collective-permute-start.14
  43.1 0.2 last_fold.2
  43.3 3.7 %collective-permute-start.7 = (bf16[8,1536]{1,0:T(8,128)(2,1)S(1)}, bf16[8,1536]{1,0:T(8,128)(2,1)S(1)}, u32[]{:S(2)}, u32[]{:S(2)}) collective-permute-start(bf16[8,1536]{1,0:T(8,128)(2,1)S(1)} %get-tuple-element.50), channel_id=1, source_target_pairs={{0,12},{1,13},{2,14},{3,15},{4,0},{5,1},{6,2},{7,3},{8,4},{9,5},{1... | collective-permute-start | bytes 73736 | tf_op jit(solution)/shard_map/ppermute | solution.py:449
  47.0 1.0 %collective-permute-start.9 = (bf16[8,1536]{1,0:T(8,128)(2,1)S(1)}, bf16[8,1536]{1,0:T(8,128)(2,1)S(1)}, u32[]{:S(2)}, u32[]{:S(2)}) collective-permute-start(bf16[8,1536]{1,0:T(8,128)(2,1)S(1)} %get-tuple-element.52), channel_id=1, source_target_pairs={{0,4},{1,5},{2,6},{3,7},{4,8},{5,9},{6,10},{7,11},{8,12},{9,13},{1... | collective-permute-start | bytes 73736 | tf_op jit(solution)/shard_map/ppermute | solution.py:449
  48.0 0.6 %collective-permute-done.14.refs_7_ = bf16[8,1536]{1,0:T(8,128)(2,1)S(1)} collective-permute-done((bf16[8,1536]{1,0:T(8,128)(2,1)S(1)}, bf16[8,1536]{1,0:T(8,128)(2,1)S(1)}, u32[]{:S(2)}, u32[]{:S(2)}) %collective-permute-start.14) | collective-permute-done | bytes 24608 | tf_op jit(solution)/shard_map/ppermute | solution.py:449
  48.6 3.1 %collective-permute-done.8.refs_2_ = bf16[8,1536]{1,0:T(8,128)(2,1)S(1)} collective-permute-done((bf16[8,1536]{1,0:T(8,128)(2,1)S(1)}, bf16[8,1536]{1,0:T(8,128)(2,1)S(1)}, u32[]{:S(2)}, u32[]{:S(2)}) %collective-permute-start.8) | collective-permute-done | bytes 24608 | tf_op jit(solution)/shard_map/ppermute | solution.py:449
  51.7 0.9 %collective-permute-done.9.refs_3_ = bf16[8,1536]{1,0:T(8,128)(2,1)S(1)} collective-permute-done((bf16[8,1536]{1,0:T(8,128)(2,1)S(1)}, bf16[8,1536]{1,0:T(8,128)(2,1)S(1)}, u32[]{:S(2)}, u32[]{:S(2)}) %collective-permute-start.9) | collective-permute-done | bytes 24608 | tf_op jit(solution)/shard_map/ppermute | solution.py:449
  52.6 0.8 %combine.1 = bf16[8,4096]{1,0:T(8,128)(2,1)} custom-call(f32[16,128]{1,0:T(8,128)S(1)} %get-tuple-element.33.share, bf16[4,16,128]{2,1,0:T(8,128)(2,1)S(1)} %get-tuple-element.34.take, bf16[8,1536]{1,0:T(8,128)(2,1)S(1)} %get-tuple-element.49.refs_0_, bf16[8,1536]{1,0:T(8,128)(2,1)S(1)} %collective-permute-done.7.refs_1_, ...), custom_call_target="tpu_custom_call" | custom-call | tf_op jit(solution)/shard_map/combine/pallas_call | solution.py:436
  (13 shorter events, 0.1 us)
Async XLA Ops:
  5.0 12.3 %collective-permute-start = (bf16[8,3072]{1,0:T(8,128)(2,1)S(1)}, bf16[8,3072]{1,0:T(8,128)(2,1)S(1)}, u32[]{:S(2)}, u32[]{:S(2)}) collective-permute-start(bf16[8,3072]{1,0:T(8,128)(2,1)S(1)} %get-tuple-element.37), channel_id=1, source_target_pairs={{0,4},{1,5},{2,6},{3,7},{4,8},{5,9},{6,10},{7,11},{8,12},{9,13},{1... | collective-permute-start | bytes 147464 | tf_op jit(solution)/shard_map/ppermute | solution.py:449
  8.1 9.2 %collective-permute-start.1 = (bf16[8,3072]{1,0:T(8,128)(2,1)S(1)}, bf16[8,3072]{1,0:T(8,128)(2,1)S(1)}, u32[]{:S(2)}, u32[]{:S(2)}) collective-permute-start(bf16[8,3072]{1,0:T(8,128)(2,1)S(1)} %get-tuple-element.38), channel_id=1, source_target_pairs={{0,8},{1,9},{2,10},{3,11},{4,12},{5,13},{6,14},{7,15},{8,0},{9,1},... | collective-permute-start | bytes 147464 | tf_op jit(solution)/shard_map/ppermute | solution.py:449
  10.6 6.7 %collective-permute-start.2 = (bf16[8,3072]{1,0:T(8,128)(2,1)S(1)}, bf16[8,3072]{1,0:T(8,128)(2,1)S(1)}, u32[]{:S(2)}, u32[]{:S(2)}) collective-permute-start(bf16[8,3072]{1,0:T(8,128)(2,1)S(1)} %get-tuple-element.39), channel_id=1, source_target_pairs={{0,12},{1,13},{2,14},{3,15},{4,0},{5,1},{6,2},{7,3},{8,4},{9,5},{1... | collective-permute-start | bytes 147464 | tf_op jit(solution)/shard_map/ppermute | solution.py:449
  17.6 6.9 %collective-permute-start.3 = (bf16[24,4096]{1,0:T(8,128)(2,1)S(1)}, bf16[24,4096]{1,0:T(8,128)(2,1)S(1)}, u32[]{:S(2)}, u32[]{:S(2)}) collective-permute-start(bf16[24,4096]{1,0:T(8,128)(2,1)S(1)} %collect.1.after.refs_1_), channel_id=1, source_target_pairs={{0,2},{1,3},{2,0},{3,1},{4,6},{5,7},{6,4},{7,5},{8,10},{9,11},{10,... | collective-permute-start | bytes 589832 | tf_op jit(solution)/shard_map/ppermute | solution.py:457
  24.5 3.3 %collective-permute-start.4 = (bf16[48,4096]{1,0:T(8,128)(2,1)S(1)}, bf16[48,4096]{1,0:T(8,128)(2,1)S(1)}, u32[]{:S(2)}, u32[]{:S(2)}) collective-permute-start(bf16[48,4096]{1,0:T(8,128)(2,1)S(1)} %join.2.after.refs_1_), channel_id=1, source_target_pairs={{0,1},{1,0},{2,3},{3,2},{4,5},{5,4},{6,7},{7,6},{8,9},{9,8},{10,11... | collective-permute-start | bytes 1179656 | tf_op jit(solution)/shard_map/ppermute | solution.py:457
  33.0 1.8 %collective-permute-start.10 = (bf16[48,2048]{1,0:T(8,128)(2,1)S(1)}, bf16[48,2048]{1,0:T(8,128)(2,1)S(1)}, u32[]{:S(2)}, u32[]{:S(2)}) collective-permute-start(bf16[48,2048]{1,0:T(8,128)(2,1)S(1)} %get-tuple-element.55), channel_id=1, source_target_pairs={{0,1},{1,0},{2,3},{3,2},{4,5},{5,4},{6,7},{7,6},{8,9},{9,8},{10,11... | collective-permute-start | bytes 589832 | tf_op jit(solution)/shard_map/ppermute | solution.py:457
  34.7 1.5 %collective-permute-start.5 = (bf16[48,2048]{1,0:T(8,128)(2,1)S(1)}, bf16[48,2048]{1,0:T(8,128)(2,1)S(1)}, u32[]{:S(2)}, u32[]{:S(2)}) collective-permute-start(bf16[48,2048]{1,0:T(8,128)(2,1)S(1)} %get-tuple-element.46), channel_id=1, source_target_pairs={{0,1},{1,0},{2,3},{3,2},{4,5},{5,4},{6,7},{7,6},{8,9},{9,8},{10,11... | collective-permute-start | bytes 589832 | tf_op jit(solution)/shard_map/ppermute | solution.py:457
  34.8 5.7 %collective-permute-start.11 = (bf16[24,2048]{1,0:T(8,128)(2,1)S(1)}, bf16[24,2048]{1,0:T(8,128)(2,1)S(1)}, u32[]{:S(2)}, u32[]{:S(2)}) collective-permute-start(bf16[24,2048]{1,0:T(8,128)(2,1)S(1)} %get-tuple-element.57), channel_id=1, source_target_pairs={{0,2},{1,3},{2,0},{3,1},{4,6},{5,7},{6,4},{7,5},{8,10},{9,11},{10,... | collective-permute-start | bytes 294920 | tf_op jit(solution)/shard_map/ppermute | solution.py:457
  36.3 6.8 %collective-permute-start.6 = (bf16[24,2048]{1,0:T(8,128)(2,1)S(1)}, bf16[24,2048]{1,0:T(8,128)(2,1)S(1)}, u32[]{:S(2)}, u32[]{:S(2)}) collective-permute-start(bf16[24,2048]{1,0:T(8,128)(2,1)S(1)} %get-tuple-element.48), channel_id=1, source_target_pairs={{0,2},{1,3},{2,0},{3,1},{4,6},{5,7},{6,4},{7,5},{8,10},{9,11},{10,... | collective-permute-start | bytes 294920 | tf_op jit(solution)/shard_map/ppermute | solution.py:457
  40.7 6.3 %collective-permute-start.12 = (bf16[8,1536]{1,0:T(8,128)(2,1)S(1)}, bf16[8,1536]{1,0:T(8,128)(2,1)S(1)}, u32[]{:S(2)}, u32[]{:S(2)}) collective-permute-start(bf16[8,1536]{1,0:T(8,128)(2,1)S(1)} %get-tuple-element.59), channel_id=1, source_target_pairs={{0,12},{1,13},{2,14},{3,15},{4,0},{5,1},{6,2},{7,3},{8,4},{9,5},{1... | collective-permute-start | bytes 73736 | tf_op jit(solution)/shard_map/ppermute | solution.py:449
  41.3 6.7 %collective-permute-start.13 = (bf16[8,1536]{1,0:T(8,128)(2,1)S(1)}, bf16[8,1536]{1,0:T(8,128)(2,1)S(1)}, u32[]{:S(2)}, u32[]{:S(2)}) collective-permute-start(bf16[8,1536]{1,0:T(8,128)(2,1)S(1)} %get-tuple-element.60), channel_id=1, source_target_pairs={{0,8},{1,9},{2,10},{3,11},{4,12},{5,13},{6,14},{7,15},{8,0},{9,1},... | collective-permute-start | bytes 73736 | tf_op jit(solution)/shard_map/ppermute | solution.py:449
  42.9 5.7 %collective-permute-start.14 = (bf16[8,1536]{1,0:T(8,128)(2,1)S(1)}, bf16[8,1536]{1,0:T(8,128)(2,1)S(1)}, u32[]{:S(2)}, u32[]{:S(2)}) collective-permute-start(bf16[8,1536]{1,0:T(8,128)(2,1)S(1)} %get-tuple-element.61), channel_id=1, source_target_pairs={{0,4},{1,5},{2,6},{3,7},{4,8},{5,9},{6,10},{7,11},{8,12},{9,13},{1... | collective-permute-start | bytes 73736 | tf_op jit(solution)/shard_map/ppermute | solution.py:449
  43.3 5.3 %collective-permute-start.7 = (bf16[8,1536]{1,0:T(8,128)(2,1)S(1)}, bf16[8,1536]{1,0:T(8,128)(2,1)S(1)}, u32[]{:S(2)}, u32[]{:S(2)}) collective-permute-start(bf16[8,1536]{1,0:T(8,128)(2,1)S(1)} %get-tuple-element.50), channel_id=1, source_target_pairs={{0,12},{1,13},{2,14},{3,15},{4,0},{5,1},{6,2},{7,3},{8,4},{9,5},{1... | collective-permute-start | bytes 73736 | tf_op jit(solution)/shard_map/ppermute | solution.py:449
  46.9 4.7 %collective-permute-start.8 = (bf16[8,1536]{1,0:T(8,128)(2,1)S(1)}, bf16[8,1536]{1,0:T(8,128)(2,1)S(1)}, u32[]{:S(2)}, u32[]{:S(2)}) collective-permute-start(bf16[8,1536]{1,0:T(8,128)(2,1)S(1)} %get-tuple-element.51), channel_id=1, source_target_pairs={{0,8},{1,9},{2,10},{3,11},{4,12},{5,13},{6,14},{7,15},{8,0},{9,1},... | collective-permute-start | bytes 73736 | tf_op jit(solution)/shard_map/ppermute | solution.py:449
  47.0 5.6 %collective-permute-start.9 = (bf16[8,1536]{1,0:T(8,128)(2,1)S(1)}, bf16[8,1536]{1,0:T(8,128)(2,1)S(1)}, u32[]{:S(2)}, u32[]{:S(2)}) collective-permute-start(bf16[8,1536]{1,0:T(8,128)(2,1)S(1)} %get-tuple-element.52), channel_id=1, source_target_pairs={{0,4},{1,5},{2,6},{3,7},{4,8},{5,9},{6,10},{7,11},{8,12},{9,13},{1... | collective-permute-start | bytes 73736 | tf_op jit(solution)/shard_map/ppermute | solution.py:449

commit v6 on v5

--- a/solution.py
+++ b/solution.py
@@ -480,15 +480,12 @@
         router_weight, routes, down_weight,
     )
 
-    gate, token = load(gate_weight, packed[0])
-    gathered = collect(token, between_planes(packed, count, 1))
-    up, token = load(up_weight, gathered)
-    gathered = join(token, gathered, swap(gathered, count, bits[0]))
+    gathered = collect(share, between_planes(packed, count, 1))
     down_rest, token = load(down_weight, gathered, down.shape[1])
-    for bit in bits[1:]:
+    for bit in bits:
         gathered = join(token, gathered, swap(gathered, count, bit))
 
-    hidden = hidden_rows(gathered, gate, up)
+    hidden = hidden_rows(gathered, gate_weight, up_weight)
     results = []
     for weight in (down, down_rest):
         held, send = down_rows(hidden, weight, gathered.shape[0])

time: 53.5 us -> 50.7 us (0.948)
  Pallas kernels: 25.9 us -> 15.7 us
  waiting for transfers between devices: 8.89 us -> 14.1 us
  starting transfers between devices: 17.8 us -> 19.9 us
    pallas_call x3 -> x1, Pallas kernels: 13.8 us -> 3.32 us  [load(): pl.pallas_call(functools.partial(load_kernel, first), out_shape=(pltpu.VM...]
    ppermute x9, waiting for transfers between devices: 4.62 us -> 8.38 us  [between_planes(): lax.ppermute(blocks[k], 'dp', [(i, (i + direction * k * plane) % count) f...]
    ppermute x6, waiting for transfers between devices: 4.27 us -> 5.76 us  [swap(): return lax.ppermute(value, 'dp', [(i, i ^ bit) for i in range(count)])]
    ppermute x6, starting transfers between devices: 3.66 us -> 4.93 us  [swap(): return lax.ppermute(value, 'dp', [(i, i ^ bit) for i in range(count)])]
    ppermute x9, starting transfers between devices: 14.1 us -> 14.9 us  [between_planes(): lax.ppermute(blocks[k], 'dp', [(i, (i + direction * k * plane) % count) f...]
  transfers between devices with their start and end apart: 15 -> 15, of which waited for: 5 -> 10; matrix products, arithmetic and copies ran while one was open for 0% -> 0% of each run, Pallas kernels for 29% -> 10%
where the time goes in v6:
time: 50.7 us; the launch traced here: 50.6 us
  starting transfers between devices  19.9 us (39%)
  Pallas kernels  15.7 us (31%)
  waiting for transfers between devices  14.1 us (28%)
  between operations  0.82 us (2%)
    ppermute x9, starting transfers between devices, between_planes(): lax.ppermute(blocks[k], 'dp', [(i, (i + direction * k * plane) % count) f...  14.9 us
    ppermute x9, waiting for transfers between devices, between_planes(): lax.ppermute(blocks[k], 'dp', [(i, (i + direction * k * plane) % count) f...  8.38 us
    ppermute x6, waiting for transfers between devices, swap(): return lax.ppermute(value, 'dp', [(i, i ^ bit) for i in range(count)])  5.76 us
    ppermute x6, starting transfers between devices, swap(): return lax.ppermute(value, 'dp', [(i, i ^ bit) for i in range(count)])  4.93 us
    pallas_call x1, Pallas kernels, attend(): pl.pallas_call(functools.partial(attend_kernel, plane), out_shape=(jax.Sh...  4.45 us
    pallas_call x1, Pallas kernels, hidden_rows(): pl.pallas_call(hidden_kernel, out_shape=jax.ShapeDtypeStruct((rows + -row...  4.12 us
    pallas_call x1, Pallas kernels, load(): pl.pallas_call(functools.partial(load_kernel, first), out_shape=(pltpu.VM...  3.32 us
    pallas_call x2, Pallas kernels, down_rows(): pl.pallas_call(down_kernel, out_shape=(jax.ShapeDtypeStruct((half, width)...  2.26 us
  transfers between devices with their start and end apart: 15, of which 10 were waited for; matrix products, arithmetic and copies ran while one was open for 0% of the time, Pallas kernels for 10%

profile of v6, /device:TPU:0, one launch (start us, length us, event | category | flops | bytes accessed | tf_op | source)
XLA Modules:
  0.0 50.6 jit_solution(14909606279074289724)
XLA Ops:
  0.7 4.5 %attend.1 = (bf16[8,4096]{1,0:T(8,128)(2,1)}, bf16[8,3072]{1,0:T(8,128)(2,1)S(1)}, bf16[8,3072]{1,0:T(8,128)(2,1)S(1)}, bf16[8,3072]{1,0:T(8,128)(2,1)S(1)}, bf1...) custom-call(bf16[8,4096]{1,0:T(8,128)(2,1)} %refs_0_.1, ...), custom_call_target="tpu_custom_call" | custom-call | tf_op jit(solution)/shard_map/attend/pallas_call | solution.py:221
  5.1 3.1 %collective-permute-start = (bf16[8,3072]{1,0:T(8,128)(2,1)S(1)}, bf16[8,3072]{1,0:T(8,128)(2,1)S(1)}, u32[]{:S(2)}, u32[]{:S(2)}) collective-permute-start(bf16[8,3072]{1,0:T(8,128)(2,1)S(1)} %get-tuple-element.32), channel_id=1, source_target_pairs={{0,4},{1,5},{2,6},{3,7},{4,8},{5,9},{6,10},{7,11},{8,12},{9,13},{1... | collective-permute-start | bytes 147464 | tf_op jit(solution)/shard_map/ppermute | solution.py:449
  8.2 2.6 %collective-permute-start.1 = (bf16[8,3072]{1,0:T(8,128)(2,1)S(1)}, bf16[8,3072]{1,0:T(8,128)(2,1)S(1)}, u32[]{:S(2)}, u32[]{:S(2)}) collective-permute-start(bf16[8,3072]{1,0:T(8,128)(2,1)S(1)} %get-tuple-element.33), channel_id=1, source_target_pairs={{0,8},{1,9},{2,10},{3,11},{4,12},{5,13},{6,14},{7,15},{8,0},{9,1},... | collective-permute-start | bytes 147464 | tf_op jit(solution)/shard_map/ppermute | solution.py:449
  10.8 1.3 %collective-permute-start.2 = (bf16[8,3072]{1,0:T(8,128)(2,1)S(1)}, bf16[8,3072]{1,0:T(8,128)(2,1)S(1)}, u32[]{:S(2)}, u32[]{:S(2)}) collective-permute-start(bf16[8,3072]{1,0:T(8,128)(2,1)S(1)} %get-tuple-element.34), channel_id=1, source_target_pairs={{0,12},{1,13},{2,14},{3,15},{4,0},{5,1},{6,2},{7,3},{8,4},{9,5},{1... | collective-permute-start | bytes 147464 | tf_op jit(solution)/shard_map/ppermute | solution.py:449
  12.1 0.3 collective-permute-done.refs_1_
  12.4 2.0 %collective-permute-done.1.refs_2_ = bf16[8,3072]{1,0:T(8,128)(2,1)S(1)} collective-permute-done((bf16[8,3072]{1,0:T(8,128)(2,1)S(1)}, bf16[8,3072]{1,0:T(8,128)(2,1)S(1)}, u32[]{:S(2)}, u32[]{:S(2)}) %collective-permute-start.1) | collective-permute-done | bytes 49184 | tf_op jit(solution)/shard_map/ppermute | solution.py:449
  14.4 0.5 collective-permute-done.2.refs_3_
  14.9 0.2 collect.1.after.refs_1_
  15.2 1.7 %collective-permute-start.3 = (bf16[24,4096]{1,0:T(8,128)(2,1)S(1)}, bf16[24,4096]{1,0:T(8,128)(2,1)S(1)}, u32[]{:S(2)}, u32[]{:S(2)}) collective-permute-start(bf16[24,4096]{1,0:T(8,128)(2,1)S(1)} %collect.1.after.refs_1_), channel_id=1, source_target_pairs={{0,2},{1,3},{2,0},{3,1},{4,6},{5,7},{6,4},{7,5},{8,10},{9,11},{10,... | collective-permute-start | bytes 589832 | tf_op jit(solution)/shard_map/ppermute | solution.py:457
  16.9 3.3 %load.1 = (bf16[1792,2048]{1,0:T(8,128)(2,1)S(1)}, f32[8,128]{1,0:T(8,128)S(1)}) custom-call(bf16[1792,4096]{1,0:T(8,128)(2,1)} %source.1, bf16[24,4096]{1,0:T(8,128)(2,1)S(1)} %collect.1.after.refs_1_), custom_call_target="tpu_custom_call" | custom-call | bytes 7340032 | tf_op jit(solution)/shard_map/load/pallas_call | solution.py:314
  20.2 0.9 %collective-permute-done.3.refs_2_ = bf16[24,4096]{1,0:T(8,128)(2,1)S(1)} collective-permute-done((bf16[24,4096]{1,0:T(8,128)(2,1)S(1)}, bf16[24,4096]{1,0:T(8,128)(2,1)S(1)}, u32[]{:S(2)}, u32[]{:S(2)}) %collective-permute-start.3) | collective-permute-done | bytes 196640 | tf_op jit(solution)/shard_map/ppermute | solution.py:457
  21.2 1.7 %collective-permute-done.4.refs_2_ = bf16[48,4096]{1,0:T(8,128)(2,1)S(1)} collective-permute-done((bf16[48,4096]{1,0:T(8,128)(2,1)S(1)}, bf16[48,4096]{1,0:T(8,128)(2,1)S(1)}, u32[]{:S(2)}, u32[]{:S(2)}) %collective-permute-start.4) | collective-permute-done | bytes 393248 | tf_op jit(solution)/shard_map/ppermute | solution.py:457
  23.1 4.1 %hidden.1 = bf16[128,1792]{1,0:T(8,128)(2,1)S(1)} custom-call(bf16[96,4096]{1,0:T(8,128)(2,1)S(1)} %join.3.inputs, bf16[4096,1792]{1,0:T(8,128)(2,1)S(1)} %bitcast.4, bf16[4096,1792]{1,0:T(8,128)(2,1)S(1)} %copy-done), custom_call_target="tpu_custom_call" | custom-call | flops 2818572288 | tf_op jit(solution)/shard_map/hidden/pallas_call | solution.py:262
  27.2 1.1 %down.3 = (f32[48,2048]{1,0:T(8,128)S(1)}, bf16[48,2048]{1,0:T(8,128)(2,1)S(1)}) custom-call(bf16[128,1792]{1,0:T(8,128)(2,1)S(1)} %hidden.1, bf16[1792,2048]{1,0:T(8,128)(2,1)S(1)} %get-tuple-element.45.down_weight), custom_call_target="tpu_custom_call" | custom-call | flops 704643072 | tf_op jit(solution)/shard_map/down/pallas_call | solution.py:287
  28.3 0.2 collective-permute-start.10
  28.5 1.1 %down.2 = (f32[48,2048]{1,0:T(8,128)S(1)}, bf16[48,2048]{1,0:T(8,128)(2,1)S(1)}) custom-call(bf16[128,1792]{1,0:T(8,128)(2,1)S(1)} %hidden.1, bf16[1792,2048]{1,0:T(8,128)(2,1)S(1)} %get-tuple-element.36.down_weight), custom_call_target="tpu_custom_call" | custom-call | flops 704643072 | tf_op jit(solution)/shard_map/down/pallas_call | solution.py:287
  29.7 0.4 collective-permute-start.5
  30.2 1.5 %collective-permute-start.11 = (bf16[24,2048]{1,0:T(8,128)(2,1)S(1)}, bf16[24,2048]{1,0:T(8,128)(2,1)S(1)}, u32[]{:S(2)}, u32[]{:S(2)}) collective-permute-start(bf16[24,2048]{1,0:T(8,128)(2,1)S(1)} %get-tuple-element.49), channel_id=1, source_target_pairs={{0,2},{1,3},{2,0},{3,1},{4,6},{5,7},{6,4},{7,5},{8,10},{9,11},{10,... | collective-permute-start | bytes 294920 | tf_op jit(solution)/shard_map/ppermute | solution.py:457
  31.7 1.0 %collective-permute-start.6 = (bf16[24,2048]{1,0:T(8,128)(2,1)S(1)}, bf16[24,2048]{1,0:T(8,128)(2,1)S(1)}, u32[]{:S(2)}, u32[]{:S(2)}) collective-permute-start(bf16[24,2048]{1,0:T(8,128)(2,1)S(1)} %get-tuple-element.40), channel_id=1, source_target_pairs={{0,2},{1,3},{2,0},{3,1},{4,6},{5,7},{6,4},{7,5},{8,10},{9,11},{10,... | collective-permute-start | bytes 294920 | tf_op jit(solution)/shard_map/ppermute | solution.py:457
  32.7 3.1 %collective-permute-done.11.arrived = bf16[24,2048]{1,0:T(8,128)(2,1)S(1)} collective-permute-done((bf16[24,2048]{1,0:T(8,128)(2,1)S(1)}, bf16[24,2048]{1,0:T(8,128)(2,1)S(1)}, u32[]{:S(2)}, u32[]{:S(2)}) %collective-permute-start.11) | collective-permute-done | bytes 98336 | tf_op jit(solution)/shard_map/ppermute | solution.py:457
  35.8 0.2 last_fold.3
  36.0 2.9 %collective-permute-start.12 = (bf16[8,1536]{1,0:T(8,128)(2,1)S(1)}, bf16[8,1536]{1,0:T(8,128)(2,1)S(1)}, u32[]{:S(2)}, u32[]{:S(2)}) collective-permute-start(bf16[8,1536]{1,0:T(8,128)(2,1)S(1)} %get-tuple-element.51), channel_id=1, source_target_pairs={{0,12},{1,13},{2,14},{3,15},{4,0},{5,1},{6,2},{7,3},{8,4},{9,5},{1... | collective-permute-start | bytes 73736 | tf_op jit(solution)/shard_map/ppermute | solution.py:449
  38.9 0.1 collective-permute-start.13
  39.0 0.5 %collective-permute-start.14 = (bf16[8,1536]{1,0:T(8,128)(2,1)S(1)}, bf16[8,1536]{1,0:T(8,128)(2,1)S(1)}, u32[]{:S(2)}, u32[]{:S(2)}) collective-permute-start(bf16[8,1536]{1,0:T(8,128)(2,1)S(1)} %get-tuple-element.53), channel_id=1, source_target_pairs={{0,4},{1,5},{2,6},{3,7},{4,8},{5,9},{6,10},{7,11},{8,12},{9,13},{1... | collective-permute-start | bytes 73736 | tf_op jit(solution)/shard_map/ppermute | solution.py:449
  39.6 0.2 last_fold.2
  39.8 3.3 %collective-permute-start.7 = (bf16[8,1536]{1,0:T(8,128)(2,1)S(1)}, bf16[8,1536]{1,0:T(8,128)(2,1)S(1)}, u32[]{:S(2)}, u32[]{:S(2)}) collective-permute-start(bf16[8,1536]{1,0:T(8,128)(2,1)S(1)} %get-tuple-element.42), channel_id=1, source_target_pairs={{0,12},{1,13},{2,14},{3,15},{4,0},{5,1},{6,2},{7,3},{8,4},{9,5},{1... | collective-permute-start | bytes 73736 | tf_op jit(solution)/shard_map/ppermute | solution.py:449
  43.1 1.0 %collective-permute-start.8 = (bf16[8,1536]{1,0:T(8,128)(2,1)S(1)}, bf16[8,1536]{1,0:T(8,128)(2,1)S(1)}, u32[]{:S(2)}, u32[]{:S(2)}) collective-permute-start(bf16[8,1536]{1,0:T(8,128)(2,1)S(1)} %get-tuple-element.43), channel_id=1, source_target_pairs={{0,8},{1,9},{2,10},{3,11},{4,12},{5,13},{6,14},{7,15},{8,0},{9,1},... | collective-permute-start | bytes 73736 | tf_op jit(solution)/shard_map/ppermute | solution.py:449
  44.1 0.7 %collective-permute-done.14.refs_7_ = bf16[8,1536]{1,0:T(8,128)(2,1)S(1)} collective-permute-done((bf16[8,1536]{1,0:T(8,128)(2,1)S(1)}, bf16[8,1536]{1,0:T(8,128)(2,1)S(1)}, u32[]{:S(2)}, u32[]{:S(2)}) %collective-permute-start.14) | collective-permute-done | bytes 24608 | tf_op jit(solution)/shard_map/ppermute | solution.py:449
  44.8 0.1 collective-permute-done.7.refs_1_
  45.0 2.8 %collective-permute-done.8.refs_2_ = bf16[8,1536]{1,0:T(8,128)(2,1)S(1)} collective-permute-done((bf16[8,1536]{1,0:T(8,128)(2,1)S(1)}, bf16[8,1536]{1,0:T(8,128)(2,1)S(1)}, u32[]{:S(2)}, u32[]{:S(2)}) %collective-permute-start.8) | collective-permute-done | bytes 24608 | tf_op jit(solution)/shard_map/ppermute | solution.py:449
  47.8 1.9 %collective-permute-done.9.refs_3_ = bf16[8,1536]{1,0:T(8,128)(2,1)S(1)} collective-permute-done((bf16[8,1536]{1,0:T(8,128)(2,1)S(1)}, bf16[8,1536]{1,0:T(8,128)(2,1)S(1)}, u32[]{:S(2)}, u32[]{:S(2)}) %collective-permute-start.9) | collective-permute-done | bytes 24608 | tf_op jit(solution)/shard_map/ppermute | solution.py:449
  49.8 0.8 %combine.1 = bf16[8,4096]{1,0:T(8,128)(2,1)} custom-call(f32[16,128]{1,0:T(8,128)S(1)} %get-tuple-element.29.token.share, bf16[4,16,128]{2,1,0:T(8,128)(2,1)S(1)} %get-tuple-element.30.take, bf16[8,1536]{1,0:T(8,128)(2,1)S(1)} %get-tuple-element.41.refs_0_, bf16[8,1536]{1,0:T(8,128)(2,1)S(1)} %collective-permute-done.7.refs_1_, ...), custom_call_target="tpu_custom_call" | custom-call | tf_op jit(solution)/shard_map/combine/pallas_call | solution.py:436
  (22 shorter events, 0.3 us)
Async XLA Ops:
  0.6 22.4 %slice-start = ((s8[14680064]{0:T(1024)(128)(4,1)}), s8[4194304]{0:T(1024)(128)(4,1)S(1)}, s32[]{:S(2)}) async-start(s8[14680064]{0:T(1024)(128)(4,1)} %bitcast.3), calls=%async_computation | async-start | bytes 8388608
  0.6 22.4 %slice-start.1 = ((s8[14680064]{0:T(1024)(128)(4,1)}), s8[4194304]{0:T(1024)(128)(4,1)S(1)}, s32[]{:S(2)}) async-start(s8[14680064]{0:T(1024)(128)(4,1)} %bitcast.3), calls=%async_computation.1 | async-start | bytes 8388608
  0.7 22.4 %copy-start = (bf16[4096,1792]{1,0:T(8,128)(2,1)S(1)}, bf16[4096,1792]{1,0:T(8,128)(2,1)}, u32[]{:S(2)}) copy-start(bf16[4096,1792]{1,0:T(8,128)(2,1)} %up_weight.1) | copy-start | bytes 44040196
  5.1 7.3 %collective-permute-start = (bf16[8,3072]{1,0:T(8,128)(2,1)S(1)}, bf16[8,3072]{1,0:T(8,128)(2,1)S(1)}, u32[]{:S(2)}, u32[]{:S(2)}) collective-permute-start(bf16[8,3072]{1,0:T(8,128)(2,1)S(1)} %get-tuple-element.32), channel_id=1, source_target_pairs={{0,4},{1,5},{2,6},{3,7},{4,8},{5,9},{6,10},{7,11},{8,12},{9,13},{1... | collective-permute-start | bytes 147464 | tf_op jit(solution)/shard_map/ppermute | solution.py:449
  8.2 6.2 %collective-permute-start.1 = (bf16[8,3072]{1,0:T(8,128)(2,1)S(1)}, bf16[8,3072]{1,0:T(8,128)(2,1)S(1)}, u32[]{:S(2)}, u32[]{:S(2)}) collective-permute-start(bf16[8,3072]{1,0:T(8,128)(2,1)S(1)} %get-tuple-element.33), channel_id=1, source_target_pairs={{0,8},{1,9},{2,10},{3,11},{4,12},{5,13},{6,14},{7,15},{8,0},{9,1},... | collective-permute-start | bytes 147464 | tf_op jit(solution)/shard_map/ppermute | solution.py:449
  10.8 4.1 %collective-permute-start.2 = (bf16[8,3072]{1,0:T(8,128)(2,1)S(1)}, bf16[8,3072]{1,0:T(8,128)(2,1)S(1)}, u32[]{:S(2)}, u32[]{:S(2)}) collective-permute-start(bf16[8,3072]{1,0:T(8,128)(2,1)S(1)} %get-tuple-element.34), channel_id=1, source_target_pairs={{0,12},{1,13},{2,14},{3,15},{4,0},{5,1},{6,2},{7,3},{8,4},{9,5},{1... | collective-permute-start | bytes 147464 | tf_op jit(solution)/shard_map/ppermute | solution.py:449
  15.2 7.9 %slice-start.2 = ((s8[14680064]{0:T(1024)(128)(4,1)}), s8[4194304]{0:T(1024)(128)(4,1)S(1)}, s32[]{:S(2)}) async-start(s8[14680064]{0:T(1024)(128)(4,1)} %bitcast.3), calls=%async_computation.2 | async-start | bytes 8388608
  15.2 7.9 %slice-start.3 = ((s8[14680064]{0:T(1024)(128)(4,1)}), s8[2097152]{0:T(1024)(128)(4,1)S(1)}, s32[]{:S(2)}) async-start(s8[14680064]{0:T(1024)(128)(4,1)} %bitcast.3), calls=%async_computation.3 | async-start | bytes 4194304
  15.2 6.0 %collective-permute-start.3 = (bf16[24,4096]{1,0:T(8,128)(2,1)S(1)}, bf16[24,4096]{1,0:T(8,128)(2,1)S(1)}, u32[]{:S(2)}, u32[]{:S(2)}) collective-permute-start(bf16[24,4096]{1,0:T(8,128)(2,1)S(1)} %collect.1.after.refs_1_), channel_id=1, source_target_pairs={{0,2},{1,3},{2,0},{3,1},{4,6},{5,7},{6,4},{7,5},{8,10},{9,11},{10,... | collective-permute-start | bytes 589832 | tf_op jit(solution)/shard_map/ppermute | solution.py:457
  21.2 1.8 %collective-permute-start.4 = (bf16[48,4096]{1,0:T(8,128)(2,1)S(1)}, bf16[48,4096]{1,0:T(8,128)(2,1)S(1)}, u32[]{:S(2)}, u32[]{:S(2)}) collective-permute-start(bf16[48,4096]{1,0:T(8,128)(2,1)S(1)} %join.2.refs_1_), channel_id=1, source_target_pairs={{0,1},{1,0},{2,3},{3,2},{4,5},{5,4},{6,7},{7,6},{8,9},{9,8},{10,11... | collective-permute-start | bytes 1179656 | tf_op jit(solution)/shard_map/ppermute | solution.py:457
  28.3 1.8 %collective-permute-start.10 = (bf16[48,2048]{1,0:T(8,128)(2,1)S(1)}, bf16[48,2048]{1,0:T(8,128)(2,1)S(1)}, u32[]{:S(2)}, u32[]{:S(2)}) collective-permute-start(bf16[48,2048]{1,0:T(8,128)(2,1)S(1)} %get-tuple-element.47), channel_id=1, source_target_pairs={{0,1},{1,0},{2,3},{3,2},{4,5},{5,4},{6,7},{7,6},{8,9},{9,8},{10,11... | collective-permute-start | bytes 589832 | tf_op jit(solution)/shard_map/ppermute | solution.py:457
  29.7 2.0 %collective-permute-start.5 = (bf16[48,2048]{1,0:T(8,128)(2,1)S(1)}, bf16[48,2048]{1,0:T(8,128)(2,1)S(1)}, u32[]{:S(2)}, u32[]{:S(2)}) collective-permute-start(bf16[48,2048]{1,0:T(8,128)(2,1)S(1)} %get-tuple-element.38), channel_id=1, source_target_pairs={{0,1},{1,0},{2,3},{3,2},{4,5},{5,4},{6,7},{7,6},{8,9},{9,8},{10,11... | collective-permute-start | bytes 589832 | tf_op jit(solution)/shard_map/ppermute | solution.py:457
  30.2 5.7 %collective-permute-start.11 = (bf16[24,2048]{1,0:T(8,128)(2,1)S(1)}, bf16[24,2048]{1,0:T(8,128)(2,1)S(1)}, u32[]{:S(2)}, u32[]{:S(2)}) collective-permute-start(bf16[24,2048]{1,0:T(8,128)(2,1)S(1)} %get-tuple-element.49), channel_id=1, source_target_pairs={{0,2},{1,3},{2,0},{3,1},{4,6},{5,7},{6,4},{7,5},{8,10},{9,11},{10,... | collective-permute-start | bytes 294920 | tf_op jit(solution)/shard_map/ppermute | solution.py:457
  31.7 7.9 %collective-permute-start.6 = (bf16[24,2048]{1,0:T(8,128)(2,1)S(1)}, bf16[24,2048]{1,0:T(8,128)(2,1)S(1)}, u32[]{:S(2)}, u32[]{:S(2)}) collective-permute-start(bf16[24,2048]{1,0:T(8,128)(2,1)S(1)} %get-tuple-element.40), channel_id=1, source_target_pairs={{0,2},{1,3},{2,0},{3,1},{4,6},{5,7},{6,4},{7,5},{8,10},{9,11},{10,... | collective-permute-start | bytes 294920 | tf_op jit(solution)/shard_map/ppermute | solution.py:457
  36.0 8.1 %collective-permute-start.12 = (bf16[8,1536]{1,0:T(8,128)(2,1)S(1)}, bf16[8,1536]{1,0:T(8,128)(2,1)S(1)}, u32[]{:S(2)}, u32[]{:S(2)}) collective-permute-start(bf16[8,1536]{1,0:T(8,128)(2,1)S(1)} %get-tuple-element.51), channel_id=1, source_target_pairs={{0,12},{1,13},{2,14},{3,15},{4,0},{5,1},{6,2},{7,3},{8,4},{9,5},{1... | collective-permute-start | bytes 73736 | tf_op jit(solution)/shard_map/ppermute | solution.py:449
  38.9 5.2 %collective-permute-start.13 = (bf16[8,1536]{1,0:T(8,128)(2,1)S(1)}, bf16[8,1536]{1,0:T(8,128)(2,1)S(1)}, u32[]{:S(2)}, u32[]{:S(2)}) collective-permute-start(bf16[8,1536]{1,0:T(8,128)(2,1)S(1)} %get-tuple-element.52), channel_id=1, source_target_pairs={{0,8},{1,9},{2,10},{3,11},{4,12},{5,13},{6,14},{7,15},{8,0},{9,1},... | collective-permute-start | bytes 73736 | tf_op jit(solution)/shard_map/ppermute | solution.py:449
  39.0 5.8 %collective-permute-start.14 = (bf16[8,1536]{1,0:T(8,128)(2,1)S(1)}, bf16[8,1536]{1,0:T(8,128)(2,1)S(1)}, u32[]{:S(2)}, u32[]{:S(2)}) collective-permute-start(bf16[8,1536]{1,0:T(8,128)(2,1)S(1)} %get-tuple-element.53), channel_id=1, source_target_pairs={{0,4},{1,5},{2,6},{3,7},{4,8},{5,9},{6,10},{7,11},{8,12},{9,13},{1... | collective-permute-start | bytes 73736 | tf_op jit(solution)/shard_map/ppermute | solution.py:449
  39.8 5.2 %collective-permute-start.7 = (bf16[8,1536]{1,0:T(8,128)(2,1)S(1)}, bf16[8,1536]{1,0:T(8,128)(2,1)S(1)}, u32[]{:S(2)}, u32[]{:S(2)}) collective-permute-start(bf16[8,1536]{1,0:T(8,128)(2,1)S(1)} %get-tuple-element.42), channel_id=1, source_target_pairs={{0,12},{1,13},{2,14},{3,15},{4,0},{5,1},{6,2},{7,3},{8,4},{9,5},{1... | collective-permute-start | bytes 73736 | tf_op jit(solution)/shard_map/ppermute | solution.py:449
  43.1 4.7 %collective-permute-start.8 = (bf16[8,1536]{1,0:T(8,128)(2,1)S(1)}, bf16[8,1536]{1,0:T(8,128)(2,1)S(1)}, u32[]{:S(2)}, u32[]{:S(2)}) collective-permute-start(bf16[8,1536]{1,0:T(8,128)(2,1)S(1)} %get-tuple-element.43), channel_id=1, source_target_pairs={{0,8},{1,9},{2,10},{3,11},{4,12},{5,13},{6,14},{7,15},{8,0},{9,1},... | collective-permute-start | bytes 73736 | tf_op jit(solution)/shard_map/ppermute | solution.py:449
  44.1 5.6 %collective-permute-start.9 = (bf16[8,1536]{1,0:T(8,128)(2,1)S(1)}, bf16[8,1536]{1,0:T(8,128)(2,1)S(1)}, u32[]{:S(2)}, u32[]{:S(2)}) collective-permute-start(bf16[8,1536]{1,0:T(8,128)(2,1)S(1)} %get-tuple-element.44), channel_id=1, source_target_pairs={{0,4},{1,5},{2,6},{3,7},{4,8},{5,9},{6,10},{7,11},{8,12},{9,13},{1... | collective-permute-start | bytes 73736 | tf_op jit(solution)/shard_map/ppermute | solution.py:449

commit v7 on v6

--- a/solution.py
+++ b/solution.py
@@ -160,7 +160,7 @@
     slot_across = jnp.zeros((8, 128), jnp.int32)
     counts = [jnp.int32(0)] * EXPERTS
     for r in range(rows):
-        names = [(routes[c, base + r] + EXPERTS - own) % EXPERTS for c in range(2)]
+        names = [routes[c, base + r] ^ own for c in range(2)]
         for choice, name in ((r, names[0]), (rows + r, names[1])):
             slot = jnp.int32(0)
             for e in range(EXPERTS):
@@ -194,8 +194,7 @@
     chosen_logits = jnp.zeros((2 * rows, 1), F32)
     for e in range(EXPERTS):
         both = jnp.concatenate([logits[e], logits[e]], axis=0)
-        relative = (e + EXPERTS - own) % EXPERTS
-        chosen_logits = jnp.where(expert_down[:, :1] == relative, both, chosen_logits)
+        chosen_logits = jnp.where(expert_down[:, :1] == (own ^ e), both, chosen_logits)
     other = jnp.concatenate([chosen_logits[rows:], chosen_logits[:rows]], axis=0)
     share[...] = jnp.broadcast_to(1.0 / (1.0 + jnp.exp(other - chosen_logits)), share.shape)
     for copy in weight:
@@ -272,32 +271,36 @@
     )(inputs, gate_weight, up_weight)
 
 
-def down_kernel(hidden, down_weight, keep, send):
-    half, width = keep.shape
+def down_kernel(hidden, *refs):
+    weights, (keep, send) = refs[:PARTS], refs[PARTS:]
+    half = keep.shape[0]
     h = hidden[...]
-    for n in range(0, width, 512):
-        terms = dot(h, down_weight[:, n : n + 512])
-        keep[:, n : n + 512] = terms[:half]
-        send[:, n : n + 512] = terms[half : 2 * half].astype(BF16)
-
-
-def down_rows(hidden, down_weight, rows):
+    first = 0
+    for weight in weights:
+        for n in range(0, weight.shape[1], 512):
+            terms = dot(h, weight[:, n : n + 512])
+            keep[:, first : first + 512] = terms[:half]
+            send[:, first : first + 512] = terms[half : 2 * half].astype(BF16)
+            first += 512
+
+
+def down_rows(hidden, weights, rows):
     columns = hidden.shape[1]
-    half, width = rows // 2, down_weight.shape[1]
+    half, width = rows // 2, sum(weight.shape[1] for weight in weights)
     return pl.pallas_call(
         down_kernel,
         out_shape=(
             jax.ShapeDtypeStruct((half, width), F32),
             jax.ShapeDtypeStruct((half, width), BF16),
         ),
-        in_specs=[VMEM] * 2,
+        in_specs=[VMEM] * (1 + PARTS),
         out_specs=(VMEM, VMEM),
         compiler_params=pltpu.CompilerParams(vmem_limit_bytes=4 * MIB * max(1, rows // 128)),
         cost_estimate=pl.CostEstimate(
             flops=2 * rows * width * columns, bytes_accessed=0, transcendentals=0
         ),
         name="down",
-    )(hidden, down_weight)
+    )(hidden, *weights)
 
 
 def load_kernel(first, source, after, target, token, semaphores):
@@ -418,39 +421,31 @@
 
 
 def combine_kernel(share, take, *refs):
-    out = refs[-1]
-    results = [refs[p * EXPERTS : (p + 1) * EXPERTS] for p in range(PARTS)]
+    results, out = refs[:-1], refs[-1]
     rows = out.shape[0]
-    quarter = refs[0].shape[1] // 3
+    quarter = results[0].shape[1] // 3
     picks = [take[i][:, : 8 * EXPERTS] for i in range(4)]
     shares = share[:, :1]
-    for part, result in enumerate(results):
-        for m, value in enumerate(unpack(picks, jnp.concatenate([x[...] for x in result], axis=0))):
-            value = value * shares
-            first = (part * 4 + m) * quarter
-            out[:, first : first + quarter] = (value[:rows] + value[rows:]).astype(BF16)
+    block = jnp.concatenate([x[...] for x in results], axis=0)
+    for m, value in enumerate(unpack(picks, block)):
+        value = value * shares
+        out[:, m * quarter : (m + 1) * quarter] = (value[:rows] + value[rows:]).astype(BF16)
 
 
 def combine(share, take, results):
-    width = results[0].shape[1] // 3 * 4
     return pl.pallas_call(
         combine_kernel,
-        out_shape=jax.ShapeDtypeStruct((share.shape[0] // 2, width * PARTS), BF16),
-        in_specs=[VMEM] * (2 + len(results)),
+        out_shape=jax.ShapeDtypeStruct((share.shape[0] // 2, results[0].shape[1] // 3 * 4), BF16),
+        in_specs=[VMEM] * (2 + EXPERTS),
         out_specs=VMEM,
         compiler_params=pltpu.CompilerParams(vmem_limit_bytes=2 * MIB),
         name="combine",
     )(share, take, *results)
 
 
-def between_planes(blocks, count, direction):
+def between_planes(blocks, count):
     plane = count // EXPERTS
-    return [blocks[0]] + [
-        lax.ppermute(
-            blocks[k], "dp", [(i, (i + direction * k * plane) % count) for i in range(count)]
-        )
-        for k in range(1, EXPERTS)
-    ]
+    return [blocks[0]] + [swap(blocks[k], count, k * plane) for k in range(1, EXPERTS)]
 
 
 def swap(value, count, bit):
@@ -480,19 +475,16 @@
         router_weight, routes, down_weight,
     )
 
-    gathered = collect(share, between_planes(packed, count, 1))
+    gathered = collect(share, between_planes(packed, count))
     down_rest, token = load(down_weight, gathered, down.shape[1])
     for bit in bits:
         gathered = join(token, gathered, swap(gathered, count, bit))
 
     hidden = hidden_rows(gathered, gate_weight, up_weight)
-    results = []
-    for weight in (down, down_rest):
-        held, send = down_rows(hidden, weight, gathered.shape[0])
-        for bit in bits[:0:-1]:
-            held, send = fold(held, swap(send, count, bit))
-        blocks = last_fold(held, swap(send, count, bits[0]))
-        results += between_planes(blocks, count, -1)
+    held, send = down_rows(hidden, (down, down_rest), gathered.shape[0])
+    for bit in bits[:0:-1]:
+        held, send = fold(held, swap(send, count, bit))
+    results = between_planes(last_fold(held, swap(send, count, bits[0])), count)
     return (attended, combine(share, take, results))
 
 

time: 50.7 us -> 48.3 us (0.953)
  starting transfers between devices: 19.9 us -> 13.5 us
  waiting for transfers between devices: 14.1 us -> 18.1 us
    ppermute x9 -> x0, starting transfers between devices: 14.9 us -> none  [between_planes(): lax.ppermute(blocks[k], 'dp', [(i, (i + direction * k * plane) % count) f...]
    ppermute x6 -> x10, waiting for transfers between devices: 5.76 us -> 18.1 us  [swap(): return lax.ppermute(value, 'dp', [(i, i ^ bit) for i in range(count)])]
    ppermute x6 -> x10, starting transfers between devices: 4.93 us -> 13.5 us  [swap(): return lax.ppermute(value, 'dp', [(i, i ^ bit) for i in range(count)])]
    ppermute x9 -> x0, waiting for transfers between devices: 8.38 us -> none  [between_planes(): lax.ppermute(blocks[k], 'dp', [(i, (i + direction * k * plane) % count) f...]
    pallas_call x2 -> x1, Pallas kernels: 2.26 us -> 2.22 us  [down_rows(): pl.pallas_call(down_kernel, out_shape=(jax.ShapeDtypeStruct((half, width)...]
  transfers between devices with their start and end apart: 15 -> 10, of which waited for: 10 -> 8; matrix products, arithmetic and copies ran while one was open for 0% -> 0% of each run, Pallas kernels for 10% -> 7%
where the time goes in v7:
time: 48.3 us; the launch traced here: 48.2 us
  waiting for transfers between devices  18.1 us (37%)
  Pallas kernels  15.7 us (33%)
  starting transfers between devices  13.5 us (28%)
  between operations  0.8 us (2%)
    ppermute x10, waiting for transfers between devices, swap(): return lax.ppermute(value, 'dp', [(i, i ^ bit) for i in range(count)])  18.1 us
    ppermute x10, starting transfers between devices, swap(): return lax.ppermute(value, 'dp', [(i, i ^ bit) for i in range(count)])  13.5 us
    pallas_call x1, Pallas kernels, attend(): pl.pallas_call(functools.partial(attend_kernel, plane), out_shape=(jax.Sh...  4.45 us
    pallas_call x1, Pallas kernels, hidden_rows(): pl.pallas_call(hidden_kernel, out_shape=jax.ShapeDtypeStruct((rows + -row...  4.11 us
    pallas_call x1, Pallas kernels, load(): pl.pallas_call(functools.partial(load_kernel, first), out_shape=(pltpu.VM...  3.45 us
    pallas_call x1, Pallas kernels, down_rows(): pl.pallas_call(down_kernel, out_shape=(jax.ShapeDtypeStruct((half, width)...  2.22 us
  transfers between devices with their start and end apart: 10, of which 8 were waited for; matrix products, arithmetic and copies ran while one was open for 0% of the time, Pallas kernels for 7%

profile of v7, /device:TPU:0, one launch (start us, length us, event | category | flops | bytes accessed | tf_op | source)
XLA Modules:
  0.0 48.2 jit_solution(11833480203682942960)
XLA Ops:
  0.6 0.0 slice-start
  0.6 0.0 slice-start.1
  0.7 4.5 %attend.1 = (bf16[8,4096]{1,0:T(8,128)(2,1)}, bf16[8,3072]{1,0:T(8,128)(2,1)S(1)}, bf16[8,3072]{1,0:T(8,128)(2,1)S(1)}, bf16[8,3072]{1,0:T(8,128)(2,1)S(1)}, bf1...) custom-call(bf16[8,4096]{1,0:T(8,128)(2,1)} %refs_0_.1, ...), custom_call_target="tpu_custom_call" | custom-call | tf_op jit(solution)/shard_map/attend/pallas_call | solution.py:220
  5.1 3.1 %collective-permute-start = (bf16[8,3072]{1,0:T(8,128)(2,1)S(1)}, bf16[8,3072]{1,0:T(8,128)(2,1)S(1)}, u32[]{:S(2)}, u32[]{:S(2)}) collective-permute-start(bf16[8,3072]{1,0:T(8,128)(2,1)S(1)} %get-tuple-element.24), channel_id=1, source_target_pairs={{0,4},{1,5},{2,6},{3,7},{4,0},{5,1},{6,2},{7,3},{8,12},{9,13},{10,... | collective-permute-start | bytes 147464 | tf_op jit(solution)/shard_map/ppermute | solution.py:452
  8.2 2.6 %collective-permute-start.1 = (bf16[8,3072]{1,0:T(8,128)(2,1)S(1)}, bf16[8,3072]{1,0:T(8,128)(2,1)S(1)}, u32[]{:S(2)}, u32[]{:S(2)}) collective-permute-start(bf16[8,3072]{1,0:T(8,128)(2,1)S(1)} %get-tuple-element.25), channel_id=1, source_target_pairs={{0,8},{1,9},{2,10},{3,11},{4,12},{5,13},{6,14},{7,15},{8,0},{9,1},... | collective-permute-start | bytes 147464 | tf_op jit(solution)/shard_map/ppermute | solution.py:452
  10.8 0.0 collective-permute-start.2
  10.8 3.3 %collective-permute-done.1.refs_2_ = bf16[8,3072]{1,0:T(8,128)(2,1)S(1)} collective-permute-done((bf16[8,3072]{1,0:T(8,128)(2,1)S(1)}, bf16[8,3072]{1,0:T(8,128)(2,1)S(1)}, u32[]{:S(2)}, u32[]{:S(2)}) %collective-permute-start.1) | collective-permute-done | bytes 49184 | tf_op jit(solution)/shard_map/ppermute | solution.py:452
  14.1 2.6 %collective-permute-done.2.refs_3_ = bf16[8,3072]{1,0:T(8,128)(2,1)S(1)} collective-permute-done((bf16[8,3072]{1,0:T(8,128)(2,1)S(1)}, bf16[8,3072]{1,0:T(8,128)(2,1)S(1)}, u32[]{:S(2)}, u32[]{:S(2)}) %collective-permute-start.2) | collective-permute-done | bytes 49184 | tf_op jit(solution)/shard_map/ppermute | solution.py:452
  16.7 0.3 collect.1.after.refs_1_
  17.0 0.0 slice-start.2
  17.0 0.0 slice-start.3
  17.0 1.6 %collective-permute-start.3 = (bf16[24,4096]{1,0:T(8,128)(2,1)S(1)}, bf16[24,4096]{1,0:T(8,128)(2,1)S(1)}, u32[]{:S(2)}, u32[]{:S(2)}) collective-permute-start(bf16[24,4096]{1,0:T(8,128)(2,1)S(1)} %collect.1.after.refs_1_), channel_id=1, source_target_pairs={{0,2},{1,3},{2,0},{3,1},{4,6},{5,7},{6,4},{7,5},{8,10},{9,11},{10,... | collective-permute-start | bytes 589832 | tf_op jit(solution)/shard_map/ppermute | solution.py:452
  18.6 3.4 %load.1 = (bf16[1792,2048]{1,0:T(8,128)(2,1)S(1)}, f32[8,128]{1,0:T(8,128)S(1)}) custom-call(bf16[1792,4096]{1,0:T(8,128)(2,1)} %source.1, bf16[24,4096]{1,0:T(8,128)(2,1)S(1)} %collect.1.after.refs_1_), custom_call_target="tpu_custom_call" | custom-call | bytes 7340032 | tf_op jit(solution)/shard_map/load/pallas_call | solution.py:317
  22.0 0.7 %collective-permute-done.3.refs_2_ = bf16[24,4096]{1,0:T(8,128)(2,1)S(1)} collective-permute-done((bf16[24,4096]{1,0:T(8,128)(2,1)S(1)}, bf16[24,4096]{1,0:T(8,128)(2,1)S(1)}, u32[]{:S(2)}, u32[]{:S(2)}) %collective-permute-start.3) | collective-permute-done | bytes 196640 | tf_op jit(solution)/shard_map/ppermute | solution.py:452
  22.7 0.1 collective-permute-start.4
  22.8 1.7 %collective-permute-done.4.refs_2_ = bf16[48,4096]{1,0:T(8,128)(2,1)S(1)} collective-permute-done((bf16[48,4096]{1,0:T(8,128)(2,1)S(1)}, bf16[48,4096]{1,0:T(8,128)(2,1)S(1)}, u32[]{:S(2)}, u32[]{:S(2)}) %collective-permute-start.4) | collective-permute-done | bytes 393248 | tf_op jit(solution)/shard_map/ppermute | solution.py:452
  24.5 0.1 join.3.inputs
  24.6 4.1 %hidden.1 = bf16[128,1792]{1,0:T(8,128)(2,1)S(1)} custom-call(bf16[96,4096]{1,0:T(8,128)(2,1)S(1)} %join.3.inputs, bf16[4096,1792]{1,0:T(8,128)(2,1)S(1)} %bitcast.4, bf16[4096,1792]{1,0:T(8,128)(2,1)S(1)} %copy-done), custom_call_target="tpu_custom_call" | custom-call | flops 2818572288 | tf_op jit(solution)/shard_map/hidden/pallas_call | solution.py:261
  28.8 2.2 %down.1 = (f32[48,4096]{1,0:T(8,128)S(1)}, bf16[48,4096]{1,0:T(8,128)(2,1)S(1)}) custom-call(bf16[128,1792]{1,0:T(8,128)(2,1)S(1)} %hidden.1, bf16[1792,2048]{1,0:T(8,128)(2,1)S(1)} %get-tuple-element.28.refs_0_, bf16[1792,2048]{1,0:T(8,128)(2,1)S(1)} %get-tuple-element.29.refs_1_), custom_call_target="tpu_custom_call" | custom-call | flops 1409286144 | tf_op jit(solution)/shard_map/down/pallas_call | solution.py:290
  31.0 0.2 collective-permute-start.5
  31.2 1.6 %collective-permute-done.5.arrived = bf16[48,4096]{1,0:T(8,128)(2,1)S(1)} collective-permute-done((bf16[48,4096]{1,0:T(8,128)(2,1)S(1)}, bf16[48,4096]{1,0:T(8,128)(2,1)S(1)}, u32[]{:S(2)}, u32[]{:S(2)}) %collective-permute-start.5) | collective-permute-done | bytes 393248 | tf_op jit(solution)/shard_map/ppermute | solution.py:452
  32.8 0.1 fold.1
  32.9 1.6 %collective-permute-start.6 = (bf16[24,4096]{1,0:T(8,128)(2,1)S(1)}, bf16[24,4096]{1,0:T(8,128)(2,1)S(1)}, u32[]{:S(2)}, u32[]{:S(2)}) collective-permute-start(bf16[24,4096]{1,0:T(8,128)(2,1)S(1)} %get-tuple-element.33), channel_id=1, source_target_pairs={{0,2},{1,3},{2,0},{3,1},{4,6},{5,7},{6,4},{7,5},{8,10},{9,11},{10,... | collective-permute-start | bytes 589832 | tf_op jit(solution)/shard_map/ppermute | solution.py:452
  34.4 5.4 %collective-permute-done.6.arrived = bf16[24,4096]{1,0:T(8,128)(2,1)S(1)} collective-permute-done((bf16[24,4096]{1,0:T(8,128)(2,1)S(1)}, bf16[24,4096]{1,0:T(8,128)(2,1)S(1)}, u32[]{:S(2)}, u32[]{:S(2)}) %collective-permute-start.6) | collective-permute-done | bytes 196640 | tf_op jit(solution)/shard_map/ppermute | solution.py:452
  39.9 0.2 last_fold.1
  40.1 0.1 collective-permute-start.7
  40.2 1.3 %collective-permute-start.8 = (bf16[8,3072]{1,0:T(8,128)(2,1)S(1)}, bf16[8,3072]{1,0:T(8,128)(2,1)S(1)}, u32[]{:S(2)}, u32[]{:S(2)}) collective-permute-start(bf16[8,3072]{1,0:T(8,128)(2,1)S(1)} %get-tuple-element.36), channel_id=1, source_target_pairs={{0,8},{1,9},{2,10},{3,11},{4,12},{5,13},{6,14},{7,15},{8,0},{9,1},... | collective-permute-start | bytes 147464 | tf_op jit(solution)/shard_map/ppermute | solution.py:452
  41.5 3.1 %collective-permute-start.9 = (bf16[8,3072]{1,0:T(8,128)(2,1)S(1)}, bf16[8,3072]{1,0:T(8,128)(2,1)S(1)}, u32[]{:S(2)}, u32[]{:S(2)}) collective-permute-start(bf16[8,3072]{1,0:T(8,128)(2,1)S(1)} %get-tuple-element.37), channel_id=1, source_target_pairs={{0,12},{1,13},{2,14},{3,15},{4,8},{5,9},{6,10},{7,11},{8,4},{9,5},... | collective-permute-start | bytes 147464 | tf_op jit(solution)/shard_map/ppermute | solution.py:452
  44.6 0.0 collective-permute-done.7.refs_1_
  44.6 1.2 %collective-permute-done.8.refs_2_ = bf16[8,3072]{1,0:T(8,128)(2,1)S(1)} collective-permute-done((bf16[8,3072]{1,0:T(8,128)(2,1)S(1)}, bf16[8,3072]{1,0:T(8,128)(2,1)S(1)}, u32[]{:S(2)}, u32[]{:S(2)}) %collective-permute-start.8) | collective-permute-done | bytes 49184 | tf_op jit(solution)/shard_map/ppermute | solution.py:452
  45.8 1.6 %collective-permute-done.9.refs_3_ = bf16[8,3072]{1,0:T(8,128)(2,1)S(1)} collective-permute-done((bf16[8,3072]{1,0:T(8,128)(2,1)S(1)}, bf16[8,3072]{1,0:T(8,128)(2,1)S(1)}, u32[]{:S(2)}, u32[]{:S(2)}) %collective-permute-start.9) | collective-permute-done | bytes 49184 | tf_op jit(solution)/shard_map/ppermute | solution.py:452
  47.4 0.8 %combine.1 = bf16[8,4096]{1,0:T(8,128)(2,1)} custom-call(f32[16,128]{1,0:T(8,128)S(1)} %get-tuple-element.21.token.share, bf16[4,16,128]{2,1,0:T(8,128)(2,1)S(1)} %get-tuple-element.22.take, bf16[8,3072]{1,0:T(8,128)(2,1)S(1)} %get-tuple-element.34.refs_0_, bf16[8,3072]{1,0:T(8,128)(2,1)S(1)} %collective-permute-done.7.refs_1_, ...), custom_call_target="tpu_custom_call" | custom-call | tf_op jit(solution)/shard_map/combine/pallas_call | solution.py:436
  (9 shorter events, 0.0 us)
Async XLA Ops:
  0.6 24.0 %slice-start = ((s8[14680064]{0:T(1024)(128)(4,1)}), s8[4194304]{0:T(1024)(128)(4,1)S(1)}, s32[]{:S(2)}) async-start(s8[14680064]{0:T(1024)(128)(4,1)} %bitcast.3), calls=%async_computation | async-start | bytes 8388608
  0.6 24.0 %slice-start.1 = ((s8[14680064]{0:T(1024)(128)(4,1)}), s8[4194304]{0:T(1024)(128)(4,1)S(1)}, s32[]{:S(2)}) async-start(s8[14680064]{0:T(1024)(128)(4,1)} %bitcast.3), calls=%async_computation.1 | async-start | bytes 8388608
  0.7 24.0 %copy-start = (bf16[4096,1792]{1,0:T(8,128)(2,1)S(1)}, bf16[4096,1792]{1,0:T(8,128)(2,1)}, u32[]{:S(2)}) copy-start(bf16[4096,1792]{1,0:T(8,128)(2,1)} %up_weight.1) | copy-start | bytes 44040196
  5.1 5.7 %collective-permute-start = (bf16[8,3072]{1,0:T(8,128)(2,1)S(1)}, bf16[8,3072]{1,0:T(8,128)(2,1)S(1)}, u32[]{:S(2)}, u32[]{:S(2)}) collective-permute-start(bf16[8,3072]{1,0:T(8,128)(2,1)S(1)} %get-tuple-element.24), channel_id=1, source_target_pairs={{0,4},{1,5},{2,6},{3,7},{4,0},{5,1},{6,2},{7,3},{8,12},{9,13},{10,... | collective-permute-start | bytes 147464 | tf_op jit(solution)/shard_map/ppermute | solution.py:452
  8.2 5.9 %collective-permute-start.1 = (bf16[8,3072]{1,0:T(8,128)(2,1)S(1)}, bf16[8,3072]{1,0:T(8,128)(2,1)S(1)}, u32[]{:S(2)}, u32[]{:S(2)}) collective-permute-start(bf16[8,3072]{1,0:T(8,128)(2,1)S(1)} %get-tuple-element.25), channel_id=1, source_target_pairs={{0,8},{1,9},{2,10},{3,11},{4,12},{5,13},{6,14},{7,15},{8,0},{9,1},... | collective-permute-start | bytes 147464 | tf_op jit(solution)/shard_map/ppermute | solution.py:452
  10.8 5.9 %collective-permute-start.2 = (bf16[8,3072]{1,0:T(8,128)(2,1)S(1)}, bf16[8,3072]{1,0:T(8,128)(2,1)S(1)}, u32[]{:S(2)}, u32[]{:S(2)}) collective-permute-start(bf16[8,3072]{1,0:T(8,128)(2,1)S(1)} %get-tuple-element.26), channel_id=1, source_target_pairs={{0,12},{1,13},{2,14},{3,15},{4,8},{5,9},{6,10},{7,11},{8,4},{9,5},... | collective-permute-start | bytes 147464 | tf_op jit(solution)/shard_map/ppermute | solution.py:452
  17.0 7.7 %slice-start.2 = ((s8[14680064]{0:T(1024)(128)(4,1)}), s8[4194304]{0:T(1024)(128)(4,1)S(1)}, s32[]{:S(2)}) async-start(s8[14680064]{0:T(1024)(128)(4,1)} %bitcast.3), calls=%async_computation.2 | async-start | bytes 8388608
  17.0 7.7 %slice-start.3 = ((s8[14680064]{0:T(1024)(128)(4,1)}), s8[2097152]{0:T(1024)(128)(4,1)S(1)}, s32[]{:S(2)}) async-start(s8[14680064]{0:T(1024)(128)(4,1)} %bitcast.3), calls=%async_computation.3 | async-start | bytes 4194304
  17.0 5.7 %collective-permute-start.3 = (bf16[24,4096]{1,0:T(8,128)(2,1)S(1)}, bf16[24,4096]{1,0:T(8,128)(2,1)S(1)}, u32[]{:S(2)}, u32[]{:S(2)}) collective-permute-start(bf16[24,4096]{1,0:T(8,128)(2,1)S(1)} %collect.1.after.refs_1_), channel_id=1, source_target_pairs={{0,2},{1,3},{2,0},{3,1},{4,6},{5,7},{6,4},{7,5},{8,10},{9,11},{10,... | collective-permute-start | bytes 589832 | tf_op jit(solution)/shard_map/ppermute | solution.py:452
  22.7 1.8 %collective-permute-start.4 = (bf16[48,4096]{1,0:T(8,128)(2,1)S(1)}, bf16[48,4096]{1,0:T(8,128)(2,1)S(1)}, u32[]{:S(2)}, u32[]{:S(2)}) collective-permute-start(bf16[48,4096]{1,0:T(8,128)(2,1)S(1)} %join.2.refs_1_), channel_id=1, source_target_pairs={{0,1},{1,0},{2,3},{3,2},{4,5},{5,4},{6,7},{7,6},{8,9},{9,8},{10,11... | collective-permute-start | bytes 1179656 | tf_op jit(solution)/shard_map/ppermute | solution.py:452
  31.0 1.8 %collective-permute-start.5 = (bf16[48,4096]{1,0:T(8,128)(2,1)S(1)}, bf16[48,4096]{1,0:T(8,128)(2,1)S(1)}, u32[]{:S(2)}, u32[]{:S(2)}) collective-permute-start(bf16[48,4096]{1,0:T(8,128)(2,1)S(1)} %get-tuple-element.31), channel_id=1, source_target_pairs={{0,1},{1,0},{2,3},{3,2},{4,5},{5,4},{6,7},{7,6},{8,9},{9,8},{10,11... | collective-permute-start | bytes 1179656 | tf_op jit(solution)/shard_map/ppermute | solution.py:452
  32.9 7.0 %collective-permute-start.6 = (bf16[24,4096]{1,0:T(8,128)(2,1)S(1)}, bf16[24,4096]{1,0:T(8,128)(2,1)S(1)}, u32[]{:S(2)}, u32[]{:S(2)}) collective-permute-start(bf16[24,4096]{1,0:T(8,128)(2,1)S(1)} %get-tuple-element.33), channel_id=1, source_target_pairs={{0,2},{1,3},{2,0},{3,1},{4,6},{5,7},{6,4},{7,5},{8,10},{9,11},{10,... | collective-permute-start | bytes 589832 | tf_op jit(solution)/shard_map/ppermute | solution.py:452
  40.1 4.5 %collective-permute-start.7 = (bf16[8,3072]{1,0:T(8,128)(2,1)S(1)}, bf16[8,3072]{1,0:T(8,128)(2,1)S(1)}, u32[]{:S(2)}, u32[]{:S(2)}) collective-permute-start(bf16[8,3072]{1,0:T(8,128)(2,1)S(1)} %get-tuple-element.35), channel_id=1, source_target_pairs={{0,4},{1,5},{2,6},{3,7},{4,0},{5,1},{6,2},{7,3},{8,12},{9,13},{10,... | collective-permute-start | bytes 147464 | tf_op jit(solution)/shard_map/ppermute | solution.py:452
  40.2 5.6 %collective-permute-start.8 = (bf16[8,3072]{1,0:T(8,128)(2,1)S(1)}, bf16[8,3072]{1,0:T(8,128)(2,1)S(1)}, u32[]{:S(2)}, u32[]{:S(2)}) collective-permute-start(bf16[8,3072]{1,0:T(8,128)(2,1)S(1)} %get-tuple-element.36), channel_id=1, source_target_pairs={{0,8},{1,9},{2,10},{3,11},{4,12},{5,13},{6,14},{7,15},{8,0},{9,1},... | collective-permute-start | bytes 147464 | tf_op jit(solution)/shard_map/ppermute | solution.py:452
  41.5 5.9 %collective-permute-start.9 = (bf16[8,3072]{1,0:T(8,128)(2,1)S(1)}, bf16[8,3072]{1,0:T(8,128)(2,1)S(1)}, u32[]{:S(2)}, u32[]{:S(2)}) collective-permute-start(bf16[8,3072]{1,0:T(8,128)(2,1)S(1)} %get-tuple-element.37), channel_id=1, source_target_pairs={{0,12},{1,13},{2,14},{3,15},{4,8},{5,9},{6,10},{7,11},{8,4},{9,5},... | collective-permute-start | bytes 147464 | tf_op jit(solution)/shard_map/ppermute | solution.py:452

commit v8 on v7

--- a/solution.py
+++ b/solution.py
@@ -238,63 +238,82 @@
     )(*[pltpu.with_memory_space_constraint(x, pltpu.HBM) for x in (*operands, weight)])
 
 
-def hidden_kernel(inputs, gate_weight, up_weight, hidden):
+def hidden_kernel(near, far, gate_weight, up_weight, hidden):
     columns = gate_weight.shape[1]
     step = 256 if columns % 256 == 0 else columns
-    x = padded(inputs[...])
+    quarter = near.shape[1] // 3
+    blocks = jnp.concatenate([near[...], far[...]], axis=0)
+    size = 128
+    row, lane = grid((size, size))
+    slot = row & 7
+    late = jnp.where(slot >= 3, 1, 0)
+    picks = [
+        one_hot((lane == row - slot + 6 + late) & (slot - 3 * late == m)) for m in range(3)
+    ]
+    tails = []
+    for first in range(0, blocks.shape[0], size):
+        some = blocks[first : first + size]
+        parts = [dot(picks[m], some[:, m * quarter : (m + 1) * quarter]) for m in range(3)]
+        tails.append((parts[0] + parts[1] + parts[2]).astype(BF16))
+    x = jnp.concatenate([blocks, jnp.concatenate(tails, axis=0)], axis=1)
     for f in range(0, columns, step):
         gate = dot(x, gate_weight[:, f : f + step])
         upper = dot(x, up_weight[:, f : f + step])
         hidden[:, f : f + step] = (gate / (1.0 + jnp.exp(-gate)) * upper).astype(BF16)
 
 
-def padded(x):
-    extra = -x.shape[0] % 128
-    if extra == 0:
-        return x
-    return jnp.concatenate([x, jnp.zeros((extra, x.shape[1]), x.dtype)], axis=0)
-
-
-def hidden_rows(inputs, gate_weight, up_weight):
-    rows, width = inputs.shape
-    columns = gate_weight.shape[1]
+def hidden_rows(near, far, gate_weight, up_weight):
+    rows = near.shape[0] + far.shape[0]
+    width, columns = gate_weight.shape
     return pl.pallas_call(
         hidden_kernel,
-        out_shape=jax.ShapeDtypeStruct((rows + -rows % 128, columns), BF16),
-        in_specs=[VMEM] * 3,
+        out_shape=jax.ShapeDtypeStruct((rows, columns), BF16),
+        in_specs=[VMEM] * 4,
         out_specs=VMEM,
         compiler_params=pltpu.CompilerParams(vmem_limit_bytes=4 * MIB * max(1, rows // 128)),
         cost_estimate=pl.CostEstimate(
             flops=4 * rows * width * columns, bytes_accessed=0, transcendentals=rows * columns
         ),
         name="hidden",
-    )(inputs, gate_weight, up_weight)
+    )(near, far, gate_weight, up_weight)
 
 
 def down_kernel(hidden, *refs):
-    weights, (keep, send) = refs[:PARTS], refs[PARTS:]
-    half = keep.shape[0]
+    weights, outs = refs[:PARTS], refs[PARTS:]
+    rows = hidden.shape[0]
+    quarter = outs[0].shape[1] // 3
+    size = 128
+    row, lane = grid((size, size))
+    slot = row & 7
+    picks = [one_hot((lane == row - slot + 3 * (slot - 6) + m) & (slot >= MOST)) for m in range(3)]
     h = hidden[...]
-    first = 0
-    for weight in weights:
-        for n in range(0, weight.shape[1], 512):
-            terms = dot(h, weight[:, n : n + 512])
-            keep[:, first : first + 512] = terms[:half]
-            send[:, first : first + 512] = terms[half : 2 * half].astype(BF16)
-            first += 512
-
-
-def down_rows(hidden, weights, rows):
-    columns = hidden.shape[1]
-    half, width = rows // 2, sum(weight.shape[1] for weight in weights)
+
+    def terms(first, count):
+        part, first = divmod(first, weights[0].shape[1])
+        return dot(h, weights[part][:, first : first + count])
+
+    step = min(512, quarter)
+    is_row = (lax.broadcasted_iota(jnp.int32, (rows, step), 0) & 7) < MOST
+    each = rows // len(outs)
+    for n in range(0, quarter, step):
+        tail = terms(3 * quarter + n, step).astype(BF16)
+        for m in range(3):
+            moved = jnp.concatenate(
+                [dot(picks[m], tail[i : i + size]) for i in range(0, rows, size)], axis=0
+            )
+            value = jnp.where(is_row, terms(m * quarter + n, step), moved).astype(BF16)
+            for k, out in enumerate(outs):
+                out[:, m * quarter + n : m * quarter + n + step] = value[k * each : (k + 1) * each]
+
+
+def down_rows(hidden, weights):
+    rows, columns = hidden.shape
+    width = sum(weight.shape[1] for weight in weights)
     return pl.pallas_call(
         down_kernel,
-        out_shape=(
-            jax.ShapeDtypeStruct((half, width), F32),
-            jax.ShapeDtypeStruct((half, width), BF16),
-        ),
+        out_shape=[jax.ShapeDtypeStruct((rows // 4, width // 4 * 3), BF16)] * 4,
         in_specs=[VMEM] * (1 + PARTS),
-        out_specs=(VMEM, VMEM),
+        out_specs=[VMEM] * 4,
         compiler_params=pltpu.CompilerParams(vmem_limit_bytes=4 * MIB * max(1, rows // 128)),
         cost_estimate=pl.CostEstimate(
             flops=2 * rows * width * columns, bytes_accessed=0, transcendentals=0
@@ -331,31 +350,6 @@
     )(pltpu.with_memory_space_constraint(source, pltpu.HBM), after)
 
 
-def collect_kernel(token, *refs):
-    arrived, gathered = refs[:-1], refs[-1]
-    row, lane = grid((MOST * EXPERTS, 8 * EXPERTS))
-    plane = sum([jnp.where(row >= MOST * e, 1, 0) for e in range(1, EXPERTS)])
-    slot = row - MOST * plane
-    late = jnp.where(slot >= 3, 1, 0)
-    picks = [one_hot(lane == plane * 8 + slot)]
-    for m in range(3):
-        picks.append(one_hot((lane == plane * 8 + 6 + late) & (slot - 3 * late == m)))
-    quarter = gathered.shape[1] // 4
-    for m, value in enumerate(unpack(picks, jnp.concatenate([x[...] for x in arrived], axis=0))):
-        gathered[:, m * quarter : (m + 1) * quarter] = value.astype(BF16)
-
-
-def collect(token, arrived):
-    return pl.pallas_call(
-        collect_kernel,
-        out_shape=jax.ShapeDtypeStruct((MOST * EXPERTS, arrived[0].shape[1] // 3 * 4), BF16),
-        in_specs=[ANY] + [VMEM] * EXPERTS,
-        out_specs=VMEM,
-        compiler_params=pltpu.CompilerParams(vmem_limit_bytes=2 * MIB),
-        name="collect",
-    )(token, *arrived)
-
-
 def join_kernel(*refs):
     out, row = refs[-1], 0
     for piece in refs[1:-1]:
@@ -375,77 +369,53 @@
     )(after, *pieces)
 
 
-def fold_kernel(held, arrived, keep, send):
-    half = keep.shape[0]
-    keep[...] = held[:half] + arrived[:half].astype(F32)
-    send[...] = (held[half:] + arrived[half:].astype(F32)).astype(BF16)
-
-
-def fold(held, arrived):
-    half, width = held.shape[0] // 2, held.shape[1]
+def fold_kernel(held, arrived, after, *outs):
+    each = outs[0].shape[0]
+    for k, out in enumerate(outs):
+        block = slice(k * each, (k + 1) * each)
+        out[...] = (held[block].astype(F32) + arrived[block].astype(F32)).astype(BF16)
+
+
+def fold(held, arrived, after):
+    rows, width = held.shape
     return pl.pallas_call(
         fold_kernel,
-        out_shape=(
-            jax.ShapeDtypeStruct((half, width), F32),
-            jax.ShapeDtypeStruct((half, width), BF16),
-        ),
-        in_specs=[VMEM] * 2,
-        out_specs=(VMEM, VMEM),
-        compiler_params=pltpu.CompilerParams(vmem_limit_bytes=4 * MIB * max(1, half // 32)),
+        out_shape=[jax.ShapeDtypeStruct((rows // 2, width), BF16)] * 2,
+        in_specs=[VMEM] * 2 + [ANY],
+        out_specs=[VMEM] * 2,
+        compiler_params=pltpu.CompilerParams(vmem_limit_bytes=MIB * max(1, rows // 64)),
+        cost_estimate=pl.CostEstimate(flops=0, bytes_accessed=16 * MIB, transcendentals=0),
         name="fold",
-    )(held, arrived)
-
-
-def last_fold_kernel(held, arrived, *packed):
-    block = (held[...] + arrived[...].astype(F32)).astype(BF16)
-    place, row = grid((8 * EXPERTS, MOST * EXPERTS))
-    plane, slot = place // 8, place % 8
-    picks = [one_hot((row == plane * MOST + slot) & (slot < MOST))]
-    for m in range(3):
-        picks.append(one_hot((row == plane * MOST + 3 * (slot - 6) + m) & (slot >= MOST)))
-    quarter = block.shape[1] // 4
-    for m, value in enumerate(pack(picks, block)):
-        for k, target in enumerate(packed):
-            target[:, m * quarter : (m + 1) * quarter] = value[8 * k : 8 * k + 8]
-
-
-def last_fold(held, arrived):
-    return pl.pallas_call(
-        last_fold_kernel,
-        out_shape=[jax.ShapeDtypeStruct((8, held.shape[1] // 4 * 3), BF16)] * EXPERTS,
-        in_specs=[VMEM] * 2,
-        out_specs=[VMEM] * EXPERTS,
-        compiler_params=pltpu.CompilerParams(vmem_limit_bytes=2 * MIB),
-        name="last_fold",
-    )(held, arrived)
-
-
-def combine_kernel(share, take, *refs):
-    results, out = refs[:-1], refs[-1]
+    )(held, arrived, after)
+
+
+def combine_kernel(first, share, take, *refs):
+    results, before, out = refs[:2], refs[2:-1], refs[-1]
     rows = out.shape[0]
     quarter = results[0].shape[1] // 3
-    picks = [take[i][:, : 8 * EXPERTS] for i in range(4)]
+    picks = [take[i][:, 8 * first : 8 * first + 16] for i in range(4)]
     shares = share[:, :1]
     block = jnp.concatenate([x[...] for x in results], axis=0)
     for m, value in enumerate(unpack(picks, block)):
+        lanes = slice(m * quarter, (m + 1) * quarter)
         value = value * shares
-        out[:, m * quarter : (m + 1) * quarter] = (value[:rows] + value[rows:]).astype(BF16)
-
-
-def combine(share, take, results):
-    return pl.pallas_call(
-        combine_kernel,
-        out_shape=jax.ShapeDtypeStruct((share.shape[0] // 2, results[0].shape[1] // 3 * 4), BF16),
-        in_specs=[VMEM] * (2 + EXPERTS),
+        value = value[:rows] + value[rows:]
+        for x in before:
+            value = value + x[:, lanes]
+        out[:, lanes] = value.astype(out.dtype)
+
+
+def combine(first, share, take, results, before, dtype):
+    width = results[0].shape[1] // 3 * 4
+    return pl.pallas_call(
+        functools.partial(combine_kernel, first),
+        out_shape=jax.ShapeDtypeStruct((share.shape[0] // 2, width), dtype),
+        in_specs=[VMEM] * (4 + len(before)),
         out_specs=VMEM,
         compiler_params=pltpu.CompilerParams(vmem_limit_bytes=2 * MIB),
+        cost_estimate=pl.CostEstimate(flops=0, bytes_accessed=16 * MIB, transcendentals=0),
         name="combine",
-    )(share, take, *results)
-
-
-def between_planes(blocks, count):
-    plane = count // EXPERTS
-    return [blocks[0]] + [swap(blocks[k], count, k * plane) for k in range(1, EXPERTS)]
+    )(share, take, *results, *before)
 
 
 def swap(value, count, bit):
@@ -475,17 +445,24 @@
         router_weight, routes, down_weight,
     )
 
-    gathered = collect(share, between_planes(packed, count))
-    down_rest, token = load(down_weight, gathered, down.shape[1])
+    packed = [packed[0]] + [swap(packed[k], count, k * plane) for k in range(1, EXPERTS)]
+    near = join(share, *packed[:2])
+    down_rest, token = load(down_weight, near, down.shape[1])
+    far = join(token, *packed[2:])
     for bit in bits:
-        gathered = join(token, gathered, swap(gathered, count, bit))
-
-    hidden = hidden_rows(gathered, gate_weight, up_weight)
-    held, send = down_rows(hidden, (down, down_rest), gathered.shape[0])
-    for bit in bits[:0:-1]:
-        held, send = fold(held, swap(send, count, bit))
-    results = between_planes(last_fold(held, swap(send, count, bits[0])), count)
-    return (attended, combine(share, take, results))
+        near = join(share, near, swap(near, count, bit))
+        far = join(share, far, swap(far, count, bit))
+
+    hidden = hidden_rows(near, far, gate_weight, up_weight)
+    near, near_send, far, far_send = down_rows(hidden, (down, down_rest))
+    for bit in reversed(bits):
+        far, far_send = fold(far, swap(far_send, count, bit), share)
+        near, near_send = fold(near, swap(near_send, count, bit), far)
+    far = swap(far, count, 2 * plane)
+    far_send = swap(far_send, count, 3 * plane)
+    near_send = swap(near_send, count, plane)
+    total = combine(2, share, take, [far, far_send], [], F32)
+    return (attended, combine(0, share, take, [near, near_send], [total], BF16))
 
 
 def solution(mesh):

time: 48.3 us -> 46.9 us (0.971)
  waiting for transfers between devices: 18.1 us -> 13.4 us
  starting transfers between devices: 13.5 us -> 16.5 us
    ppermute x10 -> x14, waiting for transfers between devices: 18.1 us -> 13.4 us  [swap(): return lax.ppermute(value, 'dp', [(i, i ^ bit) for i in range(count)])]
    ppermute x10 -> x14, starting transfers between devices: 13.5 us -> 16.5 us  [swap(): return lax.ppermute(value, 'dp', [(i, i ^ bit) for i in range(count)])]
    pallas_call x6 -> x8, Pallas kernels: 7.72 us -> 8.3 us  [the longest x1 4.4 us: hidden_rows(): pl.pallas_call(hidden_kernel, out_shape=jax.ShapeDtypeStruct((rows, colum...]
  transfers between devices with their start and end apart: 10 -> 14, of which waited for: 8 -> 7; matrix products, arithmetic and copies ran while one was open for 0% -> 0% of each run, Pallas kernels for 7% -> 8%
where the time goes in v8:
time: 46.9 us; the launch traced here: 46.7 us
  starting transfers between devices  16.5 us (35%)
  Pallas kernels  16 us (34%)
  waiting for transfers between devices  13.4 us (29%)
  between operations  0.85 us (2%)
    ppermute x14, starting transfers between devices, swap(): return lax.ppermute(value, 'dp', [(i, i ^ bit) for i in range(count)])  16.5 us
    ppermute x14, waiting for transfers between devices, swap(): return lax.ppermute(value, 'dp', [(i, i ^ bit) for i in range(count)])  13.4 us
    pallas_call x1, Pallas kernels, attend(): pl.pallas_call(functools.partial(attend_kernel, plane), out_shape=(jax.Sh...  4.45 us
    pallas_call x1, Pallas kernels, hidden_rows(): pl.pallas_call(hidden_kernel, out_shape=jax.ShapeDtypeStruct((rows, colum...  4.4 us
    pallas_call x1, Pallas kernels, load(): pl.pallas_call(functools.partial(load_kernel, first), out_shape=(pltpu.VM...  3.19 us
    pallas_call x1, Pallas kernels, down_rows(): pl.pallas_call(down_kernel, out_shape=[jax.ShapeDtypeStruct((rows // 4, w...  2.69 us
    pallas_call x2, Pallas kernels, combine(): pl.pallas_call(functools.partial(combine_kernel, first), out_shape=jax.Sh...  1.06 us
  transfers between devices with their start and end apart: 14, of which 7 were waited for; matrix products, arithmetic and copies ran while one was open for 0% of the time, Pallas kernels for 8%

profile of v8, /device:TPU:0, one launch (start us, length us, event | category | flops | bytes accessed | tf_op | source)
XLA Modules:
  0.0 46.7 jit_solution(5746778654878627408)
XLA Ops:
  0.6 0.0 slice-start
  0.6 0.0 slice-start.1
  0.7 4.5 %attend.1 = (bf16[8,4096]{1,0:T(8,128)(2,1)}, bf16[8,3072]{1,0:T(8,128)(2,1)S(1)}, bf16[8,3072]{1,0:T(8,128)(2,1)S(1)}, bf16[8,3072]{1,0:T(8,128)(2,1)S(1)}, bf1...) custom-call(bf16[8,4096]{1,0:T(8,128)(2,1)} %refs_0_.1, ...), custom_call_target="tpu_custom_call" | custom-call | tf_op jit(solution)/shard_map/attend/pallas_call | solution.py:220
  5.1 3.1 %collective-permute-start = (bf16[8,3072]{1,0:T(8,128)(2,1)S(1)}, bf16[8,3072]{1,0:T(8,128)(2,1)S(1)}, u32[]{:S(2)}, u32[]{:S(2)}) collective-permute-start(bf16[8,3072]{1,0:T(8,128)(2,1)S(1)} %get-tuple-element.28), channel_id=1, source_target_pairs={{0,4},{1,5},{2,6},{3,7},{4,0},{5,1},{6,2},{7,3},{8,12},{9,13},{10,... | collective-permute-start | bytes 147464 | tf_op jit(solution)/shard_map/ppermute | solution.py:422
  8.2 2.6 %collective-permute-start.3 = (bf16[8,3072]{1,0:T(8,128)(2,1)S(1)}, bf16[8,3072]{1,0:T(8,128)(2,1)S(1)}, u32[]{:S(2)}, u32[]{:S(2)}) collective-permute-start(bf16[8,3072]{1,0:T(8,128)(2,1)S(1)} %get-tuple-element.30), channel_id=1, source_target_pairs={{0,8},{1,9},{2,10},{3,11},{4,12},{5,13},{6,14},{7,15},{8,0},{9,1},... | collective-permute-start | bytes 147464 | tf_op jit(solution)/shard_map/ppermute | solution.py:422
  10.8 0.0 collective-permute-start.4
  10.8 0.0 slice-start.2
  10.9 1.8 %collective-permute-start.1 = (bf16[16,3072]{1,0:T(8,128)(2,1)S(1)}, bf16[16,3072]{1,0:T(8,128)(2,1)S(1)}, u32[]{:S(2)}, u32[]{:S(2)}) collective-permute-start(bf16[16,3072]{1,0:T(8,128)(2,1)S(1)} %join.6.refs_1_.after), channel_id=1, source_target_pairs={{0,2},{1,3},{2,0},{3,1},{4,6},{5,7},{6,4},{7,5},{8,10},{9,11},{10,... | collective-permute-start | bytes 294920 | tf_op jit(solution)/shard_map/ppermute | solution.py:422
  12.7 3.2 %load.1 = (bf16[1792,2048]{1,0:T(8,128)(2,1)S(1)}, f32[8,128]{1,0:T(8,128)S(1)}) custom-call(bf16[1792,4096]{1,0:T(8,128)(2,1)} %source.1, bf16[16,3072]{1,0:T(8,128)(2,1)S(1)} %join.6.refs_1_.after), custom_call_target="tpu_custom_call" | custom-call | bytes 7340032 | tf_op jit(solution)/shard_map/load/pallas_call | solution.py:336
  15.9 0.8 %collective-permute-done.4.refs_2_ = bf16[8,3072]{1,0:T(8,128)(2,1)S(1)} collective-permute-done((bf16[8,3072]{1,0:T(8,128)(2,1)S(1)}, bf16[8,3072]{1,0:T(8,128)(2,1)S(1)}, u32[]{:S(2)}, u32[]{:S(2)}) %collective-permute-start.4) | collective-permute-done | bytes 49184 | tf_op jit(solution)/shard_map/ppermute | solution.py:422
  16.7 1.6 %collective-permute-start.5 = (bf16[16,3072]{1,0:T(8,128)(2,1)S(1)}, bf16[16,3072]{1,0:T(8,128)(2,1)S(1)}, u32[]{:S(2)}, u32[]{:S(2)}) collective-permute-start(bf16[16,3072]{1,0:T(8,128)(2,1)S(1)} %join.9.refs_1_), channel_id=1, source_target_pairs={{0,2},{1,3},{2,0},{3,1},{4,6},{5,7},{6,4},{7,5},{8,10},{9,11},{10,... | collective-permute-start | bytes 294920 | tf_op jit(solution)/shard_map/ppermute | solution.py:422
  18.3 0.0 collective-permute-done.1.refs_2_
  18.3 0.1 collective-permute-start.2
  18.4 3.0 %collective-permute-done.5.refs_2_ = bf16[16,3072]{1,0:T(8,128)(2,1)S(1)} collective-permute-done((bf16[16,3072]{1,0:T(8,128)(2,1)S(1)}, bf16[16,3072]{1,0:T(8,128)(2,1)S(1)}, u32[]{:S(2)}, u32[]{:S(2)}) %collective-permute-start.5) | collective-permute-done | bytes 98336 | tf_op jit(solution)/shard_map/ppermute | solution.py:422
  21.4 0.1 collective-permute-start.6
  21.5 1.4 %collective-permute-done.6.refs_2_ = bf16[32,3072]{1,0:T(8,128)(2,1)S(1)} collective-permute-done((bf16[32,3072]{1,0:T(8,128)(2,1)S(1)}, bf16[32,3072]{1,0:T(8,128)(2,1)S(1)}, u32[]{:S(2)}, u32[]{:S(2)}) %collective-permute-start.6) | collective-permute-done | bytes 196640 | tf_op jit(solution)/shard_map/ppermute | solution.py:422
  23.0 4.4 %hidden.1 = bf16[128,1792]{1,0:T(8,128)(2,1)S(1)} custom-call(bf16[64,3072]{1,0:T(8,128)(2,1)S(1)} %join.8.near, bf16[64,3072]{1,0:T(8,128)(2,1)S(1)} %join.11.far, bf16[4096,1792]{1,0:T(8,128)(2,1)S(1)} %bitcast.4, bf16[4096,1792]{1,0:T(8,128)(2,1)S(1)} %copy-done), custom_call_target="tpu_custom_call" | custom-call | flops 3758096384 | tf_op jit(solution)/shard_map/hidden/pallas_call | solution.py:268
  27.4 2.7 %down.1 = (bf16[32,3072]{1,0:T(8,128)(2,1)S(1)}, bf16[32,3072]{1,0:T(8,128)(2,1)S(1)}, bf16[32,3072]{1,0:T(8,128)(2,1)S(1)}, bf16[32,3072]{1,0:T(8,128)(2,1)S(1)}) custom-call(bf16[128,1792]{1,0:T(8,128)(2,1)S(1)} %hidden.1, bf16[1792,2048]{1,0:T(8,128)(2,1)S(1)} %get-tuple-element.32.refs_0_, bf16[1792,2048]{1,0:T(8,128)(2,1)S(1)} %get-tuple-element.33.refs_1_), custom_call_target="tpu_custom_call" | custom-call | flops 1879048192 | tf_op jit(solution)/shard_map/down/pallas_call | solution.py:312
  30.1 0.2 collective-permute-start.8
  30.3 0.4 collective-permute-start.7
  30.7 0.9 %collective-permute-done.8.arrived = bf16[32,3072]{1,0:T(8,128)(2,1)S(1)} collective-permute-done((bf16[32,3072]{1,0:T(8,128)(2,1)S(1)}, bf16[32,3072]{1,0:T(8,128)(2,1)S(1)}, u32[]{:S(2)}, u32[]{:S(2)}) %collective-permute-start.8) | collective-permute-done | bytes 196640 | tf_op jit(solution)/shard_map/ppermute | solution.py:422
  31.7 1.6 %collective-permute-start.10 = (bf16[16,3072]{1,0:T(8,128)(2,1)S(1)}, bf16[16,3072]{1,0:T(8,128)(2,1)S(1)}, u32[]{:S(2)}, u32[]{:S(2)}) collective-permute-start(bf16[16,3072]{1,0:T(8,128)(2,1)S(1)} %get-tuple-element.41), channel_id=1, source_target_pairs={{0,2},{1,3},{2,0},{3,1},{4,6},{5,7},{6,4},{7,5},{8,10},{9,11},{10,... | collective-permute-start | bytes 294920 | tf_op jit(solution)/shard_map/ppermute | solution.py:422
  33.3 0.5 %collective-permute-start.9 = (bf16[16,3072]{1,0:T(8,128)(2,1)S(1)}, bf16[16,3072]{1,0:T(8,128)(2,1)S(1)}, u32[]{:S(2)}, u32[]{:S(2)}) collective-permute-start(bf16[16,3072]{1,0:T(8,128)(2,1)S(1)} %get-tuple-element.40), channel_id=1, source_target_pairs={{0,2},{1,3},{2,0},{3,1},{4,6},{5,7},{6,4},{7,5},{8,10},{9,11},{10,... | collective-permute-start | bytes 294920 | tf_op jit(solution)/shard_map/ppermute | solution.py:422
  33.9 3.4 %collective-permute-done.10.arrived = bf16[16,3072]{1,0:T(8,128)(2,1)S(1)} collective-permute-done((bf16[16,3072]{1,0:T(8,128)(2,1)S(1)}, bf16[16,3072]{1,0:T(8,128)(2,1)S(1)}, u32[]{:S(2)}, u32[]{:S(2)}) %collective-permute-start.10) | collective-permute-done | bytes 98336 | tf_op jit(solution)/shard_map/ppermute | solution.py:422
  37.3 3.3 %collective-permute-start.13 = (bf16[8,3072]{1,0:T(8,128)(2,1)S(1)}, bf16[8,3072]{1,0:T(8,128)(2,1)S(1)}, u32[]{:S(2)}, u32[]{:S(2)}) collective-permute-start(bf16[8,3072]{1,0:T(8,128)(2,1)S(1)} %get-tuple-element.45), channel_id=1, source_target_pairs={{0,12},{1,13},{2,14},{3,15},{4,8},{5,9},{6,10},{7,11},{8,4},{9,5},... | collective-permute-start | bytes 147464 | tf_op jit(solution)/shard_map/ppermute | solution.py:422
  40.7 0.0 collective-permute-done.9.arrived
  40.7 1.2 %collective-permute-start.11 = (bf16[8,3072]{1,0:T(8,128)(2,1)S(1)}, bf16[8,3072]{1,0:T(8,128)(2,1)S(1)}, u32[]{:S(2)}, u32[]{:S(2)}) collective-permute-start(bf16[8,3072]{1,0:T(8,128)(2,1)S(1)} %get-tuple-element.44), channel_id=1, source_target_pairs={{0,4},{1,5},{2,6},{3,7},{4,0},{5,1},{6,2},{7,3},{8,12},{9,13},{10,... | collective-permute-start | bytes 147464 | tf_op jit(solution)/shard_map/ppermute | solution.py:422
  41.9 1.5 %collective-permute-done.13.refs_1_ = bf16[8,3072]{1,0:T(8,128)(2,1)S(1)} collective-permute-done((bf16[8,3072]{1,0:T(8,128)(2,1)S(1)}, bf16[8,3072]{1,0:T(8,128)(2,1)S(1)}, u32[]{:S(2)}, u32[]{:S(2)}) %collective-permute-start.13) | collective-permute-done | bytes 49184 | tf_op jit(solution)/shard_map/ppermute | solution.py:422
  43.4 2.3 %collective-permute-done.12.refs_0_ = bf16[8,3072]{1,0:T(8,128)(2,1)S(1)} collective-permute-done((bf16[8,3072]{1,0:T(8,128)(2,1)S(1)}, bf16[8,3072]{1,0:T(8,128)(2,1)S(1)}, u32[]{:S(2)}, u32[]{:S(2)}) %collective-permute-start.12) | collective-permute-done | bytes 49184 | tf_op jit(solution)/shard_map/ppermute | solution.py:422
  45.7 0.2 combine.2.refs_2_
  45.9 0.0 collective-permute-done.11.refs_1_
  45.9 0.8 %combine.3 = bf16[8,4096]{1,0:T(8,128)(2,1)} custom-call(f32[16,128]{1,0:T(8,128)S(1)} %get-tuple-element.25.refs_0_.after.share, bf16[4,16,128]{2,1,0:T(8,128)(2,1)S(1)} %get-tuple-element.26.take, bf16[8,3072]{1,0:T(8,128)(2,1)S(1)} %get-tuple-element.43.refs_0_, bf16[8,3072]{1,0:T(8,128)(2,1)S(1)} %collective-permute-done.11.refs_1_, ...), custom_call_target="tpu_custom_call" | custom-call | bytes 16777216 | tf_op jit(solution)/shard_map/combine/pallas_call | solution.py:410
  (23 shorter events, 0.3 us)
Async XLA Ops:
  0.6 22.3 %slice-start = ((s8[14680064]{0:T(1024)(128)(4,1)}), s8[4194304]{0:T(1024)(128)(4,1)S(1)}, s32[]{:S(2)}) async-start(s8[14680064]{0:T(1024)(128)(4,1)} %bitcast.3), calls=%async_computation | async-start | bytes 8388608
  0.6 22.3 %slice-start.1 = ((s8[14680064]{0:T(1024)(128)(4,1)}), s8[4194304]{0:T(1024)(128)(4,1)S(1)}, s32[]{:S(2)}) async-start(s8[14680064]{0:T(1024)(128)(4,1)} %bitcast.3), calls=%async_computation.1 | async-start | bytes 8388608
  0.7 22.3 %copy-start = (bf16[4096,1792]{1,0:T(8,128)(2,1)S(1)}, bf16[4096,1792]{1,0:T(8,128)(2,1)}, u32[]{:S(2)}) copy-start(bf16[4096,1792]{1,0:T(8,128)(2,1)} %up_weight.1) | copy-start | bytes 44040196
  5.1 5.7 %collective-permute-start = (bf16[8,3072]{1,0:T(8,128)(2,1)S(1)}, bf16[8,3072]{1,0:T(8,128)(2,1)S(1)}, u32[]{:S(2)}, u32[]{:S(2)}) collective-permute-start(bf16[8,3072]{1,0:T(8,128)(2,1)S(1)} %get-tuple-element.28), channel_id=1, source_target_pairs={{0,4},{1,5},{2,6},{3,7},{4,0},{5,1},{6,2},{7,3},{8,12},{9,13},{10,... | collective-permute-start | bytes 147464 | tf_op jit(solution)/shard_map/ppermute | solution.py:422
  8.2 7.6 %collective-permute-start.3 = (bf16[8,3072]{1,0:T(8,128)(2,1)S(1)}, bf16[8,3072]{1,0:T(8,128)(2,1)S(1)}, u32[]{:S(2)}, u32[]{:S(2)}) collective-permute-start(bf16[8,3072]{1,0:T(8,128)(2,1)S(1)} %get-tuple-element.30), channel_id=1, source_target_pairs={{0,8},{1,9},{2,10},{3,11},{4,12},{5,13},{6,14},{7,15},{8,0},{9,1},... | collective-permute-start | bytes 147464 | tf_op jit(solution)/shard_map/ppermute | solution.py:422
  10.8 5.9 %collective-permute-start.4 = (bf16[8,3072]{1,0:T(8,128)(2,1)S(1)}, bf16[8,3072]{1,0:T(8,128)(2,1)S(1)}, u32[]{:S(2)}, u32[]{:S(2)}) collective-permute-start(bf16[8,3072]{1,0:T(8,128)(2,1)S(1)} %get-tuple-element.31), channel_id=1, source_target_pairs={{0,12},{1,13},{2,14},{3,15},{4,8},{5,9},{6,10},{7,11},{8,4},{9,5},... | collective-permute-start | bytes 147464 | tf_op jit(solution)/shard_map/ppermute | solution.py:422
  10.8 12.2 %slice-start.2 = ((s8[14680064]{0:T(1024)(128)(4,1)}), s8[4194304]{0:T(1024)(128)(4,1)S(1)}, s32[]{:S(2)}) async-start(s8[14680064]{0:T(1024)(128)(4,1)} %bitcast.3), calls=%async_computation.2 | async-start | bytes 8388608
  10.8 12.1 %slice-start.3 = ((s8[14680064]{0:T(1024)(128)(4,1)}), s8[2097152]{0:T(1024)(128)(4,1)S(1)}, s32[]{:S(2)}) async-start(s8[14680064]{0:T(1024)(128)(4,1)} %bitcast.3), calls=%async_computation.3 | async-start | bytes 4194304
  10.9 7.4 %collective-permute-start.1 = (bf16[16,3072]{1,0:T(8,128)(2,1)S(1)}, bf16[16,3072]{1,0:T(8,128)(2,1)S(1)}, u32[]{:S(2)}, u32[]{:S(2)}) collective-permute-start(bf16[16,3072]{1,0:T(8,128)(2,1)S(1)} %join.6.refs_1_.after), channel_id=1, source_target_pairs={{0,2},{1,3},{2,0},{3,1},{4,6},{5,7},{6,4},{7,5},{8,10},{9,11},{10,... | collective-permute-start | bytes 294920 | tf_op jit(solution)/shard_map/ppermute | solution.py:422
  16.7 4.7 %collective-permute-start.5 = (bf16[16,3072]{1,0:T(8,128)(2,1)S(1)}, bf16[16,3072]{1,0:T(8,128)(2,1)S(1)}, u32[]{:S(2)}, u32[]{:S(2)}) collective-permute-start(bf16[16,3072]{1,0:T(8,128)(2,1)S(1)} %join.9.refs_1_), channel_id=1, source_target_pairs={{0,2},{1,3},{2,0},{3,1},{4,6},{5,7},{6,4},{7,5},{8,10},{9,11},{10,... | collective-permute-start | bytes 294920 | tf_op jit(solution)/shard_map/ppermute | solution.py:422
  18.3 3.2 %collective-permute-start.2 = (bf16[32,3072]{1,0:T(8,128)(2,1)S(1)}, bf16[32,3072]{1,0:T(8,128)(2,1)S(1)}, u32[]{:S(2)}, u32[]{:S(2)}) collective-permute-start(bf16[32,3072]{1,0:T(8,128)(2,1)S(1)} %join.7.refs_1_), channel_id=1, source_target_pairs={{0,1},{1,0},{2,3},{3,2},{4,5},{5,4},{6,7},{7,6},{8,9},{9,8},{10,11... | collective-permute-start | bytes 589832 | tf_op jit(solution)/shard_map/ppermute | solution.py:422
  21.4 1.5 %collective-permute-start.6 = (bf16[32,3072]{1,0:T(8,128)(2,1)S(1)}, bf16[32,3072]{1,0:T(8,128)(2,1)S(1)}, u32[]{:S(2)}, u32[]{:S(2)}) collective-permute-start(bf16[32,3072]{1,0:T(8,128)(2,1)S(1)} %join.10.refs_1_), channel_id=1, source_target_pairs={{0,1},{1,0},{2,3},{3,2},{4,5},{5,4},{6,7},{7,6},{8,9},{9,8},{10,11... | collective-permute-start | bytes 589832 | tf_op jit(solution)/shard_map/ppermute | solution.py:422
  30.1 1.5 %collective-permute-start.8 = (bf16[32,3072]{1,0:T(8,128)(2,1)S(1)}, bf16[32,3072]{1,0:T(8,128)(2,1)S(1)}, u32[]{:S(2)}, u32[]{:S(2)}) collective-permute-start(bf16[32,3072]{1,0:T(8,128)(2,1)S(1)} %get-tuple-element.37), channel_id=1, source_target_pairs={{0,1},{1,0},{2,3},{3,2},{4,5},{5,4},{6,7},{7,6},{8,9},{9,8},{10,11... | collective-permute-start | bytes 589832 | tf_op jit(solution)/shard_map/ppermute | solution.py:422
  30.3 3.0 %collective-permute-start.7 = (bf16[32,3072]{1,0:T(8,128)(2,1)S(1)}, bf16[32,3072]{1,0:T(8,128)(2,1)S(1)}, u32[]{:S(2)}, u32[]{:S(2)}) collective-permute-start(bf16[32,3072]{1,0:T(8,128)(2,1)S(1)} %get-tuple-element.35), channel_id=1, source_target_pairs={{0,1},{1,0},{2,3},{3,2},{4,5},{5,4},{6,7},{7,6},{8,9},{9,8},{10,11... | collective-permute-start | bytes 589832 | tf_op jit(solution)/shard_map/ppermute | solution.py:422
  31.7 5.6 %collective-permute-start.10 = (bf16[16,3072]{1,0:T(8,128)(2,1)S(1)}, bf16[16,3072]{1,0:T(8,128)(2,1)S(1)}, u32[]{:S(2)}, u32[]{:S(2)}) collective-permute-start(bf16[16,3072]{1,0:T(8,128)(2,1)S(1)} %get-tuple-element.41), channel_id=1, source_target_pairs={{0,2},{1,3},{2,0},{3,1},{4,6},{5,7},{6,4},{7,5},{8,10},{9,11},{10,... | collective-permute-start | bytes 294920 | tf_op jit(solution)/shard_map/ppermute | solution.py:422
  33.3 7.3 %collective-permute-start.9 = (bf16[16,3072]{1,0:T(8,128)(2,1)S(1)}, bf16[16,3072]{1,0:T(8,128)(2,1)S(1)}, u32[]{:S(2)}, u32[]{:S(2)}) collective-permute-start(bf16[16,3072]{1,0:T(8,128)(2,1)S(1)} %get-tuple-element.40), channel_id=1, source_target_pairs={{0,2},{1,3},{2,0},{3,1},{4,6},{5,7},{6,4},{7,5},{8,10},{9,11},{10,... | collective-permute-start | bytes 294920 | tf_op jit(solution)/shard_map/ppermute | solution.py:422
  37.3 6.1 %collective-permute-start.13 = (bf16[8,3072]{1,0:T(8,128)(2,1)S(1)}, bf16[8,3072]{1,0:T(8,128)(2,1)S(1)}, u32[]{:S(2)}, u32[]{:S(2)}) collective-permute-start(bf16[8,3072]{1,0:T(8,128)(2,1)S(1)} %get-tuple-element.45), channel_id=1, source_target_pairs={{0,12},{1,13},{2,14},{3,15},{4,8},{5,9},{6,10},{7,11},{8,4},{9,5},... | collective-permute-start | bytes 147464 | tf_op jit(solution)/shard_map/ppermute | solution.py:422
  40.7 5.0 %collective-permute-start.12 = (bf16[8,3072]{1,0:T(8,128)(2,1)S(1)}, bf16[8,3072]{1,0:T(8,128)(2,1)S(1)}, u32[]{:S(2)}, u32[]{:S(2)}) collective-permute-start(bf16[8,3072]{1,0:T(8,128)(2,1)S(1)} %get-tuple-element.42.after), channel_id=1, source_target_pairs={{0,8},{1,9},{2,10},{3,11},{4,12},{5,13},{6,14},{7,15},{8,0},{9,1},... | collective-permute-start | bytes 147464 | tf_op jit(solution)/shard_map/ppermute | solution.py:422
  40.7 5.2 %collective-permute-start.11 = (bf16[8,3072]{1,0:T(8,128)(2,1)S(1)}, bf16[8,3072]{1,0:T(8,128)(2,1)S(1)}, u32[]{:S(2)}, u32[]{:S(2)}) collective-permute-start(bf16[8,3072]{1,0:T(8,128)(2,1)S(1)} %get-tuple-element.44), channel_id=1, source_target_pairs={{0,4},{1,5},{2,6},{3,7},{4,0},{5,1},{6,2},{7,3},{8,12},{9,13},{10,... | collective-permute-start | bytes 147464 | tf_op jit(solution)/shard_map/ppermute | solution.py:422

commit v9 on v8

--- a/solution.py
+++ b/solution.py
@@ -13,7 +13,7 @@
 EXPERTS = 4
 MIB = 1 << 20
 WAYS = 4
-PARTS = 2
+PARTS = (2, 1, 1)
 MOST = 6
 F32 = jnp.float32
 BF16 = jnp.bfloat16
@@ -70,12 +70,10 @@
         pltpu.make_async_copy(source, target, semaphores.at[i])
         for i, (source, target) in enumerate(zip(sources, held))
     ]
-    for copy in copies + weight:
+    for copy in copies[9:] + copies[:9] + weight:
         copy.start()
     (queries, cache_keys, new_keys, lengths, cache_values, new_values, residual, gain, router,
      routes) = held
-    for copy in copies[:4] + copies[9:]:
-        copy.wait()
     rows, width = queries.shape
     positions = cache_keys.shape[1]
     groups = HEADS // KV_HEADS
@@ -83,72 +81,7 @@
     every = rows * positions
     block = groups * rows
 
-    query = queries[...].astype(F32)
-    stacked = jnp.concatenate(
-        [query[:, h * HEAD_DIM : (h + 1) * HEAD_DIM] for h in range(HEADS)], axis=0
-    )
-    stacked_b = stacked.astype(BF16)
-    keys = cache_keys[...].reshape(every, KV_HEADS * HEAD_DIM)
-    newk = new_keys[...].astype(F32)
-
-    row_of = lax.broadcasted_iota(jnp.int32, (block, every), 0) % rows
-    column = lax.broadcasted_iota(jnp.int32, (block, every), 1)
-    position = column % positions
-    column_row = column // positions
-    limit = jnp.zeros((block, every), jnp.int32)
-    for r in range(rows):
-        limit = jnp.where(column_row == r, lengths[r], limit)
-    valid = (row_of == column_row) & (position < limit)
-
-    heads = range(KV_HEADS)
-    lanes = [slice(g * HEAD_DIM, (g + 1) * HEAD_DIM) for g in heads]
-    mine = [slice(g * block, (g + 1) * block) for g in heads]
-    scores = [dot(stacked_b[mine[g]], keys[:, lanes[g]], contract_last=True) for g in heads]
-    scores = [jnp.where(valid, score * scale, -jnp.inf) for score in scores]
-    own_keys = [jnp.concatenate([newk[:, lanes[g]]] * groups, axis=0) for g in heads]
-    new_scores = [
-        jnp.sum(stacked[mine[g]] * own_keys[g], axis=1, keepdims=True) * scale for g in heads
-    ]
-    peaks = [
-        jnp.maximum(jnp.max(score, axis=1, keepdims=True), new)
-        for score, new in zip(scores, new_scores)
-    ]
-    weights = [jnp.exp(score - peak) for score, peak in zip(scores, peaks)]
-    new_weights = [jnp.exp(new - peak) for new, peak in zip(new_scores, peaks)]
-    totals = [
-        jnp.sum(weight, axis=1, keepdims=True) + new
-        for weight, new in zip(weights, new_weights)
-    ]
-    probs = [(weight / total).astype(BF16) for weight, total in zip(weights, totals)]
-    new_probs = [
-        (new / total).astype(BF16).astype(F32) for new, total in zip(new_weights, totals)
-    ]
-    for copy in copies[4:9]:
-        copy.wait()
-    values = cache_values[...].reshape(every, KV_HEADS * HEAD_DIM)
-    newv = new_values[...].astype(F32)
-    mixed = [
-        dot(probs[g], values[:, lanes[g]])
-        + new_probs[g] * jnp.concatenate([newv[:, lanes[g]]] * groups, axis=0)
-        for g in heads
-    ]
-    pieces = [value[j * rows : (j + 1) * rows] for value in mixed for j in range(groups)]
-
-    states = (residual[...].astype(F32) + jnp.concatenate(pieces, axis=1)).astype(BF16)
-    attended[...] = states
-    states = states.astype(F32)
-    norm = lax.rsqrt(jnp.mean(states * states, axis=1, keepdims=True) + 1e-05)
-    gains = gain[...].astype(F32)
-    logits = [jnp.zeros((rows, 128), F32) for _ in range(EXPERTS)]
-    parts = []
-    for c in range(width // 128):
-        lanes = slice(c * 128, (c + 1) * 128)
-        part = (states[:, lanes] * norm * gains[c : c + 1]).astype(BF16).astype(F32)
-        parts.append(part)
-        for e in range(EXPERTS):
-            logits[e] += part * router[e : e + 1, lanes].astype(F32)
-    logits = [jnp.sum(value, axis=1, keepdims=True) for value in logits]
-
+    copies[9].wait()
     index = lax.axis_index("dp")
     base = index * rows
     own = index // plane
@@ -184,6 +117,76 @@
     picks = [one_hot((place == expert * 8 + slot) & chosen)]
     for m in range(3):
         picks.append(one_hot((place == expert * 8 + 6 + late) & (slot - 3 * late == m) & chosen))
+    for copy in copies[:4]:
+        copy.wait()
+
+    query = queries[...].astype(F32)
+    stacked = jnp.concatenate(
+        [query[:, h * HEAD_DIM : (h + 1) * HEAD_DIM] for h in range(HEADS)], axis=0
+    )
+    stacked_b = stacked.astype(BF16)
+    keys = cache_keys[...].reshape(every, KV_HEADS * HEAD_DIM)
+    newk = new_keys[...].astype(F32)
+
+    row_of = lax.broadcasted_iota(jnp.int32, (block, every), 0) % rows
+    column = lax.broadcasted_iota(jnp.int32, (block, every), 1)
+    position = column % positions
+    column_row = column // positions
+    limit = jnp.zeros((block, every), jnp.int32)
+    for r in range(rows):
+        limit = jnp.where(column_row == r, lengths[r], limit)
+    valid = (row_of == column_row) & (position < limit)
+
+    heads = range(KV_HEADS)
+    lanes = [slice(g * HEAD_DIM, (g + 1) * HEAD_DIM) for g in heads]
+    mine = [slice(g * block, (g + 1) * block) for g in heads]
+    scores = [dot(stacked_b[mine[g]], keys[:, lanes[g]], contract_last=True) for g in heads]
+    scores = [jnp.where(valid, score * scale, -jnp.inf) for score in scores]
+    own_keys = [jnp.concatenate([newk[:, lanes[g]]] * groups, axis=0) for g in heads]
+    new_scores = [
+        jnp.sum(stacked[mine[g]] * own_keys[g], axis=1, keepdims=True) * scale for g in heads
+    ]
+    peaks = [
+        jnp.maximum(jnp.max(score, axis=1, keepdims=True), new)
+        for score, new in zip(scores, new_scores)
+    ]
+    weights = [jnp.exp(score - peak) for score, peak in zip(scores, peaks)]
+    new_weights = [jnp.exp(new - peak) for new, peak in zip(new_scores, peaks)]
+    totals = [
+        jnp.sum(weight, axis=1, keepdims=True) + new
+        for weight, new in zip(weights, new_weights)
+    ]
+    inverses = [1.0 / total for total in totals]
+    probs = [(weight * inverse).astype(BF16) for weight, inverse in zip(weights, inverses)]
+    new_probs = [
+        (new * inverse).astype(BF16).astype(F32) for new, inverse in zip(new_weights, inverses)
+    ]
+    for copy in copies[4:9]:
+        copy.wait()
+    values = cache_values[...].reshape(every, KV_HEADS * HEAD_DIM)
+    newv = new_values[...].astype(F32)
+    mixed = [
+        dot(probs[g], values[:, lanes[g]])
+        + new_probs[g] * jnp.concatenate([newv[:, lanes[g]]] * groups, axis=0)
+        for g in heads
+    ]
+    pieces = [value[j * rows : (j + 1) * rows] for value in mixed for j in range(groups)]
+
+    states = (residual[...].astype(F32) + jnp.concatenate(pieces, axis=1)).astype(BF16)
+    attended[...] = states
+    states = states.astype(F32)
+    norm = lax.rsqrt(jnp.mean(states * states, axis=1, keepdims=True) + 1e-05)
+    gains = gain[...].astype(F32)
+    logits = [jnp.zeros((rows, 128), F32) for _ in range(EXPERTS)]
+    parts = []
+    for c in range(width // 128):
+        lanes = slice(c * 128, (c + 1) * 128)
+        part = (states[:, lanes] * norm * gains[c : c + 1]).astype(BF16).astype(F32)
+        parts.append(part)
+        for e in range(EXPERTS):
+            logits[e] += part * router[e : e + 1, lanes].astype(F32)
+    logits = [jnp.sum(value, axis=1, keepdims=True) for value in logits]
+
     normed = jnp.concatenate(parts, axis=1)
     normed = jnp.concatenate([normed, normed], axis=0).astype(BF16)
     quarter = width // 4
@@ -224,7 +227,7 @@
             *[jax.ShapeDtypeStruct((8, width * 3 // 4), BF16)] * EXPERTS,
             jax.ShapeDtypeStruct((2 * rows, 128), F32),
             jax.ShapeDtypeStruct((4, 2 * rows, 128), BF16),
-            pltpu.VMEM((weight.shape[0], weight.shape[1] // PARTS), weight.dtype),
+            pltpu.VMEM((weight.shape[0], weight.shape[1] // 4 * PARTS[0]), weight.dtype),
         ),
         in_specs=[ANY] * (len(operands) + 1),
         out_specs=(VMEM,) * (4 + EXPERTS),
@@ -250,11 +253,12 @@
     picks = [
         one_hot((lane == row - slot + 6 + late) & (slot - 3 * late == m)) for m in range(3)
     ]
+    picks = jnp.concatenate(picks, axis=1)
     tails = []
     for first in range(0, blocks.shape[0], size):
         some = blocks[first : first + size]
-        parts = [dot(picks[m], some[:, m * quarter : (m + 1) * quarter]) for m in range(3)]
-        tails.append((parts[0] + parts[1] + parts[2]).astype(BF16))
+        parts = [some[:, m * quarter : (m + 1) * quarter] for m in range(3)]
+        tails.append(dot(picks, jnp.concatenate(parts, axis=0)).astype(BF16))
     x = jnp.concatenate([blocks, jnp.concatenate(tails, axis=0)], axis=1)
     for f in range(0, columns, step):
         gate = dot(x, gate_weight[:, f : f + step])
@@ -279,28 +283,30 @@
 
 
 def down_kernel(hidden, *refs):
-    weights, outs = refs[:PARTS], refs[PARTS:]
+    weights, outs = refs[: len(PARTS)], refs[len(PARTS) :]
     rows = hidden.shape[0]
     quarter = outs[0].shape[1] // 3
     size = 128
     row, lane = grid((size, size))
     slot = row & 7
     picks = [one_hot((lane == row - slot + 3 * (slot - 6) + m) & (slot >= MOST)) for m in range(3)]
+    picks = jnp.concatenate(picks, axis=0)
     h = hidden[...]
 
     def terms(first, count):
-        part, first = divmod(first, weights[0].shape[1])
-        return dot(h, weights[part][:, first : first + count])
+        for weight in weights:
+            if first < weight.shape[1]:
+                return dot(h, weight[:, first : first + count])
+            first -= weight.shape[1]
 
     step = min(512, quarter)
     is_row = (lax.broadcasted_iota(jnp.int32, (rows, step), 0) & 7) < MOST
     each = rows // len(outs)
     for n in range(0, quarter, step):
         tail = terms(3 * quarter + n, step).astype(BF16)
+        tails = [dot(picks, tail[i : i + size]) for i in range(0, rows, size)]
         for m in range(3):
-            moved = jnp.concatenate(
-                [dot(picks[m], tail[i : i + size]) for i in range(0, rows, size)], axis=0
-            )
+            moved = jnp.concatenate([x[m * size : (m + 1) * size] for x in tails], axis=0)
             value = jnp.where(is_row, terms(m * quarter + n, step), moved).astype(BF16)
             for k, out in enumerate(outs):
                 out[:, m * quarter + n : m * quarter + n + step] = value[k * each : (k + 1) * each]
@@ -312,7 +318,7 @@
     return pl.pallas_call(
         down_kernel,
         out_shape=[jax.ShapeDtypeStruct((rows // 4, width // 4 * 3), BF16)] * 4,
-        in_specs=[VMEM] * (1 + PARTS),
+        in_specs=[VMEM] * (1 + len(PARTS)),
         out_specs=[VMEM] * 4,
         compiler_params=pltpu.CompilerParams(vmem_limit_bytes=4 * MIB * max(1, rows // 128)),
         cost_estimate=pl.CostEstimate(
@@ -331,8 +337,8 @@
         copy.wait()
 
 
-def load(source, after, first=0):
-    shape = (source.shape[0], source.shape[1] - first)
+def load(source, after, first, columns):
+    shape = (source.shape[0], columns)
     return pl.pallas_call(
         functools.partial(load_kernel, first),
         out_shape=(
@@ -447,16 +453,19 @@
 
     packed = [packed[0]] + [swap(packed[k], count, k * plane) for k in range(1, EXPERTS)]
     near = join(share, *packed[:2])
-    down_rest, token = load(down_weight, near, down.shape[1])
+    quarter = down_weight.shape[1] // 4
+    down_2, token = load(down_weight, near, quarter * PARTS[0], quarter * PARTS[1])
     far = join(token, *packed[2:])
+    down_3, token = load(down_weight, far, quarter * sum(PARTS[:2]), quarter * PARTS[2])
     for bit in bits:
         near = join(share, near, swap(near, count, bit))
-        far = join(share, far, swap(far, count, bit))
+        far = join(token, far, swap(far, count, bit))
 
     hidden = hidden_rows(near, far, gate_weight, up_weight)
-    near, near_send, far, far_send = down_rows(hidden, (down, down_rest))
+    near, near_send, far, far_send = down_rows(hidden, (down, down_2, down_3))
     for bit in reversed(bits):
         far, far_send = fold(far, swap(far_send, count, bit), share)
+    for bit in reversed(bits):
         near, near_send = fold(near, swap(near_send, count, bit), far)
     far = swap(far, count, 2 * plane)
     far_send = swap(far_send, count, 3 * plane)

time: 46.9 us -> 46.3 us (0.987)
  Pallas kernels: 16 us -> 18.1 us
  waiting for transfers between devices: 13.4 us -> 12 us
  starting transfers between devices: 16.5 us -> 15.2 us
    pallas_call x1 -> x2, Pallas kernels: 3.19 us -> 5.6 us  [load(): pl.pallas_call(functools.partial(load_kernel, first), out_shape=(pltpu.VM...]
    ppermute x14, waiting for transfers between devices: 13.4 us -> 12 us  [swap(): return lax.ppermute(value, 'dp', [(i, i ^ bit) for i in range(count)])]
    ppermute x14, starting transfers between devices: 16.5 us -> 15.2 us  [swap(): return lax.ppermute(value, 'dp', [(i, i ^ bit) for i in range(count)])]
  transfers between devices with their start and end apart: 14 -> 14, of which waited for: 7 -> 9; matrix products, arithmetic and copies ran while one was open for 0% -> 0% of each run, Pallas kernels for 8% -> 13%
where the time goes in v9:
time: 46.3 us; the launch traced here: 46.2 us
  Pallas kernels  18.1 us (39%)
  starting transfers between devices  15.2 us (33%)
  waiting for transfers between devices  12 us (26%)
  between operations  0.9 us (2%)
    ppermute x14, starting transfers between devices, swap(): return lax.ppermute(value, 'dp', [(i, i ^ bit) for i in range(count)])  15.2 us
    ppermute x14, waiting for transfers between devices, swap(): return lax.ppermute(value, 'dp', [(i, i ^ bit) for i in range(count)])  12 us
    pallas_call x2, Pallas kernels, load(): pl.pallas_call(functools.partial(load_kernel, first), out_shape=(pltpu.VM...  5.6 us
    pallas_call x1, Pallas kernels, attend(): pl.pallas_call(functools.partial(attend_kernel, plane), out_shape=(jax.Sh...  4.46 us
    pallas_call x1, Pallas kernels, hidden_rows(): pl.pallas_call(hidden_kernel, out_shape=jax.ShapeDtypeStruct((rows, colum...  4.13 us
    pallas_call x1, Pallas kernels, down_rows(): pl.pallas_call(down_kernel, out_shape=[jax.ShapeDtypeStruct((rows // 4, w...  2.55 us
    pallas_call x2, Pallas kernels, combine(): pl.pallas_call(functools.partial(combine_kernel, first), out_shape=jax.Sh...  1.07 us
  transfers between devices with their start and end apart: 14, of which 9 were waited for; matrix products, arithmetic and copies ran while one was open for 0% of the time, Pallas kernels for 13%

profile of v9, /device:TPU:0, one launch (start us, length us, event | category | flops | bytes accessed | tf_op | source)
XLA Modules:
  0.0 46.2 jit_solution(2380326066270806390)
XLA Ops:
  0.7 4.5 %attend.1 = (bf16[8,4096]{1,0:T(8,128)(2,1)}, bf16[8,3072]{1,0:T(8,128)(2,1)S(1)}, bf16[8,3072]{1,0:T(8,128)(2,1)S(1)}, bf16[8,3072]{1,0:T(8,128)(2,1)S(1)}, bf1...) custom-call(bf16[8,4096]{1,0:T(8,128)(2,1)} %refs_0_.1, ...), custom_call_target="tpu_custom_call" | custom-call | tf_op jit(solution)/shard_map/attend/pallas_call | solution.py:223
  5.1 3.1 %collective-permute-start = (bf16[8,3072]{1,0:T(8,128)(2,1)S(1)}, bf16[8,3072]{1,0:T(8,128)(2,1)S(1)}, u32[]{:S(2)}, u32[]{:S(2)}) collective-permute-start(bf16[8,3072]{1,0:T(8,128)(2,1)S(1)} %get-tuple-element.30), channel_id=1, source_target_pairs={{0,4},{1,5},{2,6},{3,7},{4,0},{5,1},{6,2},{7,3},{8,12},{9,13},{10,... | collective-permute-start | bytes 147464 | tf_op jit(solution)/shard_map/ppermute | solution.py:428
  8.2 2.6 %collective-permute-start.3 = (bf16[8,3072]{1,0:T(8,128)(2,1)S(1)}, bf16[8,3072]{1,0:T(8,128)(2,1)S(1)}, u32[]{:S(2)}, u32[]{:S(2)}) collective-permute-start(bf16[8,3072]{1,0:T(8,128)(2,1)S(1)} %get-tuple-element.32), channel_id=1, source_target_pairs={{0,8},{1,9},{2,10},{3,11},{4,12},{5,13},{6,14},{7,15},{8,0},{9,1},... | collective-permute-start | bytes 147464 | tf_op jit(solution)/shard_map/ppermute | solution.py:428
  10.8 0.0 slice-start.6
  10.9 1.8 %collective-permute-start.1 = (bf16[16,3072]{1,0:T(8,128)(2,1)S(1)}, bf16[16,3072]{1,0:T(8,128)(2,1)S(1)}, u32[]{:S(2)}, u32[]{:S(2)}) collective-permute-start(bf16[16,3072]{1,0:T(8,128)(2,1)S(1)} %join.6.refs_1_.after), channel_id=1, source_target_pairs={{0,2},{1,3},{2,0},{3,1},{4,6},{5,7},{6,4},{7,5},{8,10},{9,11},{10,... | collective-permute-start | bytes 294920 | tf_op jit(solution)/shard_map/ppermute | solution.py:428
  12.7 2.8 %load.2 = (bf16[1792,1024]{1,0:T(8,128)(2,1)S(1)}, f32[8,128]{1,0:T(8,128)S(1)}) custom-call(bf16[1792,4096]{1,0:T(8,128)(2,1)} %source.3, bf16[16,3072]{1,0:T(8,128)(2,1)S(1)} %join.6.refs_1_.after), custom_call_target="tpu_custom_call" | custom-call | bytes 3670016 | tf_op jit(solution)/shard_map/load/pallas_call | solution.py:342
  15.5 1.2 %collective-permute-done.4.refs_2_ = bf16[8,3072]{1,0:T(8,128)(2,1)S(1)} collective-permute-done((bf16[8,3072]{1,0:T(8,128)(2,1)S(1)}, bf16[8,3072]{1,0:T(8,128)(2,1)S(1)}, u32[]{:S(2)}, u32[]{:S(2)}) %collective-permute-start.4) | collective-permute-done | bytes 49184 | tf_op jit(solution)/shard_map/ppermute | solution.py:428
  16.7 0.0 slice-start.2
  16.7 1.6 %collective-permute-start.5 = (bf16[16,3072]{1,0:T(8,128)(2,1)S(1)}, bf16[16,3072]{1,0:T(8,128)(2,1)S(1)}, u32[]{:S(2)}, u32[]{:S(2)}) collective-permute-start(bf16[16,3072]{1,0:T(8,128)(2,1)S(1)} %join.9.after.refs_1_), channel_id=1, source_target_pairs={{0,2},{1,3},{2,0},{3,1},{4,6},{5,7},{6,4},{7,5},{8,10},{9,11},{10,... | collective-permute-start | bytes 294920 | tf_op jit(solution)/shard_map/ppermute | solution.py:428
  18.3 2.8 %load.3 = (bf16[1792,1024]{1,0:T(8,128)(2,1)S(1)}, f32[8,128]{1,0:T(8,128)S(1)}) custom-call(bf16[1792,4096]{1,0:T(8,128)(2,1)} %source.3, bf16[16,3072]{1,0:T(8,128)(2,1)S(1)} %join.9.after.refs_1_), custom_call_target="tpu_custom_call" | custom-call | bytes 3670016 | tf_op jit(solution)/shard_map/load/pallas_call | solution.py:342
  21.1 0.1 collective-permute-start.2
  21.2 0.2 collective-permute-done.5.refs_2_
  21.4 0.4 collective-permute-start.6
  21.8 0.8 %collective-permute-done.2.refs_2_ = bf16[32,3072]{1,0:T(8,128)(2,1)S(1)} collective-permute-done((bf16[32,3072]{1,0:T(8,128)(2,1)S(1)}, bf16[32,3072]{1,0:T(8,128)(2,1)S(1)}, u32[]{:S(2)}, u32[]{:S(2)}) %collective-permute-start.2) | collective-permute-done | bytes 196640 | tf_op jit(solution)/shard_map/ppermute | solution.py:428
  22.7 0.3 collective-permute-done.6.refs_2_
  23.1 4.1 %hidden.1 = bf16[128,1792]{1,0:T(8,128)(2,1)S(1)} custom-call(bf16[64,3072]{1,0:T(8,128)(2,1)S(1)} %join.8.near, bf16[64,3072]{1,0:T(8,128)(2,1)S(1)} %join.11.far, bf16[4096,1792]{1,0:T(8,128)(2,1)S(1)} %bitcast.4, bf16[4096,1792]{1,0:T(8,128)(2,1)S(1)} %bitcast.6), custom_call_target="tpu_custom_call" | custom-call | flops 3758096384 | tf_op jit(solution)/shard_map/hidden/pallas_call | solution.py:272
  27.2 2.6 %down.1 = (bf16[32,3072]{1,0:T(8,128)(2,1)S(1)}, bf16[32,3072]{1,0:T(8,128)(2,1)S(1)}, bf16[32,3072]{1,0:T(8,128)(2,1)S(1)}, bf16[32,3072]{1,0:T(8,128)(2,1)S(1)}) custom-call(bf16[128,1792]{1,0:T(8,128)(2,1)S(1)} %hidden.1, bf16[1792,2048]{1,0:T(8,128)(2,1)S(1)} %get-tuple-element.35.refs_0_, bf16[1792,1024]{1,0:T(8,128)(2,1)S(1)} %get-tuple-element.36.refs_1_, ...), custom_call_target="tpu_custom_call" | custom-call | flops 1879048192 | tf_op jit(solution)/shard_map/down/pallas_call | solution.py:318
  29.8 0.4 collective-permute-start.8
  30.1 0.2 collective-permute-start.7
  30.3 0.9 %collective-permute-done.8.arrived = bf16[32,3072]{1,0:T(8,128)(2,1)S(1)} collective-permute-done((bf16[32,3072]{1,0:T(8,128)(2,1)S(1)}, bf16[32,3072]{1,0:T(8,128)(2,1)S(1)}, u32[]{:S(2)}, u32[]{:S(2)}) %collective-permute-start.8) | collective-permute-done | bytes 196640 | tf_op jit(solution)/shard_map/ppermute | solution.py:428
  31.3 1.6 %collective-permute-start.9 = (bf16[16,3072]{1,0:T(8,128)(2,1)S(1)}, bf16[16,3072]{1,0:T(8,128)(2,1)S(1)}, u32[]{:S(2)}, u32[]{:S(2)}) collective-permute-start(bf16[16,3072]{1,0:T(8,128)(2,1)S(1)} %get-tuple-element.43), channel_id=1, source_target_pairs={{0,2},{1,3},{2,0},{3,1},{4,6},{5,7},{6,4},{7,5},{8,10},{9,11},{10,... | collective-permute-start | bytes 294920 | tf_op jit(solution)/shard_map/ppermute | solution.py:428
  32.9 3.5 %collective-permute-done.9.arrived = bf16[16,3072]{1,0:T(8,128)(2,1)S(1)} collective-permute-done((bf16[16,3072]{1,0:T(8,128)(2,1)S(1)}, bf16[16,3072]{1,0:T(8,128)(2,1)S(1)}, u32[]{:S(2)}, u32[]{:S(2)}) %collective-permute-start.9) | collective-permute-done | bytes 98336 | tf_op jit(solution)/shard_map/ppermute | solution.py:428
  36.4 0.1 fold.6
  36.5 1.4 %collective-permute-start.10 = (bf16[16,3072]{1,0:T(8,128)(2,1)S(1)}, bf16[16,3072]{1,0:T(8,128)(2,1)S(1)}, u32[]{:S(2)}, u32[]{:S(2)}) collective-permute-start(bf16[16,3072]{1,0:T(8,128)(2,1)S(1)} %get-tuple-element.46), channel_id=1, source_target_pairs={{0,2},{1,3},{2,0},{3,1},{4,6},{5,7},{6,4},{7,5},{8,10},{9,11},{10,... | collective-permute-start | bytes 294920 | tf_op jit(solution)/shard_map/ppermute | solution.py:428
  37.9 0.4 collective-permute-start.12
  38.3 1.4 %collective-permute-start.13 = (bf16[8,3072]{1,0:T(8,128)(2,1)S(1)}, bf16[8,3072]{1,0:T(8,128)(2,1)S(1)}, u32[]{:S(2)}, u32[]{:S(2)}) collective-permute-start(bf16[8,3072]{1,0:T(8,128)(2,1)S(1)} %get-tuple-element.49), channel_id=1, source_target_pairs={{0,12},{1,13},{2,14},{3,15},{4,8},{5,9},{6,10},{7,11},{8,4},{9,5},... | collective-permute-start | bytes 147464 | tf_op jit(solution)/shard_map/ppermute | solution.py:428
  39.7 1.5 %collective-permute-done.10.arrived = bf16[16,3072]{1,0:T(8,128)(2,1)S(1)} collective-permute-done((bf16[16,3072]{1,0:T(8,128)(2,1)S(1)}, bf16[16,3072]{1,0:T(8,128)(2,1)S(1)}, u32[]{:S(2)}, u32[]{:S(2)}) %collective-permute-start.10) | collective-permute-done | bytes 98336 | tf_op jit(solution)/shard_map/ppermute | solution.py:428
  41.2 0.3 collective-permute-start.11
  41.5 2.8 %collective-permute-done.13.refs_1_ = bf16[8,3072]{1,0:T(8,128)(2,1)S(1)} collective-permute-done((bf16[8,3072]{1,0:T(8,128)(2,1)S(1)}, bf16[8,3072]{1,0:T(8,128)(2,1)S(1)}, u32[]{:S(2)}, u32[]{:S(2)}) %collective-permute-start.13) | collective-permute-done | bytes 49184 | tf_op jit(solution)/shard_map/ppermute | solution.py:428
  44.3 0.2 combine.2.refs_2_
  44.5 0.8 %collective-permute-done.11.refs_1_ = bf16[8,3072]{1,0:T(8,128)(2,1)S(1)} collective-permute-done((bf16[8,3072]{1,0:T(8,128)(2,1)S(1)}, bf16[8,3072]{1,0:T(8,128)(2,1)S(1)}, u32[]{:S(2)}, u32[]{:S(2)}) %collective-permute-start.11) | collective-permute-done | bytes 49184 | tf_op jit(solution)/shard_map/ppermute | solution.py:428
  45.4 0.8 %combine.3 = bf16[8,4096]{1,0:T(8,128)(2,1)} custom-call(f32[16,128]{1,0:T(8,128)S(1)} %get-tuple-element.27.refs_0_.after.share, bf16[4,16,128]{2,1,0:T(8,128)(2,1)S(1)} %get-tuple-element.28.take, bf16[8,3072]{1,0:T(8,128)(2,1)S(1)} %get-tuple-element.47.refs_0_, bf16[8,3072]{1,0:T(8,128)(2,1)S(1)} %collective-permute-done.11.refs_1_, ...), custom_call_target="tpu_custom_call" | custom-call | bytes 16777216 | tf_op jit(solution)/shard_map/combine/pallas_call | solution.py:416
  (31 shorter events, 0.3 us)
Async XLA Ops:
  0.6 22.3 %slice-start.4 = ((s8[14680064]{0:T(1024)(128)(4,1)}), s8[4194304]{0:T(1024)(128)(4,1)S(1)}, s32[]{:S(2)}) async-start(s8[14680064]{0:T(1024)(128)(4,1)} %bitcast.5), calls=%async_computation.4 | async-start | bytes 8388608
  0.6 22.3 %slice-start.5 = ((s8[14680064]{0:T(1024)(128)(4,1)}), s8[4194304]{0:T(1024)(128)(4,1)S(1)}, s32[]{:S(2)}) async-start(s8[14680064]{0:T(1024)(128)(4,1)} %bitcast.5), calls=%async_computation.5 | async-start | bytes 8388608
  5.1 5.7 %collective-permute-start = (bf16[8,3072]{1,0:T(8,128)(2,1)S(1)}, bf16[8,3072]{1,0:T(8,128)(2,1)S(1)}, u32[]{:S(2)}, u32[]{:S(2)}) collective-permute-start(bf16[8,3072]{1,0:T(8,128)(2,1)S(1)} %get-tuple-element.30), channel_id=1, source_target_pairs={{0,4},{1,5},{2,6},{3,7},{4,0},{5,1},{6,2},{7,3},{8,12},{9,13},{10,... | collective-permute-start | bytes 147464 | tf_op jit(solution)/shard_map/ppermute | solution.py:428
  8.2 7.3 %collective-permute-start.3 = (bf16[8,3072]{1,0:T(8,128)(2,1)S(1)}, bf16[8,3072]{1,0:T(8,128)(2,1)S(1)}, u32[]{:S(2)}, u32[]{:S(2)}) collective-permute-start(bf16[8,3072]{1,0:T(8,128)(2,1)S(1)} %get-tuple-element.32), channel_id=1, source_target_pairs={{0,8},{1,9},{2,10},{3,11},{4,12},{5,13},{6,14},{7,15},{8,0},{9,1},... | collective-permute-start | bytes 147464 | tf_op jit(solution)/shard_map/ppermute | solution.py:428
  10.8 5.9 %collective-permute-start.4 = (bf16[8,3072]{1,0:T(8,128)(2,1)S(1)}, bf16[8,3072]{1,0:T(8,128)(2,1)S(1)}, u32[]{:S(2)}, u32[]{:S(2)}) collective-permute-start(bf16[8,3072]{1,0:T(8,128)(2,1)S(1)} %get-tuple-element.33), channel_id=1, source_target_pairs={{0,12},{1,13},{2,14},{3,15},{4,8},{5,9},{6,10},{7,11},{8,4},{9,5},... | collective-permute-start | bytes 147464 | tf_op jit(solution)/shard_map/ppermute | solution.py:428
  10.8 12.2 %slice-start = ((s8[14680064]{0:T(1024)(128)(4,1)}), s8[4194304]{0:T(1024)(128)(4,1)S(1)}, s32[]{:S(2)}) async-start(s8[14680064]{0:T(1024)(128)(4,1)} %bitcast.3), calls=%async_computation | async-start | bytes 8388608
  10.8 12.2 %slice-start.1 = ((s8[14680064]{0:T(1024)(128)(4,1)}), s8[4194304]{0:T(1024)(128)(4,1)S(1)}, s32[]{:S(2)}) async-start(s8[14680064]{0:T(1024)(128)(4,1)} %bitcast.3), calls=%async_computation.1 | async-start | bytes 8388608
  10.8 12.2 %slice-start.6 = ((s8[14680064]{0:T(1024)(128)(4,1)}), s8[4194304]{0:T(1024)(128)(4,1)S(1)}, s32[]{:S(2)}) async-start(s8[14680064]{0:T(1024)(128)(4,1)} %bitcast.5), calls=%async_computation.6 | async-start | bytes 8388608
  10.9 10.3 %collective-permute-start.1 = (bf16[16,3072]{1,0:T(8,128)(2,1)S(1)}, bf16[16,3072]{1,0:T(8,128)(2,1)S(1)}, u32[]{:S(2)}, u32[]{:S(2)}) collective-permute-start(bf16[16,3072]{1,0:T(8,128)(2,1)S(1)} %join.6.refs_1_.after), channel_id=1, source_target_pairs={{0,2},{1,3},{2,0},{3,1},{4,6},{5,7},{6,4},{7,5},{8,10},{9,11},{10,... | collective-permute-start | bytes 294920 | tf_op jit(solution)/shard_map/ppermute | solution.py:428
  16.7 6.3 %slice-start.2 = ((s8[14680064]{0:T(1024)(128)(4,1)}), s8[4194304]{0:T(1024)(128)(4,1)S(1)}, s32[]{:S(2)}) async-start(s8[14680064]{0:T(1024)(128)(4,1)} %bitcast.3), calls=%async_computation.2 | async-start | bytes 8388608
  16.7 6.3 %slice-start.3 = ((s8[14680064]{0:T(1024)(128)(4,1)}), s8[2097152]{0:T(1024)(128)(4,1)S(1)}, s32[]{:S(2)}) async-start(s8[14680064]{0:T(1024)(128)(4,1)} %bitcast.3), calls=%async_computation.3 | async-start | bytes 4194304
  16.7 6.3 %slice-start.7 = ((s8[14680064]{0:T(1024)(128)(4,1)}), s8[2097152]{0:T(1024)(128)(4,1)S(1)}, s32[]{:S(2)}) async-start(s8[14680064]{0:T(1024)(128)(4,1)} %bitcast.5), calls=%async_computation.7 | async-start | bytes 4194304
  16.7 4.7 %collective-permute-start.5 = (bf16[16,3072]{1,0:T(8,128)(2,1)S(1)}, bf16[16,3072]{1,0:T(8,128)(2,1)S(1)}, u32[]{:S(2)}, u32[]{:S(2)}) collective-permute-start(bf16[16,3072]{1,0:T(8,128)(2,1)S(1)} %join.9.after.refs_1_), channel_id=1, source_target_pairs={{0,2},{1,3},{2,0},{3,1},{4,6},{5,7},{6,4},{7,5},{8,10},{9,11},{10,... | collective-permute-start | bytes 294920 | tf_op jit(solution)/shard_map/ppermute | solution.py:428
  21.1 1.5 %collective-permute-start.2 = (bf16[32,3072]{1,0:T(8,128)(2,1)S(1)}, bf16[32,3072]{1,0:T(8,128)(2,1)S(1)}, u32[]{:S(2)}, u32[]{:S(2)}) collective-permute-start(bf16[32,3072]{1,0:T(8,128)(2,1)S(1)} %join.7.refs_1_), channel_id=1, source_target_pairs={{0,1},{1,0},{2,3},{3,2},{4,5},{5,4},{6,7},{7,6},{8,9},{9,8},{10,11... | collective-permute-start | bytes 589832 | tf_op jit(solution)/shard_map/ppermute | solution.py:428
  21.4 1.5 %collective-permute-start.6 = (bf16[32,3072]{1,0:T(8,128)(2,1)S(1)}, bf16[32,3072]{1,0:T(8,128)(2,1)S(1)}, u32[]{:S(2)}, u32[]{:S(2)}) collective-permute-start(bf16[32,3072]{1,0:T(8,128)(2,1)S(1)} %join.10.refs_1_), channel_id=1, source_target_pairs={{0,1},{1,0},{2,3},{3,2},{4,5},{5,4},{6,7},{7,6},{8,9},{9,8},{10,11... | collective-permute-start | bytes 589832 | tf_op jit(solution)/shard_map/ppermute | solution.py:428
  29.8 1.5 %collective-permute-start.8 = (bf16[32,3072]{1,0:T(8,128)(2,1)S(1)}, bf16[32,3072]{1,0:T(8,128)(2,1)S(1)}, u32[]{:S(2)}, u32[]{:S(2)}) collective-permute-start(bf16[32,3072]{1,0:T(8,128)(2,1)S(1)} %get-tuple-element.41), channel_id=1, source_target_pairs={{0,1},{1,0},{2,3},{3,2},{4,5},{5,4},{6,7},{7,6},{8,9},{9,8},{10,11... | collective-permute-start | bytes 589832 | tf_op jit(solution)/shard_map/ppermute | solution.py:428
  30.1 6.3 %collective-permute-start.7 = (bf16[32,3072]{1,0:T(8,128)(2,1)S(1)}, bf16[32,3072]{1,0:T(8,128)(2,1)S(1)}, u32[]{:S(2)}, u32[]{:S(2)}) collective-permute-start(bf16[32,3072]{1,0:T(8,128)(2,1)S(1)} %get-tuple-element.39), channel_id=1, source_target_pairs={{0,1},{1,0},{2,3},{3,2},{4,5},{5,4},{6,7},{7,6},{8,9},{9,8},{10,11... | collective-permute-start | bytes 589832 | tf_op jit(solution)/shard_map/ppermute | solution.py:428
  31.3 5.1 %collective-permute-start.9 = (bf16[16,3072]{1,0:T(8,128)(2,1)S(1)}, bf16[16,3072]{1,0:T(8,128)(2,1)S(1)}, u32[]{:S(2)}, u32[]{:S(2)}) collective-permute-start(bf16[16,3072]{1,0:T(8,128)(2,1)S(1)} %get-tuple-element.43), channel_id=1, source_target_pairs={{0,2},{1,3},{2,0},{3,1},{4,6},{5,7},{6,4},{7,5},{8,10},{9,11},{10,... | collective-permute-start | bytes 294920 | tf_op jit(solution)/shard_map/ppermute | solution.py:428
  36.5 4.7 %collective-permute-start.10 = (bf16[16,3072]{1,0:T(8,128)(2,1)S(1)}, bf16[16,3072]{1,0:T(8,128)(2,1)S(1)}, u32[]{:S(2)}, u32[]{:S(2)}) collective-permute-start(bf16[16,3072]{1,0:T(8,128)(2,1)S(1)} %get-tuple-element.46), channel_id=1, source_target_pairs={{0,2},{1,3},{2,0},{3,1},{4,6},{5,7},{6,4},{7,5},{8,10},{9,11},{10,... | collective-permute-start | bytes 294920 | tf_op jit(solution)/shard_map/ppermute | solution.py:428
  37.9 6.3 %collective-permute-start.12 = (bf16[8,3072]{1,0:T(8,128)(2,1)S(1)}, bf16[8,3072]{1,0:T(8,128)(2,1)S(1)}, u32[]{:S(2)}, u32[]{:S(2)}) collective-permute-start(bf16[8,3072]{1,0:T(8,128)(2,1)S(1)} %get-tuple-element.44.after), channel_id=1, source_target_pairs={{0,8},{1,9},{2,10},{3,11},{4,12},{5,13},{6,14},{7,15},{8,0},{9,1},... | collective-permute-start | bytes 147464 | tf_op jit(solution)/shard_map/ppermute | solution.py:428
  38.3 6.0 %collective-permute-start.13 = (bf16[8,3072]{1,0:T(8,128)(2,1)S(1)}, bf16[8,3072]{1,0:T(8,128)(2,1)S(1)}, u32[]{:S(2)}, u32[]{:S(2)}) collective-permute-start(bf16[8,3072]{1,0:T(8,128)(2,1)S(1)} %get-tuple-element.49), channel_id=1, source_target_pairs={{0,12},{1,13},{2,14},{3,15},{4,8},{5,9},{6,10},{7,11},{8,4},{9,5},... | collective-permute-start | bytes 147464 | tf_op jit(solution)/shard_map/ppermute | solution.py:428
  41.2 4.2 %collective-permute-start.11 = (bf16[8,3072]{1,0:T(8,128)(2,1)S(1)}, bf16[8,3072]{1,0:T(8,128)(2,1)S(1)}, u32[]{:S(2)}, u32[]{:S(2)}) collective-permute-start(bf16[8,3072]{1,0:T(8,128)(2,1)S(1)} %get-tuple-element.48), channel_id=1, source_target_pairs={{0,4},{1,5},{2,6},{3,7},{4,0},{5,1},{6,2},{7,3},{8,12},{9,13},{10,... | collective-permute-start | bytes 147464 | tf_op jit(solution)/shard_map/ppermute | solution.py:428

commit v10 on v9

--- a/solution.py
+++ b/solution.py
@@ -12,8 +12,7 @@
 HEAD_DIM = 128
 EXPERTS = 4
 MIB = 1 << 20
-WAYS = 4
-PARTS = (2, 1, 1)
+HINTS = 3
 MOST = 6
 F32 = jnp.float32
 BF16 = jnp.bfloat16
@@ -26,18 +25,6 @@
     return lax.dot_general(a, b, dims, preferred_element_type=F32)
 
 
-def weight_copies(source, target, semaphores, first=0):
-    step, columns = source.shape[0] // WAYS, target.shape[1]
-    return [
-        pltpu.make_async_copy(
-            source.at[pl.ds(i * step, step), pl.ds(first, columns)],
-            target.at[pl.ds(i * step, step)],
-            semaphores.at[i],
-        )
-        for i in range(WAYS)
-    ]
-
-
 def one_hot(mask):
     return mask.astype(F32).astype(BF16)
 
@@ -62,15 +49,15 @@
 
 
 def attend_kernel(plane, *refs):
+    refs = refs[:10] + refs[10 + HINTS :]
     sources, attended, packed, (share, take), held, semaphores = (
-        refs[:10], refs[11], refs[12:16], refs[16:18], refs[19:29], refs[29]
-    )
-    weight = weight_copies(refs[10], refs[18], refs[30])
+        refs[:10], refs[10], refs[11:15], refs[15:17], refs[17:27], refs[27]
+    )
     copies = [
         pltpu.make_async_copy(source, target, semaphores.at[i])
         for i, (source, target) in enumerate(zip(sources, held))
     ]
-    for copy in copies[9:] + copies[:9] + weight:
+    for copy in copies[9:] + copies[:9]:
         copy.start()
     (queries, cache_keys, new_keys, lengths, cache_values, new_values, residual, gain, router,
      routes) = held
@@ -200,8 +187,6 @@
         chosen_logits = jnp.where(expert_down[:, :1] == (own ^ e), both, chosen_logits)
     other = jnp.concatenate([chosen_logits[rows:], chosen_logits[:rows]], axis=0)
     share[...] = jnp.broadcast_to(1.0 / (1.0 + jnp.exp(other - chosen_logits)), share.shape)
-    for copy in weight:
-        copy.wait()
 
 
 def attend(plane, queries, new_keys, new_values, cache_keys, cache_values, lengths, residual,
@@ -227,25 +212,31 @@
             *[jax.ShapeDtypeStruct((8, width * 3 // 4), BF16)] * EXPERTS,
             jax.ShapeDtypeStruct((2 * rows, 128), F32),
             jax.ShapeDtypeStruct((4, 2 * rows, 128), BF16),
-            pltpu.VMEM((weight.shape[0], weight.shape[1] // 4 * PARTS[0]), weight.dtype),
         ),
-        in_specs=[ANY] * (len(operands) + 1),
-        out_specs=(VMEM,) * (4 + EXPERTS),
+        in_specs=[ANY] * (len(operands) + HINTS),
+        out_specs=(VMEM,) * (3 + EXPERTS),
         scratch_shapes=[
             (pltpu.SMEM if i in in_smem else pltpu.VMEM)(operand.shape, operand.dtype)
             for i, operand in enumerate(operands)
         ]
-        + [pltpu.SemaphoreType.DMA((len(operands),)), pltpu.SemaphoreType.DMA((WAYS,))],
+        + [pltpu.SemaphoreType.DMA((len(operands),))],
         compiler_params=pltpu.CompilerParams(vmem_limit_bytes=5 * MIB),
         name="attend",
-    )(*[pltpu.with_memory_space_constraint(x, pltpu.HBM) for x in (*operands, weight)])
-
-
-def hidden_kernel(near, far, gate_weight, up_weight, hidden):
-    columns = gate_weight.shape[1]
-    step = 256 if columns % 256 == 0 else columns
-    quarter = near.shape[1] // 3
-    blocks = jnp.concatenate([near[...], far[...]], axis=0)
+    )(*[pltpu.with_memory_space_constraint(x, pltpu.HBM) for x in operands + (weight,) * HINTS])
+
+
+def expert_kernel(near, far, gate_weight, up_weight, down_weight, *refs):
+    outs, (hidden, down, semaphores) = refs[:4], refs[4:]
+    rows = near.shape[0] + far.shape[0]
+    width, columns = gate_weight.shape
+    quarter = width // 4
+    order = (3, 0, 1, 2)
+    copies = {}
+    for m in order:
+        lanes = pl.ds(m * quarter, quarter)
+        copies[m] = pltpu.make_async_copy(down_weight.at[:, lanes], down.at[m], semaphores.at[m])
+        copies[m].start()
+
     size = 128
     row, lane = grid((size, size))
     slot = row & 7
@@ -254,125 +245,83 @@
         one_hot((lane == row - slot + 6 + late) & (slot - 3 * late == m)) for m in range(3)
     ]
     picks = jnp.concatenate(picks, axis=1)
+    blocks = jnp.concatenate([near[...], far[...]], axis=0)
     tails = []
-    for first in range(0, blocks.shape[0], size):
+    for first in range(0, rows, size):
         some = blocks[first : first + size]
         parts = [some[:, m * quarter : (m + 1) * quarter] for m in range(3)]
         tails.append(dot(picks, jnp.concatenate(parts, axis=0)).astype(BF16))
     x = jnp.concatenate([blocks, jnp.concatenate(tails, axis=0)], axis=1)
+    step = 256 if columns % 256 == 0 else columns
     for f in range(0, columns, step):
         gate = dot(x, gate_weight[:, f : f + step])
         upper = dot(x, up_weight[:, f : f + step])
         hidden[:, f : f + step] = (gate / (1.0 + jnp.exp(-gate)) * upper).astype(BF16)
 
-
-def hidden_rows(near, far, gate_weight, up_weight):
+    picks = [one_hot((lane == row - slot + 3 * (slot - 6) + m) & (slot >= MOST)) for m in range(3)]
+    picks = jnp.concatenate(picks, axis=0)
+    h = hidden[...]
+    step = min(512, quarter)
+    is_row = (lax.broadcasted_iota(jnp.int32, (rows, step), 0) & 7) < MOST
+    each = rows // len(outs)
+    moved = {}
+    for m in order:
+        copies[m].wait()
+        for n in range(0, quarter, step):
+            terms = dot(h, down[m, :, n : n + step])
+            if m == 3:
+                tail = terms.astype(BF16)
+                tails = [dot(picks, tail[i : i + size]) for i in range(0, rows, size)]
+                for k in range(3):
+                    moved[k, n] = jnp.concatenate(
+                        [t[k * size : (k + 1) * size] for t in tails], axis=0
+                    ).astype(BF16)
+                continue
+            value = jnp.where(is_row, terms, moved[m, n].astype(F32)).astype(BF16)
+            for k, out in enumerate(outs):
+                out[:, m * quarter + n : m * quarter + n + step] = value[k * each : (k + 1) * each]
+
+
+def expert_rows(near, far, gate_weight, up_weight, down_weight):
     rows = near.shape[0] + far.shape[0]
     width, columns = gate_weight.shape
     return pl.pallas_call(
-        hidden_kernel,
-        out_shape=jax.ShapeDtypeStruct((rows, columns), BF16),
-        in_specs=[VMEM] * 4,
-        out_specs=VMEM,
-        compiler_params=pltpu.CompilerParams(vmem_limit_bytes=4 * MIB * max(1, rows // 128)),
+        expert_kernel,
+        out_shape=[jax.ShapeDtypeStruct((rows // 4, width // 4 * 3), BF16)] * 4,
+        in_specs=[VMEM] * 4 + [ANY],
+        out_specs=[VMEM] * 4,
+        scratch_shapes=[
+            pltpu.VMEM((rows, columns), BF16),
+            pltpu.VMEM((4, columns, width // 4), BF16),
+            pltpu.SemaphoreType.DMA((4,)),
+        ],
+        compiler_params=pltpu.CompilerParams(
+            vmem_limit_bytes=2 * columns * width + 4 * MIB * max(1, rows // 128)
+        ),
         cost_estimate=pl.CostEstimate(
-            flops=4 * rows * width * columns, bytes_accessed=0, transcendentals=rows * columns
+            flops=6 * rows * width * columns, bytes_accessed=0, transcendentals=rows * columns
         ),
-        name="hidden",
-    )(near, far, gate_weight, up_weight)
-
-
-def down_kernel(hidden, *refs):
-    weights, outs = refs[: len(PARTS)], refs[len(PARTS) :]
-    rows = hidden.shape[0]
-    quarter = outs[0].shape[1] // 3
-    size = 128
-    row, lane = grid((size, size))
-    slot = row & 7
-    picks = [one_hot((lane == row - slot + 3 * (slot - 6) + m) & (slot >= MOST)) for m in range(3)]
-    picks = jnp.concatenate(picks, axis=0)
-    h = hidden[...]
-
-    def terms(first, count):
-        for weight in weights:
-            if first < weight.shape[1]:
-                return dot(h, weight[:, first : first + count])
-            first -= weight.shape[1]
-
-    step = min(512, quarter)
-    is_row = (lax.broadcasted_iota(jnp.int32, (rows, step), 0) & 7) < MOST
-    each = rows // len(outs)
-    for n in range(0, quarter, step):
-        tail = terms(3 * quarter + n, step).astype(BF16)
-        tails = [dot(picks, tail[i : i + size]) for i in range(0, rows, size)]
-        for m in range(3):
-            moved = jnp.concatenate([x[m * size : (m + 1) * size] for x in tails], axis=0)
-            value = jnp.where(is_row, terms(m * quarter + n, step), moved).astype(BF16)
-            for k, out in enumerate(outs):
-                out[:, m * quarter + n : m * quarter + n + step] = value[k * each : (k + 1) * each]
-
-
-def down_rows(hidden, weights):
-    rows, columns = hidden.shape
-    width = sum(weight.shape[1] for weight in weights)
-    return pl.pallas_call(
-        down_kernel,
-        out_shape=[jax.ShapeDtypeStruct((rows // 4, width // 4 * 3), BF16)] * 4,
-        in_specs=[VMEM] * (1 + len(PARTS)),
-        out_specs=[VMEM] * 4,
-        compiler_params=pltpu.CompilerParams(vmem_limit_bytes=4 * MIB * max(1, rows // 128)),
-        cost_estimate=pl.CostEstimate(
-            flops=2 * rows * width * columns, bytes_accessed=0, transcendentals=0
-        ),
-        name="down",
-    )(hidden, *weights)
-
-
-def load_kernel(first, source, after, target, token, semaphores):
-    copies = weight_copies(source, target, semaphores, first)
-    for copy in copies:
-        copy.start()
-    token[...] = jnp.zeros(token.shape, token.dtype)
-    for copy in copies:
-        copy.wait()
-
-
-def load(source, after, first, columns):
-    shape = (source.shape[0], columns)
-    return pl.pallas_call(
-        functools.partial(load_kernel, first),
-        out_shape=(
-            pltpu.VMEM(shape, source.dtype),
-            jax.ShapeDtypeStruct((8, 128), F32),
-        ),
-        in_specs=[ANY, ANY],
-        out_specs=(VMEM, VMEM),
-        scratch_shapes=[pltpu.SemaphoreType.DMA((WAYS,))],
-        compiler_params=pltpu.CompilerParams(vmem_limit_bytes=MIB),
-        cost_estimate=pl.CostEstimate(
-            flops=0, bytes_accessed=2 * shape[0] * shape[1], transcendentals=0
-        ),
-        name="load",
-    )(pltpu.with_memory_space_constraint(source, pltpu.HBM), after)
+        name="experts",
+    )(near, far, gate_weight, up_weight, pltpu.with_memory_space_constraint(down_weight, pltpu.HBM))
 
 
 def join_kernel(*refs):
     out, row = refs[-1], 0
-    for piece in refs[1:-1]:
+    for piece in refs[:-1]:
         out[row : row + piece.shape[0]] = piece[...]
         row += piece.shape[0]
 
 
-def join(after, *pieces):
+def join(*pieces):
     rows = sum(piece.shape[0] for piece in pieces)
     return pl.pallas_call(
         join_kernel,
         out_shape=jax.ShapeDtypeStruct((rows, pieces[0].shape[1]), BF16),
-        in_specs=[ANY] + [VMEM] * len(pieces),
+        in_specs=[VMEM] * len(pieces),
         out_specs=VMEM,
         compiler_params=pltpu.CompilerParams(vmem_limit_bytes=1 * MIB),
         name="join",
-    )(after, *pieces)
+    )(*pieces)
 
 
 def fold_kernel(held, arrived, after, *outs):
@@ -446,23 +395,21 @@
     count = lax.axis_size("dp")
     plane = count // EXPERTS
     bits = [1 << k for k in reversed(range(plane.bit_length() - 1))]
-    attended, *packed, share, take, down = attend(
+    attended, *packed, share, take = attend(
         plane, queries, new_keys, new_values, cache_keys, cache_values, lengths, residual, norm_gain,
         router_weight, routes, down_weight,
     )
 
     packed = [packed[0]] + [swap(packed[k], count, k * plane) for k in range(1, EXPERTS)]
-    near = join(share, *packed[:2])
-    quarter = down_weight.shape[1] // 4
-    down_2, token = load(down_weight, near, quarter * PARTS[0], quarter * PARTS[1])
-    far = join(token, *packed[2:])
-    down_3, token = load(down_weight, far, quarter * sum(PARTS[:2]), quarter * PARTS[2])
+    near = join(*packed[:2])
+    far = join(*packed[2:])
     for bit in bits:
-        near = join(share, near, swap(near, count, bit))
-        far = join(token, far, swap(far, count, bit))
-
-    hidden = hidden_rows(near, far, gate_weight, up_weight)
-    near, near_send, far, far_send = down_rows(hidden, (down, down_2, down_3))
+        near = join(near, swap(near, count, bit))
+        far = join(far, swap(far, count, bit))
+
+    near, near_send, far, far_send = expert_rows(
+        near, far, gate_weight, up_weight, down_weight
+    )
     for bit in reversed(bits):
         far, far_send = fold(far, swap(far_send, count, bit), share)
     for bit in reversed(bits):

time: 46.3 us -> 47.5 us (1.026)
  waiting for transfers between devices: 12 us -> 17.7 us
  Pallas kernels: 18.1 us -> 13.9 us
    ppermute x14, waiting for transfers between devices: 12 us -> 17.7 us  [swap(): return lax.ppermute(value, 'dp', [(i, i ^ bit) for i in range(count)])]
    pallas_call x4 -> x1, Pallas kernels: 12.3 us -> 9.95 us  [expert_rows(): pl.pallas_call(expert_kernel, out_shape=[jax.ShapeDtypeStruct((rows // 4,...]
    pallas_call x1, Pallas kernels: 4.46 us -> 2.65 us  [attend(): pl.pallas_call(functools.partial(attend_kernel, plane), out_shape=(jax.Sh...]
  transfers between devices with their start and end apart: 14 -> 14, of which waited for: 9 -> 9; matrix products, arithmetic and copies ran while one was open for 0% -> 0% of each run, Pallas kernels for 13% -> 1%
where the time goes in v10:
time: 47.5 us; the launch traced here: 47.3 us
  waiting for transfers between devices  17.7 us (37%)
  starting transfers between devices  15 us (32%)
  Pallas kernels  13.9 us (29%)
  between operations  0.77 us (2%)
    ppermute x14, waiting for transfers between devices, swap(): return lax.ppermute(value, 'dp', [(i, i ^ bit) for i in range(count)])  17.7 us
    ppermute x14, starting transfers between devices, swap(): return lax.ppermute(value, 'dp', [(i, i ^ bit) for i in range(count)])  15 us
    pallas_call x1, Pallas kernels, expert_rows(): pl.pallas_call(expert_kernel, out_shape=[jax.ShapeDtypeStruct((rows // 4,...  9.95 us
    pallas_call x1, Pallas kernels, attend(): pl.pallas_call(functools.partial(attend_kernel, plane), out_shape=(jax.Sh...  2.65 us
    pallas_call x2, Pallas kernels, combine(): pl.pallas_call(functools.partial(combine_kernel, first), out_shape=jax.Sh...  1.06 us
  transfers between devices with their start and end apart: 14, of which 9 were waited for; matrix products, arithmetic and copies ran while one was open for 0% of the time, Pallas kernels for 1%

profile of v10, /device:TPU:0, one launch (start us, length us, event | category | flops | bytes accessed | tf_op | source)
XLA Modules:
  0.0 47.3 jit_solution(11935757327057952398)
XLA Ops:
  0.7 2.7 %attend.1 = (bf16[8,4096]{1,0:T(8,128)(2,1)}, bf16[8,3072]{1,0:T(8,128)(2,1)S(1)}, bf16[8,3072]{1,0:T(8,128)(2,1)S(1)}, bf16[8,3072]{1,0:T(8,128)(2,1)S(1)}, bf1...) custom-call(bf16[8,4096]{1,0:T(8,128)(2,1)} %refs_0_.1, ...), custom_call_target="tpu_custom_call" | custom-call | tf_op jit(solution)/shard_map/attend/pallas_call | solution.py:208
  3.3 3.1 %collective-permute-start = (bf16[8,3072]{1,0:T(8,128)(2,1)S(1)}, bf16[8,3072]{1,0:T(8,128)(2,1)S(1)}, u32[]{:S(2)}, u32[]{:S(2)}) collective-permute-start(bf16[8,3072]{1,0:T(8,128)(2,1)S(1)} %get-tuple-element.25), channel_id=1, source_target_pairs={{0,4},{1,5},{2,6},{3,7},{4,0},{5,1},{6,2},{7,3},{8,12},{9,13},{10,... | collective-permute-start | bytes 147464 | tf_op jit(solution)/shard_map/ppermute | solution.py:377
  6.4 2.6 %collective-permute-start.3 = (bf16[8,3072]{1,0:T(8,128)(2,1)S(1)}, bf16[8,3072]{1,0:T(8,128)(2,1)S(1)}, u32[]{:S(2)}, u32[]{:S(2)}) collective-permute-start(bf16[8,3072]{1,0:T(8,128)(2,1)S(1)} %get-tuple-element.26), channel_id=1, source_target_pairs={{0,8},{1,9},{2,10},{3,11},{4,12},{5,13},{6,14},{7,15},{8,0},{9,1},... | collective-permute-start | bytes 147464 | tf_op jit(solution)/shard_map/ppermute | solution.py:377
  9.0 0.0 collective-permute-start.4
  9.0 0.0 collective-permute-done.refs_1_
  9.0 1.8 %collective-permute-start.1 = (bf16[16,3072]{1,0:T(8,128)(2,1)S(1)}, bf16[16,3072]{1,0:T(8,128)(2,1)S(1)}, u32[]{:S(2)}, u32[]{:S(2)}) collective-permute-start(bf16[16,3072]{1,0:T(8,128)(2,1)S(1)} %join.6.refs_0_), channel_id=1, source_target_pairs={{0,2},{1,3},{2,0},{3,1},{4,6},{5,7},{6,4},{7,5},{8,10},{9,11},{10,... | collective-permute-start | bytes 294920 | tf_op jit(solution)/shard_map/ppermute | solution.py:377
  10.8 1.5 %collective-permute-done.3.refs_0_ = bf16[8,3072]{1,0:T(8,128)(2,1)S(1)} collective-permute-done((bf16[8,3072]{1,0:T(8,128)(2,1)S(1)}, bf16[8,3072]{1,0:T(8,128)(2,1)S(1)}, u32[]{:S(2)}, u32[]{:S(2)}) %collective-permute-start.3) | collective-permute-done | bytes 49184 | tf_op jit(solution)/shard_map/ppermute | solution.py:377
  12.3 2.6 %collective-permute-done.4.refs_1_ = bf16[8,3072]{1,0:T(8,128)(2,1)S(1)} collective-permute-done((bf16[8,3072]{1,0:T(8,128)(2,1)S(1)}, bf16[8,3072]{1,0:T(8,128)(2,1)S(1)}, u32[]{:S(2)}, u32[]{:S(2)}) %collective-permute-start.4) | collective-permute-done | bytes 49184 | tf_op jit(solution)/shard_map/ppermute | solution.py:377
  14.9 1.6 %collective-permute-start.5 = (bf16[16,3072]{1,0:T(8,128)(2,1)S(1)}, bf16[16,3072]{1,0:T(8,128)(2,1)S(1)}, u32[]{:S(2)}, u32[]{:S(2)}) collective-permute-start(bf16[16,3072]{1,0:T(8,128)(2,1)S(1)} %join.9.refs_0_), channel_id=1, source_target_pairs={{0,2},{1,3},{2,0},{3,1},{4,6},{5,7},{6,4},{7,5},{8,10},{9,11},{10,... | collective-permute-start | bytes 294920 | tf_op jit(solution)/shard_map/ppermute | solution.py:377
  16.5 0.0 collective-permute-done.1.refs_1_
  16.5 0.1 collective-permute-start.2
  16.6 3.0 %collective-permute-done.5.refs_1_ = bf16[16,3072]{1,0:T(8,128)(2,1)S(1)} collective-permute-done((bf16[16,3072]{1,0:T(8,128)(2,1)S(1)}, bf16[16,3072]{1,0:T(8,128)(2,1)S(1)}, u32[]{:S(2)}, u32[]{:S(2)}) %collective-permute-start.5) | collective-permute-done | bytes 98336 | tf_op jit(solution)/shard_map/ppermute | solution.py:377
  19.6 0.1 collective-permute-start.6
  19.7 0.0 collective-permute-done.2.refs_1_
  19.7 1.4 %collective-permute-done.6.refs_1_ = bf16[32,3072]{1,0:T(8,128)(2,1)S(1)} collective-permute-done((bf16[32,3072]{1,0:T(8,128)(2,1)S(1)}, bf16[32,3072]{1,0:T(8,128)(2,1)S(1)}, u32[]{:S(2)}, u32[]{:S(2)}) %collective-permute-start.6) | collective-permute-done | bytes 196640 | tf_op jit(solution)/shard_map/ppermute | solution.py:377
  21.1 9.9 %experts.1 = (bf16[32,3072]{1,0:T(8,128)(2,1)S(1)}, bf16[32,3072]{1,0:T(8,128)(2,1)S(1)}, bf16[32,3072]{1,0:T(8,128)(2,1)S(1)}, bf16[32,3072]{1,0:T(8,128)(2,1)S(1)}) custom-call(bf16[64,3072]{1,0:T(8,128)(2,1)S(1)} %join.8.near, bf16[64,3072]{1,0:T(8,128)(2,1)S(1)} %join.11.far, bf16[4096,1792]{1,0:T(8,128)(2,1)S(1)} %copy-done, ...), custom_call_target="tpu_custom_call" | custom-call | flops 5637144576 | tf_op jit(solution)/shard_map/experts/pallas_call | solution.py:288
  31.1 0.2 collective-permute-start.8
  31.3 0.4 collective-permute-start.7
  31.7 0.9 %collective-permute-done.8.arrived = bf16[32,3072]{1,0:T(8,128)(2,1)S(1)} collective-permute-done((bf16[32,3072]{1,0:T(8,128)(2,1)S(1)}, bf16[32,3072]{1,0:T(8,128)(2,1)S(1)}, u32[]{:S(2)}, u32[]{:S(2)}) %collective-permute-start.8) | collective-permute-done | bytes 196640 | tf_op jit(solution)/shard_map/ppermute | solution.py:377
  32.7 1.6 %collective-permute-start.9 = (bf16[16,3072]{1,0:T(8,128)(2,1)S(1)}, bf16[16,3072]{1,0:T(8,128)(2,1)S(1)}, u32[]{:S(2)}, u32[]{:S(2)}) collective-permute-start(bf16[16,3072]{1,0:T(8,128)(2,1)S(1)} %get-tuple-element.33), channel_id=1, source_target_pairs={{0,2},{1,3},{2,0},{3,1},{4,6},{5,7},{6,4},{7,5},{8,10},{9,11},{10,... | collective-permute-start | bytes 294920 | tf_op jit(solution)/shard_map/ppermute | solution.py:377
  34.2 3.3 %collective-permute-done.9.arrived = bf16[16,3072]{1,0:T(8,128)(2,1)S(1)} collective-permute-done((bf16[16,3072]{1,0:T(8,128)(2,1)S(1)}, bf16[16,3072]{1,0:T(8,128)(2,1)S(1)}, u32[]{:S(2)}, u32[]{:S(2)}) %collective-permute-start.9) | collective-permute-done | bytes 98336 | tf_op jit(solution)/shard_map/ppermute | solution.py:377
  37.6 0.0 collective-permute-done.7.arrived
  37.6 0.1 fold.6
  37.7 1.6 %collective-permute-start.10 = (bf16[16,3072]{1,0:T(8,128)(2,1)S(1)}, bf16[16,3072]{1,0:T(8,128)(2,1)S(1)}, u32[]{:S(2)}, u32[]{:S(2)}) collective-permute-start(bf16[16,3072]{1,0:T(8,128)(2,1)S(1)} %get-tuple-element.36), channel_id=1, source_target_pairs={{0,2},{1,3},{2,0},{3,1},{4,6},{5,7},{6,4},{7,5},{8,10},{9,11},{10,... | collective-permute-start | bytes 294920 | tf_op jit(solution)/shard_map/ppermute | solution.py:377
  39.2 0.4 collective-permute-start.12
  39.6 1.2 %collective-permute-start.13 = (bf16[8,3072]{1,0:T(8,128)(2,1)S(1)}, bf16[8,3072]{1,0:T(8,128)(2,1)S(1)}, u32[]{:S(2)}, u32[]{:S(2)}) collective-permute-start(bf16[8,3072]{1,0:T(8,128)(2,1)S(1)} %get-tuple-element.39), channel_id=1, source_target_pairs={{0,12},{1,13},{2,14},{3,15},{4,8},{5,9},{6,10},{7,11},{8,4},{9,5},... | collective-permute-start | bytes 147464 | tf_op jit(solution)/shard_map/ppermute | solution.py:377
  40.8 1.6 %collective-permute-done.10.arrived = bf16[16,3072]{1,0:T(8,128)(2,1)S(1)} collective-permute-done((bf16[16,3072]{1,0:T(8,128)(2,1)S(1)}, bf16[16,3072]{1,0:T(8,128)(2,1)S(1)}, u32[]{:S(2)}, u32[]{:S(2)}) %collective-permute-start.10) | collective-permute-done | bytes 98336 | tf_op jit(solution)/shard_map/ppermute | solution.py:377
  42.4 0.5 collective-permute-start.11
  42.8 2.7 %collective-permute-done.13.refs_1_ = bf16[8,3072]{1,0:T(8,128)(2,1)S(1)} collective-permute-done((bf16[8,3072]{1,0:T(8,128)(2,1)S(1)}, bf16[8,3072]{1,0:T(8,128)(2,1)S(1)}, u32[]{:S(2)}, u32[]{:S(2)}) %collective-permute-start.13) | collective-permute-done | bytes 49184 | tf_op jit(solution)/shard_map/ppermute | solution.py:377
  45.5 0.2 combine.2.refs_2_
  45.8 0.8 %collective-permute-done.11.refs_1_ = bf16[8,3072]{1,0:T(8,128)(2,1)S(1)} collective-permute-done((bf16[8,3072]{1,0:T(8,128)(2,1)S(1)}, bf16[8,3072]{1,0:T(8,128)(2,1)S(1)}, u32[]{:S(2)}, u32[]{:S(2)}) %collective-permute-start.11) | collective-permute-done | bytes 49184 | tf_op jit(solution)/shard_map/ppermute | solution.py:377
  46.5 0.8 %combine.3 = bf16[8,4096]{1,0:T(8,128)(2,1)} custom-call(f32[16,128]{1,0:T(8,128)S(1)} %get-tuple-element.22.after.share, bf16[4,16,128]{2,1,0:T(8,128)(2,1)S(1)} %get-tuple-element.23.take, bf16[8,3072]{1,0:T(8,128)(2,1)S(1)} %get-tuple-element.37.refs_0_, bf16[8,3072]{1,0:T(8,128)(2,1)S(1)} %collective-permute-done.11.refs_1_, f32[8,4096]{1,0:T(8,128)S(1)} %combine.2.refs_2_), custom_call_target="tpu_custom_call" | custom-call | bytes 16777216 | tf_op jit(solution)/shard_map/combine/pallas_call | solution.py:365
  (14 shorter events, 0.2 us)
Async XLA Ops:
  0.6 20.5 %copy-start = (bf16[4096,1792]{1,0:T(8,128)(2,1)S(1)}, bf16[4096,1792]{1,0:T(8,128)(2,1)}, u32[]{:S(2)}) copy-start(bf16[4096,1792]{1,0:T(8,128)(2,1)} %gate_weight.1) | copy-start | bytes 44040196
  0.6 20.5 %copy-start.1 = (bf16[4096,1792]{1,0:T(8,128)(2,1)S(1)}, bf16[4096,1792]{1,0:T(8,128)(2,1)}, u32[]{:S(2)}) copy-start(bf16[4096,1792]{1,0:T(8,128)(2,1)} %up_weight.1) | copy-start | bytes 44040196
  3.3 5.7 %collective-permute-start = (bf16[8,3072]{1,0:T(8,128)(2,1)S(1)}, bf16[8,3072]{1,0:T(8,128)(2,1)S(1)}, u32[]{:S(2)}, u32[]{:S(2)}) collective-permute-start(bf16[8,3072]{1,0:T(8,128)(2,1)S(1)} %get-tuple-element.25), channel_id=1, source_target_pairs={{0,4},{1,5},{2,6},{3,7},{4,0},{5,1},{6,2},{7,3},{8,12},{9,13},{10,... | collective-permute-start | bytes 147464 | tf_op jit(solution)/shard_map/ppermute | solution.py:377
  6.4 5.9 %collective-permute-start.3 = (bf16[8,3072]{1,0:T(8,128)(2,1)S(1)}, bf16[8,3072]{1,0:T(8,128)(2,1)S(1)}, u32[]{:S(2)}, u32[]{:S(2)}) collective-permute-start(bf16[8,3072]{1,0:T(8,128)(2,1)S(1)} %get-tuple-element.26), channel_id=1, source_target_pairs={{0,8},{1,9},{2,10},{3,11},{4,12},{5,13},{6,14},{7,15},{8,0},{9,1},... | collective-permute-start | bytes 147464 | tf_op jit(solution)/shard_map/ppermute | solution.py:377
  9.0 5.9 %collective-permute-start.4 = (bf16[8,3072]{1,0:T(8,128)(2,1)S(1)}, bf16[8,3072]{1,0:T(8,128)(2,1)S(1)}, u32[]{:S(2)}, u32[]{:S(2)}) collective-permute-start(bf16[8,3072]{1,0:T(8,128)(2,1)S(1)} %get-tuple-element.27), channel_id=1, source_target_pairs={{0,12},{1,13},{2,14},{3,15},{4,8},{5,9},{6,10},{7,11},{8,4},{9,5},... | collective-permute-start | bytes 147464 | tf_op jit(solution)/shard_map/ppermute | solution.py:377
  9.0 7.5 %collective-permute-start.1 = (bf16[16,3072]{1,0:T(8,128)(2,1)S(1)}, bf16[16,3072]{1,0:T(8,128)(2,1)S(1)}, u32[]{:S(2)}, u32[]{:S(2)}) collective-permute-start(bf16[16,3072]{1,0:T(8,128)(2,1)S(1)} %join.6.refs_0_), channel_id=1, source_target_pairs={{0,2},{1,3},{2,0},{3,1},{4,6},{5,7},{6,4},{7,5},{8,10},{9,11},{10,... | collective-permute-start | bytes 294920 | tf_op jit(solution)/shard_map/ppermute | solution.py:377
  14.9 4.7 %collective-permute-start.5 = (bf16[16,3072]{1,0:T(8,128)(2,1)S(1)}, bf16[16,3072]{1,0:T(8,128)(2,1)S(1)}, u32[]{:S(2)}, u32[]{:S(2)}) collective-permute-start(bf16[16,3072]{1,0:T(8,128)(2,1)S(1)} %join.9.refs_0_), channel_id=1, source_target_pairs={{0,2},{1,3},{2,0},{3,1},{4,6},{5,7},{6,4},{7,5},{8,10},{9,11},{10,... | collective-permute-start | bytes 294920 | tf_op jit(solution)/shard_map/ppermute | solution.py:377
  16.5 3.2 %collective-permute-start.2 = (bf16[32,3072]{1,0:T(8,128)(2,1)S(1)}, bf16[32,3072]{1,0:T(8,128)(2,1)S(1)}, u32[]{:S(2)}, u32[]{:S(2)}) collective-permute-start(bf16[32,3072]{1,0:T(8,128)(2,1)S(1)} %join.7.refs_0_), channel_id=1, source_target_pairs={{0,1},{1,0},{2,3},{3,2},{4,5},{5,4},{6,7},{7,6},{8,9},{9,8},{10,11... | collective-permute-start | bytes 589832 | tf_op jit(solution)/shard_map/ppermute | solution.py:377
  19.6 1.5 %collective-permute-start.6 = (bf16[32,3072]{1,0:T(8,128)(2,1)S(1)}, bf16[32,3072]{1,0:T(8,128)(2,1)S(1)}, u32[]{:S(2)}, u32[]{:S(2)}) collective-permute-start(bf16[32,3072]{1,0:T(8,128)(2,1)S(1)} %join.10.refs_0_), channel_id=1, source_target_pairs={{0,1},{1,0},{2,3},{3,2},{4,5},{5,4},{6,7},{7,6},{8,9},{9,8},{10,11... | collective-permute-start | bytes 589832 | tf_op jit(solution)/shard_map/ppermute | solution.py:377
  31.1 1.5 %collective-permute-start.8 = (bf16[32,3072]{1,0:T(8,128)(2,1)S(1)}, bf16[32,3072]{1,0:T(8,128)(2,1)S(1)}, u32[]{:S(2)}, u32[]{:S(2)}) collective-permute-start(bf16[32,3072]{1,0:T(8,128)(2,1)S(1)} %get-tuple-element.31), channel_id=1, source_target_pairs={{0,1},{1,0},{2,3},{3,2},{4,5},{5,4},{6,7},{7,6},{8,9},{9,8},{10,11... | collective-permute-start | bytes 589832 | tf_op jit(solution)/shard_map/ppermute | solution.py:377
  31.3 6.3 %collective-permute-start.7 = (bf16[32,3072]{1,0:T(8,128)(2,1)S(1)}, bf16[32,3072]{1,0:T(8,128)(2,1)S(1)}, u32[]{:S(2)}, u32[]{:S(2)}) collective-permute-start(bf16[32,3072]{1,0:T(8,128)(2,1)S(1)} %get-tuple-element.29), channel_id=1, source_target_pairs={{0,1},{1,0},{2,3},{3,2},{4,5},{5,4},{6,7},{7,6},{8,9},{9,8},{10,11... | collective-permute-start | bytes 589832 | tf_op jit(solution)/shard_map/ppermute | solution.py:377
  32.7 4.9 %collective-permute-start.9 = (bf16[16,3072]{1,0:T(8,128)(2,1)S(1)}, bf16[16,3072]{1,0:T(8,128)(2,1)S(1)}, u32[]{:S(2)}, u32[]{:S(2)}) collective-permute-start(bf16[16,3072]{1,0:T(8,128)(2,1)S(1)} %get-tuple-element.33), channel_id=1, source_target_pairs={{0,2},{1,3},{2,0},{3,1},{4,6},{5,7},{6,4},{7,5},{8,10},{9,11},{10,... | collective-permute-start | bytes 294920 | tf_op jit(solution)/shard_map/ppermute | solution.py:377
  37.7 4.7 %collective-permute-start.10 = (bf16[16,3072]{1,0:T(8,128)(2,1)S(1)}, bf16[16,3072]{1,0:T(8,128)(2,1)S(1)}, u32[]{:S(2)}, u32[]{:S(2)}) collective-permute-start(bf16[16,3072]{1,0:T(8,128)(2,1)S(1)} %get-tuple-element.36), channel_id=1, source_target_pairs={{0,2},{1,3},{2,0},{3,1},{4,6},{5,7},{6,4},{7,5},{8,10},{9,11},{10,... | collective-permute-start | bytes 294920 | tf_op jit(solution)/shard_map/ppermute | solution.py:377
  39.2 6.2 %collective-permute-start.12 = (bf16[8,3072]{1,0:T(8,128)(2,1)S(1)}, bf16[8,3072]{1,0:T(8,128)(2,1)S(1)}, u32[]{:S(2)}, u32[]{:S(2)}) collective-permute-start(bf16[8,3072]{1,0:T(8,128)(2,1)S(1)} %get-tuple-element.34.after), channel_id=1, source_target_pairs={{0,8},{1,9},{2,10},{3,11},{4,12},{5,13},{6,14},{7,15},{8,0},{9,1},... | collective-permute-start | bytes 147464 | tf_op jit(solution)/shard_map/ppermute | solution.py:377
  39.6 5.9 %collective-permute-start.13 = (bf16[8,3072]{1,0:T(8,128)(2,1)S(1)}, bf16[8,3072]{1,0:T(8,128)(2,1)S(1)}, u32[]{:S(2)}, u32[]{:S(2)}) collective-permute-start(bf16[8,3072]{1,0:T(8,128)(2,1)S(1)} %get-tuple-element.39), channel_id=1, source_target_pairs={{0,12},{1,13},{2,14},{3,15},{4,8},{5,9},{6,10},{7,11},{8,4},{9,5},... | collective-permute-start | bytes 147464 | tf_op jit(solution)/shard_map/ppermute | solution.py:377
  42.4 4.2 %collective-permute-start.11 = (bf16[8,3072]{1,0:T(8,128)(2,1)S(1)}, bf16[8,3072]{1,0:T(8,128)(2,1)S(1)}, u32[]{:S(2)}, u32[]{:S(2)}) collective-permute-start(bf16[8,3072]{1,0:T(8,128)(2,1)S(1)} %get-tuple-element.38), channel_id=1, source_target_pairs={{0,4},{1,5},{2,6},{3,7},{4,0},{5,1},{6,2},{7,3},{8,12},{9,13},{10,... | collective-permute-start | bytes 147464 | tf_op jit(solution)/shard_map/ppermute | solution.py:377

commit v11 on v10

--- a/solution.py
+++ b/solution.py
@@ -12,7 +12,8 @@
 HEAD_DIM = 128
 EXPERTS = 4
 MIB = 1 << 20
-HINTS = 3
+HINTS = 4
+WAYS = 2
 MOST = 6
 F32 = jnp.float32
 BF16 = jnp.bfloat16
@@ -225,17 +226,55 @@
     )(*[pltpu.with_memory_space_constraint(x, pltpu.HBM) for x in operands + (weight,) * HINTS])
 
 
-def expert_kernel(near, far, gate_weight, up_weight, down_weight, *refs):
-    outs, (hidden, down, semaphores) = refs[:4], refs[4:]
+def row_copies(source, target, semaphores, first):
+    step = target.shape[0] // WAYS
+    return [
+        pltpu.make_async_copy(
+            source.at[pl.ds(first + i * step, step)],
+            target.at[pl.ds(i * step, step)],
+            semaphores.at[i],
+        )
+        for i in range(WAYS)
+    ]
+
+
+def load_kernel(source, after, target, token, semaphores):
+    copies = row_copies(source, target, semaphores, 0)
+    for copy in copies:
+        copy.start()
+    token[...] = jnp.zeros(token.shape, token.dtype)
+    for copy in copies:
+        copy.wait()
+
+
+def load(source, rows, after):
+    return pl.pallas_call(
+        load_kernel,
+        out_shape=(
+            pltpu.VMEM((rows, source.shape[1]), source.dtype),
+            jax.ShapeDtypeStruct((8, 128), F32),
+        ),
+        in_specs=[ANY, ANY],
+        out_specs=(VMEM, VMEM),
+        scratch_shapes=[pltpu.SemaphoreType.DMA((WAYS,))],
+        compiler_params=pltpu.CompilerParams(vmem_limit_bytes=MIB),
+        cost_estimate=pl.CostEstimate(
+            flops=0, bytes_accessed=2 * rows * source.shape[1], transcendentals=0
+        ),
+        name="load",
+    )(pltpu.with_memory_space_constraint(source, pltpu.HBM), after)
+
+
+def expert_kernel(near, far, gate_weight, up_weight, down_top, down_weight, *refs):
+    outs, (hidden, down_rest, semaphores) = refs[:4], refs[4:]
     rows = near.shape[0] + far.shape[0]
     width, columns = gate_weight.shape
+    top = down_top.shape[0]
     quarter = width // 4
     order = (3, 0, 1, 2)
-    copies = {}
-    for m in order:
-        lanes = pl.ds(m * quarter, quarter)
-        copies[m] = pltpu.make_async_copy(down_weight.at[:, lanes], down.at[m], semaphores.at[m])
-        copies[m].start()
+    copies = row_copies(down_weight, down_rest, semaphores, top)
+    for copy in copies:
+        copy.start()
 
     size = 128
     row, lane = grid((size, size))
@@ -261,14 +300,16 @@
     picks = [one_hot((lane == row - slot + 3 * (slot - 6) + m) & (slot >= MOST)) for m in range(3)]
     picks = jnp.concatenate(picks, axis=0)
     h = hidden[...]
+    for copy in copies:
+        copy.wait()
     step = min(512, quarter)
     is_row = (lax.broadcasted_iota(jnp.int32, (rows, step), 0) & 7) < MOST
     each = rows // len(outs)
     moved = {}
     for m in order:
-        copies[m].wait()
         for n in range(0, quarter, step):
-            terms = dot(h, down[m, :, n : n + step])
+            lanes = slice(m * quarter + n, m * quarter + n + step)
+            terms = dot(h[:, :top], down_top[:, lanes]) + dot(h[:, top:], down_rest[:, lanes])
             if m == 3:
                 tail = terms.astype(BF16)
                 tails = [dot(picks, tail[i : i + size]) for i in range(0, rows, size)]
@@ -279,49 +320,57 @@
                 continue
             value = jnp.where(is_row, terms, moved[m, n].astype(F32)).astype(BF16)
             for k, out in enumerate(outs):
-                out[:, m * quarter + n : m * quarter + n + step] = value[k * each : (k + 1) * each]
-
-
-def expert_rows(near, far, gate_weight, up_weight, down_weight):
+                out[:, lanes] = value[k * each : (k + 1) * each]
+
+
+def expert_rows(near, far, gate_weight, up_weight, down_top, down_weight):
     rows = near.shape[0] + far.shape[0]
     width, columns = gate_weight.shape
     return pl.pallas_call(
         expert_kernel,
         out_shape=[jax.ShapeDtypeStruct((rows // 4, width // 4 * 3), BF16)] * 4,
-        in_specs=[VMEM] * 4 + [ANY],
+        in_specs=[VMEM] * 5 + [ANY],
         out_specs=[VMEM] * 4,
         scratch_shapes=[
             pltpu.VMEM((rows, columns), BF16),
-            pltpu.VMEM((4, columns, width // 4), BF16),
-            pltpu.SemaphoreType.DMA((4,)),
+            pltpu.VMEM((columns - down_top.shape[0], width), BF16),
+            pltpu.SemaphoreType.DMA((WAYS,)),
         ],
         compiler_params=pltpu.CompilerParams(
-            vmem_limit_bytes=2 * columns * width + 4 * MIB * max(1, rows // 128)
+            vmem_limit_bytes=2 * (columns - down_top.shape[0]) * width
+            + 4 * MIB * max(1, rows // 128)
         ),
         cost_estimate=pl.CostEstimate(
             flops=6 * rows * width * columns, bytes_accessed=0, transcendentals=rows * columns
         ),
         name="experts",
-    )(near, far, gate_weight, up_weight, pltpu.with_memory_space_constraint(down_weight, pltpu.HBM))
+    )(
+        near,
+        far,
+        gate_weight,
+        up_weight,
+        down_top,
+        pltpu.with_memory_space_constraint(down_weight, pltpu.HBM),
+    )
 
 
 def join_kernel(*refs):
     out, row = refs[-1], 0
-    for piece in refs[:-1]:
+    for piece in refs[1:-1]:
         out[row : row + piece.shape[0]] = piece[...]
         row += piece.shape[0]
 
 
-def join(*pieces):
+def join(after, *pieces):
     rows = sum(piece.shape[0] for piece in pieces)
     return pl.pallas_call(
         join_kernel,
         out_shape=jax.ShapeDtypeStruct((rows, pieces[0].shape[1]), BF16),
-        in_specs=[VMEM] * len(pieces),
+        in_specs=[ANY] + [VMEM] * len(pieces),
         out_specs=VMEM,
         compiler_params=pltpu.CompilerParams(vmem_limit_bytes=1 * MIB),
         name="join",
-    )(*pieces)
+    )(after, *pieces)
 
 
 def fold_kernel(held, arrived, after, *outs):
@@ -401,14 +450,16 @@
     )
 
     packed = [packed[0]] + [swap(packed[k], count, k * plane) for k in range(1, EXPERTS)]
-    near = join(*packed[:2])
-    far = join(*packed[2:])
+    near = join(share, *packed[:2])
+    far = join(share, *packed[2:])
+    columns = down_weight.shape[0]
+    down_top, token = load(down_weight, max(256, columns // 512 * 256), far)
     for bit in bits:
-        near = join(near, swap(near, count, bit))
-        far = join(far, swap(far, count, bit))
+        near = join(share, near, swap(near, count, bit))
+        far = join(token, far, swap(far, count, bit))
 
     near, near_send, far, far_send = expert_rows(
-        near, far, gate_weight, up_weight, down_weight
+        near, far, gate_weight, up_weight, down_top, down_weight
     )
     for bit in reversed(bits):
         far, far_send = fold(far, swap(far_send, count, bit), share)

time: 47.5 us -> 47.9 us (level)
  Pallas kernels: 13.9 us -> 16.8 us
  waiting for transfers between devices: 17.7 us -> 15.3 us
    pallas_call x0 -> x1, Pallas kernels: none -> 2.86 us  [load(): pl.pallas_call(load_kernel, out_shape=(pltpu.VMEM((rows, source.shape[1])...]
    ppermute x14, waiting for transfers between devices: 17.7 us -> 15.3 us  [swap(): return lax.ppermute(value, 'dp', [(i, i ^ bit) for i in range(count)])]
  transfers between devices with their start and end apart: 14 -> 14, of which waited for: 9 -> 10; matrix products, arithmetic and copies ran while one was open for 0% -> 0% of each run, Pallas kernels for 1% -> 7%
where the time goes in v11:
time: 47.9 us; the launch traced here: 47.8 us
  Pallas kernels  16.8 us (35%)
  waiting for transfers between devices  15.3 us (32%)
  starting transfers between devices  14.8 us (31%)
  between operations  0.89 us (2%)
    ppermute x14, waiting for transfers between devices, swap(): return lax.ppermute(value, 'dp', [(i, i ^ bit) for i in range(count)])  15.3 us
    ppermute x14, starting transfers between devices, swap(): return lax.ppermute(value, 'dp', [(i, i ^ bit) for i in range(count)])  14.8 us
    pallas_call x1, Pallas kernels, expert_rows(): pl.pallas_call(expert_kernel, out_shape=[jax.ShapeDtypeStruct((rows // 4,...  10 us
    pallas_call x1, Pallas kernels, load(): pl.pallas_call(load_kernel, out_shape=(pltpu.VMEM((rows, source.shape[1])...  2.86 us
    pallas_call x1, Pallas kernels, attend(): pl.pallas_call(functools.partial(attend_kernel, plane), out_shape=(jax.Sh...  2.65 us
    pallas_call x2, Pallas kernels, combine(): pl.pallas_call(functools.partial(combine_kernel, first), out_shape=jax.Sh...  1.06 us
  transfers between devices with their start and end apart: 14, of which 10 were waited for; matrix products, arithmetic and copies ran while one was open for 0% of the time, Pallas kernels for 7%

profile of v11, /device:TPU:0, one launch (start us, length us, event | category | flops | bytes accessed | tf_op | source)
XLA Modules:
  0.0 47.8 jit_solution(17989606278681337486)
XLA Ops:
  0.6 0.0 slice-start
  0.6 0.0 slice-start.4
  0.7 0.0 slice-start.3
  0.7 2.7 %attend.1 = (bf16[8,4096]{1,0:T(8,128)(2,1)}, bf16[8,3072]{1,0:T(8,128)(2,1)S(1)}, bf16[8,3072]{1,0:T(8,128)(2,1)S(1)}, bf16[8,3072]{1,0:T(8,128)(2,1)S(1)}, bf1...) custom-call(bf16[8,4096]{1,0:T(8,128)(2,1)} %refs_0_.1, ...), custom_call_target="tpu_custom_call" | custom-call | tf_op jit(solution)/shard_map/attend/pallas_call | solution.py:209
  3.4 3.1 %collective-permute-start = (bf16[8,3072]{1,0:T(8,128)(2,1)S(1)}, bf16[8,3072]{1,0:T(8,128)(2,1)S(1)}, u32[]{:S(2)}, u32[]{:S(2)}) collective-permute-start(bf16[8,3072]{1,0:T(8,128)(2,1)S(1)} %get-tuple-element.27), channel_id=1, source_target_pairs={{0,4},{1,5},{2,6},{3,7},{4,0},{5,1},{6,2},{7,3},{8,12},{9,13},{10,... | collective-permute-start | bytes 147464 | tf_op jit(solution)/shard_map/ppermute | solution.py:426
  6.5 2.6 %collective-permute-start.3 = (bf16[8,3072]{1,0:T(8,128)(2,1)S(1)}, bf16[8,3072]{1,0:T(8,128)(2,1)S(1)}, u32[]{:S(2)}, u32[]{:S(2)}) collective-permute-start(bf16[8,3072]{1,0:T(8,128)(2,1)S(1)} %get-tuple-element.28), channel_id=1, source_target_pairs={{0,8},{1,9},{2,10},{3,11},{4,12},{5,13},{6,14},{7,15},{8,0},{9,1},... | collective-permute-start | bytes 147464 | tf_op jit(solution)/shard_map/ppermute | solution.py:426
  9.1 1.8 %collective-permute-start.1 = (bf16[16,3072]{1,0:T(8,128)(2,1)S(1)}, bf16[16,3072]{1,0:T(8,128)(2,1)S(1)}, u32[]{:S(2)}, u32[]{:S(2)}) collective-permute-start(bf16[16,3072]{1,0:T(8,128)(2,1)S(1)} %join.6.refs_1_), channel_id=1, source_target_pairs={{0,2},{1,3},{2,0},{3,1},{4,6},{5,7},{6,4},{7,5},{8,10},{9,11},{10,... | collective-permute-start | bytes 294920 | tf_op jit(solution)/shard_map/ppermute | solution.py:426
  10.9 1.5 %collective-permute-done.3.refs_1_ = bf16[8,3072]{1,0:T(8,128)(2,1)S(1)} collective-permute-done((bf16[8,3072]{1,0:T(8,128)(2,1)S(1)}, bf16[8,3072]{1,0:T(8,128)(2,1)S(1)}, u32[]{:S(2)}, u32[]{:S(2)}) %collective-permute-start.3) | collective-permute-done | bytes 49184 | tf_op jit(solution)/shard_map/ppermute | solution.py:426
  12.4 2.6 %collective-permute-done.4.refs_2_ = bf16[8,3072]{1,0:T(8,128)(2,1)S(1)} collective-permute-done((bf16[8,3072]{1,0:T(8,128)(2,1)S(1)}, bf16[8,3072]{1,0:T(8,128)(2,1)S(1)}, u32[]{:S(2)}, u32[]{:S(2)}) %collective-permute-start.4) | collective-permute-done | bytes 49184 | tf_op jit(solution)/shard_map/ppermute | solution.py:426
  15.0 1.6 %collective-permute-start.5 = (bf16[16,3072]{1,0:T(8,128)(2,1)S(1)}, bf16[16,3072]{1,0:T(8,128)(2,1)S(1)}, u32[]{:S(2)}, u32[]{:S(2)}) collective-permute-start(bf16[16,3072]{1,0:T(8,128)(2,1)S(1)} %join.9.after.refs_1_), channel_id=1, source_target_pairs={{0,2},{1,3},{2,0},{3,1},{4,6},{5,7},{6,4},{7,5},{8,10},{9,11},{10,... | collective-permute-start | bytes 294920 | tf_op jit(solution)/shard_map/ppermute | solution.py:426
  16.5 2.9 %load.1 = (bf16[768,4096]{1,0:T(8,128)(2,1)S(1)}, f32[8,128]{1,0:T(8,128)S(1)}) custom-call(bf16[1792,4096]{1,0:T(8,128)(2,1)} %down_weight.1, bf16[16,3072]{1,0:T(8,128)(2,1)S(1)} %join.9.after.refs_1_), custom_call_target="tpu_custom_call" | custom-call | bytes 6291456 | tf_op jit(solution)/shard_map/load/pallas_call | solution.py:251
  19.4 0.1 collective-permute-start.2
  19.5 0.1 collective-permute-done.5.refs_2_
  19.7 0.5 collective-permute-start.6
  20.1 0.8 %collective-permute-done.2.refs_2_ = bf16[32,3072]{1,0:T(8,128)(2,1)S(1)} collective-permute-done((bf16[32,3072]{1,0:T(8,128)(2,1)S(1)}, bf16[32,3072]{1,0:T(8,128)(2,1)S(1)}, u32[]{:S(2)}, u32[]{:S(2)}) %collective-permute-start.2) | collective-permute-done | bytes 196640 | tf_op jit(solution)/shard_map/ppermute | solution.py:426
  21.0 0.3 collective-permute-done.6.refs_2_
  21.4 10.0 %experts.1 = (bf16[32,3072]{1,0:T(8,128)(2,1)S(1)}, bf16[32,3072]{1,0:T(8,128)(2,1)S(1)}, bf16[32,3072]{1,0:T(8,128)(2,1)S(1)}, bf16[32,3072]{1,0:T(8,128)(2,1)S(1)}) custom-call(bf16[64,3072]{1,0:T(8,128)(2,1)S(1)} %join.8.near, bf16[64,3072]{1,0:T(8,128)(2,1)S(1)} %join.11.far, bf16[4096,1792]{1,0:T(8,128)(2,1)S(1)} %bitcast.4, ...), custom_call_target="tpu_custom_call" | custom-call | flops 5637144576 | tf_op jit(solution)/shard_map/experts/pallas_call | solution.py:329
  31.4 0.4 collective-permute-start.8
  31.8 0.2 collective-permute-start.7
  32.0 0.9 %collective-permute-done.8.arrived = bf16[32,3072]{1,0:T(8,128)(2,1)S(1)} collective-permute-done((bf16[32,3072]{1,0:T(8,128)(2,1)S(1)}, bf16[32,3072]{1,0:T(8,128)(2,1)S(1)}, u32[]{:S(2)}, u32[]{:S(2)}) %collective-permute-start.8) | collective-permute-done | bytes 196640 | tf_op jit(solution)/shard_map/ppermute | solution.py:426
  32.9 1.5 %collective-permute-start.9 = (bf16[16,3072]{1,0:T(8,128)(2,1)S(1)}, bf16[16,3072]{1,0:T(8,128)(2,1)S(1)}, u32[]{:S(2)}, u32[]{:S(2)}) collective-permute-start(bf16[16,3072]{1,0:T(8,128)(2,1)S(1)} %get-tuple-element.37), channel_id=1, source_target_pairs={{0,2},{1,3},{2,0},{3,1},{4,6},{5,7},{6,4},{7,5},{8,10},{9,11},{10,... | collective-permute-start | bytes 294920 | tf_op jit(solution)/shard_map/ppermute | solution.py:426
  34.5 3.6 %collective-permute-done.9.arrived = bf16[16,3072]{1,0:T(8,128)(2,1)S(1)} collective-permute-done((bf16[16,3072]{1,0:T(8,128)(2,1)S(1)}, bf16[16,3072]{1,0:T(8,128)(2,1)S(1)}, u32[]{:S(2)}, u32[]{:S(2)}) %collective-permute-start.9) | collective-permute-done | bytes 98336 | tf_op jit(solution)/shard_map/ppermute | solution.py:426
  38.1 0.1 fold.6
  38.1 1.3 %collective-permute-start.10 = (bf16[16,3072]{1,0:T(8,128)(2,1)S(1)}, bf16[16,3072]{1,0:T(8,128)(2,1)S(1)}, u32[]{:S(2)}, u32[]{:S(2)}) collective-permute-start(bf16[16,3072]{1,0:T(8,128)(2,1)S(1)} %get-tuple-element.40), channel_id=1, source_target_pairs={{0,2},{1,3},{2,0},{3,1},{4,6},{5,7},{6,4},{7,5},{8,10},{9,11},{10,... | collective-permute-start | bytes 294920 | tf_op jit(solution)/shard_map/ppermute | solution.py:426
  39.5 0.4 collective-permute-start.12
  39.8 1.2 %collective-permute-start.13 = (bf16[8,3072]{1,0:T(8,128)(2,1)S(1)}, bf16[8,3072]{1,0:T(8,128)(2,1)S(1)}, u32[]{:S(2)}, u32[]{:S(2)}) collective-permute-start(bf16[8,3072]{1,0:T(8,128)(2,1)S(1)} %get-tuple-element.43), channel_id=1, source_target_pairs={{0,12},{1,13},{2,14},{3,15},{4,8},{5,9},{6,10},{7,11},{8,4},{9,5},... | collective-permute-start | bytes 147464 | tf_op jit(solution)/shard_map/ppermute | solution.py:426
  41.0 1.8 %collective-permute-done.10.arrived = bf16[16,3072]{1,0:T(8,128)(2,1)S(1)} collective-permute-done((bf16[16,3072]{1,0:T(8,128)(2,1)S(1)}, bf16[16,3072]{1,0:T(8,128)(2,1)S(1)}, u32[]{:S(2)}, u32[]{:S(2)}) %collective-permute-start.10) | collective-permute-done | bytes 98336 | tf_op jit(solution)/shard_map/ppermute | solution.py:426
  42.8 0.2 collective-permute-start.11
  43.0 2.7 %collective-permute-done.13.refs_1_ = bf16[8,3072]{1,0:T(8,128)(2,1)S(1)} collective-permute-done((bf16[8,3072]{1,0:T(8,128)(2,1)S(1)}, bf16[8,3072]{1,0:T(8,128)(2,1)S(1)}, u32[]{:S(2)}, u32[]{:S(2)}) %collective-permute-start.13) | collective-permute-done | bytes 49184 | tf_op jit(solution)/shard_map/ppermute | solution.py:426
  45.7 0.2 combine.2.refs_2_
  46.0 1.0 %collective-permute-done.11.refs_1_ = bf16[8,3072]{1,0:T(8,128)(2,1)S(1)} collective-permute-done((bf16[8,3072]{1,0:T(8,128)(2,1)S(1)}, bf16[8,3072]{1,0:T(8,128)(2,1)S(1)}, u32[]{:S(2)}, u32[]{:S(2)}) %collective-permute-start.11) | collective-permute-done | bytes 49184 | tf_op jit(solution)/shard_map/ppermute | solution.py:426
  47.0 0.8 %combine.3 = bf16[8,4096]{1,0:T(8,128)(2,1)} custom-call(f32[16,128]{1,0:T(8,128)S(1)} %get-tuple-element.24.refs_0_.after.share, bf16[4,16,128]{2,1,0:T(8,128)(2,1)S(1)} %get-tuple-element.25.take, bf16[8,3072]{1,0:T(8,128)(2,1)S(1)} %get-tuple-element.41.refs_0_, bf16[8,3072]{1,0:T(8,128)(2,1)S(1)} %collective-permute-done.11.refs_1_, ...), custom_call_target="tpu_custom_call" | custom-call | bytes 16777216 | tf_op jit(solution)/shard_map/combine/pallas_call | solution.py:414
  (29 shorter events, 0.2 us)
Async XLA Ops:
  0.6 20.6 %slice-start = ((s8[14680064]{0:T(1024)(128)(4,1)}), s8[4194304]{0:T(1024)(128)(4,1)S(1)}, s32[]{:S(2)}) async-start(s8[14680064]{0:T(1024)(128)(4,1)} %bitcast.3), calls=%async_computation | async-start | bytes 8388608
  0.6 20.6 %slice-start.4 = ((s8[14680064]{0:T(1024)(128)(4,1)}), s8[4194304]{0:T(1024)(128)(4,1)S(1)}, s32[]{:S(2)}) async-start(s8[14680064]{0:T(1024)(128)(4,1)} %bitcast.5), calls=%async_computation.4 | async-start | bytes 8388608
  0.7 20.6 %slice-start.1 = ((s8[14680064]{0:T(1024)(128)(4,1)}), s8[4194304]{0:T(1024)(128)(4,1)S(1)}, s32[]{:S(2)}) async-start(s8[14680064]{0:T(1024)(128)(4,1)} %bitcast.3), calls=%async_computation.1 | async-start | bytes 8388608
  0.7 20.6 %slice-start.2 = ((s8[14680064]{0:T(1024)(128)(4,1)}), s8[4194304]{0:T(1024)(128)(4,1)S(1)}, s32[]{:S(2)}) async-start(s8[14680064]{0:T(1024)(128)(4,1)} %bitcast.3), calls=%async_computation.2 | async-start | bytes 8388608
  0.7 20.6 %slice-start.3 = ((s8[14680064]{0:T(1024)(128)(4,1)}), s8[2097152]{0:T(1024)(128)(4,1)S(1)}, s32[]{:S(2)}) async-start(s8[14680064]{0:T(1024)(128)(4,1)} %bitcast.3), calls=%async_computation.3 | async-start | bytes 4194304
  0.7 20.6 %slice-start.5 = ((s8[14680064]{0:T(1024)(128)(4,1)}), s8[4194304]{0:T(1024)(128)(4,1)S(1)}, s32[]{:S(2)}) async-start(s8[14680064]{0:T(1024)(128)(4,1)} %bitcast.5), calls=%async_computation.5 | async-start | bytes 8388608
  0.7 20.6 %slice-start.6 = ((s8[14680064]{0:T(1024)(128)(4,1)}), s8[4194304]{0:T(1024)(128)(4,1)S(1)}, s32[]{:S(2)}) async-start(s8[14680064]{0:T(1024)(128)(4,1)} %bitcast.5), calls=%async_computation.6 | async-start | bytes 8388608
  0.7 20.6 %slice-start.7 = ((s8[14680064]{0:T(1024)(128)(4,1)}), s8[2097152]{0:T(1024)(128)(4,1)S(1)}, s32[]{:S(2)}) async-start(s8[14680064]{0:T(1024)(128)(4,1)} %bitcast.5), calls=%async_computation.7 | async-start | bytes 4194304
  3.4 5.7 %collective-permute-start = (bf16[8,3072]{1,0:T(8,128)(2,1)S(1)}, bf16[8,3072]{1,0:T(8,128)(2,1)S(1)}, u32[]{:S(2)}, u32[]{:S(2)}) collective-permute-start(bf16[8,3072]{1,0:T(8,128)(2,1)S(1)} %get-tuple-element.27), channel_id=1, source_target_pairs={{0,4},{1,5},{2,6},{3,7},{4,0},{5,1},{6,2},{7,3},{8,12},{9,13},{10,... | collective-permute-start | bytes 147464 | tf_op jit(solution)/shard_map/ppermute | solution.py:426
  6.5 5.9 %collective-permute-start.3 = (bf16[8,3072]{1,0:T(8,128)(2,1)S(1)}, bf16[8,3072]{1,0:T(8,128)(2,1)S(1)}, u32[]{:S(2)}, u32[]{:S(2)}) collective-permute-start(bf16[8,3072]{1,0:T(8,128)(2,1)S(1)} %get-tuple-element.28), channel_id=1, source_target_pairs={{0,8},{1,9},{2,10},{3,11},{4,12},{5,13},{6,14},{7,15},{8,0},{9,1},... | collective-permute-start | bytes 147464 | tf_op jit(solution)/shard_map/ppermute | solution.py:426
  9.1 5.9 %collective-permute-start.4 = (bf16[8,3072]{1,0:T(8,128)(2,1)S(1)}, bf16[8,3072]{1,0:T(8,128)(2,1)S(1)}, u32[]{:S(2)}, u32[]{:S(2)}) collective-permute-start(bf16[8,3072]{1,0:T(8,128)(2,1)S(1)} %get-tuple-element.29), channel_id=1, source_target_pairs={{0,12},{1,13},{2,14},{3,15},{4,8},{5,9},{6,10},{7,11},{8,4},{9,5},... | collective-permute-start | bytes 147464 | tf_op jit(solution)/shard_map/ppermute | solution.py:426
  9.1 10.3 %collective-permute-start.1 = (bf16[16,3072]{1,0:T(8,128)(2,1)S(1)}, bf16[16,3072]{1,0:T(8,128)(2,1)S(1)}, u32[]{:S(2)}, u32[]{:S(2)}) collective-permute-start(bf16[16,3072]{1,0:T(8,128)(2,1)S(1)} %join.6.refs_1_), channel_id=1, source_target_pairs={{0,2},{1,3},{2,0},{3,1},{4,6},{5,7},{6,4},{7,5},{8,10},{9,11},{10,... | collective-permute-start | bytes 294920 | tf_op jit(solution)/shard_map/ppermute | solution.py:426
  15.0 4.7 %collective-permute-start.5 = (bf16[16,3072]{1,0:T(8,128)(2,1)S(1)}, bf16[16,3072]{1,0:T(8,128)(2,1)S(1)}, u32[]{:S(2)}, u32[]{:S(2)}) collective-permute-start(bf16[16,3072]{1,0:T(8,128)(2,1)S(1)} %join.9.after.refs_1_), channel_id=1, source_target_pairs={{0,2},{1,3},{2,0},{3,1},{4,6},{5,7},{6,4},{7,5},{8,10},{9,11},{10,... | collective-permute-start | bytes 294920 | tf_op jit(solution)/shard_map/ppermute | solution.py:426
  19.4 1.5 %collective-permute-start.2 = (bf16[32,3072]{1,0:T(8,128)(2,1)S(1)}, bf16[32,3072]{1,0:T(8,128)(2,1)S(1)}, u32[]{:S(2)}, u32[]{:S(2)}) collective-permute-start(bf16[32,3072]{1,0:T(8,128)(2,1)S(1)} %join.7.refs_1_), channel_id=1, source_target_pairs={{0,1},{1,0},{2,3},{3,2},{4,5},{5,4},{6,7},{7,6},{8,9},{9,8},{10,11... | collective-permute-start | bytes 589832 | tf_op jit(solution)/shard_map/ppermute | solution.py:426
  19.7 1.6 %collective-permute-start.6 = (bf16[32,3072]{1,0:T(8,128)(2,1)S(1)}, bf16[32,3072]{1,0:T(8,128)(2,1)S(1)}, u32[]{:S(2)}, u32[]{:S(2)}) collective-permute-start(bf16[32,3072]{1,0:T(8,128)(2,1)S(1)} %join.10.refs_1_), channel_id=1, source_target_pairs={{0,1},{1,0},{2,3},{3,2},{4,5},{5,4},{6,7},{7,6},{8,9},{9,8},{10,11... | collective-permute-start | bytes 589832 | tf_op jit(solution)/shard_map/ppermute | solution.py:426
  31.4 1.5 %collective-permute-start.8 = (bf16[32,3072]{1,0:T(8,128)(2,1)S(1)}, bf16[32,3072]{1,0:T(8,128)(2,1)S(1)}, u32[]{:S(2)}, u32[]{:S(2)}) collective-permute-start(bf16[32,3072]{1,0:T(8,128)(2,1)S(1)} %get-tuple-element.35), channel_id=1, source_target_pairs={{0,1},{1,0},{2,3},{3,2},{4,5},{5,4},{6,7},{7,6},{8,9},{9,8},{10,11... | collective-permute-start | bytes 589832 | tf_op jit(solution)/shard_map/ppermute | solution.py:426
  31.8 6.3 %collective-permute-start.7 = (bf16[32,3072]{1,0:T(8,128)(2,1)S(1)}, bf16[32,3072]{1,0:T(8,128)(2,1)S(1)}, u32[]{:S(2)}, u32[]{:S(2)}) collective-permute-start(bf16[32,3072]{1,0:T(8,128)(2,1)S(1)} %get-tuple-element.33), channel_id=1, source_target_pairs={{0,1},{1,0},{2,3},{3,2},{4,5},{5,4},{6,7},{7,6},{8,9},{9,8},{10,11... | collective-permute-start | bytes 589832 | tf_op jit(solution)/shard_map/ppermute | solution.py:426
  32.9 5.1 %collective-permute-start.9 = (bf16[16,3072]{1,0:T(8,128)(2,1)S(1)}, bf16[16,3072]{1,0:T(8,128)(2,1)S(1)}, u32[]{:S(2)}, u32[]{:S(2)}) collective-permute-start(bf16[16,3072]{1,0:T(8,128)(2,1)S(1)} %get-tuple-element.37), channel_id=1, source_target_pairs={{0,2},{1,3},{2,0},{3,1},{4,6},{5,7},{6,4},{7,5},{8,10},{9,11},{10,... | collective-permute-start | bytes 294920 | tf_op jit(solution)/shard_map/ppermute | solution.py:426
  38.1 4.7 %collective-permute-start.10 = (bf16[16,3072]{1,0:T(8,128)(2,1)S(1)}, bf16[16,3072]{1,0:T(8,128)(2,1)S(1)}, u32[]{:S(2)}, u32[]{:S(2)}) collective-permute-start(bf16[16,3072]{1,0:T(8,128)(2,1)S(1)} %get-tuple-element.40), channel_id=1, source_target_pairs={{0,2},{1,3},{2,0},{3,1},{4,6},{5,7},{6,4},{7,5},{8,10},{9,11},{10,... | collective-permute-start | bytes 294920 | tf_op jit(solution)/shard_map/ppermute | solution.py:426
  39.5 6.3 %collective-permute-start.12 = (bf16[8,3072]{1,0:T(8,128)(2,1)S(1)}, bf16[8,3072]{1,0:T(8,128)(2,1)S(1)}, u32[]{:S(2)}, u32[]{:S(2)}) collective-permute-start(bf16[8,3072]{1,0:T(8,128)(2,1)S(1)} %get-tuple-element.38.after), channel_id=1, source_target_pairs={{0,8},{1,9},{2,10},{3,11},{4,12},{5,13},{6,14},{7,15},{8,0},{9,1},... | collective-permute-start | bytes 147464 | tf_op jit(solution)/shard_map/ppermute | solution.py:426
  39.8 5.9 %collective-permute-start.13 = (bf16[8,3072]{1,0:T(8,128)(2,1)S(1)}, bf16[8,3072]{1,0:T(8,128)(2,1)S(1)}, u32[]{:S(2)}, u32[]{:S(2)}) collective-permute-start(bf16[8,3072]{1,0:T(8,128)(2,1)S(1)} %get-tuple-element.43), channel_id=1, source_target_pairs={{0,12},{1,13},{2,14},{3,15},{4,8},{5,9},{6,10},{7,11},{8,4},{9,5},... | collective-permute-start | bytes 147464 | tf_op jit(solution)/shard_map/ppermute | solution.py:426
  42.8 4.2 %collective-permute-start.11 = (bf16[8,3072]{1,0:T(8,128)(2,1)S(1)}, bf16[8,3072]{1,0:T(8,128)(2,1)S(1)}, u32[]{:S(2)}, u32[]{:S(2)}) collective-permute-start(bf16[8,3072]{1,0:T(8,128)(2,1)S(1)} %get-tuple-element.42), channel_id=1, source_target_pairs={{0,4},{1,5},{2,6},{3,7},{4,0},{5,1},{6,2},{7,3},{8,12},{9,13},{10,... | collective-permute-start | bytes 147464 | tf_op jit(solution)/shard_map/ppermute | solution.py:426

commit v12 on v10

--- a/solution.py
+++ b/solution.py
@@ -12,7 +12,7 @@
 HEAD_DIM = 128
 EXPERTS = 4
 MIB = 1 << 20
-HINTS = 3
+HINTS = 4
 MOST = 6
 F32 = jnp.float32
 BF16 = jnp.bfloat16
@@ -225,18 +225,11 @@
     )(*[pltpu.with_memory_space_constraint(x, pltpu.HBM) for x in operands + (weight,) * HINTS])
 
 
-def expert_kernel(near, far, gate_weight, up_weight, down_weight, *refs):
-    outs, (hidden, down, semaphores) = refs[:4], refs[4:]
-    rows = near.shape[0] + far.shape[0]
-    width, columns = gate_weight.shape
-    quarter = width // 4
-    order = (3, 0, 1, 2)
-    copies = {}
-    for m in order:
-        lanes = pl.ds(m * quarter, quarter)
-        copies[m] = pltpu.make_async_copy(down_weight.at[:, lanes], down.at[m], semaphores.at[m])
-        copies[m].start()
-
+def hidden_kernel(near, far, gate_weight, up_weight, down_weight, hidden):
+    columns = gate_weight.shape[1]
+    step = 256 if columns % 256 == 0 else columns
+    quarter = near.shape[1] // 3
+    blocks = jnp.concatenate([near[...], far[...]], axis=0)
     size = 128
     row, lane = grid((size, size))
     slot = row & 7
@@ -245,64 +238,74 @@
         one_hot((lane == row - slot + 6 + late) & (slot - 3 * late == m)) for m in range(3)
     ]
     picks = jnp.concatenate(picks, axis=1)
-    blocks = jnp.concatenate([near[...], far[...]], axis=0)
     tails = []
-    for first in range(0, rows, size):
+    for first in range(0, blocks.shape[0], size):
         some = blocks[first : first + size]
         parts = [some[:, m * quarter : (m + 1) * quarter] for m in range(3)]
         tails.append(dot(picks, jnp.concatenate(parts, axis=0)).astype(BF16))
     x = jnp.concatenate([blocks, jnp.concatenate(tails, axis=0)], axis=1)
-    step = 256 if columns % 256 == 0 else columns
     for f in range(0, columns, step):
         gate = dot(x, gate_weight[:, f : f + step])
         upper = dot(x, up_weight[:, f : f + step])
         hidden[:, f : f + step] = (gate / (1.0 + jnp.exp(-gate)) * upper).astype(BF16)
 
+
+def hidden_rows(near, far, gate_weight, up_weight, down_weight):
+    rows = near.shape[0] + far.shape[0]
+    width, columns = gate_weight.shape
+    return pl.pallas_call(
+        hidden_kernel,
+        out_shape=jax.ShapeDtypeStruct((rows, columns), BF16),
+        in_specs=[VMEM] * 5,
+        out_specs=VMEM,
+        compiler_params=pltpu.CompilerParams(vmem_limit_bytes=4 * MIB * max(1, rows // 128)),
+        cost_estimate=pl.CostEstimate(
+            flops=4 * rows * width * columns, bytes_accessed=0, transcendentals=rows * columns
+        ),
+        name="hidden",
+    )(near, far, gate_weight, up_weight, down_weight)
+
+
+def down_kernel(hidden, weight, *outs):
+    rows = hidden.shape[0]
+    quarter = outs[0].shape[1] // 3
+    size = 128
+    row, lane = grid((size, size))
+    slot = row & 7
     picks = [one_hot((lane == row - slot + 3 * (slot - 6) + m) & (slot >= MOST)) for m in range(3)]
     picks = jnp.concatenate(picks, axis=0)
     h = hidden[...]
+
+    def terms(first, count):
+        return dot(h, weight[:, first : first + count])
+
     step = min(512, quarter)
     is_row = (lax.broadcasted_iota(jnp.int32, (rows, step), 0) & 7) < MOST
     each = rows // len(outs)
-    moved = {}
-    for m in order:
-        copies[m].wait()
-        for n in range(0, quarter, step):
-            terms = dot(h, down[m, :, n : n + step])
-            if m == 3:
-                tail = terms.astype(BF16)
-                tails = [dot(picks, tail[i : i + size]) for i in range(0, rows, size)]
-                for k in range(3):
-                    moved[k, n] = jnp.concatenate(
-                        [t[k * size : (k + 1) * size] for t in tails], axis=0
-                    ).astype(BF16)
-                continue
-            value = jnp.where(is_row, terms, moved[m, n].astype(F32)).astype(BF16)
+    for n in range(0, quarter, step):
+        tail = terms(3 * quarter + n, step).astype(BF16)
+        tails = [dot(picks, tail[i : i + size]) for i in range(0, rows, size)]
+        for m in range(3):
+            moved = jnp.concatenate([x[m * size : (m + 1) * size] for x in tails], axis=0)
+            value = jnp.where(is_row, terms(m * quarter + n, step), moved).astype(BF16)
             for k, out in enumerate(outs):
                 out[:, m * quarter + n : m * quarter + n + step] = value[k * each : (k + 1) * each]
 
 
-def expert_rows(near, far, gate_weight, up_weight, down_weight):
-    rows = near.shape[0] + far.shape[0]
-    width, columns = gate_weight.shape
-    return pl.pallas_call(
-        expert_kernel,
+def down_rows(hidden, weight):
+    rows, columns = hidden.shape
+    width = weight.shape[1]
+    return pl.pallas_call(
+        down_kernel,
         out_shape=[jax.ShapeDtypeStruct((rows // 4, width // 4 * 3), BF16)] * 4,
-        in_specs=[VMEM] * 4 + [ANY],
+        in_specs=[VMEM] * 2,
         out_specs=[VMEM] * 4,
-        scratch_shapes=[
-            pltpu.VMEM((rows, columns), BF16),
-            pltpu.VMEM((4, columns, width // 4), BF16),
-            pltpu.SemaphoreType.DMA((4,)),
-        ],
-        compiler_params=pltpu.CompilerParams(
-            vmem_limit_bytes=2 * columns * width + 4 * MIB * max(1, rows // 128)
+        compiler_params=pltpu.CompilerParams(vmem_limit_bytes=4 * MIB * max(1, rows // 128)),
+        cost_estimate=pl.CostEstimate(
+            flops=2 * rows * width * columns, bytes_accessed=0, transcendentals=0
         ),
-        cost_estimate=pl.CostEstimate(
-            flops=6 * rows * width * columns, bytes_accessed=0, transcendentals=rows * columns
-        ),
-        name="experts",
-    )(near, far, gate_weight, up_weight, pltpu.with_memory_space_constraint(down_weight, pltpu.HBM))
+        name="down",
+    )(hidden, weight)
 
 
 def join_kernel(*refs):
@@ -407,9 +410,8 @@
         near = join(near, swap(near, count, bit))
         far = join(far, swap(far, count, bit))
 
-    near, near_send, far, far_send = expert_rows(
-        near, far, gate_weight, up_weight, down_weight
-    )
+    hidden = hidden_rows(near, far, gate_weight, up_weight, down_weight)
+    near, near_send, far, far_send = down_rows(hidden, down_weight)
     for bit in reversed(bits):
         far, far_send = fold(far, swap(far_send, count, bit), share)
     for bit in reversed(bits):

time: 47.5 us -> 44.3 us (0.933)
  Pallas kernels: 13.9 us -> 10.6 us
    pallas_call x1 -> x2, Pallas kernels: 9.95 us -> 6.68 us  [the longest x1 4.13 us: hidden_rows(): pl.pallas_call(hidden_kernel, out_shape=jax.ShapeDtypeStruct((rows, colum...]
where the time goes in v12:
time: 44.3 us; the launch traced here: 44.1 us
  waiting for transfers between devices  17.7 us (40%)
  starting transfers between devices  15 us (34%)
  Pallas kernels  10.6 us (24%)
  between operations  0.8 us (2%)
    ppermute x14, waiting for transfers between devices, swap(): return lax.ppermute(value, 'dp', [(i, i ^ bit) for i in range(count)])  17.7 us
    ppermute x14, starting transfers between devices, swap(): return lax.ppermute(value, 'dp', [(i, i ^ bit) for i in range(count)])  15 us
    pallas_call x1, Pallas kernels, hidden_rows(): pl.pallas_call(hidden_kernel, out_shape=jax.ShapeDtypeStruct((rows, colum...  4.13 us
    pallas_call x1, Pallas kernels, attend(): pl.pallas_call(functools.partial(attend_kernel, plane), out_shape=(jax.Sh...  2.65 us
    pallas_call x1, Pallas kernels, down_rows(): pl.pallas_call(down_kernel, out_shape=[jax.ShapeDtypeStruct((rows // 4, w...  2.55 us
    pallas_call x2, Pallas kernels, combine(): pl.pallas_call(functools.partial(combine_kernel, first), out_shape=jax.Sh...  1.06 us
  transfers between devices with their start and end apart: 14, of which 9 were waited for; matrix products, arithmetic and copies ran while one was open for 0% of the time, Pallas kernels for 1%

profile of v12, /device:TPU:0, one launch (start us, length us, event | category | flops | bytes accessed | tf_op | source)
XLA Modules:
  0.0 44.1 jit_solution(5942527908263203738)
XLA Ops:
  0.7 2.7 %attend.1 = (bf16[8,4096]{1,0:T(8,128)(2,1)}, bf16[8,3072]{1,0:T(8,128)(2,1)S(1)}, bf16[8,3072]{1,0:T(8,128)(2,1)S(1)}, bf16[8,3072]{1,0:T(8,128)(2,1)S(1)}, bf1...) custom-call(bf16[8,4096]{1,0:T(8,128)(2,1)} %refs_0_.1, ...), custom_call_target="tpu_custom_call" | custom-call | tf_op jit(solution)/shard_map/attend/pallas_call | solution.py:208
  3.3 3.1 %collective-permute-start = (bf16[8,3072]{1,0:T(8,128)(2,1)S(1)}, bf16[8,3072]{1,0:T(8,128)(2,1)S(1)}, u32[]{:S(2)}, u32[]{:S(2)}) collective-permute-start(bf16[8,3072]{1,0:T(8,128)(2,1)S(1)} %get-tuple-element.25), channel_id=1, source_target_pairs={{0,4},{1,5},{2,6},{3,7},{4,0},{5,1},{6,2},{7,3},{8,12},{9,13},{10,... | collective-permute-start | bytes 147464 | tf_op jit(solution)/shard_map/ppermute | solution.py:380
  6.4 2.6 %collective-permute-start.3 = (bf16[8,3072]{1,0:T(8,128)(2,1)S(1)}, bf16[8,3072]{1,0:T(8,128)(2,1)S(1)}, u32[]{:S(2)}, u32[]{:S(2)}) collective-permute-start(bf16[8,3072]{1,0:T(8,128)(2,1)S(1)} %get-tuple-element.26), channel_id=1, source_target_pairs={{0,8},{1,9},{2,10},{3,11},{4,12},{5,13},{6,14},{7,15},{8,0},{9,1},... | collective-permute-start | bytes 147464 | tf_op jit(solution)/shard_map/ppermute | solution.py:380
  9.0 0.0 collective-permute-start.4
  9.0 0.0 collective-permute-done.refs_1_
  9.0 1.8 %collective-permute-start.1 = (bf16[16,3072]{1,0:T(8,128)(2,1)S(1)}, bf16[16,3072]{1,0:T(8,128)(2,1)S(1)}, u32[]{:S(2)}, u32[]{:S(2)}) collective-permute-start(bf16[16,3072]{1,0:T(8,128)(2,1)S(1)} %join.6.refs_0_), channel_id=1, source_target_pairs={{0,2},{1,3},{2,0},{3,1},{4,6},{5,7},{6,4},{7,5},{8,10},{9,11},{10,... | collective-permute-start | bytes 294920 | tf_op jit(solution)/shard_map/ppermute | solution.py:380
  10.8 1.5 %collective-permute-done.3.refs_0_ = bf16[8,3072]{1,0:T(8,128)(2,1)S(1)} collective-permute-done((bf16[8,3072]{1,0:T(8,128)(2,1)S(1)}, bf16[8,3072]{1,0:T(8,128)(2,1)S(1)}, u32[]{:S(2)}, u32[]{:S(2)}) %collective-permute-start.3) | collective-permute-done | bytes 49184 | tf_op jit(solution)/shard_map/ppermute | solution.py:380
  12.3 2.6 %collective-permute-done.4.refs_1_ = bf16[8,3072]{1,0:T(8,128)(2,1)S(1)} collective-permute-done((bf16[8,3072]{1,0:T(8,128)(2,1)S(1)}, bf16[8,3072]{1,0:T(8,128)(2,1)S(1)}, u32[]{:S(2)}, u32[]{:S(2)}) %collective-permute-start.4) | collective-permute-done | bytes 49184 | tf_op jit(solution)/shard_map/ppermute | solution.py:380
  14.9 1.6 %collective-permute-start.5 = (bf16[16,3072]{1,0:T(8,128)(2,1)S(1)}, bf16[16,3072]{1,0:T(8,128)(2,1)S(1)}, u32[]{:S(2)}, u32[]{:S(2)}) collective-permute-start(bf16[16,3072]{1,0:T(8,128)(2,1)S(1)} %join.9.refs_0_), channel_id=1, source_target_pairs={{0,2},{1,3},{2,0},{3,1},{4,6},{5,7},{6,4},{7,5},{8,10},{9,11},{10,... | collective-permute-start | bytes 294920 | tf_op jit(solution)/shard_map/ppermute | solution.py:380
  16.5 0.0 collective-permute-done.1.refs_1_
  16.5 0.1 collective-permute-start.2
  16.6 3.0 %collective-permute-done.5.refs_1_ = bf16[16,3072]{1,0:T(8,128)(2,1)S(1)} collective-permute-done((bf16[16,3072]{1,0:T(8,128)(2,1)S(1)}, bf16[16,3072]{1,0:T(8,128)(2,1)S(1)}, u32[]{:S(2)}, u32[]{:S(2)}) %collective-permute-start.5) | collective-permute-done | bytes 98336 | tf_op jit(solution)/shard_map/ppermute | solution.py:380
  19.6 0.1 collective-permute-start.6
  19.7 1.4 %collective-permute-done.6.refs_1_ = bf16[32,3072]{1,0:T(8,128)(2,1)S(1)} collective-permute-done((bf16[32,3072]{1,0:T(8,128)(2,1)S(1)}, bf16[32,3072]{1,0:T(8,128)(2,1)S(1)}, u32[]{:S(2)}, u32[]{:S(2)}) %collective-permute-start.6) | collective-permute-done | bytes 196640 | tf_op jit(solution)/shard_map/ppermute | solution.py:380
  21.2 4.1 %hidden.1 = bf16[128,1792]{1,0:T(8,128)(2,1)S(1)} custom-call(bf16[64,3072]{1,0:T(8,128)(2,1)S(1)} %join.8.near, bf16[64,3072]{1,0:T(8,128)(2,1)S(1)} %join.11.far, bf16[4096,1792]{1,0:T(8,128)(2,1)S(1)} %copy-done.1, bf16[4096,1792]{1,0:T(8,128)(2,1)S(1)} %copy-done.2, bf16[1792,4096]{1,0:T(8,128)(2,1)S(1)} %copy-done), custom_call_target="tpu_custom_call" | custom-call | flops 3758096384 | tf_op jit(solution)/shard_map/hidden/pallas_call | solution.py:256
  25.3 2.6 %down.1 = (bf16[32,3072]{1,0:T(8,128)(2,1)S(1)}, bf16[32,3072]{1,0:T(8,128)(2,1)S(1)}, bf16[32,3072]{1,0:T(8,128)(2,1)S(1)}, bf16[32,3072]{1,0:T(8,128)(2,1)S(1)}) custom-call(bf16[128,1792]{1,0:T(8,128)(2,1)S(1)} %hidden.1, bf16[1792,4096]{1,0:T(8,128)(2,1)S(1)} %copy-done), custom_call_target="tpu_custom_call" | custom-call | flops 1879048192 | tf_op jit(solution)/shard_map/down/pallas_call | solution.py:298
  27.9 0.2 collective-permute-start.8
  28.1 0.4 collective-permute-start.7
  28.4 0.9 %collective-permute-done.8.arrived = bf16[32,3072]{1,0:T(8,128)(2,1)S(1)} collective-permute-done((bf16[32,3072]{1,0:T(8,128)(2,1)S(1)}, bf16[32,3072]{1,0:T(8,128)(2,1)S(1)}, u32[]{:S(2)}, u32[]{:S(2)}) %collective-permute-start.8) | collective-permute-done | bytes 196640 | tf_op jit(solution)/shard_map/ppermute | solution.py:380
  29.4 1.6 %collective-permute-start.9 = (bf16[16,3072]{1,0:T(8,128)(2,1)S(1)}, bf16[16,3072]{1,0:T(8,128)(2,1)S(1)}, u32[]{:S(2)}, u32[]{:S(2)}) collective-permute-start(bf16[16,3072]{1,0:T(8,128)(2,1)S(1)} %get-tuple-element.33), channel_id=1, source_target_pairs={{0,2},{1,3},{2,0},{3,1},{4,6},{5,7},{6,4},{7,5},{8,10},{9,11},{10,... | collective-permute-start | bytes 294920 | tf_op jit(solution)/shard_map/ppermute | solution.py:380
  31.0 3.3 %collective-permute-done.9.arrived = bf16[16,3072]{1,0:T(8,128)(2,1)S(1)} collective-permute-done((bf16[16,3072]{1,0:T(8,128)(2,1)S(1)}, bf16[16,3072]{1,0:T(8,128)(2,1)S(1)}, u32[]{:S(2)}, u32[]{:S(2)}) %collective-permute-start.9) | collective-permute-done | bytes 98336 | tf_op jit(solution)/shard_map/ppermute | solution.py:380
  34.4 0.0 collective-permute-done.7.arrived
  34.4 0.1 fold.6
  34.4 1.6 %collective-permute-start.10 = (bf16[16,3072]{1,0:T(8,128)(2,1)S(1)}, bf16[16,3072]{1,0:T(8,128)(2,1)S(1)}, u32[]{:S(2)}, u32[]{:S(2)}) collective-permute-start(bf16[16,3072]{1,0:T(8,128)(2,1)S(1)} %get-tuple-element.36), channel_id=1, source_target_pairs={{0,2},{1,3},{2,0},{3,1},{4,6},{5,7},{6,4},{7,5},{8,10},{9,11},{10,... | collective-permute-start | bytes 294920 | tf_op jit(solution)/shard_map/ppermute | solution.py:380
  36.0 0.4 collective-permute-start.12
  36.4 1.2 %collective-permute-start.13 = (bf16[8,3072]{1,0:T(8,128)(2,1)S(1)}, bf16[8,3072]{1,0:T(8,128)(2,1)S(1)}, u32[]{:S(2)}, u32[]{:S(2)}) collective-permute-start(bf16[8,3072]{1,0:T(8,128)(2,1)S(1)} %get-tuple-element.39), channel_id=1, source_target_pairs={{0,12},{1,13},{2,14},{3,15},{4,8},{5,9},{6,10},{7,11},{8,4},{9,5},... | collective-permute-start | bytes 147464 | tf_op jit(solution)/shard_map/ppermute | solution.py:380
  37.5 1.6 %collective-permute-done.10.arrived = bf16[16,3072]{1,0:T(8,128)(2,1)S(1)} collective-permute-done((bf16[16,3072]{1,0:T(8,128)(2,1)S(1)}, bf16[16,3072]{1,0:T(8,128)(2,1)S(1)}, u32[]{:S(2)}, u32[]{:S(2)}) %collective-permute-start.10) | collective-permute-done | bytes 98336 | tf_op jit(solution)/shard_map/ppermute | solution.py:380
  39.1 0.5 %collective-permute-start.11 = (bf16[8,3072]{1,0:T(8,128)(2,1)S(1)}, bf16[8,3072]{1,0:T(8,128)(2,1)S(1)}, u32[]{:S(2)}, u32[]{:S(2)}) collective-permute-start(bf16[8,3072]{1,0:T(8,128)(2,1)S(1)} %get-tuple-element.38), channel_id=1, source_target_pairs={{0,4},{1,5},{2,6},{3,7},{4,0},{5,1},{6,2},{7,3},{8,12},{9,13},{10,... | collective-permute-start | bytes 147464 | tf_op jit(solution)/shard_map/ppermute | solution.py:380
  39.6 2.7 %collective-permute-done.13.refs_1_ = bf16[8,3072]{1,0:T(8,128)(2,1)S(1)} collective-permute-done((bf16[8,3072]{1,0:T(8,128)(2,1)S(1)}, bf16[8,3072]{1,0:T(8,128)(2,1)S(1)}, u32[]{:S(2)}, u32[]{:S(2)}) %collective-permute-start.13) | collective-permute-done | bytes 49184 | tf_op jit(solution)/shard_map/ppermute | solution.py:380
  42.3 0.2 combine.2.refs_2_
  42.5 0.8 %collective-permute-done.11.refs_1_ = bf16[8,3072]{1,0:T(8,128)(2,1)S(1)} collective-permute-done((bf16[8,3072]{1,0:T(8,128)(2,1)S(1)}, bf16[8,3072]{1,0:T(8,128)(2,1)S(1)}, u32[]{:S(2)}, u32[]{:S(2)}) %collective-permute-start.11) | collective-permute-done | bytes 49184 | tf_op jit(solution)/shard_map/ppermute | solution.py:380
  43.3 0.8 %combine.3 = bf16[8,4096]{1,0:T(8,128)(2,1)} custom-call(f32[16,128]{1,0:T(8,128)S(1)} %get-tuple-element.22.after.share, bf16[4,16,128]{2,1,0:T(8,128)(2,1)S(1)} %get-tuple-element.23.take, bf16[8,3072]{1,0:T(8,128)(2,1)S(1)} %get-tuple-element.37.refs_0_, bf16[8,3072]{1,0:T(8,128)(2,1)S(1)} %collective-permute-done.11.refs_1_, f32[8,4096]{1,0:T(8,128)S(1)} %combine.2.refs_2_), custom_call_target="tpu_custom_call" | custom-call | bytes 16777216 | tf_op jit(solution)/shard_map/combine/pallas_call | solution.py:368
  (17 shorter events, 0.2 us)
Async XLA Ops:
  0.6 20.5 %copy-start = (bf16[1792,4096]{1,0:T(8,128)(2,1)S(1)}, bf16[1792,4096]{1,0:T(8,128)(2,1)}, u32[]{:S(2)}) copy-start(bf16[1792,4096]{1,0:T(8,128)(2,1)} %weight.1) | copy-start | bytes 44040196
  0.6 20.5 %copy-start.1 = (bf16[4096,1792]{1,0:T(8,128)(2,1)S(1)}, bf16[4096,1792]{1,0:T(8,128)(2,1)}, u32[]{:S(2)}) copy-start(bf16[4096,1792]{1,0:T(8,128)(2,1)} %gate_weight.1) | copy-start | bytes 44040196
  0.7 20.5 %copy-start.2 = (bf16[4096,1792]{1,0:T(8,128)(2,1)S(1)}, bf16[4096,1792]{1,0:T(8,128)(2,1)}, u32[]{:S(2)}) copy-start(bf16[4096,1792]{1,0:T(8,128)(2,1)} %up_weight.1) | copy-start | bytes 44040196
  3.3 5.7 %collective-permute-start = (bf16[8,3072]{1,0:T(8,128)(2,1)S(1)}, bf16[8,3072]{1,0:T(8,128)(2,1)S(1)}, u32[]{:S(2)}, u32[]{:S(2)}) collective-permute-start(bf16[8,3072]{1,0:T(8,128)(2,1)S(1)} %get-tuple-element.25), channel_id=1, source_target_pairs={{0,4},{1,5},{2,6},{3,7},{4,0},{5,1},{6,2},{7,3},{8,12},{9,13},{10,... | collective-permute-start | bytes 147464 | tf_op jit(solution)/shard_map/ppermute | solution.py:380
  6.4 5.9 %collective-permute-start.3 = (bf16[8,3072]{1,0:T(8,128)(2,1)S(1)}, bf16[8,3072]{1,0:T(8,128)(2,1)S(1)}, u32[]{:S(2)}, u32[]{:S(2)}) collective-permute-start(bf16[8,3072]{1,0:T(8,128)(2,1)S(1)} %get-tuple-element.26), channel_id=1, source_target_pairs={{0,8},{1,9},{2,10},{3,11},{4,12},{5,13},{6,14},{7,15},{8,0},{9,1},... | collective-permute-start | bytes 147464 | tf_op jit(solution)/shard_map/ppermute | solution.py:380
  9.0 5.9 %collective-permute-start.4 = (bf16[8,3072]{1,0:T(8,128)(2,1)S(1)}, bf16[8,3072]{1,0:T(8,128)(2,1)S(1)}, u32[]{:S(2)}, u32[]{:S(2)}) collective-permute-start(bf16[8,3072]{1,0:T(8,128)(2,1)S(1)} %get-tuple-element.27), channel_id=1, source_target_pairs={{0,12},{1,13},{2,14},{3,15},{4,8},{5,9},{6,10},{7,11},{8,4},{9,5},... | collective-permute-start | bytes 147464 | tf_op jit(solution)/shard_map/ppermute | solution.py:380
  9.0 7.5 %collective-permute-start.1 = (bf16[16,3072]{1,0:T(8,128)(2,1)S(1)}, bf16[16,3072]{1,0:T(8,128)(2,1)S(1)}, u32[]{:S(2)}, u32[]{:S(2)}) collective-permute-start(bf16[16,3072]{1,0:T(8,128)(2,1)S(1)} %join.6.refs_0_), channel_id=1, source_target_pairs={{0,2},{1,3},{2,0},{3,1},{4,6},{5,7},{6,4},{7,5},{8,10},{9,11},{10,... | collective-permute-start | bytes 294920 | tf_op jit(solution)/shard_map/ppermute | solution.py:380
  14.9 4.7 %collective-permute-start.5 = (bf16[16,3072]{1,0:T(8,128)(2,1)S(1)}, bf16[16,3072]{1,0:T(8,128)(2,1)S(1)}, u32[]{:S(2)}, u32[]{:S(2)}) collective-permute-start(bf16[16,3072]{1,0:T(8,128)(2,1)S(1)} %join.9.refs_0_), channel_id=1, source_target_pairs={{0,2},{1,3},{2,0},{3,1},{4,6},{5,7},{6,4},{7,5},{8,10},{9,11},{10,... | collective-permute-start | bytes 294920 | tf_op jit(solution)/shard_map/ppermute | solution.py:380
  16.5 3.2 %collective-permute-start.2 = (bf16[32,3072]{1,0:T(8,128)(2,1)S(1)}, bf16[32,3072]{1,0:T(8,128)(2,1)S(1)}, u32[]{:S(2)}, u32[]{:S(2)}) collective-permute-start(bf16[32,3072]{1,0:T(8,128)(2,1)S(1)} %join.7.refs_0_), channel_id=1, source_target_pairs={{0,1},{1,0},{2,3},{3,2},{4,5},{5,4},{6,7},{7,6},{8,9},{9,8},{10,11... | collective-permute-start | bytes 589832 | tf_op jit(solution)/shard_map/ppermute | solution.py:380
  19.6 1.5 %collective-permute-start.6 = (bf16[32,3072]{1,0:T(8,128)(2,1)S(1)}, bf16[32,3072]{1,0:T(8,128)(2,1)S(1)}, u32[]{:S(2)}, u32[]{:S(2)}) collective-permute-start(bf16[32,3072]{1,0:T(8,128)(2,1)S(1)} %join.10.refs_0_), channel_id=1, source_target_pairs={{0,1},{1,0},{2,3},{3,2},{4,5},{5,4},{6,7},{7,6},{8,9},{9,8},{10,11... | collective-permute-start | bytes 589832 | tf_op jit(solution)/shard_map/ppermute | solution.py:380
  27.9 1.5 %collective-permute-start.8 = (bf16[32,3072]{1,0:T(8,128)(2,1)S(1)}, bf16[32,3072]{1,0:T(8,128)(2,1)S(1)}, u32[]{:S(2)}, u32[]{:S(2)}) collective-permute-start(bf16[32,3072]{1,0:T(8,128)(2,1)S(1)} %get-tuple-element.31), channel_id=1, source_target_pairs={{0,1},{1,0},{2,3},{3,2},{4,5},{5,4},{6,7},{7,6},{8,9},{9,8},{10,11... | collective-permute-start | bytes 589832 | tf_op jit(solution)/shard_map/ppermute | solution.py:380
  28.1 6.3 %collective-permute-start.7 = (bf16[32,3072]{1,0:T(8,128)(2,1)S(1)}, bf16[32,3072]{1,0:T(8,128)(2,1)S(1)}, u32[]{:S(2)}, u32[]{:S(2)}) collective-permute-start(bf16[32,3072]{1,0:T(8,128)(2,1)S(1)} %get-tuple-element.29), channel_id=1, source_target_pairs={{0,1},{1,0},{2,3},{3,2},{4,5},{5,4},{6,7},{7,6},{8,9},{9,8},{10,11... | collective-permute-start | bytes 589832 | tf_op jit(solution)/shard_map/ppermute | solution.py:380
  29.4 4.9 %collective-permute-start.9 = (bf16[16,3072]{1,0:T(8,128)(2,1)S(1)}, bf16[16,3072]{1,0:T(8,128)(2,1)S(1)}, u32[]{:S(2)}, u32[]{:S(2)}) collective-permute-start(bf16[16,3072]{1,0:T(8,128)(2,1)S(1)} %get-tuple-element.33), channel_id=1, source_target_pairs={{0,2},{1,3},{2,0},{3,1},{4,6},{5,7},{6,4},{7,5},{8,10},{9,11},{10,... | collective-permute-start | bytes 294920 | tf_op jit(solution)/shard_map/ppermute | solution.py:380
  34.4 4.7 %collective-permute-start.10 = (bf16[16,3072]{1,0:T(8,128)(2,1)S(1)}, bf16[16,3072]{1,0:T(8,128)(2,1)S(1)}, u32[]{:S(2)}, u32[]{:S(2)}) collective-permute-start(bf16[16,3072]{1,0:T(8,128)(2,1)S(1)} %get-tuple-element.36), channel_id=1, source_target_pairs={{0,2},{1,3},{2,0},{3,1},{4,6},{5,7},{6,4},{7,5},{8,10},{9,11},{10,... | collective-permute-start | bytes 294920 | tf_op jit(solution)/shard_map/ppermute | solution.py:380
  36.0 6.3 %collective-permute-start.12 = (bf16[8,3072]{1,0:T(8,128)(2,1)S(1)}, bf16[8,3072]{1,0:T(8,128)(2,1)S(1)}, u32[]{:S(2)}, u32[]{:S(2)}) collective-permute-start(bf16[8,3072]{1,0:T(8,128)(2,1)S(1)} %get-tuple-element.34.after), channel_id=1, source_target_pairs={{0,8},{1,9},{2,10},{3,11},{4,12},{5,13},{6,14},{7,15},{8,0},{9,1},... | collective-permute-start | bytes 147464 | tf_op jit(solution)/shard_map/ppermute | solution.py:380
  36.4 5.9 %collective-permute-start.13 = (bf16[8,3072]{1,0:T(8,128)(2,1)S(1)}, bf16[8,3072]{1,0:T(8,128)(2,1)S(1)}, u32[]{:S(2)}, u32[]{:S(2)}) collective-permute-start(bf16[8,3072]{1,0:T(8,128)(2,1)S(1)} %get-tuple-element.39), channel_id=1, source_target_pairs={{0,12},{1,13},{2,14},{3,15},{4,8},{5,9},{6,10},{7,11},{8,4},{9,5},... | collective-permute-start | bytes 147464 | tf_op jit(solution)/shard_map/ppermute | solution.py:380
  39.1 4.2 %collective-permute-start.11 = (bf16[8,3072]{1,0:T(8,128)(2,1)S(1)}, bf16[8,3072]{1,0:T(8,128)(2,1)S(1)}, u32[]{:S(2)}, u32[]{:S(2)}) collective-permute-start(bf16[8,3072]{1,0:T(8,128)(2,1)S(1)} %get-tuple-element.38), channel_id=1, source_target_pairs={{0,4},{1,5},{2,6},{3,7},{4,0},{5,1},{6,2},{7,3},{8,12},{9,13},{10,... | collective-permute-start | bytes 147464 | tf_op jit(solution)/shard_map/ppermute | solution.py:380

commit v13 on v12

--- a/solution.py
+++ b/solution.py
@@ -225,11 +225,12 @@
     )(*[pltpu.with_memory_space_constraint(x, pltpu.HBM) for x in operands + (weight,) * HINTS])
 
 
-def hidden_kernel(near, far, gate_weight, up_weight, down_weight, hidden):
+def hidden_kernel(gate_weight, up_weight, down_weight, *refs):
+    waves, hidden = refs[:-1], refs[-1]
     columns = gate_weight.shape[1]
     step = 256 if columns % 256 == 0 else columns
-    quarter = near.shape[1] // 3
-    blocks = jnp.concatenate([near[...], far[...]], axis=0)
+    quarter = waves[0].shape[1] // 3
+    blocks = jnp.concatenate([wave[...] for wave in waves], axis=0)
     size = 128
     row, lane = grid((size, size))
     slot = row & 7
@@ -250,20 +251,20 @@
         hidden[:, f : f + step] = (gate / (1.0 + jnp.exp(-gate)) * upper).astype(BF16)
 
 
-def hidden_rows(near, far, gate_weight, up_weight, down_weight):
-    rows = near.shape[0] + far.shape[0]
+def hidden_rows(waves, gate_weight, up_weight, down_weight):
+    rows = sum(wave.shape[0] for wave in waves)
     width, columns = gate_weight.shape
     return pl.pallas_call(
         hidden_kernel,
         out_shape=jax.ShapeDtypeStruct((rows, columns), BF16),
-        in_specs=[VMEM] * 5,
+        in_specs=[VMEM] * (3 + len(waves)),
         out_specs=VMEM,
         compiler_params=pltpu.CompilerParams(vmem_limit_bytes=4 * MIB * max(1, rows // 128)),
         cost_estimate=pl.CostEstimate(
             flops=4 * rows * width * columns, bytes_accessed=0, transcendentals=rows * columns
         ),
         name="hidden",
-    )(near, far, gate_weight, up_weight, down_weight)
+    )(gate_weight, up_weight, down_weight, *waves)
 
 
 def down_kernel(hidden, weight, *outs):
@@ -281,50 +282,61 @@
 
     step = min(512, quarter)
     is_row = (lax.broadcasted_iota(jnp.int32, (rows, step), 0) & 7) < MOST
-    each = rows // len(outs)
     for n in range(0, quarter, step):
         tail = terms(3 * quarter + n, step).astype(BF16)
         tails = [dot(picks, tail[i : i + size]) for i in range(0, rows, size)]
         for m in range(3):
             moved = jnp.concatenate([x[m * size : (m + 1) * size] for x in tails], axis=0)
             value = jnp.where(is_row, terms(m * quarter + n, step), moved).astype(BF16)
-            for k, out in enumerate(outs):
-                out[:, m * quarter + n : m * quarter + n + step] = value[k * each : (k + 1) * each]
+            lanes = slice(m * quarter + n, m * quarter + n + step)
+            for out, blocks in zip(outs, ways_back(rows // 32)):
+                for i, b in enumerate(blocks):
+                    out[8 * i : 8 * i + 8, lanes] = value[8 * b : 8 * b + 8]
+
+
+def ways_back(places):
+    near = [2 * p + j for high in range(0, places, 2) for j in (0, 1) for p in (high, high + 1)]
+    two = [2 * places + 2 * p for p in range(places)]
+    three = [b + 1 for b in two]
+    return [half for w in (near, two, three) for half in (w[: len(w) // 2], w[len(w) // 2 :])]
 
 
 def down_rows(hidden, weight):
     rows, columns = hidden.shape
     width = weight.shape[1]
-    return pl.pallas_call(
+    sizes = [8 * len(blocks) for blocks in ways_back(rows // 32)]
+    outs = pl.pallas_call(
         down_kernel,
-        out_shape=[jax.ShapeDtypeStruct((rows // 4, width // 4 * 3), BF16)] * 4,
+        out_shape=[jax.ShapeDtypeStruct((size, width // 4 * 3), BF16) for size in sizes],
         in_specs=[VMEM] * 2,
-        out_specs=[VMEM] * 4,
+        out_specs=[VMEM] * len(sizes),
         compiler_params=pltpu.CompilerParams(vmem_limit_bytes=4 * MIB * max(1, rows // 128)),
         cost_estimate=pl.CostEstimate(
             flops=2 * rows * width * columns, bytes_accessed=0, transcendentals=0
         ),
         name="down",
     )(hidden, weight)
+    return outs[0:2], outs[2:4], outs[4:6]
 
 
 def join_kernel(*refs):
     out, row = refs[-1], 0
-    for piece in refs[:-1]:
+    for piece in refs[1:-1]:
         out[row : row + piece.shape[0]] = piece[...]
         row += piece.shape[0]
 
 
-def join(*pieces):
+def join(after, *pieces):
     rows = sum(piece.shape[0] for piece in pieces)
     return pl.pallas_call(
         join_kernel,
         out_shape=jax.ShapeDtypeStruct((rows, pieces[0].shape[1]), BF16),
-        in_specs=[VMEM] * len(pieces),
+        in_specs=[ANY] + [VMEM] * len(pieces),
         out_specs=VMEM,
         compiler_params=pltpu.CompilerParams(vmem_limit_bytes=1 * MIB),
+        cost_estimate=pl.CostEstimate(flops=0, bytes_accessed=0, transcendentals=0),
         name="join",
-    )(*pieces)
+    )(after, *pieces)
 
 
 def fold_kernel(held, arrived, after, *outs):
@@ -334,15 +346,15 @@
         out[...] = (held[block].astype(F32) + arrived[block].astype(F32)).astype(BF16)
 
 
-def fold(held, arrived, after):
+def fold(held, arrived, after, parts):
     rows, width = held.shape
     return pl.pallas_call(
         fold_kernel,
-        out_shape=[jax.ShapeDtypeStruct((rows // 2, width), BF16)] * 2,
+        out_shape=[jax.ShapeDtypeStruct((rows // parts, width), BF16)] * parts,
         in_specs=[VMEM] * 2 + [ANY],
-        out_specs=[VMEM] * 2,
+        out_specs=[VMEM] * parts,
         compiler_params=pltpu.CompilerParams(vmem_limit_bytes=MIB * max(1, rows // 64)),
-        cost_estimate=pl.CostEstimate(flops=0, bytes_accessed=16 * MIB, transcendentals=0),
+        cost_estimate=pl.CostEstimate(flops=0, bytes_accessed=0, transcendentals=0),
         name="fold",
     )(held, arrived, after)
 
@@ -404,23 +416,36 @@
     )
 
     packed = [packed[0]] + [swap(packed[k], count, k * plane) for k in range(1, EXPERTS)]
-    near = join(*packed[:2])
-    far = join(*packed[2:])
+    waves = [join(share, *packed[:2]), join(share, *packed[2:])]
     for bit in bits:
-        near = join(near, swap(near, count, bit))
-        far = join(far, swap(far, count, bit))
-
-    hidden = hidden_rows(near, far, gate_weight, up_weight, down_weight)
-    near, near_send, far, far_send = down_rows(hidden, down_weight)
-    for bit in reversed(bits):
-        far, far_send = fold(far, swap(far_send, count, bit), share)
-    for bit in reversed(bits):
-        near, near_send = fold(near, swap(near_send, count, bit), far)
-    far = swap(far, count, 2 * plane)
-    far_send = swap(far_send, count, 3 * plane)
-    near_send = swap(near_send, count, plane)
-    total = combine(2, share, take, [far, far_send], [], F32)
-    return (attended, combine(0, share, take, [near, near_send], [total], BF16))
+        waves = [join(share, wave, swap(wave, count, bit)) for wave in waves]
+
+    hidden = hidden_rows(waves, gate_weight, up_weight, down_weight)
+
+    near, two, three = down_rows(hidden, down_weight)
+
+    def back(wave, stage, after, parts=2):
+        return fold(wave[0], swap(wave[1], count, bits[-1 - stage]), after, parts)
+
+    last = len(bits) - 1
+    token = share
+    for stage in range(last):
+        two = back(two, stage, token)
+        three = back(three, stage, two[0])
+        token = three[0]
+        near = back(near, stage, token, 4 if stage == last - 1 else 2)
+    two = back(two, last, near[0], 1)
+    three = back(three, last, two[0], 1)
+    one = back(near[2:4], last, three[0], 1)
+    zero = back(near[0:2], last, one[0], 1)
+    results = [
+        zero[0],
+        swap(one[0], count, plane),
+        swap(two[0], count, 2 * plane),
+        swap(three[0], count, 3 * plane),
+    ]
+    total = combine(2, share, take, results[2:], [], F32)
+    return (attended, combine(0, share, take, results[:2], [total], BF16))
 
 
 def solution(mesh):

time: 44.3 us -> 42.6 us (0.962)
  waiting for transfers between devices: 17.7 us -> 14.3 us
  starting transfers between devices: 15 us -> 16.6 us
    ppermute x14 -> x17, waiting for transfers between devices: 17.7 us -> 14.3 us  [swap(): return lax.ppermute(value, 'dp', [(i, i ^ bit) for i in range(count)])]
    ppermute x14 -> x17, starting transfers between devices: 15 us -> 16.6 us  [swap(): return lax.ppermute(value, 'dp', [(i, i ^ bit) for i in range(count)])]
    pallas_call x5 -> x8, Pallas kernels: 2.7 us -> 2.71 us  [the longest x1 2.55 us: down_rows(): pl.pallas_call(down_kernel, out_shape=[jax.ShapeDtypeStruct((size, width...]
  transfers between devices with their start and end apart: 14 -> 17, of which waited for: 9 -> 8; matrix products, arithmetic and copies ran while one was open for 0% -> 0% of each run, Pallas kernels for 1% -> 1%
where the time goes in v13:
time: 42.6 us; the launch traced here: 42.4 us
  starting transfers between devices  16.6 us (39%)
  waiting for transfers between devices  14.3 us (34%)
  Pallas kernels  10.7 us (25%)
  between operations  0.81 us (2%)
    ppermute x17, starting transfers between devices, swap(): return lax.ppermute(value, 'dp', [(i, i ^ bit) for i in range(count)])  16.6 us
    ppermute x17, waiting for transfers between devices, swap(): return lax.ppermute(value, 'dp', [(i, i ^ bit) for i in range(count)])  14.3 us
    pallas_call x1, Pallas kernels, hidden_rows(): pl.pallas_call(hidden_kernel, out_shape=jax.ShapeDtypeStruct((rows, colum...  4.13 us
    pallas_call x1, Pallas kernels, attend(): pl.pallas_call(functools.partial(attend_kernel, plane), out_shape=(jax.Sh...  2.65 us
    pallas_call x1, Pallas kernels, down_rows(): pl.pallas_call(down_kernel, out_shape=[jax.ShapeDtypeStruct((size, width...  2.55 us
    pallas_call x2, Pallas kernels, combine(): pl.pallas_call(functools.partial(combine_kernel, first), out_shape=jax.Sh...  1.07 us
  transfers between devices with their start and end apart: 17, of which 8 were waited for; matrix products, arithmetic and copies ran while one was open for 0% of the time, Pallas kernels for 1%

profile of v13, /device:TPU:0, one launch (start us, length us, event | category | flops | bytes accessed | tf_op | source)
XLA Modules:
  0.0 42.4 jit_solution(12271713171560708230)
XLA Ops:
  0.7 2.7 %attend.1 = (bf16[8,4096]{1,0:T(8,128)(2,1)}, bf16[8,3072]{1,0:T(8,128)(2,1)S(1)}, bf16[8,3072]{1,0:T(8,128)(2,1)S(1)}, bf16[8,3072]{1,0:T(8,128)(2,1)S(1)}, bf1...) custom-call(bf16[8,4096]{1,0:T(8,128)(2,1)} %refs_0_.1, ...), custom_call_target="tpu_custom_call" | custom-call | tf_op jit(solution)/shard_map/attend/pallas_call | solution.py:208
  3.3 3.1 %collective-permute-start = (bf16[8,3072]{1,0:T(8,128)(2,1)S(1)}, bf16[8,3072]{1,0:T(8,128)(2,1)S(1)}, u32[]{:S(2)}, u32[]{:S(2)}) collective-permute-start(bf16[8,3072]{1,0:T(8,128)(2,1)S(1)} %get-tuple-element.27), channel_id=1, source_target_pairs={{0,4},{1,5},{2,6},{3,7},{4,0},{5,1},{6,2},{7,3},{8,12},{9,13},{10,... | collective-permute-start | bytes 147464 | tf_op jit(solution)/shard_map/ppermute | solution.py:392
  6.4 2.6 %collective-permute-start.3 = (bf16[8,3072]{1,0:T(8,128)(2,1)S(1)}, bf16[8,3072]{1,0:T(8,128)(2,1)S(1)}, u32[]{:S(2)}, u32[]{:S(2)}) collective-permute-start(bf16[8,3072]{1,0:T(8,128)(2,1)S(1)} %get-tuple-element.28), channel_id=1, source_target_pairs={{0,8},{1,9},{2,10},{3,11},{4,12},{5,13},{6,14},{7,15},{8,0},{9,1},... | collective-permute-start | bytes 147464 | tf_op jit(solution)/shard_map/ppermute | solution.py:392
  9.0 0.0 collective-permute-start.4
  9.0 0.0 collective-permute-done.refs_2_
  9.0 1.8 %collective-permute-start.1 = (bf16[16,3072]{1,0:T(8,128)(2,1)S(1)}, bf16[16,3072]{1,0:T(8,128)(2,1)S(1)}, u32[]{:S(2)}, u32[]{:S(2)}) collective-permute-start(bf16[16,3072]{1,0:T(8,128)(2,1)S(1)} %join.6.refs_1_), channel_id=1, source_target_pairs={{0,2},{1,3},{2,0},{3,1},{4,6},{5,7},{6,4},{7,5},{8,10},{9,11},{10,... | collective-permute-start | bytes 294920 | tf_op jit(solution)/shard_map/ppermute | solution.py:392
  10.8 1.5 %collective-permute-done.3.refs_1_ = bf16[8,3072]{1,0:T(8,128)(2,1)S(1)} collective-permute-done((bf16[8,3072]{1,0:T(8,128)(2,1)S(1)}, bf16[8,3072]{1,0:T(8,128)(2,1)S(1)}, u32[]{:S(2)}, u32[]{:S(2)}) %collective-permute-start.3) | collective-permute-done | bytes 49184 | tf_op jit(solution)/shard_map/ppermute | solution.py:392
  12.3 2.6 %collective-permute-done.4.refs_2_ = bf16[8,3072]{1,0:T(8,128)(2,1)S(1)} collective-permute-done((bf16[8,3072]{1,0:T(8,128)(2,1)S(1)}, bf16[8,3072]{1,0:T(8,128)(2,1)S(1)}, u32[]{:S(2)}, u32[]{:S(2)}) %collective-permute-start.4) | collective-permute-done | bytes 49184 | tf_op jit(solution)/shard_map/ppermute | solution.py:392
  14.9 1.6 %collective-permute-start.5 = (bf16[16,3072]{1,0:T(8,128)(2,1)S(1)}, bf16[16,3072]{1,0:T(8,128)(2,1)S(1)}, u32[]{:S(2)}, u32[]{:S(2)}) collective-permute-start(bf16[16,3072]{1,0:T(8,128)(2,1)S(1)} %join.9.refs_1_), channel_id=1, source_target_pairs={{0,2},{1,3},{2,0},{3,1},{4,6},{5,7},{6,4},{7,5},{8,10},{9,11},{10,... | collective-permute-start | bytes 294920 | tf_op jit(solution)/shard_map/ppermute | solution.py:392
  16.5 0.1 collective-permute-start.2
  16.6 3.0 %collective-permute-done.5.refs_2_ = bf16[16,3072]{1,0:T(8,128)(2,1)S(1)} collective-permute-done((bf16[16,3072]{1,0:T(8,128)(2,1)S(1)}, bf16[16,3072]{1,0:T(8,128)(2,1)S(1)}, u32[]{:S(2)}, u32[]{:S(2)}) %collective-permute-start.5) | collective-permute-done | bytes 98336 | tf_op jit(solution)/shard_map/ppermute | solution.py:392
  19.6 0.1 collective-permute-start.6
  19.7 1.4 %collective-permute-done.6.refs_2_ = bf16[32,3072]{1,0:T(8,128)(2,1)S(1)} collective-permute-done((bf16[32,3072]{1,0:T(8,128)(2,1)S(1)}, bf16[32,3072]{1,0:T(8,128)(2,1)S(1)}, u32[]{:S(2)}, u32[]{:S(2)}) %collective-permute-start.6) | collective-permute-done | bytes 196640 | tf_op jit(solution)/shard_map/ppermute | solution.py:392
  21.2 4.1 %hidden.1 = bf16[128,1792]{1,0:T(8,128)(2,1)S(1)} custom-call(bf16[4096,1792]{1,0:T(8,128)(2,1)S(1)} %copy-done.1, bf16[4096,1792]{1,0:T(8,128)(2,1)S(1)} %copy-done.2, bf16[1792,4096]{1,0:T(8,128)(2,1)S(1)} %copy-done, bf16[64,3072]{1,0:T(8,128)(2,1)S(1)} %join.8.refs_0_, bf16[64,3072]{1,0:T(8,128)(2,1)S(1)} %join.11.refs_1_), custom_call_target="tpu_custom_call" | custom-call | flops 3758096384 | tf_op jit(solution)/shard_map/hidden/pallas_call | solution.py:257
  25.3 2.6 %down.1 = (bf16[32,3072]{1,0:T(8,128)(2,1)S(1)}, bf16[32,3072]{1,0:T(8,128)(2,1)S(1)}, bf16[16,3072]{1,0:T(8,128)(2,1)S(1)}, bf16[16,3072]{1,0:T(8,128)(2,1)S(1)...) custom-call(bf16[128,1792]{1,0:T(8,128)(2,1)S(1)} %hidden.1, bf16[1792,4096]{1,0:T(8,128)(2,1)S(1)} %copy-done), custom_call_target="tpu_custom_call" | custom-call | flops 1879048192 | tf_op jit(solution)/shard_map/down/pallas_call | solution.py:308
  27.9 0.2 collective-permute-start.7
  28.1 0.4 collective-permute-start.9
  28.4 0.1 collective-permute-start.8
  28.6 0.9 %collective-permute-done.9.arrived = bf16[16,3072]{1,0:T(8,128)(2,1)S(1)} collective-permute-done((bf16[16,3072]{1,0:T(8,128)(2,1)S(1)}, bf16[16,3072]{1,0:T(8,128)(2,1)S(1)}, u32[]{:S(2)}, u32[]{:S(2)}) %collective-permute-start.9) | collective-permute-done | bytes 98336 | tf_op jit(solution)/shard_map/ppermute | solution.py:392
  29.5 1.6 %collective-permute-start.13 = (bf16[8,3072]{1,0:T(8,128)(2,1)S(1)}, bf16[8,3072]{1,0:T(8,128)(2,1)S(1)}, u32[]{:S(2)}, u32[]{:S(2)}) collective-permute-start(bf16[8,3072]{1,0:T(8,128)(2,1)S(1)} %get-tuple-element.43), channel_id=1, source_target_pairs={{0,2},{1,3},{2,0},{3,1},{4,6},{5,7},{6,4},{7,5},{8,10},{9,11},{10,... | collective-permute-start | bytes 147464 | tf_op jit(solution)/shard_map/ppermute | solution.py:392
  31.2 0.6 %collective-permute-start.12 = (bf16[8,3072]{1,0:T(8,128)(2,1)S(1)}, bf16[8,3072]{1,0:T(8,128)(2,1)S(1)}, u32[]{:S(2)}, u32[]{:S(2)}) collective-permute-start(bf16[8,3072]{1,0:T(8,128)(2,1)S(1)} %get-tuple-element.42), channel_id=1, source_target_pairs={{0,2},{1,3},{2,0},{3,1},{4,6},{5,7},{6,4},{7,5},{8,10},{9,11},{10,... | collective-permute-start | bytes 147464 | tf_op jit(solution)/shard_map/ppermute | solution.py:392
  31.8 1.6 %collective-permute-start.11 = (bf16[8,3072]{1,0:T(8,128)(2,1)S(1)}, bf16[8,3072]{1,0:T(8,128)(2,1)S(1)}, u32[]{:S(2)}, u32[]{:S(2)}) collective-permute-start(bf16[8,3072]{1,0:T(8,128)(2,1)S(1)} %get-tuple-element.41), channel_id=1, source_target_pairs={{0,2},{1,3},{2,0},{3,1},{4,6},{5,7},{6,4},{7,5},{8,10},{9,11},{10,... | collective-permute-start | bytes 147464 | tf_op jit(solution)/shard_map/ppermute | solution.py:392
  33.4 0.5 %collective-permute-start.10 = (bf16[8,3072]{1,0:T(8,128)(2,1)S(1)}, bf16[8,3072]{1,0:T(8,128)(2,1)S(1)}, u32[]{:S(2)}, u32[]{:S(2)}) collective-permute-start(bf16[8,3072]{1,0:T(8,128)(2,1)S(1)} %get-tuple-element.39), channel_id=1, source_target_pairs={{0,2},{1,3},{2,0},{3,1},{4,6},{5,7},{6,4},{7,5},{8,10},{9,11},{10,... | collective-permute-start | bytes 147464 | tf_op jit(solution)/shard_map/ppermute | solution.py:392
  33.9 0.0 collective-permute-done.13.arrived
  33.9 0.4 %collective-permute-start.15 = (bf16[8,3072]{1,0:T(8,128)(2,1)S(1)}, bf16[8,3072]{1,0:T(8,128)(2,1)S(1)}, u32[]{:S(2)}, u32[]{:S(2)}) collective-permute-start(bf16[8,3072]{1,0:T(8,128)(2,1)S(1)} %fold.10.after), channel_id=1, source_target_pairs={{0,8},{1,9},{2,10},{3,11},{4,12},{5,13},{6,14},{7,15},{8,0},{9,1},... | collective-permute-start | bytes 147464 | tf_op jit(solution)/shard_map/ppermute | solution.py:392
  34.3 1.0 %collective-permute-done.12.arrived = bf16[8,3072]{1,0:T(8,128)(2,1)S(1)} collective-permute-done((bf16[8,3072]{1,0:T(8,128)(2,1)S(1)}, bf16[8,3072]{1,0:T(8,128)(2,1)S(1)}, u32[]{:S(2)}, u32[]{:S(2)}) %collective-permute-start.12) | collective-permute-done | bytes 49184 | tf_op jit(solution)/shard_map/ppermute | solution.py:392
  35.4 0.8 %collective-permute-start.16 = (bf16[8,3072]{1,0:T(8,128)(2,1)S(1)}, bf16[8,3072]{1,0:T(8,128)(2,1)S(1)}, u32[]{:S(2)}, u32[]{:S(2)}) collective-permute-start(bf16[8,3072]{1,0:T(8,128)(2,1)S(1)} %fold.11.after), channel_id=1, source_target_pairs={{0,12},{1,13},{2,14},{3,15},{4,8},{5,9},{6,10},{7,11},{8,4},{9,5},... | collective-permute-start | bytes 147464 | tf_op jit(solution)/shard_map/ppermute | solution.py:392
  36.2 0.2 collective-permute-done.11.arrived
  36.4 1.2 %collective-permute-start.14 = (bf16[8,3072]{1,0:T(8,128)(2,1)S(1)}, bf16[8,3072]{1,0:T(8,128)(2,1)S(1)}, u32[]{:S(2)}, u32[]{:S(2)}) collective-permute-start(bf16[8,3072]{1,0:T(8,128)(2,1)S(1)} %fold.12.after), channel_id=1, source_target_pairs={{0,4},{1,5},{2,6},{3,7},{4,0},{5,1},{6,2},{7,3},{8,12},{9,13},{10,... | collective-permute-start | bytes 147464 | tf_op jit(solution)/shard_map/ppermute | solution.py:392
  37.6 3.7 %collective-permute-done.16.refs_1_ = bf16[8,3072]{1,0:T(8,128)(2,1)S(1)} collective-permute-done((bf16[8,3072]{1,0:T(8,128)(2,1)S(1)}, bf16[8,3072]{1,0:T(8,128)(2,1)S(1)}, u32[]{:S(2)}, u32[]{:S(2)}) %collective-permute-start.16) | collective-permute-done | bytes 49184 | tf_op jit(solution)/shard_map/ppermute | solution.py:392
  41.3 0.2 combine.2.refs_2_
  41.6 0.8 %combine.3 = bf16[8,4096]{1,0:T(8,128)(2,1)} custom-call(f32[16,128]{1,0:T(8,128)S(1)} %get-tuple-element.24.refs_0_.after.share, bf16[4,16,128]{2,1,0:T(8,128)(2,1)S(1)} %get-tuple-element.25.take, bf16[8,3072]{1,0:T(8,128)(2,1)S(1)} %fold.13.refs_0_, bf16[8,3072]{1,0:T(8,128)(2,1)S(1)} %collective-permute-done.14.refs_1_, f32[8,4096]{1,0:T(8,128)S(1)} %combine.2.refs_2_), custom_call_target="tpu_custom_call" | custom-call | bytes 16777216 | tf_op jit(solution)/shard_map/combine/pallas_call | solution.py:380
  (26 shorter events, 0.3 us)
Async XLA Ops:
  0.6 20.5 %copy-start = (bf16[1792,4096]{1,0:T(8,128)(2,1)S(1)}, bf16[1792,4096]{1,0:T(8,128)(2,1)}, u32[]{:S(2)}) copy-start(bf16[1792,4096]{1,0:T(8,128)(2,1)} %weight.1) | copy-start | bytes 44040196
  0.6 20.5 %copy-start.1 = (bf16[4096,1792]{1,0:T(8,128)(2,1)S(1)}, bf16[4096,1792]{1,0:T(8,128)(2,1)}, u32[]{:S(2)}) copy-start(bf16[4096,1792]{1,0:T(8,128)(2,1)} %gate_weight.1) | copy-start | bytes 44040196
  0.7 20.5 %copy-start.2 = (bf16[4096,1792]{1,0:T(8,128)(2,1)S(1)}, bf16[4096,1792]{1,0:T(8,128)(2,1)}, u32[]{:S(2)}) copy-start(bf16[4096,1792]{1,0:T(8,128)(2,1)} %up_weight.1) | copy-start | bytes 44040196
  3.3 5.7 %collective-permute-start = (bf16[8,3072]{1,0:T(8,128)(2,1)S(1)}, bf16[8,3072]{1,0:T(8,128)(2,1)S(1)}, u32[]{:S(2)}, u32[]{:S(2)}) collective-permute-start(bf16[8,3072]{1,0:T(8,128)(2,1)S(1)} %get-tuple-element.27), channel_id=1, source_target_pairs={{0,4},{1,5},{2,6},{3,7},{4,0},{5,1},{6,2},{7,3},{8,12},{9,13},{10,... | collective-permute-start | bytes 147464 | tf_op jit(solution)/shard_map/ppermute | solution.py:392
  6.4 5.9 %collective-permute-start.3 = (bf16[8,3072]{1,0:T(8,128)(2,1)S(1)}, bf16[8,3072]{1,0:T(8,128)(2,1)S(1)}, u32[]{:S(2)}, u32[]{:S(2)}) collective-permute-start(bf16[8,3072]{1,0:T(8,128)(2,1)S(1)} %get-tuple-element.28), channel_id=1, source_target_pairs={{0,8},{1,9},{2,10},{3,11},{4,12},{5,13},{6,14},{7,15},{8,0},{9,1},... | collective-permute-start | bytes 147464 | tf_op jit(solution)/shard_map/ppermute | solution.py:392
  9.0 5.9 %collective-permute-start.4 = (bf16[8,3072]{1,0:T(8,128)(2,1)S(1)}, bf16[8,3072]{1,0:T(8,128)(2,1)S(1)}, u32[]{:S(2)}, u32[]{:S(2)}) collective-permute-start(bf16[8,3072]{1,0:T(8,128)(2,1)S(1)} %get-tuple-element.29), channel_id=1, source_target_pairs={{0,12},{1,13},{2,14},{3,15},{4,8},{5,9},{6,10},{7,11},{8,4},{9,5},... | collective-permute-start | bytes 147464 | tf_op jit(solution)/shard_map/ppermute | solution.py:392
  9.0 7.5 %collective-permute-start.1 = (bf16[16,3072]{1,0:T(8,128)(2,1)S(1)}, bf16[16,3072]{1,0:T(8,128)(2,1)S(1)}, u32[]{:S(2)}, u32[]{:S(2)}) collective-permute-start(bf16[16,3072]{1,0:T(8,128)(2,1)S(1)} %join.6.refs_1_), channel_id=1, source_target_pairs={{0,2},{1,3},{2,0},{3,1},{4,6},{5,7},{6,4},{7,5},{8,10},{9,11},{10,... | collective-permute-start | bytes 294920 | tf_op jit(solution)/shard_map/ppermute | solution.py:392
  14.9 4.7 %collective-permute-start.5 = (bf16[16,3072]{1,0:T(8,128)(2,1)S(1)}, bf16[16,3072]{1,0:T(8,128)(2,1)S(1)}, u32[]{:S(2)}, u32[]{:S(2)}) collective-permute-start(bf16[16,3072]{1,0:T(8,128)(2,1)S(1)} %join.9.refs_1_), channel_id=1, source_target_pairs={{0,2},{1,3},{2,0},{3,1},{4,6},{5,7},{6,4},{7,5},{8,10},{9,11},{10,... | collective-permute-start | bytes 294920 | tf_op jit(solution)/shard_map/ppermute | solution.py:392
  16.5 3.2 %collective-permute-start.2 = (bf16[32,3072]{1,0:T(8,128)(2,1)S(1)}, bf16[32,3072]{1,0:T(8,128)(2,1)S(1)}, u32[]{:S(2)}, u32[]{:S(2)}) collective-permute-start(bf16[32,3072]{1,0:T(8,128)(2,1)S(1)} %join.7.refs_1_), channel_id=1, source_target_pairs={{0,1},{1,0},{2,3},{3,2},{4,5},{5,4},{6,7},{7,6},{8,9},{9,8},{10,11... | collective-permute-start | bytes 589832 | tf_op jit(solution)/shard_map/ppermute | solution.py:392
  19.6 1.5 %collective-permute-start.6 = (bf16[32,3072]{1,0:T(8,128)(2,1)S(1)}, bf16[32,3072]{1,0:T(8,128)(2,1)S(1)}, u32[]{:S(2)}, u32[]{:S(2)}) collective-permute-start(bf16[32,3072]{1,0:T(8,128)(2,1)S(1)} %join.10.refs_1_), channel_id=1, source_target_pairs={{0,1},{1,0},{2,3},{3,2},{4,5},{5,4},{6,7},{7,6},{8,9},{9,8},{10,11... | collective-permute-start | bytes 589832 | tf_op jit(solution)/shard_map/ppermute | solution.py:392
  27.9 3.9 %collective-permute-start.7 = (bf16[32,3072]{1,0:T(8,128)(2,1)S(1)}, bf16[32,3072]{1,0:T(8,128)(2,1)S(1)}, u32[]{:S(2)}, u32[]{:S(2)}) collective-permute-start(bf16[32,3072]{1,0:T(8,128)(2,1)S(1)} %get-tuple-element.31), channel_id=1, source_target_pairs={{0,1},{1,0},{2,3},{3,2},{4,5},{5,4},{6,7},{7,6},{8,9},{9,8},{10,11... | collective-permute-start | bytes 589832 | tf_op jit(solution)/shard_map/ppermute | solution.py:392
  28.1 1.4 %collective-permute-start.9 = (bf16[16,3072]{1,0:T(8,128)(2,1)S(1)}, bf16[16,3072]{1,0:T(8,128)(2,1)S(1)}, u32[]{:S(2)}, u32[]{:S(2)}) collective-permute-start(bf16[16,3072]{1,0:T(8,128)(2,1)S(1)} %get-tuple-element.35), channel_id=1, source_target_pairs={{0,1},{1,0},{2,3},{3,2},{4,5},{5,4},{6,7},{7,6},{8,9},{9,8},{10,11... | collective-permute-start | bytes 294920 | tf_op jit(solution)/shard_map/ppermute | solution.py:392
  28.4 2.7 %collective-permute-start.8 = (bf16[16,3072]{1,0:T(8,128)(2,1)S(1)}, bf16[16,3072]{1,0:T(8,128)(2,1)S(1)}, u32[]{:S(2)}, u32[]{:S(2)}) collective-permute-start(bf16[16,3072]{1,0:T(8,128)(2,1)S(1)} %get-tuple-element.33), channel_id=1, source_target_pairs={{0,1},{1,0},{2,3},{3,2},{4,5},{5,4},{6,7},{7,6},{8,9},{9,8},{10,11... | collective-permute-start | bytes 294920 | tf_op jit(solution)/shard_map/ppermute | solution.py:392
  29.5 4.3 %collective-permute-start.13 = (bf16[8,3072]{1,0:T(8,128)(2,1)S(1)}, bf16[8,3072]{1,0:T(8,128)(2,1)S(1)}, u32[]{:S(2)}, u32[]{:S(2)}) collective-permute-start(bf16[8,3072]{1,0:T(8,128)(2,1)S(1)} %get-tuple-element.43), channel_id=1, source_target_pairs={{0,2},{1,3},{2,0},{3,1},{4,6},{5,7},{6,4},{7,5},{8,10},{9,11},{10,... | collective-permute-start | bytes 147464 | tf_op jit(solution)/shard_map/ppermute | solution.py:392
  31.2 4.2 %collective-permute-start.12 = (bf16[8,3072]{1,0:T(8,128)(2,1)S(1)}, bf16[8,3072]{1,0:T(8,128)(2,1)S(1)}, u32[]{:S(2)}, u32[]{:S(2)}) collective-permute-start(bf16[8,3072]{1,0:T(8,128)(2,1)S(1)} %get-tuple-element.42), channel_id=1, source_target_pairs={{0,2},{1,3},{2,0},{3,1},{4,6},{5,7},{6,4},{7,5},{8,10},{9,11},{10,... | collective-permute-start | bytes 147464 | tf_op jit(solution)/shard_map/ppermute | solution.py:392
  31.8 4.6 %collective-permute-start.11 = (bf16[8,3072]{1,0:T(8,128)(2,1)S(1)}, bf16[8,3072]{1,0:T(8,128)(2,1)S(1)}, u32[]{:S(2)}, u32[]{:S(2)}) collective-permute-start(bf16[8,3072]{1,0:T(8,128)(2,1)S(1)} %get-tuple-element.41), channel_id=1, source_target_pairs={{0,2},{1,3},{2,0},{3,1},{4,6},{5,7},{6,4},{7,5},{8,10},{9,11},{10,... | collective-permute-start | bytes 147464 | tf_op jit(solution)/shard_map/ppermute | solution.py:392
  33.4 4.3 %collective-permute-start.10 = (bf16[8,3072]{1,0:T(8,128)(2,1)S(1)}, bf16[8,3072]{1,0:T(8,128)(2,1)S(1)}, u32[]{:S(2)}, u32[]{:S(2)}) collective-permute-start(bf16[8,3072]{1,0:T(8,128)(2,1)S(1)} %get-tuple-element.39), channel_id=1, source_target_pairs={{0,2},{1,3},{2,0},{3,1},{4,6},{5,7},{6,4},{7,5},{8,10},{9,11},{10,... | collective-permute-start | bytes 147464 | tf_op jit(solution)/shard_map/ppermute | solution.py:392
  33.9 7.4 %collective-permute-start.15 = (bf16[8,3072]{1,0:T(8,128)(2,1)S(1)}, bf16[8,3072]{1,0:T(8,128)(2,1)S(1)}, u32[]{:S(2)}, u32[]{:S(2)}) collective-permute-start(bf16[8,3072]{1,0:T(8,128)(2,1)S(1)} %fold.10.after), channel_id=1, source_target_pairs={{0,8},{1,9},{2,10},{3,11},{4,12},{5,13},{6,14},{7,15},{8,0},{9,1},... | collective-permute-start | bytes 147464 | tf_op jit(solution)/shard_map/ppermute | solution.py:392
  35.4 6.0 %collective-permute-start.16 = (bf16[8,3072]{1,0:T(8,128)(2,1)S(1)}, bf16[8,3072]{1,0:T(8,128)(2,1)S(1)}, u32[]{:S(2)}, u32[]{:S(2)}) collective-permute-start(bf16[8,3072]{1,0:T(8,128)(2,1)S(1)} %fold.11.after), channel_id=1, source_target_pairs={{0,12},{1,13},{2,14},{3,15},{4,8},{5,9},{6,10},{7,11},{8,4},{9,5},... | collective-permute-start | bytes 147464 | tf_op jit(solution)/shard_map/ppermute | solution.py:392
  36.4 5.2 %collective-permute-start.14 = (bf16[8,3072]{1,0:T(8,128)(2,1)S(1)}, bf16[8,3072]{1,0:T(8,128)(2,1)S(1)}, u32[]{:S(2)}, u32[]{:S(2)}) collective-permute-start(bf16[8,3072]{1,0:T(8,128)(2,1)S(1)} %fold.12.after), channel_id=1, source_target_pairs={{0,4},{1,5},{2,6},{3,7},{4,0},{5,1},{6,2},{7,3},{8,12},{9,13},{10,... | collective-permute-start | bytes 147464 | tf_op jit(solution)/shard_map/ppermute | solution.py:392

commit v14 on v13

--- a/solution.py
+++ b/solution.py
@@ -433,9 +433,10 @@
         two = back(two, stage, token)
         three = back(three, stage, two[0])
         token = three[0]
-        near = back(near, stage, token, 4 if stage == last - 1 else 2)
-    two = back(two, last, near[0], 1)
-    three = back(three, last, two[0], 1)
+    two = back(two, last, token, 1)
+    for stage in range(last):
+        near = back(near, stage, two[0], 4 if stage == last - 1 else 2)
+    three = back(three, last, near[0], 1)
     one = back(near[2:4], last, three[0], 1)
     zero = back(near[0:2], last, one[0], 1)
     results = [

time: 42.6 us -> 43.6 us (1.023)
  starting transfers between devices: 16.6 us -> 17.4 us
    ppermute x17, starting transfers between devices: 16.6 us -> 17.4 us  [swap(): return lax.ppermute(value, 'dp', [(i, i ^ bit) for i in range(count)])]
  transfers between devices with their start and end apart: 17 -> 17, of which waited for: 8 -> 11; matrix products, arithmetic and copies ran while one was open for 0% -> 0% of each run, Pallas kernels for 1% -> 1%
where the time goes in v14:
time: 43.6 us; the launch traced here: 43.4 us
  starting transfers between devices  17.4 us (40%)
  waiting for transfers between devices  14.6 us (33%)
  Pallas kernels  10.7 us (25%)
  between operations  0.81 us (2%)
    ppermute x17, starting transfers between devices, swap(): return lax.ppermute(value, 'dp', [(i, i ^ bit) for i in range(count)])  17.4 us
    ppermute x17, waiting for transfers between devices, swap(): return lax.ppermute(value, 'dp', [(i, i ^ bit) for i in range(count)])  14.6 us
    pallas_call x1, Pallas kernels, hidden_rows(): pl.pallas_call(hidden_kernel, out_shape=jax.ShapeDtypeStruct((rows, colum...  4.13 us
    pallas_call x1, Pallas kernels, attend(): pl.pallas_call(functools.partial(attend_kernel, plane), out_shape=(jax.Sh...  2.65 us
    pallas_call x1, Pallas kernels, down_rows(): pl.pallas_call(down_kernel, out_shape=[jax.ShapeDtypeStruct((size, width...  2.55 us
    pallas_call x2, Pallas kernels, combine(): pl.pallas_call(functools.partial(combine_kernel, first), out_shape=jax.Sh...  1.06 us
  transfers between devices with their start and end apart: 17, of which 11 were waited for; matrix products, arithmetic and copies ran while one was open for 0% of the time, Pallas kernels for 1%

profile of v14, /device:TPU:0, one launch (start us, length us, event | category | flops | bytes accessed | tf_op | source)
XLA Modules:
  0.0 43.4 jit_solution(9398376798145553212)
XLA Ops:
  0.7 2.7 %attend.1 = (bf16[8,4096]{1,0:T(8,128)(2,1)}, bf16[8,3072]{1,0:T(8,128)(2,1)S(1)}, bf16[8,3072]{1,0:T(8,128)(2,1)S(1)}, bf16[8,3072]{1,0:T(8,128)(2,1)S(1)}, bf1...) custom-call(bf16[8,4096]{1,0:T(8,128)(2,1)} %refs_0_.1, ...), custom_call_target="tpu_custom_call" | custom-call | tf_op jit(solution)/shard_map/attend/pallas_call | solution.py:208
  3.3 3.1 %collective-permute-start = (bf16[8,3072]{1,0:T(8,128)(2,1)S(1)}, bf16[8,3072]{1,0:T(8,128)(2,1)S(1)}, u32[]{:S(2)}, u32[]{:S(2)}) collective-permute-start(bf16[8,3072]{1,0:T(8,128)(2,1)S(1)} %get-tuple-element.27), channel_id=1, source_target_pairs={{0,4},{1,5},{2,6},{3,7},{4,0},{5,1},{6,2},{7,3},{8,12},{9,13},{10,... | collective-permute-start | bytes 147464 | tf_op jit(solution)/shard_map/ppermute | solution.py:392
  6.4 2.6 %collective-permute-start.3 = (bf16[8,3072]{1,0:T(8,128)(2,1)S(1)}, bf16[8,3072]{1,0:T(8,128)(2,1)S(1)}, u32[]{:S(2)}, u32[]{:S(2)}) collective-permute-start(bf16[8,3072]{1,0:T(8,128)(2,1)S(1)} %get-tuple-element.28), channel_id=1, source_target_pairs={{0,8},{1,9},{2,10},{3,11},{4,12},{5,13},{6,14},{7,15},{8,0},{9,1},... | collective-permute-start | bytes 147464 | tf_op jit(solution)/shard_map/ppermute | solution.py:392
  9.0 1.8 %collective-permute-start.1 = (bf16[16,3072]{1,0:T(8,128)(2,1)S(1)}, bf16[16,3072]{1,0:T(8,128)(2,1)S(1)}, u32[]{:S(2)}, u32[]{:S(2)}) collective-permute-start(bf16[16,3072]{1,0:T(8,128)(2,1)S(1)} %join.6.refs_1_), channel_id=1, source_target_pairs={{0,2},{1,3},{2,0},{3,1},{4,6},{5,7},{6,4},{7,5},{8,10},{9,11},{10,... | collective-permute-start | bytes 294920 | tf_op jit(solution)/shard_map/ppermute | solution.py:392
  10.8 1.5 %collective-permute-done.3.refs_1_ = bf16[8,3072]{1,0:T(8,128)(2,1)S(1)} collective-permute-done((bf16[8,3072]{1,0:T(8,128)(2,1)S(1)}, bf16[8,3072]{1,0:T(8,128)(2,1)S(1)}, u32[]{:S(2)}, u32[]{:S(2)}) %collective-permute-start.3) | collective-permute-done | bytes 49184 | tf_op jit(solution)/shard_map/ppermute | solution.py:392
  12.3 2.6 %collective-permute-done.4.refs_2_ = bf16[8,3072]{1,0:T(8,128)(2,1)S(1)} collective-permute-done((bf16[8,3072]{1,0:T(8,128)(2,1)S(1)}, bf16[8,3072]{1,0:T(8,128)(2,1)S(1)}, u32[]{:S(2)}, u32[]{:S(2)}) %collective-permute-start.4) | collective-permute-done | bytes 49184 | tf_op jit(solution)/shard_map/ppermute | solution.py:392
  14.9 1.6 %collective-permute-start.5 = (bf16[16,3072]{1,0:T(8,128)(2,1)S(1)}, bf16[16,3072]{1,0:T(8,128)(2,1)S(1)}, u32[]{:S(2)}, u32[]{:S(2)}) collective-permute-start(bf16[16,3072]{1,0:T(8,128)(2,1)S(1)} %join.9.refs_1_), channel_id=1, source_target_pairs={{0,2},{1,3},{2,0},{3,1},{4,6},{5,7},{6,4},{7,5},{8,10},{9,11},{10,... | collective-permute-start | bytes 294920 | tf_op jit(solution)/shard_map/ppermute | solution.py:392
  16.5 0.1 collective-permute-start.2
  16.6 3.0 %collective-permute-done.5.refs_2_ = bf16[16,3072]{1,0:T(8,128)(2,1)S(1)} collective-permute-done((bf16[16,3072]{1,0:T(8,128)(2,1)S(1)}, bf16[16,3072]{1,0:T(8,128)(2,1)S(1)}, u32[]{:S(2)}, u32[]{:S(2)}) %collective-permute-start.5) | collective-permute-done | bytes 98336 | tf_op jit(solution)/shard_map/ppermute | solution.py:392
  19.6 0.1 collective-permute-start.6
  19.7 1.4 %collective-permute-done.6.refs_2_ = bf16[32,3072]{1,0:T(8,128)(2,1)S(1)} collective-permute-done((bf16[32,3072]{1,0:T(8,128)(2,1)S(1)}, bf16[32,3072]{1,0:T(8,128)(2,1)S(1)}, u32[]{:S(2)}, u32[]{:S(2)}) %collective-permute-start.6) | collective-permute-done | bytes 196640 | tf_op jit(solution)/shard_map/ppermute | solution.py:392
  21.2 4.1 %hidden.1 = bf16[128,1792]{1,0:T(8,128)(2,1)S(1)} custom-call(bf16[4096,1792]{1,0:T(8,128)(2,1)S(1)} %copy-done.1, bf16[4096,1792]{1,0:T(8,128)(2,1)S(1)} %copy-done.2, bf16[1792,4096]{1,0:T(8,128)(2,1)S(1)} %copy-done, bf16[64,3072]{1,0:T(8,128)(2,1)S(1)} %join.8.refs_0_, bf16[64,3072]{1,0:T(8,128)(2,1)S(1)} %join.11.refs_1_), custom_call_target="tpu_custom_call" | custom-call | flops 3758096384 | tf_op jit(solution)/shard_map/hidden/pallas_call | solution.py:257
  25.3 2.6 %down.1 = (bf16[32,3072]{1,0:T(8,128)(2,1)S(1)}, bf16[32,3072]{1,0:T(8,128)(2,1)S(1)}, bf16[16,3072]{1,0:T(8,128)(2,1)S(1)}, bf16[16,3072]{1,0:T(8,128)(2,1)S(1)...) custom-call(bf16[128,1792]{1,0:T(8,128)(2,1)S(1)} %hidden.1, bf16[1792,4096]{1,0:T(8,128)(2,1)S(1)} %copy-done), custom_call_target="tpu_custom_call" | custom-call | flops 1879048192 | tf_op jit(solution)/shard_map/down/pallas_call | solution.py:308
  27.9 0.2 collective-permute-start.7
  28.1 0.4 collective-permute-start.8
  28.4 0.1 collective-permute-start.10
  28.6 0.9 %collective-permute-done.8.arrived = bf16[16,3072]{1,0:T(8,128)(2,1)S(1)} collective-permute-done((bf16[16,3072]{1,0:T(8,128)(2,1)S(1)}, bf16[16,3072]{1,0:T(8,128)(2,1)S(1)}, u32[]{:S(2)}, u32[]{:S(2)}) %collective-permute-start.8) | collective-permute-done | bytes 98336 | tf_op jit(solution)/shard_map/ppermute | solution.py:392
  29.5 1.6 %collective-permute-start.9 = (bf16[8,3072]{1,0:T(8,128)(2,1)S(1)}, bf16[8,3072]{1,0:T(8,128)(2,1)S(1)}, u32[]{:S(2)}, u32[]{:S(2)}) collective-permute-start(bf16[8,3072]{1,0:T(8,128)(2,1)S(1)} %get-tuple-element.35), channel_id=1, source_target_pairs={{0,2},{1,3},{2,0},{3,1},{4,6},{5,7},{6,4},{7,5},{8,10},{9,11},{10,... | collective-permute-start | bytes 147464 | tf_op jit(solution)/shard_map/ppermute | solution.py:392
  31.2 0.6 %collective-permute-start.13 = (bf16[8,3072]{1,0:T(8,128)(2,1)S(1)}, bf16[8,3072]{1,0:T(8,128)(2,1)S(1)}, u32[]{:S(2)}, u32[]{:S(2)}) collective-permute-start(bf16[8,3072]{1,0:T(8,128)(2,1)S(1)} %get-tuple-element.43), channel_id=1, source_target_pairs={{0,2},{1,3},{2,0},{3,1},{4,6},{5,7},{6,4},{7,5},{8,10},{9,11},{10,... | collective-permute-start | bytes 147464 | tf_op jit(solution)/shard_map/ppermute | solution.py:392
  31.7 2.0 %collective-permute-done.9.arrived = bf16[8,3072]{1,0:T(8,128)(2,1)S(1)} collective-permute-done((bf16[8,3072]{1,0:T(8,128)(2,1)S(1)}, bf16[8,3072]{1,0:T(8,128)(2,1)S(1)}, u32[]{:S(2)}, u32[]{:S(2)}) %collective-permute-start.9) | collective-permute-done | bytes 49184 | tf_op jit(solution)/shard_map/ppermute | solution.py:392
  33.8 1.9 %collective-permute-start.12 = (bf16[8,3072]{1,0:T(8,128)(2,1)S(1)}, bf16[8,3072]{1,0:T(8,128)(2,1)S(1)}, u32[]{:S(2)}, u32[]{:S(2)}) collective-permute-start(bf16[8,3072]{1,0:T(8,128)(2,1)S(1)} %get-tuple-element.42), channel_id=1, source_target_pairs={{0,2},{1,3},{2,0},{3,1},{4,6},{5,7},{6,4},{7,5},{8,10},{9,11},{10,... | collective-permute-start | bytes 147464 | tf_op jit(solution)/shard_map/ppermute | solution.py:392
  35.7 0.4 collective-permute-start.15
  36.0 0.2 collective-permute-start.11
  36.3 1.2 %collective-permute-start.16 = (bf16[8,3072]{1,0:T(8,128)(2,1)S(1)}, bf16[8,3072]{1,0:T(8,128)(2,1)S(1)}, u32[]{:S(2)}, u32[]{:S(2)}) collective-permute-start(bf16[8,3072]{1,0:T(8,128)(2,1)S(1)} %fold.11.after), channel_id=1, source_target_pairs={{0,12},{1,13},{2,14},{3,15},{4,8},{5,9},{6,10},{7,11},{8,4},{9,5},... | collective-permute-start | bytes 147464 | tf_op jit(solution)/shard_map/ppermute | solution.py:392
  37.5 0.4 collective-permute-done.12.arrived
  38.0 1.6 %collective-permute-start.14 = (bf16[8,3072]{1,0:T(8,128)(2,1)S(1)}, bf16[8,3072]{1,0:T(8,128)(2,1)S(1)}, u32[]{:S(2)}, u32[]{:S(2)}) collective-permute-start(bf16[8,3072]{1,0:T(8,128)(2,1)S(1)} %fold.12.after), channel_id=1, source_target_pairs={{0,4},{1,5},{2,6},{3,7},{4,0},{5,1},{6,2},{7,3},{8,12},{9,13},{10,... | collective-permute-start | bytes 147464 | tf_op jit(solution)/shard_map/ppermute | solution.py:392
  39.5 0.6 %collective-permute-done.11.arrived = bf16[8,3072]{1,0:T(8,128)(2,1)S(1)} collective-permute-done((bf16[8,3072]{1,0:T(8,128)(2,1)S(1)}, bf16[8,3072]{1,0:T(8,128)(2,1)S(1)}, u32[]{:S(2)}, u32[]{:S(2)}) %collective-permute-start.11) | collective-permute-done | bytes 49184 | tf_op jit(solution)/shard_map/ppermute | solution.py:392
  40.1 0.5 %collective-permute-done.15.refs_0_ = bf16[8,3072]{1,0:T(8,128)(2,1)S(1)} collective-permute-done((bf16[8,3072]{1,0:T(8,128)(2,1)S(1)}, bf16[8,3072]{1,0:T(8,128)(2,1)S(1)}, u32[]{:S(2)}, u32[]{:S(2)}) %collective-permute-start.15) | collective-permute-done | bytes 49184 | tf_op jit(solution)/shard_map/ppermute | solution.py:392
  40.7 1.6 %collective-permute-done.16.refs_1_ = bf16[8,3072]{1,0:T(8,128)(2,1)S(1)} collective-permute-done((bf16[8,3072]{1,0:T(8,128)(2,1)S(1)}, bf16[8,3072]{1,0:T(8,128)(2,1)S(1)}, u32[]{:S(2)}, u32[]{:S(2)}) %collective-permute-start.16) | collective-permute-done | bytes 49184 | tf_op jit(solution)/shard_map/ppermute | solution.py:392
  42.3 0.2 combine.2.refs_2_
  42.6 0.1 collective-permute-done.14.refs_1_
  42.6 0.8 %combine.3 = bf16[8,4096]{1,0:T(8,128)(2,1)} custom-call(f32[16,128]{1,0:T(8,128)S(1)} %get-tuple-element.24.refs_0_.after.share, bf16[4,16,128]{2,1,0:T(8,128)(2,1)S(1)} %get-tuple-element.25.take, bf16[8,3072]{1,0:T(8,128)(2,1)S(1)} %fold.13.refs_0_, bf16[8,3072]{1,0:T(8,128)(2,1)S(1)} %collective-permute-done.14.refs_1_, f32[8,4096]{1,0:T(8,128)S(1)} %combine.2.refs_2_), custom_call_target="tpu_custom_call" | custom-call | bytes 16777216 | tf_op jit(solution)/shard_map/combine/pallas_call | solution.py:380
  (26 shorter events, 0.3 us)
Async XLA Ops:
  0.6 20.5 %copy-start = (bf16[1792,4096]{1,0:T(8,128)(2,1)S(1)}, bf16[1792,4096]{1,0:T(8,128)(2,1)}, u32[]{:S(2)}) copy-start(bf16[1792,4096]{1,0:T(8,128)(2,1)} %weight.1) | copy-start | bytes 44040196
  0.6 20.5 %copy-start.1 = (bf16[4096,1792]{1,0:T(8,128)(2,1)S(1)}, bf16[4096,1792]{1,0:T(8,128)(2,1)}, u32[]{:S(2)}) copy-start(bf16[4096,1792]{1,0:T(8,128)(2,1)} %gate_weight.1) | copy-start | bytes 44040196
  0.7 20.5 %copy-start.2 = (bf16[4096,1792]{1,0:T(8,128)(2,1)S(1)}, bf16[4096,1792]{1,0:T(8,128)(2,1)}, u32[]{:S(2)}) copy-start(bf16[4096,1792]{1,0:T(8,128)(2,1)} %up_weight.1) | copy-start | bytes 44040196
  3.3 5.7 %collective-permute-start = (bf16[8,3072]{1,0:T(8,128)(2,1)S(1)}, bf16[8,3072]{1,0:T(8,128)(2,1)S(1)}, u32[]{:S(2)}, u32[]{:S(2)}) collective-permute-start(bf16[8,3072]{1,0:T(8,128)(2,1)S(1)} %get-tuple-element.27), channel_id=1, source_target_pairs={{0,4},{1,5},{2,6},{3,7},{4,0},{5,1},{6,2},{7,3},{8,12},{9,13},{10,... | collective-permute-start | bytes 147464 | tf_op jit(solution)/shard_map/ppermute | solution.py:392
  6.4 5.9 %collective-permute-start.3 = (bf16[8,3072]{1,0:T(8,128)(2,1)S(1)}, bf16[8,3072]{1,0:T(8,128)(2,1)S(1)}, u32[]{:S(2)}, u32[]{:S(2)}) collective-permute-start(bf16[8,3072]{1,0:T(8,128)(2,1)S(1)} %get-tuple-element.28), channel_id=1, source_target_pairs={{0,8},{1,9},{2,10},{3,11},{4,12},{5,13},{6,14},{7,15},{8,0},{9,1},... | collective-permute-start | bytes 147464 | tf_op jit(solution)/shard_map/ppermute | solution.py:392
  9.0 5.9 %collective-permute-start.4 = (bf16[8,3072]{1,0:T(8,128)(2,1)S(1)}, bf16[8,3072]{1,0:T(8,128)(2,1)S(1)}, u32[]{:S(2)}, u32[]{:S(2)}) collective-permute-start(bf16[8,3072]{1,0:T(8,128)(2,1)S(1)} %get-tuple-element.29), channel_id=1, source_target_pairs={{0,12},{1,13},{2,14},{3,15},{4,8},{5,9},{6,10},{7,11},{8,4},{9,5},... | collective-permute-start | bytes 147464 | tf_op jit(solution)/shard_map/ppermute | solution.py:392
  9.0 7.5 %collective-permute-start.1 = (bf16[16,3072]{1,0:T(8,128)(2,1)S(1)}, bf16[16,3072]{1,0:T(8,128)(2,1)S(1)}, u32[]{:S(2)}, u32[]{:S(2)}) collective-permute-start(bf16[16,3072]{1,0:T(8,128)(2,1)S(1)} %join.6.refs_1_), channel_id=1, source_target_pairs={{0,2},{1,3},{2,0},{3,1},{4,6},{5,7},{6,4},{7,5},{8,10},{9,11},{10,... | collective-permute-start | bytes 294920 | tf_op jit(solution)/shard_map/ppermute | solution.py:392
  14.9 4.7 %collective-permute-start.5 = (bf16[16,3072]{1,0:T(8,128)(2,1)S(1)}, bf16[16,3072]{1,0:T(8,128)(2,1)S(1)}, u32[]{:S(2)}, u32[]{:S(2)}) collective-permute-start(bf16[16,3072]{1,0:T(8,128)(2,1)S(1)} %join.9.refs_1_), channel_id=1, source_target_pairs={{0,2},{1,3},{2,0},{3,1},{4,6},{5,7},{6,4},{7,5},{8,10},{9,11},{10,... | collective-permute-start | bytes 294920 | tf_op jit(solution)/shard_map/ppermute | solution.py:392
  16.5 3.2 %collective-permute-start.2 = (bf16[32,3072]{1,0:T(8,128)(2,1)S(1)}, bf16[32,3072]{1,0:T(8,128)(2,1)S(1)}, u32[]{:S(2)}, u32[]{:S(2)}) collective-permute-start(bf16[32,3072]{1,0:T(8,128)(2,1)S(1)} %join.7.refs_1_), channel_id=1, source_target_pairs={{0,1},{1,0},{2,3},{3,2},{4,5},{5,4},{6,7},{7,6},{8,9},{9,8},{10,11... | collective-permute-start | bytes 589832 | tf_op jit(solution)/shard_map/ppermute | solution.py:392
  19.6 1.5 %collective-permute-start.6 = (bf16[32,3072]{1,0:T(8,128)(2,1)S(1)}, bf16[32,3072]{1,0:T(8,128)(2,1)S(1)}, u32[]{:S(2)}, u32[]{:S(2)}) collective-permute-start(bf16[32,3072]{1,0:T(8,128)(2,1)S(1)} %join.10.refs_1_), channel_id=1, source_target_pairs={{0,1},{1,0},{2,3},{3,2},{4,5},{5,4},{6,7},{7,6},{8,9},{9,8},{10,11... | collective-permute-start | bytes 589832 | tf_op jit(solution)/shard_map/ppermute | solution.py:392
  27.9 5.9 %collective-permute-start.7 = (bf16[32,3072]{1,0:T(8,128)(2,1)S(1)}, bf16[32,3072]{1,0:T(8,128)(2,1)S(1)}, u32[]{:S(2)}, u32[]{:S(2)}) collective-permute-start(bf16[32,3072]{1,0:T(8,128)(2,1)S(1)} %get-tuple-element.31), channel_id=1, source_target_pairs={{0,1},{1,0},{2,3},{3,2},{4,5},{5,4},{6,7},{7,6},{8,9},{9,8},{10,11... | collective-permute-start | bytes 589832 | tf_op jit(solution)/shard_map/ppermute | solution.py:392
  28.1 1.4 %collective-permute-start.8 = (bf16[16,3072]{1,0:T(8,128)(2,1)S(1)}, bf16[16,3072]{1,0:T(8,128)(2,1)S(1)}, u32[]{:S(2)}, u32[]{:S(2)}) collective-permute-start(bf16[16,3072]{1,0:T(8,128)(2,1)S(1)} %get-tuple-element.33), channel_id=1, source_target_pairs={{0,1},{1,0},{2,3},{3,2},{4,5},{5,4},{6,7},{7,6},{8,9},{9,8},{10,11... | collective-permute-start | bytes 294920 | tf_op jit(solution)/shard_map/ppermute | solution.py:392
  28.4 2.7 %collective-permute-start.10 = (bf16[16,3072]{1,0:T(8,128)(2,1)S(1)}, bf16[16,3072]{1,0:T(8,128)(2,1)S(1)}, u32[]{:S(2)}, u32[]{:S(2)}) collective-permute-start(bf16[16,3072]{1,0:T(8,128)(2,1)S(1)} %get-tuple-element.37), channel_id=1, source_target_pairs={{0,1},{1,0},{2,3},{3,2},{4,5},{5,4},{6,7},{7,6},{8,9},{9,8},{10,11... | collective-permute-start | bytes 294920 | tf_op jit(solution)/shard_map/ppermute | solution.py:392
  29.5 4.2 %collective-permute-start.9 = (bf16[8,3072]{1,0:T(8,128)(2,1)S(1)}, bf16[8,3072]{1,0:T(8,128)(2,1)S(1)}, u32[]{:S(2)}, u32[]{:S(2)}) collective-permute-start(bf16[8,3072]{1,0:T(8,128)(2,1)S(1)} %get-tuple-element.35), channel_id=1, source_target_pairs={{0,2},{1,3},{2,0},{3,1},{4,6},{5,7},{6,4},{7,5},{8,10},{9,11},{10,... | collective-permute-start | bytes 147464 | tf_op jit(solution)/shard_map/ppermute | solution.py:392
  31.2 5.1 %collective-permute-start.13 = (bf16[8,3072]{1,0:T(8,128)(2,1)S(1)}, bf16[8,3072]{1,0:T(8,128)(2,1)S(1)}, u32[]{:S(2)}, u32[]{:S(2)}) collective-permute-start(bf16[8,3072]{1,0:T(8,128)(2,1)S(1)} %get-tuple-element.43), channel_id=1, source_target_pairs={{0,2},{1,3},{2,0},{3,1},{4,6},{5,7},{6,4},{7,5},{8,10},{9,11},{10,... | collective-permute-start | bytes 147464 | tf_op jit(solution)/shard_map/ppermute | solution.py:392
  33.8 4.2 %collective-permute-start.12 = (bf16[8,3072]{1,0:T(8,128)(2,1)S(1)}, bf16[8,3072]{1,0:T(8,128)(2,1)S(1)}, u32[]{:S(2)}, u32[]{:S(2)}) collective-permute-start(bf16[8,3072]{1,0:T(8,128)(2,1)S(1)} %get-tuple-element.42), channel_id=1, source_target_pairs={{0,2},{1,3},{2,0},{3,1},{4,6},{5,7},{6,4},{7,5},{8,10},{9,11},{10,... | collective-permute-start | bytes 147464 | tf_op jit(solution)/shard_map/ppermute | solution.py:392
  35.7 5.0 %collective-permute-start.15 = (bf16[8,3072]{1,0:T(8,128)(2,1)S(1)}, bf16[8,3072]{1,0:T(8,128)(2,1)S(1)}, u32[]{:S(2)}, u32[]{:S(2)}) collective-permute-start(bf16[8,3072]{1,0:T(8,128)(2,1)S(1)} %fold.9.after), channel_id=1, source_target_pairs={{0,8},{1,9},{2,10},{3,11},{4,12},{5,13},{6,14},{7,15},{8,0},{9,1},... | collective-permute-start | bytes 147464 | tf_op jit(solution)/shard_map/ppermute | solution.py:392
  36.0 4.1 %collective-permute-start.11 = (bf16[8,3072]{1,0:T(8,128)(2,1)S(1)}, bf16[8,3072]{1,0:T(8,128)(2,1)S(1)}, u32[]{:S(2)}, u32[]{:S(2)}) collective-permute-start(bf16[8,3072]{1,0:T(8,128)(2,1)S(1)} %get-tuple-element.40), channel_id=1, source_target_pairs={{0,2},{1,3},{2,0},{3,1},{4,6},{5,7},{6,4},{7,5},{8,10},{9,11},{10,... | collective-permute-start | bytes 147464 | tf_op jit(solution)/shard_map/ppermute | solution.py:392
  36.3 6.1 %collective-permute-start.16 = (bf16[8,3072]{1,0:T(8,128)(2,1)S(1)}, bf16[8,3072]{1,0:T(8,128)(2,1)S(1)}, u32[]{:S(2)}, u32[]{:S(2)}) collective-permute-start(bf16[8,3072]{1,0:T(8,128)(2,1)S(1)} %fold.11.after), channel_id=1, source_target_pairs={{0,12},{1,13},{2,14},{3,15},{4,8},{5,9},{6,10},{7,11},{8,4},{9,5},... | collective-permute-start | bytes 147464 | tf_op jit(solution)/shard_map/ppermute | solution.py:392
  38.0 4.7 %collective-permute-start.14 = (bf16[8,3072]{1,0:T(8,128)(2,1)S(1)}, bf16[8,3072]{1,0:T(8,128)(2,1)S(1)}, u32[]{:S(2)}, u32[]{:S(2)}) collective-permute-start(bf16[8,3072]{1,0:T(8,128)(2,1)S(1)} %fold.12.after), channel_id=1, source_target_pairs={{0,4},{1,5},{2,6},{3,7},{4,0},{5,1},{6,2},{7,3},{8,12},{9,13},{10,... | collective-permute-start | bytes 147464 | tf_op jit(solution)/shard_map/ppermute | solution.py:392

commit v15 on v14

--- a/solution.py
+++ b/solution.py
@@ -295,10 +295,11 @@
 
 
 def ways_back(places):
-    near = [2 * p + j for high in range(0, places, 2) for j in (0, 1) for p in (high, high + 1)]
-    two = [2 * places + 2 * p for p in range(places)]
-    three = [b + 1 for b in two]
-    return [half for w in (near, two, three) for half in (w[: len(w) // 2], w[len(w) // 2 :])]
+    blocks = []
+    for k in range(EXPERTS):
+        groups = [k // 2 * 2 * places + 2 * p + k % 2 for p in range(places)]
+        blocks += [groups[: places // 2], groups[places // 2 :]]
+    return blocks
 
 
 def down_rows(hidden, weight):
@@ -316,7 +317,7 @@
         ),
         name="down",
     )(hidden, weight)
-    return outs[0:2], outs[2:4], outs[4:6]
+    return [outs[2 * k : 2 * k + 2] for k in range(EXPERTS)]
 
 
 def join_kernel(*refs):
@@ -422,29 +423,26 @@
 
     hidden = hidden_rows(waves, gate_weight, up_weight, down_weight)
 
-    near, two, three = down_rows(hidden, down_weight)
-
-    def back(wave, stage, after, parts=2):
-        return fold(wave[0], swap(wave[1], count, bits[-1 - stage]), after, parts)
+    blocks = down_rows(hidden, down_weight)
+
+    def back(k, stage, after):
+        held, send = blocks[k]
+        parts = 1 if stage == last else 2
+        blocks[k] = fold(held, swap(send, count, bits[-1 - stage]), after, parts)
+        return blocks[k][0]
 
     last = len(bits) - 1
     token = share
     for stage in range(last):
-        two = back(two, stage, token)
-        three = back(three, stage, two[0])
-        token = three[0]
-    two = back(two, last, token, 1)
+        for k in (3, 2, 1):
+            token = back(k, stage, token)
+    token = back(3, last, token)
     for stage in range(last):
-        near = back(near, stage, two[0], 4 if stage == last - 1 else 2)
-    three = back(three, last, near[0], 1)
-    one = back(near[2:4], last, three[0], 1)
-    zero = back(near[0:2], last, one[0], 1)
-    results = [
-        zero[0],
-        swap(one[0], count, plane),
-        swap(two[0], count, 2 * plane),
-        swap(three[0], count, 3 * plane),
-    ]
+        back(0, stage, token)
+    token = back(2, last, token)
+    token = back(1, last, token)
+    back(0, last, token)
+    results = [blocks[0][0]] + [swap(blocks[k][0], count, k * plane) for k in (1, 2, 3)]
     total = combine(2, share, take, results[2:], [], F32)
     return (attended, combine(0, share, take, results[:2], [total], BF16))
 

time: 43.6 us -> 43.5 us (level)
  waiting for transfers between devices: 14.6 us -> 11.5 us
  starting transfers between devices: 17.4 us -> 20.4 us
    ppermute x17 -> x18, waiting for transfers between devices: 14.6 us -> 11.5 us  [swap(): return lax.ppermute(value, 'dp', [(i, i ^ bit) for i in range(count)])]
    ppermute x17 -> x18, starting transfers between devices: 17.4 us -> 20.4 us  [swap(): return lax.ppermute(value, 'dp', [(i, i ^ bit) for i in range(count)])]
  transfers between devices with their start and end apart: 17 -> 18, of which waited for: 11 -> 8; matrix products, arithmetic and copies ran while one was open for 0% -> 0% of each run, Pallas kernels for 1% -> 1%
where the time goes in v15:
time: 43.5 us; the launch traced here: 43.4 us
  starting transfers between devices  20.4 us (47%)
  waiting for transfers between devices  11.5 us (26%)
  Pallas kernels  10.7 us (25%)
  between operations  0.84 us (2%)
    ppermute x18, starting transfers between devices, swap(): return lax.ppermute(value, 'dp', [(i, i ^ bit) for i in range(count)])  20.4 us
    ppermute x18, waiting for transfers between devices, swap(): return lax.ppermute(value, 'dp', [(i, i ^ bit) for i in range(count)])  11.5 us
    pallas_call x1, Pallas kernels, hidden_rows(): pl.pallas_call(hidden_kernel, out_shape=jax.ShapeDtypeStruct((rows, colum...  4.13 us
    pallas_call x1, Pallas kernels, attend(): pl.pallas_call(functools.partial(attend_kernel, plane), out_shape=(jax.Sh...  2.65 us
    pallas_call x1, Pallas kernels, down_rows(): pl.pallas_call(down_kernel, out_shape=[jax.ShapeDtypeStruct((size, width...  2.55 us
    pallas_call x2, Pallas kernels, combine(): pl.pallas_call(functools.partial(combine_kernel, first), out_shape=jax.Sh...  1.07 us
  transfers between devices with their start and end apart: 18, of which 8 were waited for; matrix products, arithmetic and copies ran while one was open for 0% of the time, Pallas kernels for 1%

profile of v15, /device:TPU:0, one launch (start us, length us, event | category | flops | bytes accessed | tf_op | source)
XLA Modules:
  0.0 43.4 jit_solution(1461884925079528297)
XLA Ops:
  0.7 2.7 %attend.1 = (bf16[8,4096]{1,0:T(8,128)(2,1)}, bf16[8,3072]{1,0:T(8,128)(2,1)S(1)}, bf16[8,3072]{1,0:T(8,128)(2,1)S(1)}, bf16[8,3072]{1,0:T(8,128)(2,1)S(1)}, bf1...) custom-call(bf16[8,4096]{1,0:T(8,128)(2,1)} %refs_0_.1, ...), custom_call_target="tpu_custom_call" | custom-call | tf_op jit(solution)/shard_map/attend/pallas_call | solution.py:208
  3.3 3.1 %collective-permute-start = (bf16[8,3072]{1,0:T(8,128)(2,1)S(1)}, bf16[8,3072]{1,0:T(8,128)(2,1)S(1)}, u32[]{:S(2)}, u32[]{:S(2)}) collective-permute-start(bf16[8,3072]{1,0:T(8,128)(2,1)S(1)} %get-tuple-element.29), channel_id=1, source_target_pairs={{0,4},{1,5},{2,6},{3,7},{4,0},{5,1},{6,2},{7,3},{8,12},{9,13},{10,... | collective-permute-start | bytes 147464 | tf_op jit(solution)/shard_map/ppermute | solution.py:393
  6.4 2.6 %collective-permute-start.3 = (bf16[8,3072]{1,0:T(8,128)(2,1)S(1)}, bf16[8,3072]{1,0:T(8,128)(2,1)S(1)}, u32[]{:S(2)}, u32[]{:S(2)}) collective-permute-start(bf16[8,3072]{1,0:T(8,128)(2,1)S(1)} %get-tuple-element.30), channel_id=1, source_target_pairs={{0,8},{1,9},{2,10},{3,11},{4,12},{5,13},{6,14},{7,15},{8,0},{9,1},... | collective-permute-start | bytes 147464 | tf_op jit(solution)/shard_map/ppermute | solution.py:393
  9.0 0.0 collective-permute-start.4
  9.0 0.0 collective-permute-done.refs_2_
  9.0 1.8 %collective-permute-start.1 = (bf16[16,3072]{1,0:T(8,128)(2,1)S(1)}, bf16[16,3072]{1,0:T(8,128)(2,1)S(1)}, u32[]{:S(2)}, u32[]{:S(2)}) collective-permute-start(bf16[16,3072]{1,0:T(8,128)(2,1)S(1)} %join.6.refs_1_), channel_id=1, source_target_pairs={{0,2},{1,3},{2,0},{3,1},{4,6},{5,7},{6,4},{7,5},{8,10},{9,11},{10,... | collective-permute-start | bytes 294920 | tf_op jit(solution)/shard_map/ppermute | solution.py:393
  10.8 1.5 %collective-permute-done.3.refs_1_ = bf16[8,3072]{1,0:T(8,128)(2,1)S(1)} collective-permute-done((bf16[8,3072]{1,0:T(8,128)(2,1)S(1)}, bf16[8,3072]{1,0:T(8,128)(2,1)S(1)}, u32[]{:S(2)}, u32[]{:S(2)}) %collective-permute-start.3) | collective-permute-done | bytes 49184 | tf_op jit(solution)/shard_map/ppermute | solution.py:393
  12.3 2.6 %collective-permute-done.4.refs_2_ = bf16[8,3072]{1,0:T(8,128)(2,1)S(1)} collective-permute-done((bf16[8,3072]{1,0:T(8,128)(2,1)S(1)}, bf16[8,3072]{1,0:T(8,128)(2,1)S(1)}, u32[]{:S(2)}, u32[]{:S(2)}) %collective-permute-start.4) | collective-permute-done | bytes 49184 | tf_op jit(solution)/shard_map/ppermute | solution.py:393
  14.9 1.6 %collective-permute-start.5 = (bf16[16,3072]{1,0:T(8,128)(2,1)S(1)}, bf16[16,3072]{1,0:T(8,128)(2,1)S(1)}, u32[]{:S(2)}, u32[]{:S(2)}) collective-permute-start(bf16[16,3072]{1,0:T(8,128)(2,1)S(1)} %join.9.refs_1_), channel_id=1, source_target_pairs={{0,2},{1,3},{2,0},{3,1},{4,6},{5,7},{6,4},{7,5},{8,10},{9,11},{10,... | collective-permute-start | bytes 294920 | tf_op jit(solution)/shard_map/ppermute | solution.py:393
  16.5 0.1 collective-permute-start.2
  16.6 3.0 %collective-permute-done.5.refs_2_ = bf16[16,3072]{1,0:T(8,128)(2,1)S(1)} collective-permute-done((bf16[16,3072]{1,0:T(8,128)(2,1)S(1)}, bf16[16,3072]{1,0:T(8,128)(2,1)S(1)}, u32[]{:S(2)}, u32[]{:S(2)}) %collective-permute-start.5) | collective-permute-done | bytes 98336 | tf_op jit(solution)/shard_map/ppermute | solution.py:393
  19.6 0.1 collective-permute-start.6
  19.7 1.4 %collective-permute-done.6.refs_2_ = bf16[32,3072]{1,0:T(8,128)(2,1)S(1)} collective-permute-done((bf16[32,3072]{1,0:T(8,128)(2,1)S(1)}, bf16[32,3072]{1,0:T(8,128)(2,1)S(1)}, u32[]{:S(2)}, u32[]{:S(2)}) %collective-permute-start.6) | collective-permute-done | bytes 196640 | tf_op jit(solution)/shard_map/ppermute | solution.py:393
  21.2 4.1 %hidden.1 = bf16[128,1792]{1,0:T(8,128)(2,1)S(1)} custom-call(bf16[4096,1792]{1,0:T(8,128)(2,1)S(1)} %copy-done.1, bf16[4096,1792]{1,0:T(8,128)(2,1)S(1)} %copy-done.2, bf16[1792,4096]{1,0:T(8,128)(2,1)S(1)} %copy-done, bf16[64,3072]{1,0:T(8,128)(2,1)S(1)} %join.8.refs_0_, bf16[64,3072]{1,0:T(8,128)(2,1)S(1)} %join.11.refs_1_), custom_call_target="tpu_custom_call" | custom-call | flops 3758096384 | tf_op jit(solution)/shard_map/hidden/pallas_call | solution.py:257
  25.3 2.6 %down.1 = (bf16[16,3072]{1,0:T(8,128)(2,1)S(1)}, bf16[16,3072]{1,0:T(8,128)(2,1)S(1)}, bf16[16,3072]{1,0:T(8,128)(2,1)S(1)}, bf16[16,3072]{1,0:T(8,128)(2,1)S(1)...) custom-call(bf16[128,1792]{1,0:T(8,128)(2,1)S(1)} %hidden.1, ...), custom_call_target="tpu_custom_call" | custom-call | flops 1879048192 | tf_op jit(solution)/shard_map/down/pallas_call | solution.py:309
  27.9 0.2 collective-permute-start.8
  28.1 0.4 collective-permute-start.11
  28.4 0.1 collective-permute-start.10
  28.6 0.4 collective-permute-start.7
  28.9 0.3 collective-permute-done.8.arrived
  29.3 1.6 %collective-permute-start.9 = (bf16[8,3072]{1,0:T(8,128)(2,1)S(1)}, bf16[8,3072]{1,0:T(8,128)(2,1)S(1)}, u32[]{:S(2)}, u32[]{:S(2)}) collective-permute-start(bf16[8,3072]{1,0:T(8,128)(2,1)S(1)} %get-tuple-element.37), channel_id=1, source_target_pairs={{0,2},{1,3},{2,0},{3,1},{4,6},{5,7},{6,4},{7,5},{8,10},{9,11},{10,... | collective-permute-start | bytes 147464 | tf_op jit(solution)/shard_map/ppermute | solution.py:393
  30.9 0.6 %collective-permute-start.14 = (bf16[8,3072]{1,0:T(8,128)(2,1)S(1)}, bf16[8,3072]{1,0:T(8,128)(2,1)S(1)}, u32[]{:S(2)}, u32[]{:S(2)}) collective-permute-start(bf16[8,3072]{1,0:T(8,128)(2,1)S(1)} %get-tuple-element.47), channel_id=1, source_target_pairs={{0,2},{1,3},{2,0},{3,1},{4,6},{5,7},{6,4},{7,5},{8,10},{9,11},{10,... | collective-permute-start | bytes 147464 | tf_op jit(solution)/shard_map/ppermute | solution.py:393
  31.5 1.6 %collective-permute-start.13 = (bf16[8,3072]{1,0:T(8,128)(2,1)S(1)}, bf16[8,3072]{1,0:T(8,128)(2,1)S(1)}, u32[]{:S(2)}, u32[]{:S(2)}) collective-permute-start(bf16[8,3072]{1,0:T(8,128)(2,1)S(1)} %get-tuple-element.46), channel_id=1, source_target_pairs={{0,2},{1,3},{2,0},{3,1},{4,6},{5,7},{6,4},{7,5},{8,10},{9,11},{10,... | collective-permute-start | bytes 147464 | tf_op jit(solution)/shard_map/ppermute | solution.py:393
  33.1 0.3 collective-permute-done.9.arrived
  33.5 1.8 %collective-permute-start.12 = (bf16[8,3072]{1,0:T(8,128)(2,1)S(1)}, bf16[8,3072]{1,0:T(8,128)(2,1)S(1)}, u32[]{:S(2)}, u32[]{:S(2)}) collective-permute-start(bf16[8,3072]{1,0:T(8,128)(2,1)S(1)} %get-tuple-element.45), channel_id=1, source_target_pairs={{0,2},{1,3},{2,0},{3,1},{4,6},{5,7},{6,4},{7,5},{8,10},{9,11},{10,... | collective-permute-start | bytes 147464 | tf_op jit(solution)/shard_map/ppermute | solution.py:393
  35.3 0.7 %collective-permute-start.17 = (bf16[8,3072]{1,0:T(8,128)(2,1)S(1)}, bf16[8,3072]{1,0:T(8,128)(2,1)S(1)}, u32[]{:S(2)}, u32[]{:S(2)}) collective-permute-start(bf16[8,3072]{1,0:T(8,128)(2,1)S(1)} %fold.11.after), channel_id=1, source_target_pairs={{0,12},{1,13},{2,14},{3,15},{4,8},{5,9},{6,10},{7,11},{8,4},{9,5},... | collective-permute-start | bytes 147464 | tf_op jit(solution)/shard_map/ppermute | solution.py:393
  36.1 0.1 collective-permute-start.16
  36.2 3.7 %collective-permute-start.15 = (bf16[8,3072]{1,0:T(8,128)(2,1)S(1)}, bf16[8,3072]{1,0:T(8,128)(2,1)S(1)}, u32[]{:S(2)}, u32[]{:S(2)}) collective-permute-start(bf16[8,3072]{1,0:T(8,128)(2,1)S(1)} %fold.14.after), channel_id=1, source_target_pairs={{0,4},{1,5},{2,6},{3,7},{4,0},{5,1},{6,2},{7,3},{8,12},{9,13},{10,... | collective-permute-start | bytes 147464 | tf_op jit(solution)/shard_map/ppermute | solution.py:393
  39.9 1.4 %collective-permute-done.17.refs_1_ = bf16[8,3072]{1,0:T(8,128)(2,1)S(1)} collective-permute-done((bf16[8,3072]{1,0:T(8,128)(2,1)S(1)}, bf16[8,3072]{1,0:T(8,128)(2,1)S(1)}, u32[]{:S(2)}, u32[]{:S(2)}) %collective-permute-start.17) | collective-permute-done | bytes 49184 | tf_op jit(solution)/shard_map/ppermute | solution.py:393
  41.3 1.0 %collective-permute-done.16.refs_0_ = bf16[8,3072]{1,0:T(8,128)(2,1)S(1)} collective-permute-done((bf16[8,3072]{1,0:T(8,128)(2,1)S(1)}, bf16[8,3072]{1,0:T(8,128)(2,1)S(1)}, u32[]{:S(2)}, u32[]{:S(2)}) %collective-permute-start.16) | collective-permute-done | bytes 49184 | tf_op jit(solution)/shard_map/ppermute | solution.py:393
  42.3 0.2 combine.2.refs_2_
  42.5 0.8 %combine.3 = bf16[8,4096]{1,0:T(8,128)(2,1)} custom-call(f32[16,128]{1,0:T(8,128)S(1)} %get-tuple-element.26.refs_0_.after.share, bf16[4,16,128]{2,1,0:T(8,128)(2,1)S(1)} %get-tuple-element.27.take, bf16[8,3072]{1,0:T(8,128)(2,1)S(1)} %fold.15.refs_0_, bf16[8,3072]{1,0:T(8,128)(2,1)S(1)} %collective-permute-done.15.refs_1_, f32[8,4096]{1,0:T(8,128)S(1)} %combine.2.refs_2_), custom_call_target="tpu_custom_call" | custom-call | bytes 16777216 | tf_op jit(solution)/shard_map/combine/pallas_call | solution.py:381
  (29 shorter events, 0.3 us)
Async XLA Ops:
  0.6 20.5 %copy-start = (bf16[1792,4096]{1,0:T(8,128)(2,1)S(1)}, bf16[1792,4096]{1,0:T(8,128)(2,1)}, u32[]{:S(2)}) copy-start(bf16[1792,4096]{1,0:T(8,128)(2,1)} %weight.1) | copy-start | bytes 44040196
  0.6 20.5 %copy-start.1 = (bf16[4096,1792]{1,0:T(8,128)(2,1)S(1)}, bf16[4096,1792]{1,0:T(8,128)(2,1)}, u32[]{:S(2)}) copy-start(bf16[4096,1792]{1,0:T(8,128)(2,1)} %gate_weight.1) | copy-start | bytes 44040196
  0.7 20.5 %copy-start.2 = (bf16[4096,1792]{1,0:T(8,128)(2,1)S(1)}, bf16[4096,1792]{1,0:T(8,128)(2,1)}, u32[]{:S(2)}) copy-start(bf16[4096,1792]{1,0:T(8,128)(2,1)} %up_weight.1) | copy-start | bytes 44040196
  3.3 5.7 %collective-permute-start = (bf16[8,3072]{1,0:T(8,128)(2,1)S(1)}, bf16[8,3072]{1,0:T(8,128)(2,1)S(1)}, u32[]{:S(2)}, u32[]{:S(2)}) collective-permute-start(bf16[8,3072]{1,0:T(8,128)(2,1)S(1)} %get-tuple-element.29), channel_id=1, source_target_pairs={{0,4},{1,5},{2,6},{3,7},{4,0},{5,1},{6,2},{7,3},{8,12},{9,13},{10,... | collective-permute-start | bytes 147464 | tf_op jit(solution)/shard_map/ppermute | solution.py:393
  6.4 5.9 %collective-permute-start.3 = (bf16[8,3072]{1,0:T(8,128)(2,1)S(1)}, bf16[8,3072]{1,0:T(8,128)(2,1)S(1)}, u32[]{:S(2)}, u32[]{:S(2)}) collective-permute-start(bf16[8,3072]{1,0:T(8,128)(2,1)S(1)} %get-tuple-element.30), channel_id=1, source_target_pairs={{0,8},{1,9},{2,10},{3,11},{4,12},{5,13},{6,14},{7,15},{8,0},{9,1},... | collective-permute-start | bytes 147464 | tf_op jit(solution)/shard_map/ppermute | solution.py:393
  9.0 5.9 %collective-permute-start.4 = (bf16[8,3072]{1,0:T(8,128)(2,1)S(1)}, bf16[8,3072]{1,0:T(8,128)(2,1)S(1)}, u32[]{:S(2)}, u32[]{:S(2)}) collective-permute-start(bf16[8,3072]{1,0:T(8,128)(2,1)S(1)} %get-tuple-element.31), channel_id=1, source_target_pairs={{0,12},{1,13},{2,14},{3,15},{4,8},{5,9},{6,10},{7,11},{8,4},{9,5},... | collective-permute-start | bytes 147464 | tf_op jit(solution)/shard_map/ppermute | solution.py:393
  9.0 7.5 %collective-permute-start.1 = (bf16[16,3072]{1,0:T(8,128)(2,1)S(1)}, bf16[16,3072]{1,0:T(8,128)(2,1)S(1)}, u32[]{:S(2)}, u32[]{:S(2)}) collective-permute-start(bf16[16,3072]{1,0:T(8,128)(2,1)S(1)} %join.6.refs_1_), channel_id=1, source_target_pairs={{0,2},{1,3},{2,0},{3,1},{4,6},{5,7},{6,4},{7,5},{8,10},{9,11},{10,... | collective-permute-start | bytes 294920 | tf_op jit(solution)/shard_map/ppermute | solution.py:393
  14.9 4.7 %collective-permute-start.5 = (bf16[16,3072]{1,0:T(8,128)(2,1)S(1)}, bf16[16,3072]{1,0:T(8,128)(2,1)S(1)}, u32[]{:S(2)}, u32[]{:S(2)}) collective-permute-start(bf16[16,3072]{1,0:T(8,128)(2,1)S(1)} %join.9.refs_1_), channel_id=1, source_target_pairs={{0,2},{1,3},{2,0},{3,1},{4,6},{5,7},{6,4},{7,5},{8,10},{9,11},{10,... | collective-permute-start | bytes 294920 | tf_op jit(solution)/shard_map/ppermute | solution.py:393
  16.5 3.2 %collective-permute-start.2 = (bf16[32,3072]{1,0:T(8,128)(2,1)S(1)}, bf16[32,3072]{1,0:T(8,128)(2,1)S(1)}, u32[]{:S(2)}, u32[]{:S(2)}) collective-permute-start(bf16[32,3072]{1,0:T(8,128)(2,1)S(1)} %join.7.refs_1_), channel_id=1, source_target_pairs={{0,1},{1,0},{2,3},{3,2},{4,5},{5,4},{6,7},{7,6},{8,9},{9,8},{10,11... | collective-permute-start | bytes 589832 | tf_op jit(solution)/shard_map/ppermute | solution.py:393
  19.6 1.5 %collective-permute-start.6 = (bf16[32,3072]{1,0:T(8,128)(2,1)S(1)}, bf16[32,3072]{1,0:T(8,128)(2,1)S(1)}, u32[]{:S(2)}, u32[]{:S(2)}) collective-permute-start(bf16[32,3072]{1,0:T(8,128)(2,1)S(1)} %join.10.refs_1_), channel_id=1, source_target_pairs={{0,1},{1,0},{2,3},{3,2},{4,5},{5,4},{6,7},{7,6},{8,9},{9,8},{10,11... | collective-permute-start | bytes 589832 | tf_op jit(solution)/shard_map/ppermute | solution.py:393
  27.9 1.4 %collective-permute-start.8 = (bf16[16,3072]{1,0:T(8,128)(2,1)S(1)}, bf16[16,3072]{1,0:T(8,128)(2,1)S(1)}, u32[]{:S(2)}, u32[]{:S(2)}) collective-permute-start(bf16[16,3072]{1,0:T(8,128)(2,1)S(1)} %get-tuple-element.35), channel_id=1, source_target_pairs={{0,1},{1,0},{2,3},{3,2},{4,5},{5,4},{6,7},{7,6},{8,9},{9,8},{10,11... | collective-permute-start | bytes 294920 | tf_op jit(solution)/shard_map/ppermute | solution.py:393
  28.1 2.8 %collective-permute-start.11 = (bf16[16,3072]{1,0:T(8,128)(2,1)S(1)}, bf16[16,3072]{1,0:T(8,128)(2,1)S(1)}, u32[]{:S(2)}, u32[]{:S(2)}) collective-permute-start(bf16[16,3072]{1,0:T(8,128)(2,1)S(1)} %get-tuple-element.41), channel_id=1, source_target_pairs={{0,1},{1,0},{2,3},{3,2},{4,5},{5,4},{6,7},{7,6},{8,9},{9,8},{10,11... | collective-permute-start | bytes 294920 | tf_op jit(solution)/shard_map/ppermute | solution.py:393
  28.4 3.0 %collective-permute-start.10 = (bf16[16,3072]{1,0:T(8,128)(2,1)S(1)}, bf16[16,3072]{1,0:T(8,128)(2,1)S(1)}, u32[]{:S(2)}, u32[]{:S(2)}) collective-permute-start(bf16[16,3072]{1,0:T(8,128)(2,1)S(1)} %get-tuple-element.39), channel_id=1, source_target_pairs={{0,1},{1,0},{2,3},{3,2},{4,5},{5,4},{6,7},{7,6},{8,9},{9,8},{10,11... | collective-permute-start | bytes 294920 | tf_op jit(solution)/shard_map/ppermute | solution.py:393
  28.6 4.9 %collective-permute-start.7 = (bf16[16,3072]{1,0:T(8,128)(2,1)S(1)}, bf16[16,3072]{1,0:T(8,128)(2,1)S(1)}, u32[]{:S(2)}, u32[]{:S(2)}) collective-permute-start(bf16[16,3072]{1,0:T(8,128)(2,1)S(1)} %get-tuple-element.33), channel_id=1, source_target_pairs={{0,1},{1,0},{2,3},{3,2},{4,5},{5,4},{6,7},{7,6},{8,9},{9,8},{10,11... | collective-permute-start | bytes 294920 | tf_op jit(solution)/shard_map/ppermute | solution.py:393
  29.3 4.2 %collective-permute-start.9 = (bf16[8,3072]{1,0:T(8,128)(2,1)S(1)}, bf16[8,3072]{1,0:T(8,128)(2,1)S(1)}, u32[]{:S(2)}, u32[]{:S(2)}) collective-permute-start(bf16[8,3072]{1,0:T(8,128)(2,1)S(1)} %get-tuple-element.37), channel_id=1, source_target_pairs={{0,2},{1,3},{2,0},{3,1},{4,6},{5,7},{6,4},{7,5},{8,10},{9,11},{10,... | collective-permute-start | bytes 147464 | tf_op jit(solution)/shard_map/ppermute | solution.py:393
  30.9 5.2 %collective-permute-start.14 = (bf16[8,3072]{1,0:T(8,128)(2,1)S(1)}, bf16[8,3072]{1,0:T(8,128)(2,1)S(1)}, u32[]{:S(2)}, u32[]{:S(2)}) collective-permute-start(bf16[8,3072]{1,0:T(8,128)(2,1)S(1)} %get-tuple-element.47), channel_id=1, source_target_pairs={{0,2},{1,3},{2,0},{3,1},{4,6},{5,7},{6,4},{7,5},{8,10},{9,11},{10,... | collective-permute-start | bytes 147464 | tf_op jit(solution)/shard_map/ppermute | solution.py:393
  31.5 4.7 %collective-permute-start.13 = (bf16[8,3072]{1,0:T(8,128)(2,1)S(1)}, bf16[8,3072]{1,0:T(8,128)(2,1)S(1)}, u32[]{:S(2)}, u32[]{:S(2)}) collective-permute-start(bf16[8,3072]{1,0:T(8,128)(2,1)S(1)} %get-tuple-element.46), channel_id=1, source_target_pairs={{0,2},{1,3},{2,0},{3,1},{4,6},{5,7},{6,4},{7,5},{8,10},{9,11},{10,... | collective-permute-start | bytes 147464 | tf_op jit(solution)/shard_map/ppermute | solution.py:393
  33.5 6.4 %collective-permute-start.12 = (bf16[8,3072]{1,0:T(8,128)(2,1)S(1)}, bf16[8,3072]{1,0:T(8,128)(2,1)S(1)}, u32[]{:S(2)}, u32[]{:S(2)}) collective-permute-start(bf16[8,3072]{1,0:T(8,128)(2,1)S(1)} %get-tuple-element.45), channel_id=1, source_target_pairs={{0,2},{1,3},{2,0},{3,1},{4,6},{5,7},{6,4},{7,5},{8,10},{9,11},{10,... | collective-permute-start | bytes 147464 | tf_op jit(solution)/shard_map/ppermute | solution.py:393
  35.3 6.0 %collective-permute-start.17 = (bf16[8,3072]{1,0:T(8,128)(2,1)S(1)}, bf16[8,3072]{1,0:T(8,128)(2,1)S(1)}, u32[]{:S(2)}, u32[]{:S(2)}) collective-permute-start(bf16[8,3072]{1,0:T(8,128)(2,1)S(1)} %fold.11.after), channel_id=1, source_target_pairs={{0,12},{1,13},{2,14},{3,15},{4,8},{5,9},{6,10},{7,11},{8,4},{9,5},... | collective-permute-start | bytes 147464 | tf_op jit(solution)/shard_map/ppermute | solution.py:393
  36.1 6.2 %collective-permute-start.16 = (bf16[8,3072]{1,0:T(8,128)(2,1)S(1)}, bf16[8,3072]{1,0:T(8,128)(2,1)S(1)}, u32[]{:S(2)}, u32[]{:S(2)}) collective-permute-start(bf16[8,3072]{1,0:T(8,128)(2,1)S(1)} %fold.13.after), channel_id=1, source_target_pairs={{0,8},{1,9},{2,10},{3,11},{4,12},{5,13},{6,14},{7,15},{8,0},{9,1},... | collective-permute-start | bytes 147464 | tf_op jit(solution)/shard_map/ppermute | solution.py:393
  36.2 6.4 %collective-permute-start.15 = (bf16[8,3072]{1,0:T(8,128)(2,1)S(1)}, bf16[8,3072]{1,0:T(8,128)(2,1)S(1)}, u32[]{:S(2)}, u32[]{:S(2)}) collective-permute-start(bf16[8,3072]{1,0:T(8,128)(2,1)S(1)} %fold.14.after), channel_id=1, source_target_pairs={{0,4},{1,5},{2,6},{3,7},{4,0},{5,1},{6,2},{7,3},{8,12},{9,13},{10,... | collective-permute-start | bytes 147464 | tf_op jit(solution)/shard_map/ppermute | solution.py:393

commit v16 on v13

--- a/solution.py
+++ b/solution.py
@@ -51,8 +51,9 @@
 def attend_kernel(plane, *refs):
     refs = refs[:10] + refs[10 + HINTS :]
     sources, attended, packed, (share, take), held, semaphores = (
-        refs[:10], refs[10], refs[11:15], refs[15:17], refs[17:27], refs[27]
+        refs[:10], refs[10], refs[11:15], refs[15:17], refs[17:27], refs[28]
     )
+    kept = refs[27]
     copies = [
         pltpu.make_async_copy(source, target, semaphores.at[i])
         for i, (source, target) in enumerate(zip(sources, held))
@@ -160,7 +161,9 @@
     pieces = [value[j * rows : (j + 1) * rows] for value in mixed for j in range(groups)]
 
     states = (residual[...].astype(F32) + jnp.concatenate(pieces, axis=1)).astype(BF16)
-    attended[...] = states
+    attended_copy = pltpu.make_async_copy(kept, attended, semaphores.at[len(copies)])
+    kept[...] = states
+    attended_copy.start()
     states = states.astype(F32)
     norm = lax.rsqrt(jnp.mean(states * states, axis=1, keepdims=True) + 1e-05)
     gains = gain[...].astype(F32)
@@ -187,6 +190,7 @@
         chosen_logits = jnp.where(expert_down[:, :1] == (own ^ e), both, chosen_logits)
     other = jnp.concatenate([chosen_logits[rows:], chosen_logits[:rows]], axis=0)
     share[...] = jnp.broadcast_to(1.0 / (1.0 + jnp.exp(other - chosen_logits)), share.shape)
+    attended_copy.wait()
 
 
 def attend(plane, queries, new_keys, new_values, cache_keys, cache_values, lengths, residual,
@@ -214,12 +218,12 @@
             jax.ShapeDtypeStruct((4, 2 * rows, 128), BF16),
         ),
         in_specs=[ANY] * (len(operands) + HINTS),
-        out_specs=(VMEM,) * (3 + EXPERTS),
+        out_specs=(ANY,) + (VMEM,) * (2 + EXPERTS),
         scratch_shapes=[
             (pltpu.SMEM if i in in_smem else pltpu.VMEM)(operand.shape, operand.dtype)
             for i, operand in enumerate(operands)
         ]
-        + [pltpu.SemaphoreType.DMA((len(operands),))],
+        + [pltpu.VMEM((rows, width), BF16), pltpu.SemaphoreType.DMA((len(operands) + 1,))],
         compiler_params=pltpu.CompilerParams(vmem_limit_bytes=5 * MIB),
         name="attend",
     )(*[pltpu.with_memory_space_constraint(x, pltpu.HBM) for x in operands + (weight,) * HINTS])
@@ -228,7 +232,7 @@
 def hidden_kernel(gate_weight, up_weight, down_weight, *refs):
     waves, hidden = refs[:-1], refs[-1]
     columns = gate_weight.shape[1]
-    step = 256 if columns % 256 == 0 else columns
+    step = 512
     quarter = waves[0].shape[1] // 3
     blocks = jnp.concatenate([wave[...] for wave in waves], axis=0)
     size = 128
@@ -246,9 +250,10 @@
         tails.append(dot(picks, jnp.concatenate(parts, axis=0)).astype(BF16))
     x = jnp.concatenate([blocks, jnp.concatenate(tails, axis=0)], axis=1)
     for f in range(0, columns, step):
-        gate = dot(x, gate_weight[:, f : f + step])
-        upper = dot(x, up_weight[:, f : f + step])
-        hidden[:, f : f + step] = (gate / (1.0 + jnp.exp(-gate)) * upper).astype(BF16)
+        last = min(f + step, columns)
+        gate = dot(x, gate_weight[:, f:last])
+        upper = dot(x, up_weight[:, f:last])
+        hidden[:, f:last] = (gate / (1.0 + jnp.exp(-gate)) * upper).astype(BF16)
 
 
 def hidden_rows(waves, gate_weight, up_weight, down_weight):
@@ -280,7 +285,7 @@
     def terms(first, count):
         return dot(h, weight[:, first : first + count])
 
-    step = min(512, quarter)
+    step = min(1024, quarter)
     is_row = (lax.broadcasted_iota(jnp.int32, (rows, step), 0) & 7) < MOST
     for n in range(0, quarter, step):
         tail = terms(3 * quarter + n, step).astype(BF16)
@@ -359,33 +364,57 @@
     )(held, arrived, after)
 
 
-def combine_kernel(first, share, take, *refs):
-    results, before, out = refs[:2], refs[2:-1], refs[-1]
-    rows = out.shape[0]
-    quarter = results[0].shape[1] // 3
+def combined(first, share, take, results):
     picks = [take[i][:, 8 * first : 8 * first + 16] for i in range(4)]
-    shares = share[:, :1]
+    rows = share.shape[0] // 2
     block = jnp.concatenate([x[...] for x in results], axis=0)
-    for m, value in enumerate(unpack(picks, block)):
-        lanes = slice(m * quarter, (m + 1) * quarter)
-        value = value * shares
-        value = value[:rows] + value[rows:]
-        for x in before:
-            value = value + x[:, lanes]
-        out[:, lanes] = value.astype(out.dtype)
-
-
-def combine(first, share, take, results, before, dtype):
-    width = results[0].shape[1] // 3 * 4
+    values = [value * share[:, :1] for value in unpack(picks, block)]
+    return [value[:rows] + value[rows:] for value in values]
+
+
+def combine_far_kernel(share, take, two, three, total):
+    quarter = two.shape[1] // 3
+    for m, value in enumerate(combined(2, share, take, (two, three))):
+        total[:, m * quarter : (m + 1) * quarter] = value
+
+
+def combine_kernel(share, take, zero, one, total, out, held, semaphores):
+    quarter = zero.shape[1] // 3
+    copies = []
+    for m, value in enumerate(combined(0, share, take, (zero, one))):
+        lanes = pl.ds(m * quarter, quarter)
+        held[:, lanes] = (value + total[:, lanes]).astype(BF16)
+        copies.append(
+            pltpu.make_async_copy(held.at[:, lanes], out.at[:, lanes], semaphores.at[m])
+        )
+        copies[m].start()
+    for copy in copies:
+        copy.wait()
+
+
+def combine(share, take, results):
+    rows, width = share.shape[0] // 2, results[0].shape[1] // 3 * 4
+    params = pltpu.CompilerParams(vmem_limit_bytes=2 * MIB)
+    cost = pl.CostEstimate(flops=0, bytes_accessed=16 * MIB, transcendentals=0)
+    total = pl.pallas_call(
+        combine_far_kernel,
+        out_shape=jax.ShapeDtypeStruct((rows, width), F32),
+        in_specs=[VMEM] * 4,
+        out_specs=VMEM,
+        compiler_params=params,
+        cost_estimate=cost,
+        name="combine_far",
+    )(share, take, *results[2:])
     return pl.pallas_call(
-        functools.partial(combine_kernel, first),
-        out_shape=jax.ShapeDtypeStruct((share.shape[0] // 2, width), dtype),
-        in_specs=[VMEM] * (4 + len(before)),
-        out_specs=VMEM,
-        compiler_params=pltpu.CompilerParams(vmem_limit_bytes=2 * MIB),
-        cost_estimate=pl.CostEstimate(flops=0, bytes_accessed=16 * MIB, transcendentals=0),
+        combine_kernel,
+        out_shape=jax.ShapeDtypeStruct((rows, width), BF16),
+        in_specs=[VMEM] * 5,
+        out_specs=ANY,
+        scratch_shapes=[pltpu.VMEM((rows, width), BF16), pltpu.SemaphoreType.DMA((4,))],
+        compiler_params=params,
+        cost_estimate=cost,
         name="combine",
-    )(share, take, *results, *before)
+    )(share, take, *results[:2], total)
 
 
 def swap(value, count, bit):
@@ -444,8 +473,7 @@
         swap(two[0], count, 2 * plane),
         swap(three[0], count, 3 * plane),
     ]
-    total = combine(2, share, take, results[2:], [], F32)
-    return (attended, combine(0, share, take, results[:2], [total], BF16))
+    return (attended, combine(share, take, results))
 
 
 def solution(mesh):

time: 42.6 us -> 42.3 us (level)
  no operation moved by 1% of the time
where the time goes in v16:
time: 42.3 us; the launch traced here: 42.2 us
  starting transfers between devices  16.6 us (39%)
  waiting for transfers between devices  14.3 us (34%)
  Pallas kernels  10.4 us (25%)
  between operations  0.81 us (2%)
    ppermute x17, starting transfers between devices, swap(): return lax.ppermute(value, 'dp', [(i, i ^ bit) for i in range(count)])  16.6 us
    ppermute x17, waiting for transfers between devices, swap(): return lax.ppermute(value, 'dp', [(i, i ^ bit) for i in range(count)])  14.3 us
    pallas_call x1, Pallas kernels, hidden_rows(): pl.pallas_call(hidden_kernel, out_shape=jax.ShapeDtypeStruct((rows, colum...  4.12 us
    pallas_call x1, Pallas kernels, attend(): pl.pallas_call(functools.partial(attend_kernel, plane), out_shape=(jax.Sh...  2.66 us
    pallas_call x1, Pallas kernels, down_rows(): pl.pallas_call(down_kernel, out_shape=[jax.ShapeDtypeStruct((size, width...  2.3 us
  transfers between devices with their start and end apart: 17, of which 8 were waited for; matrix products, arithmetic and copies ran while one was open for 0% of the time, Pallas kernels for 1%

profile of v16, /device:TPU:0, one launch (start us, length us, event | category | flops | bytes accessed | tf_op | source)
XLA Modules:
  0.0 42.2 jit_solution(1046408133610816940)
XLA Ops:
  0.7 2.7 %attend.1 = (bf16[8,4096]{1,0:T(8,128)(2,1)}, bf16[8,3072]{1,0:T(8,128)(2,1)S(1)}, bf16[8,3072]{1,0:T(8,128)(2,1)S(1)}, bf16[8,3072]{1,0:T(8,128)(2,1)S(1)}, bf1...) custom-call(bf16[8,4096]{1,0:T(8,128)(2,1)} %refs_0_.1, ...), custom_call_target="tpu_custom_call" | custom-call | tf_op jit(solution)/shard_map/attend/pallas_call | solution.py:212
  3.3 3.1 %collective-permute-start = (bf16[8,3072]{1,0:T(8,128)(2,1)S(1)}, bf16[8,3072]{1,0:T(8,128)(2,1)S(1)}, u32[]{:S(2)}, u32[]{:S(2)}) collective-permute-start(bf16[8,3072]{1,0:T(8,128)(2,1)S(1)} %get-tuple-element.27), channel_id=1, source_target_pairs={{0,4},{1,5},{2,6},{3,7},{4,0},{5,1},{6,2},{7,3},{8,12},{9,13},{10,... | collective-permute-start | bytes 147464 | tf_op jit(solution)/shard_map/ppermute | solution.py:421
  6.4 2.6 %collective-permute-start.3 = (bf16[8,3072]{1,0:T(8,128)(2,1)S(1)}, bf16[8,3072]{1,0:T(8,128)(2,1)S(1)}, u32[]{:S(2)}, u32[]{:S(2)}) collective-permute-start(bf16[8,3072]{1,0:T(8,128)(2,1)S(1)} %get-tuple-element.28), channel_id=1, source_target_pairs={{0,8},{1,9},{2,10},{3,11},{4,12},{5,13},{6,14},{7,15},{8,0},{9,1},... | collective-permute-start | bytes 147464 | tf_op jit(solution)/shard_map/ppermute | solution.py:421
  9.0 0.0 collective-permute-start.4
  9.0 0.0 collective-permute-done.refs_2_
  9.0 1.8 %collective-permute-start.1 = (bf16[16,3072]{1,0:T(8,128)(2,1)S(1)}, bf16[16,3072]{1,0:T(8,128)(2,1)S(1)}, u32[]{:S(2)}, u32[]{:S(2)}) collective-permute-start(bf16[16,3072]{1,0:T(8,128)(2,1)S(1)} %join.6.refs_1_), channel_id=1, source_target_pairs={{0,2},{1,3},{2,0},{3,1},{4,6},{5,7},{6,4},{7,5},{8,10},{9,11},{10,... | collective-permute-start | bytes 294920 | tf_op jit(solution)/shard_map/ppermute | solution.py:421
  10.8 1.5 %collective-permute-done.3.refs_1_ = bf16[8,3072]{1,0:T(8,128)(2,1)S(1)} collective-permute-done((bf16[8,3072]{1,0:T(8,128)(2,1)S(1)}, bf16[8,3072]{1,0:T(8,128)(2,1)S(1)}, u32[]{:S(2)}, u32[]{:S(2)}) %collective-permute-start.3) | collective-permute-done | bytes 49184 | tf_op jit(solution)/shard_map/ppermute | solution.py:421
  12.3 2.6 %collective-permute-done.4.refs_2_ = bf16[8,3072]{1,0:T(8,128)(2,1)S(1)} collective-permute-done((bf16[8,3072]{1,0:T(8,128)(2,1)S(1)}, bf16[8,3072]{1,0:T(8,128)(2,1)S(1)}, u32[]{:S(2)}, u32[]{:S(2)}) %collective-permute-start.4) | collective-permute-done | bytes 49184 | tf_op jit(solution)/shard_map/ppermute | solution.py:421
  14.9 1.6 %collective-permute-start.5 = (bf16[16,3072]{1,0:T(8,128)(2,1)S(1)}, bf16[16,3072]{1,0:T(8,128)(2,1)S(1)}, u32[]{:S(2)}, u32[]{:S(2)}) collective-permute-start(bf16[16,3072]{1,0:T(8,128)(2,1)S(1)} %join.9.refs_1_), channel_id=1, source_target_pairs={{0,2},{1,3},{2,0},{3,1},{4,6},{5,7},{6,4},{7,5},{8,10},{9,11},{10,... | collective-permute-start | bytes 294920 | tf_op jit(solution)/shard_map/ppermute | solution.py:421
  16.5 0.0 collective-permute-done.1.refs_2_
  16.5 0.1 collective-permute-start.2
  16.6 3.0 %collective-permute-done.5.refs_2_ = bf16[16,3072]{1,0:T(8,128)(2,1)S(1)} collective-permute-done((bf16[16,3072]{1,0:T(8,128)(2,1)S(1)}, bf16[16,3072]{1,0:T(8,128)(2,1)S(1)}, u32[]{:S(2)}, u32[]{:S(2)}) %collective-permute-start.5) | collective-permute-done | bytes 98336 | tf_op jit(solution)/shard_map/ppermute | solution.py:421
  19.6 0.1 collective-permute-start.6
  19.7 1.4 %collective-permute-done.6.refs_2_ = bf16[32,3072]{1,0:T(8,128)(2,1)S(1)} collective-permute-done((bf16[32,3072]{1,0:T(8,128)(2,1)S(1)}, bf16[32,3072]{1,0:T(8,128)(2,1)S(1)}, u32[]{:S(2)}, u32[]{:S(2)}) %collective-permute-start.6) | collective-permute-done | bytes 196640 | tf_op jit(solution)/shard_map/ppermute | solution.py:421
  21.2 4.1 %hidden.1 = bf16[128,1792]{1,0:T(8,128)(2,1)S(1)} custom-call(bf16[4096,1792]{1,0:T(8,128)(2,1)S(1)} %copy-done.1, bf16[4096,1792]{1,0:T(8,128)(2,1)S(1)} %copy-done.2, bf16[1792,4096]{1,0:T(8,128)(2,1)S(1)} %copy-done, bf16[64,3072]{1,0:T(8,128)(2,1)S(1)} %join.8.refs_0_, bf16[64,3072]{1,0:T(8,128)(2,1)S(1)} %join.11.refs_1_), custom_call_target="tpu_custom_call" | custom-call | flops 3758096384 | tf_op jit(solution)/shard_map/hidden/pallas_call | solution.py:262
  25.3 2.3 %down.1 = (bf16[32,3072]{1,0:T(8,128)(2,1)S(1)}, bf16[32,3072]{1,0:T(8,128)(2,1)S(1)}, bf16[16,3072]{1,0:T(8,128)(2,1)S(1)}, bf16[16,3072]{1,0:T(8,128)(2,1)S(1)...) custom-call(bf16[128,1792]{1,0:T(8,128)(2,1)S(1)} %hidden.1, bf16[1792,4096]{1,0:T(8,128)(2,1)S(1)} %copy-done), custom_call_target="tpu_custom_call" | custom-call | flops 1879048192 | tf_op jit(solution)/shard_map/down/pallas_call | solution.py:313
  27.6 0.2 collective-permute-start.7
  27.8 0.4 collective-permute-start.9
  28.2 0.1 collective-permute-start.8
  28.3 0.9 %collective-permute-done.9.arrived = bf16[16,3072]{1,0:T(8,128)(2,1)S(1)} collective-permute-done((bf16[16,3072]{1,0:T(8,128)(2,1)S(1)}, bf16[16,3072]{1,0:T(8,128)(2,1)S(1)}, u32[]{:S(2)}, u32[]{:S(2)}) %collective-permute-start.9) | collective-permute-done | bytes 98336 | tf_op jit(solution)/shard_map/ppermute | solution.py:421
  29.3 1.6 %collective-permute-start.13 = (bf16[8,3072]{1,0:T(8,128)(2,1)S(1)}, bf16[8,3072]{1,0:T(8,128)(2,1)S(1)}, u32[]{:S(2)}, u32[]{:S(2)}) collective-permute-start(bf16[8,3072]{1,0:T(8,128)(2,1)S(1)} %get-tuple-element.43), channel_id=1, source_target_pairs={{0,2},{1,3},{2,0},{3,1},{4,6},{5,7},{6,4},{7,5},{8,10},{9,11},{10,... | collective-permute-start | bytes 147464 | tf_op jit(solution)/shard_map/ppermute | solution.py:421
  30.9 0.6 %collective-permute-start.12 = (bf16[8,3072]{1,0:T(8,128)(2,1)S(1)}, bf16[8,3072]{1,0:T(8,128)(2,1)S(1)}, u32[]{:S(2)}, u32[]{:S(2)}) collective-permute-start(bf16[8,3072]{1,0:T(8,128)(2,1)S(1)} %get-tuple-element.42), channel_id=1, source_target_pairs={{0,2},{1,3},{2,0},{3,1},{4,6},{5,7},{6,4},{7,5},{8,10},{9,11},{10,... | collective-permute-start | bytes 147464 | tf_op jit(solution)/shard_map/ppermute | solution.py:421
  31.5 1.6 %collective-permute-start.11 = (bf16[8,3072]{1,0:T(8,128)(2,1)S(1)}, bf16[8,3072]{1,0:T(8,128)(2,1)S(1)}, u32[]{:S(2)}, u32[]{:S(2)}) collective-permute-start(bf16[8,3072]{1,0:T(8,128)(2,1)S(1)} %get-tuple-element.41), channel_id=1, source_target_pairs={{0,2},{1,3},{2,0},{3,1},{4,6},{5,7},{6,4},{7,5},{8,10},{9,11},{10,... | collective-permute-start | bytes 147464 | tf_op jit(solution)/shard_map/ppermute | solution.py:421
  33.1 0.5 %collective-permute-start.10 = (bf16[8,3072]{1,0:T(8,128)(2,1)S(1)}, bf16[8,3072]{1,0:T(8,128)(2,1)S(1)}, u32[]{:S(2)}, u32[]{:S(2)}) collective-permute-start(bf16[8,3072]{1,0:T(8,128)(2,1)S(1)} %get-tuple-element.39), channel_id=1, source_target_pairs={{0,2},{1,3},{2,0},{3,1},{4,6},{5,7},{6,4},{7,5},{8,10},{9,11},{10,... | collective-permute-start | bytes 147464 | tf_op jit(solution)/shard_map/ppermute | solution.py:421
  33.6 0.4 %collective-permute-start.15 = (bf16[8,3072]{1,0:T(8,128)(2,1)S(1)}, bf16[8,3072]{1,0:T(8,128)(2,1)S(1)}, u32[]{:S(2)}, u32[]{:S(2)}) collective-permute-start(bf16[8,3072]{1,0:T(8,128)(2,1)S(1)} %fold.10.after), channel_id=1, source_target_pairs={{0,8},{1,9},{2,10},{3,11},{4,12},{5,13},{6,14},{7,15},{8,0},{9,1},... | collective-permute-start | bytes 147464 | tf_op jit(solution)/shard_map/ppermute | solution.py:421
  34.1 1.0 %collective-permute-done.12.arrived = bf16[8,3072]{1,0:T(8,128)(2,1)S(1)} collective-permute-done((bf16[8,3072]{1,0:T(8,128)(2,1)S(1)}, bf16[8,3072]{1,0:T(8,128)(2,1)S(1)}, u32[]{:S(2)}, u32[]{:S(2)}) %collective-permute-start.12) | collective-permute-done | bytes 49184 | tf_op jit(solution)/shard_map/ppermute | solution.py:421
  35.1 0.8 %collective-permute-start.16 = (bf16[8,3072]{1,0:T(8,128)(2,1)S(1)}, bf16[8,3072]{1,0:T(8,128)(2,1)S(1)}, u32[]{:S(2)}, u32[]{:S(2)}) collective-permute-start(bf16[8,3072]{1,0:T(8,128)(2,1)S(1)} %fold.11.after), channel_id=1, source_target_pairs={{0,12},{1,13},{2,14},{3,15},{4,8},{5,9},{6,10},{7,11},{8,4},{9,5},... | collective-permute-start | bytes 147464 | tf_op jit(solution)/shard_map/ppermute | solution.py:421
  35.9 0.2 collective-permute-done.11.arrived
  36.2 1.2 %collective-permute-start.14 = (bf16[8,3072]{1,0:T(8,128)(2,1)S(1)}, bf16[8,3072]{1,0:T(8,128)(2,1)S(1)}, u32[]{:S(2)}, u32[]{:S(2)}) collective-permute-start(bf16[8,3072]{1,0:T(8,128)(2,1)S(1)} %fold.12.after), channel_id=1, source_target_pairs={{0,4},{1,5},{2,6},{3,7},{4,0},{5,1},{6,2},{7,3},{8,12},{9,13},{10,... | collective-permute-start | bytes 147464 | tf_op jit(solution)/shard_map/ppermute | solution.py:421
  37.4 3.7 %collective-permute-done.16.three = bf16[8,3072]{1,0:T(8,128)(2,1)S(1)} collective-permute-done((bf16[8,3072]{1,0:T(8,128)(2,1)S(1)}, bf16[8,3072]{1,0:T(8,128)(2,1)S(1)}, u32[]{:S(2)}, u32[]{:S(2)}) %collective-permute-start.16) | collective-permute-done | bytes 49184 | tf_op jit(solution)/shard_map/ppermute | solution.py:421
  41.1 0.2 combine_far.1.total
  41.3 0.8 %combine.1 = bf16[8,4096]{1,0:T(8,128)(2,1)} custom-call(f32[16,128]{1,0:T(8,128)S(1)} %get-tuple-element.24.refs_0_.after.share, bf16[4,16,128]{2,1,0:T(8,128)(2,1)S(1)} %get-tuple-element.25.take, bf16[8,3072]{1,0:T(8,128)(2,1)S(1)} %fold.13.zero, bf16[8,3072]{1,0:T(8,128)(2,1)S(1)} %collective-permute-done.14.one, f32[8,4096]{1,0:T(8,128)S(1)} %combine_far.1.total), custom_call_target="tpu_custom_call" | custom-call | bytes 16777216 | tf_op jit(solution)/shard_map/combine/pallas_call | solution.py:408
  (26 shorter events, 0.3 us)
Async XLA Ops:
  0.6 20.5 %copy-start = (bf16[1792,4096]{1,0:T(8,128)(2,1)S(1)}, bf16[1792,4096]{1,0:T(8,128)(2,1)}, u32[]{:S(2)}) copy-start(bf16[1792,4096]{1,0:T(8,128)(2,1)} %weight.1) | copy-start | bytes 44040196
  0.6 20.5 %copy-start.1 = (bf16[4096,1792]{1,0:T(8,128)(2,1)S(1)}, bf16[4096,1792]{1,0:T(8,128)(2,1)}, u32[]{:S(2)}) copy-start(bf16[4096,1792]{1,0:T(8,128)(2,1)} %gate_weight.1) | copy-start | bytes 44040196
  0.7 20.5 %copy-start.2 = (bf16[4096,1792]{1,0:T(8,128)(2,1)S(1)}, bf16[4096,1792]{1,0:T(8,128)(2,1)}, u32[]{:S(2)}) copy-start(bf16[4096,1792]{1,0:T(8,128)(2,1)} %up_weight.1) | copy-start | bytes 44040196
  3.3 5.7 %collective-permute-start = (bf16[8,3072]{1,0:T(8,128)(2,1)S(1)}, bf16[8,3072]{1,0:T(8,128)(2,1)S(1)}, u32[]{:S(2)}, u32[]{:S(2)}) collective-permute-start(bf16[8,3072]{1,0:T(8,128)(2,1)S(1)} %get-tuple-element.27), channel_id=1, source_target_pairs={{0,4},{1,5},{2,6},{3,7},{4,0},{5,1},{6,2},{7,3},{8,12},{9,13},{10,... | collective-permute-start | bytes 147464 | tf_op jit(solution)/shard_map/ppermute | solution.py:421
  6.4 5.9 %collective-permute-start.3 = (bf16[8,3072]{1,0:T(8,128)(2,1)S(1)}, bf16[8,3072]{1,0:T(8,128)(2,1)S(1)}, u32[]{:S(2)}, u32[]{:S(2)}) collective-permute-start(bf16[8,3072]{1,0:T(8,128)(2,1)S(1)} %get-tuple-element.28), channel_id=1, source_target_pairs={{0,8},{1,9},{2,10},{3,11},{4,12},{5,13},{6,14},{7,15},{8,0},{9,1},... | collective-permute-start | bytes 147464 | tf_op jit(solution)/shard_map/ppermute | solution.py:421
  9.0 5.9 %collective-permute-start.4 = (bf16[8,3072]{1,0:T(8,128)(2,1)S(1)}, bf16[8,3072]{1,0:T(8,128)(2,1)S(1)}, u32[]{:S(2)}, u32[]{:S(2)}) collective-permute-start(bf16[8,3072]{1,0:T(8,128)(2,1)S(1)} %get-tuple-element.29), channel_id=1, source_target_pairs={{0,12},{1,13},{2,14},{3,15},{4,8},{5,9},{6,10},{7,11},{8,4},{9,5},... | collective-permute-start | bytes 147464 | tf_op jit(solution)/shard_map/ppermute | solution.py:421
  9.0 7.5 %collective-permute-start.1 = (bf16[16,3072]{1,0:T(8,128)(2,1)S(1)}, bf16[16,3072]{1,0:T(8,128)(2,1)S(1)}, u32[]{:S(2)}, u32[]{:S(2)}) collective-permute-start(bf16[16,3072]{1,0:T(8,128)(2,1)S(1)} %join.6.refs_1_), channel_id=1, source_target_pairs={{0,2},{1,3},{2,0},{3,1},{4,6},{5,7},{6,4},{7,5},{8,10},{9,11},{10,... | collective-permute-start | bytes 294920 | tf_op jit(solution)/shard_map/ppermute | solution.py:421
  14.9 4.7 %collective-permute-start.5 = (bf16[16,3072]{1,0:T(8,128)(2,1)S(1)}, bf16[16,3072]{1,0:T(8,128)(2,1)S(1)}, u32[]{:S(2)}, u32[]{:S(2)}) collective-permute-start(bf16[16,3072]{1,0:T(8,128)(2,1)S(1)} %join.9.refs_1_), channel_id=1, source_target_pairs={{0,2},{1,3},{2,0},{3,1},{4,6},{5,7},{6,4},{7,5},{8,10},{9,11},{10,... | collective-permute-start | bytes 294920 | tf_op jit(solution)/shard_map/ppermute | solution.py:421
  16.5 3.2 %collective-permute-start.2 = (bf16[32,3072]{1,0:T(8,128)(2,1)S(1)}, bf16[32,3072]{1,0:T(8,128)(2,1)S(1)}, u32[]{:S(2)}, u32[]{:S(2)}) collective-permute-start(bf16[32,3072]{1,0:T(8,128)(2,1)S(1)} %join.7.refs_1_), channel_id=1, source_target_pairs={{0,1},{1,0},{2,3},{3,2},{4,5},{5,4},{6,7},{7,6},{8,9},{9,8},{10,11... | collective-permute-start | bytes 589832 | tf_op jit(solution)/shard_map/ppermute | solution.py:421
  19.6 1.5 %collective-permute-start.6 = (bf16[32,3072]{1,0:T(8,128)(2,1)S(1)}, bf16[32,3072]{1,0:T(8,128)(2,1)S(1)}, u32[]{:S(2)}, u32[]{:S(2)}) collective-permute-start(bf16[32,3072]{1,0:T(8,128)(2,1)S(1)} %join.10.refs_1_), channel_id=1, source_target_pairs={{0,1},{1,0},{2,3},{3,2},{4,5},{5,4},{6,7},{7,6},{8,9},{9,8},{10,11... | collective-permute-start | bytes 589832 | tf_op jit(solution)/shard_map/ppermute | solution.py:421
  27.6 3.9 %collective-permute-start.7 = (bf16[32,3072]{1,0:T(8,128)(2,1)S(1)}, bf16[32,3072]{1,0:T(8,128)(2,1)S(1)}, u32[]{:S(2)}, u32[]{:S(2)}) collective-permute-start(bf16[32,3072]{1,0:T(8,128)(2,1)S(1)} %get-tuple-element.31), channel_id=1, source_target_pairs={{0,1},{1,0},{2,3},{3,2},{4,5},{5,4},{6,7},{7,6},{8,9},{9,8},{10,11... | collective-permute-start | bytes 589832 | tf_op jit(solution)/shard_map/ppermute | solution.py:421
  27.8 1.4 %collective-permute-start.9 = (bf16[16,3072]{1,0:T(8,128)(2,1)S(1)}, bf16[16,3072]{1,0:T(8,128)(2,1)S(1)}, u32[]{:S(2)}, u32[]{:S(2)}) collective-permute-start(bf16[16,3072]{1,0:T(8,128)(2,1)S(1)} %get-tuple-element.35), channel_id=1, source_target_pairs={{0,1},{1,0},{2,3},{3,2},{4,5},{5,4},{6,7},{7,6},{8,9},{9,8},{10,11... | collective-permute-start | bytes 294920 | tf_op jit(solution)/shard_map/ppermute | solution.py:421
  28.2 2.7 %collective-permute-start.8 = (bf16[16,3072]{1,0:T(8,128)(2,1)S(1)}, bf16[16,3072]{1,0:T(8,128)(2,1)S(1)}, u32[]{:S(2)}, u32[]{:S(2)}) collective-permute-start(bf16[16,3072]{1,0:T(8,128)(2,1)S(1)} %get-tuple-element.33), channel_id=1, source_target_pairs={{0,1},{1,0},{2,3},{3,2},{4,5},{5,4},{6,7},{7,6},{8,9},{9,8},{10,11... | collective-permute-start | bytes 294920 | tf_op jit(solution)/shard_map/ppermute | solution.py:421
  29.3 4.3 %collective-permute-start.13 = (bf16[8,3072]{1,0:T(8,128)(2,1)S(1)}, bf16[8,3072]{1,0:T(8,128)(2,1)S(1)}, u32[]{:S(2)}, u32[]{:S(2)}) collective-permute-start(bf16[8,3072]{1,0:T(8,128)(2,1)S(1)} %get-tuple-element.43), channel_id=1, source_target_pairs={{0,2},{1,3},{2,0},{3,1},{4,6},{5,7},{6,4},{7,5},{8,10},{9,11},{10,... | collective-permute-start | bytes 147464 | tf_op jit(solution)/shard_map/ppermute | solution.py:421
  30.9 4.2 %collective-permute-start.12 = (bf16[8,3072]{1,0:T(8,128)(2,1)S(1)}, bf16[8,3072]{1,0:T(8,128)(2,1)S(1)}, u32[]{:S(2)}, u32[]{:S(2)}) collective-permute-start(bf16[8,3072]{1,0:T(8,128)(2,1)S(1)} %get-tuple-element.42), channel_id=1, source_target_pairs={{0,2},{1,3},{2,0},{3,1},{4,6},{5,7},{6,4},{7,5},{8,10},{9,11},{10,... | collective-permute-start | bytes 147464 | tf_op jit(solution)/shard_map/ppermute | solution.py:421
  31.5 4.6 %collective-permute-start.11 = (bf16[8,3072]{1,0:T(8,128)(2,1)S(1)}, bf16[8,3072]{1,0:T(8,128)(2,1)S(1)}, u32[]{:S(2)}, u32[]{:S(2)}) collective-permute-start(bf16[8,3072]{1,0:T(8,128)(2,1)S(1)} %get-tuple-element.41), channel_id=1, source_target_pairs={{0,2},{1,3},{2,0},{3,1},{4,6},{5,7},{6,4},{7,5},{8,10},{9,11},{10,... | collective-permute-start | bytes 147464 | tf_op jit(solution)/shard_map/ppermute | solution.py:421
  33.1 4.3 %collective-permute-start.10 = (bf16[8,3072]{1,0:T(8,128)(2,1)S(1)}, bf16[8,3072]{1,0:T(8,128)(2,1)S(1)}, u32[]{:S(2)}, u32[]{:S(2)}) collective-permute-start(bf16[8,3072]{1,0:T(8,128)(2,1)S(1)} %get-tuple-element.39), channel_id=1, source_target_pairs={{0,2},{1,3},{2,0},{3,1},{4,6},{5,7},{6,4},{7,5},{8,10},{9,11},{10,... | collective-permute-start | bytes 147464 | tf_op jit(solution)/shard_map/ppermute | solution.py:421
  33.6 7.4 %collective-permute-start.15 = (bf16[8,3072]{1,0:T(8,128)(2,1)S(1)}, bf16[8,3072]{1,0:T(8,128)(2,1)S(1)}, u32[]{:S(2)}, u32[]{:S(2)}) collective-permute-start(bf16[8,3072]{1,0:T(8,128)(2,1)S(1)} %fold.10.after), channel_id=1, source_target_pairs={{0,8},{1,9},{2,10},{3,11},{4,12},{5,13},{6,14},{7,15},{8,0},{9,1},... | collective-permute-start | bytes 147464 | tf_op jit(solution)/shard_map/ppermute | solution.py:421
  35.1 6.0 %collective-permute-start.16 = (bf16[8,3072]{1,0:T(8,128)(2,1)S(1)}, bf16[8,3072]{1,0:T(8,128)(2,1)S(1)}, u32[]{:S(2)}, u32[]{:S(2)}) collective-permute-start(bf16[8,3072]{1,0:T(8,128)(2,1)S(1)} %fold.11.after), channel_id=1, source_target_pairs={{0,12},{1,13},{2,14},{3,15},{4,8},{5,9},{6,10},{7,11},{8,4},{9,5},... | collective-permute-start | bytes 147464 | tf_op jit(solution)/shard_map/ppermute | solution.py:421
  36.2 5.2 %collective-permute-start.14 = (bf16[8,3072]{1,0:T(8,128)(2,1)S(1)}, bf16[8,3072]{1,0:T(8,128)(2,1)S(1)}, u32[]{:S(2)}, u32[]{:S(2)}) collective-permute-start(bf16[8,3072]{1,0:T(8,128)(2,1)S(1)} %fold.12.after), channel_id=1, source_target_pairs={{0,4},{1,5},{2,6},{3,7},{4,0},{5,1},{6,2},{7,3},{8,12},{9,13},{10,... | collective-permute-start | bytes 147464 | tf_op jit(solution)/shard_map/ppermute | solution.py:421

commit v17 on v16

--- a/solution.py
+++ b/solution.py
@@ -300,10 +300,16 @@
 
 
 def ways_back(places):
-    near = [2 * p + j for high in range(0, places, 2) for j in (0, 1) for p in (high, high + 1)]
-    two = [2 * places + 2 * p for p in range(places)]
-    three = [b + 1 for b in two]
-    return [half for w in (near, two, three) for half in (w[: len(w) // 2], w[len(w) // 2 :])]
+    halves = []
+    for w in (0, 1):
+        groups = [
+            2 * places * w + 2 * p + j
+            for high in range(0, places, 2)
+            for j in (0, 1)
+            for p in (high, high + 1)
+        ]
+        halves += [groups[:places], groups[places:]]
+    return halves
 
 
 def down_rows(hidden, weight):
@@ -321,7 +327,7 @@
         ),
         name="down",
     )(hidden, weight)
-    return outs[0:2], outs[2:4], outs[4:6]
+    return outs[0:2], outs[2:4]
 
 
 def join_kernel(*refs):
@@ -451,7 +457,7 @@
 
     hidden = hidden_rows(waves, gate_weight, up_weight, down_weight)
 
-    near, two, three = down_rows(hidden, down_weight)
+    near, far = down_rows(hidden, down_weight)
 
     def back(wave, stage, after, parts=2):
         return fold(wave[0], swap(wave[1], count, bits[-1 - stage]), after, parts)
@@ -459,12 +465,12 @@
     last = len(bits) - 1
     token = share
     for stage in range(last):
-        two = back(two, stage, token)
-        three = back(three, stage, two[0])
-        token = three[0]
-        near = back(near, stage, token, 4 if stage == last - 1 else 2)
-    two = back(two, last, near[0], 1)
-    three = back(three, last, two[0], 1)
+        parts = 4 if stage == last - 1 else 2
+        far = back(far, stage, token, parts)
+        near = back(near, stage, far[0], parts)
+        token = near[0]
+    two = back(far[0:2], last, token, 1)
+    three = back(far[2:4], last, two[0], 1)
     one = back(near[2:4], last, three[0], 1)
     zero = back(near[0:2], last, one[0], 1)
     results = [

time: 42.3 us -> 42.3 us (level)
    ppermute x17 -> x16, starting transfers between devices: 16.6 us -> 16.5 us  [swap(): return lax.ppermute(value, 'dp', [(i, i ^ bit) for i in range(count)])]
    ppermute x17 -> x16, waiting for transfers between devices: 14.3 us -> 14.4 us  [swap(): return lax.ppermute(value, 'dp', [(i, i ^ bit) for i in range(count)])]
  transfers between devices with their start and end apart: 17 -> 16, of which waited for: 8 -> 8; matrix products, arithmetic and copies ran while one was open for 0% -> 0% of each run, Pallas kernels for 1% -> 1%
where the time goes in v17:
time: 42.3 us; the launch traced here: 42.2 us
  starting transfers between devices  16.5 us (39%)
  waiting for transfers between devices  14.4 us (34%)
  Pallas kernels  10.4 us (25%)
  between operations  0.8 us (2%)
    ppermute x16, starting transfers between devices, swap(): return lax.ppermute(value, 'dp', [(i, i ^ bit) for i in range(count)])  16.5 us
    ppermute x16, waiting for transfers between devices, swap(): return lax.ppermute(value, 'dp', [(i, i ^ bit) for i in range(count)])  14.4 us
    pallas_call x1, Pallas kernels, hidden_rows(): pl.pallas_call(hidden_kernel, out_shape=jax.ShapeDtypeStruct((rows, colum...  4.12 us
    pallas_call x1, Pallas kernels, attend(): pl.pallas_call(functools.partial(attend_kernel, plane), out_shape=(jax.Sh...  2.66 us
    pallas_call x1, Pallas kernels, down_rows(): pl.pallas_call(down_kernel, out_shape=[jax.ShapeDtypeStruct((size, width...  2.3 us
  transfers between devices with their start and end apart: 16, of which 8 were waited for; matrix products, arithmetic and copies ran while one was open for 0% of the time, Pallas kernels for 1%

profile of v17, /device:TPU:0, one launch (start us, length us, event | category | flops | bytes accessed | tf_op | source)
XLA Modules:
  0.0 42.2 jit_solution(17089309360101729568)
XLA Ops:
  0.7 2.7 %attend.1 = (bf16[8,4096]{1,0:T(8,128)(2,1)}, bf16[8,3072]{1,0:T(8,128)(2,1)S(1)}, bf16[8,3072]{1,0:T(8,128)(2,1)S(1)}, bf16[8,3072]{1,0:T(8,128)(2,1)S(1)}, bf1...) custom-call(bf16[8,4096]{1,0:T(8,128)(2,1)} %refs_0_.1, ...), custom_call_target="tpu_custom_call" | custom-call | tf_op jit(solution)/shard_map/attend/pallas_call | solution.py:212
  3.3 3.1 %collective-permute-start = (bf16[8,3072]{1,0:T(8,128)(2,1)S(1)}, bf16[8,3072]{1,0:T(8,128)(2,1)S(1)}, u32[]{:S(2)}, u32[]{:S(2)}) collective-permute-start(bf16[8,3072]{1,0:T(8,128)(2,1)S(1)} %get-tuple-element.25), channel_id=1, source_target_pairs={{0,4},{1,5},{2,6},{3,7},{4,0},{5,1},{6,2},{7,3},{8,12},{9,13},{10,... | collective-permute-start | bytes 147464 | tf_op jit(solution)/shard_map/ppermute | solution.py:427
  6.4 2.6 %collective-permute-start.3 = (bf16[8,3072]{1,0:T(8,128)(2,1)S(1)}, bf16[8,3072]{1,0:T(8,128)(2,1)S(1)}, u32[]{:S(2)}, u32[]{:S(2)}) collective-permute-start(bf16[8,3072]{1,0:T(8,128)(2,1)S(1)} %get-tuple-element.26), channel_id=1, source_target_pairs={{0,8},{1,9},{2,10},{3,11},{4,12},{5,13},{6,14},{7,15},{8,0},{9,1},... | collective-permute-start | bytes 147464 | tf_op jit(solution)/shard_map/ppermute | solution.py:427
  9.0 0.0 collective-permute-start.4
  9.0 0.0 collective-permute-done.refs_2_
  9.0 1.8 %collective-permute-start.1 = (bf16[16,3072]{1,0:T(8,128)(2,1)S(1)}, bf16[16,3072]{1,0:T(8,128)(2,1)S(1)}, u32[]{:S(2)}, u32[]{:S(2)}) collective-permute-start(bf16[16,3072]{1,0:T(8,128)(2,1)S(1)} %join.6.refs_1_), channel_id=1, source_target_pairs={{0,2},{1,3},{2,0},{3,1},{4,6},{5,7},{6,4},{7,5},{8,10},{9,11},{10,... | collective-permute-start | bytes 294920 | tf_op jit(solution)/shard_map/ppermute | solution.py:427
  10.8 1.5 %collective-permute-done.3.refs_1_ = bf16[8,3072]{1,0:T(8,128)(2,1)S(1)} collective-permute-done((bf16[8,3072]{1,0:T(8,128)(2,1)S(1)}, bf16[8,3072]{1,0:T(8,128)(2,1)S(1)}, u32[]{:S(2)}, u32[]{:S(2)}) %collective-permute-start.3) | collective-permute-done | bytes 49184 | tf_op jit(solution)/shard_map/ppermute | solution.py:427
  12.3 2.6 %collective-permute-done.4.refs_2_ = bf16[8,3072]{1,0:T(8,128)(2,1)S(1)} collective-permute-done((bf16[8,3072]{1,0:T(8,128)(2,1)S(1)}, bf16[8,3072]{1,0:T(8,128)(2,1)S(1)}, u32[]{:S(2)}, u32[]{:S(2)}) %collective-permute-start.4) | collective-permute-done | bytes 49184 | tf_op jit(solution)/shard_map/ppermute | solution.py:427
  14.9 1.6 %collective-permute-start.5 = (bf16[16,3072]{1,0:T(8,128)(2,1)S(1)}, bf16[16,3072]{1,0:T(8,128)(2,1)S(1)}, u32[]{:S(2)}, u32[]{:S(2)}) collective-permute-start(bf16[16,3072]{1,0:T(8,128)(2,1)S(1)} %join.9.refs_1_), channel_id=1, source_target_pairs={{0,2},{1,3},{2,0},{3,1},{4,6},{5,7},{6,4},{7,5},{8,10},{9,11},{10,... | collective-permute-start | bytes 294920 | tf_op jit(solution)/shard_map/ppermute | solution.py:427
  16.5 0.0 collective-permute-done.1.refs_2_
  16.5 0.1 collective-permute-start.2
  16.6 3.0 %collective-permute-done.5.refs_2_ = bf16[16,3072]{1,0:T(8,128)(2,1)S(1)} collective-permute-done((bf16[16,3072]{1,0:T(8,128)(2,1)S(1)}, bf16[16,3072]{1,0:T(8,128)(2,1)S(1)}, u32[]{:S(2)}, u32[]{:S(2)}) %collective-permute-start.5) | collective-permute-done | bytes 98336 | tf_op jit(solution)/shard_map/ppermute | solution.py:427
  19.6 0.1 collective-permute-start.6
  19.7 1.4 %collective-permute-done.6.refs_2_ = bf16[32,3072]{1,0:T(8,128)(2,1)S(1)} collective-permute-done((bf16[32,3072]{1,0:T(8,128)(2,1)S(1)}, bf16[32,3072]{1,0:T(8,128)(2,1)S(1)}, u32[]{:S(2)}, u32[]{:S(2)}) %collective-permute-start.6) | collective-permute-done | bytes 196640 | tf_op jit(solution)/shard_map/ppermute | solution.py:427
  21.2 4.1 %hidden.1 = bf16[128,1792]{1,0:T(8,128)(2,1)S(1)} custom-call(bf16[4096,1792]{1,0:T(8,128)(2,1)S(1)} %copy-done.1, bf16[4096,1792]{1,0:T(8,128)(2,1)S(1)} %copy-done.2, bf16[1792,4096]{1,0:T(8,128)(2,1)S(1)} %copy-done, bf16[64,3072]{1,0:T(8,128)(2,1)S(1)} %join.8.refs_0_, bf16[64,3072]{1,0:T(8,128)(2,1)S(1)} %join.11.refs_1_), custom_call_target="tpu_custom_call" | custom-call | flops 3758096384 | tf_op jit(solution)/shard_map/hidden/pallas_call | solution.py:262
  25.3 2.3 %down.1 = (bf16[32,3072]{1,0:T(8,128)(2,1)S(1)}, bf16[32,3072]{1,0:T(8,128)(2,1)S(1)}, bf16[32,3072]{1,0:T(8,128)(2,1)S(1)}, bf16[32,3072]{1,0:T(8,128)(2,1)S(1)}) custom-call(bf16[128,1792]{1,0:T(8,128)(2,1)S(1)} %hidden.1, bf16[1792,4096]{1,0:T(8,128)(2,1)S(1)} %copy-done), custom_call_target="tpu_custom_call" | custom-call | flops 1879048192 | tf_op jit(solution)/shard_map/down/pallas_call | solution.py:319
  27.6 0.2 collective-permute-start.8
  27.8 0.4 collective-permute-start.7
  28.2 0.9 %collective-permute-done.8.arrived = bf16[32,3072]{1,0:T(8,128)(2,1)S(1)} collective-permute-done((bf16[32,3072]{1,0:T(8,128)(2,1)S(1)}, bf16[32,3072]{1,0:T(8,128)(2,1)S(1)}, u32[]{:S(2)}, u32[]{:S(2)}) %collective-permute-start.8) | collective-permute-done | bytes 196640 | tf_op jit(solution)/shard_map/ppermute | solution.py:427
  29.2 1.6 %collective-permute-start.12 = (bf16[8,3072]{1,0:T(8,128)(2,1)S(1)}, bf16[8,3072]{1,0:T(8,128)(2,1)S(1)}, u32[]{:S(2)}, u32[]{:S(2)}) collective-permute-start(bf16[8,3072]{1,0:T(8,128)(2,1)S(1)} %get-tuple-element.39), channel_id=1, source_target_pairs={{0,2},{1,3},{2,0},{3,1},{4,6},{5,7},{6,4},{7,5},{8,10},{9,11},{10,... | collective-permute-start | bytes 147464 | tf_op jit(solution)/shard_map/ppermute | solution.py:427
  30.8 0.5 %collective-permute-start.11 = (bf16[8,3072]{1,0:T(8,128)(2,1)S(1)}, bf16[8,3072]{1,0:T(8,128)(2,1)S(1)}, u32[]{:S(2)}, u32[]{:S(2)}) collective-permute-start(bf16[8,3072]{1,0:T(8,128)(2,1)S(1)} %get-tuple-element.38), channel_id=1, source_target_pairs={{0,2},{1,3},{2,0},{3,1},{4,6},{5,7},{6,4},{7,5},{8,10},{9,11},{10,... | collective-permute-start | bytes 147464 | tf_op jit(solution)/shard_map/ppermute | solution.py:427
  31.3 1.6 %collective-permute-start.10 = (bf16[8,3072]{1,0:T(8,128)(2,1)S(1)}, bf16[8,3072]{1,0:T(8,128)(2,1)S(1)}, u32[]{:S(2)}, u32[]{:S(2)}) collective-permute-start(bf16[8,3072]{1,0:T(8,128)(2,1)S(1)} %get-tuple-element.36), channel_id=1, source_target_pairs={{0,2},{1,3},{2,0},{3,1},{4,6},{5,7},{6,4},{7,5},{8,10},{9,11},{10,... | collective-permute-start | bytes 147464 | tf_op jit(solution)/shard_map/ppermute | solution.py:427
  32.9 0.5 %collective-permute-start.9 = (bf16[8,3072]{1,0:T(8,128)(2,1)S(1)}, bf16[8,3072]{1,0:T(8,128)(2,1)S(1)}, u32[]{:S(2)}, u32[]{:S(2)}) collective-permute-start(bf16[8,3072]{1,0:T(8,128)(2,1)S(1)} %get-tuple-element.34), channel_id=1, source_target_pairs={{0,2},{1,3},{2,0},{3,1},{4,6},{5,7},{6,4},{7,5},{8,10},{9,11},{10,... | collective-permute-start | bytes 147464 | tf_op jit(solution)/shard_map/ppermute | solution.py:427
  33.4 0.1 collective-permute-done.12.arrived
  33.5 0.4 %collective-permute-start.14 = (bf16[8,3072]{1,0:T(8,128)(2,1)S(1)}, bf16[8,3072]{1,0:T(8,128)(2,1)S(1)}, u32[]{:S(2)}, u32[]{:S(2)}) collective-permute-start(bf16[8,3072]{1,0:T(8,128)(2,1)S(1)} %fold.8.after), channel_id=1, source_target_pairs={{0,8},{1,9},{2,10},{3,11},{4,12},{5,13},{6,14},{7,15},{8,0},{9,1},... | collective-permute-start | bytes 147464 | tf_op jit(solution)/shard_map/ppermute | solution.py:427
  34.0 1.1 %collective-permute-done.11.arrived = bf16[8,3072]{1,0:T(8,128)(2,1)S(1)} collective-permute-done((bf16[8,3072]{1,0:T(8,128)(2,1)S(1)}, bf16[8,3072]{1,0:T(8,128)(2,1)S(1)}, u32[]{:S(2)}, u32[]{:S(2)}) %collective-permute-start.11) | collective-permute-done | bytes 49184 | tf_op jit(solution)/shard_map/ppermute | solution.py:427
  35.1 0.8 %collective-permute-start.15 = (bf16[8,3072]{1,0:T(8,128)(2,1)S(1)}, bf16[8,3072]{1,0:T(8,128)(2,1)S(1)}, u32[]{:S(2)}, u32[]{:S(2)}) collective-permute-start(bf16[8,3072]{1,0:T(8,128)(2,1)S(1)} %fold.9.after), channel_id=1, source_target_pairs={{0,12},{1,13},{2,14},{3,15},{4,8},{5,9},{6,10},{7,11},{8,4},{9,5},... | collective-permute-start | bytes 147464 | tf_op jit(solution)/shard_map/ppermute | solution.py:427
  35.9 0.0 collective-permute-done.10.arrived
  36.0 1.3 %collective-permute-start.13 = (bf16[8,3072]{1,0:T(8,128)(2,1)S(1)}, bf16[8,3072]{1,0:T(8,128)(2,1)S(1)}, u32[]{:S(2)}, u32[]{:S(2)}) collective-permute-start(bf16[8,3072]{1,0:T(8,128)(2,1)S(1)} %fold.10.after), channel_id=1, source_target_pairs={{0,4},{1,5},{2,6},{3,7},{4,0},{5,1},{6,2},{7,3},{8,12},{9,13},{10,... | collective-permute-start | bytes 147464 | tf_op jit(solution)/shard_map/ppermute | solution.py:427
  37.3 3.8 %collective-permute-done.15.three = bf16[8,3072]{1,0:T(8,128)(2,1)S(1)} collective-permute-done((bf16[8,3072]{1,0:T(8,128)(2,1)S(1)}, bf16[8,3072]{1,0:T(8,128)(2,1)S(1)}, u32[]{:S(2)}, u32[]{:S(2)}) %collective-permute-start.15) | collective-permute-done | bytes 49184 | tf_op jit(solution)/shard_map/ppermute | solution.py:427
  41.1 0.2 combine_far.1.total
  41.3 0.8 %combine.1 = bf16[8,4096]{1,0:T(8,128)(2,1)} custom-call(f32[16,128]{1,0:T(8,128)S(1)} %get-tuple-element.22.refs_0_.after.share, bf16[4,16,128]{2,1,0:T(8,128)(2,1)S(1)} %get-tuple-element.23.take, bf16[8,3072]{1,0:T(8,128)(2,1)S(1)} %fold.11.zero, bf16[8,3072]{1,0:T(8,128)(2,1)S(1)} %collective-permute-done.13.one, f32[8,4096]{1,0:T(8,128)S(1)} %combine_far.1.total), custom_call_target="tpu_custom_call" | custom-call | bytes 16777216 | tf_op jit(solution)/shard_map/combine/pallas_call | solution.py:414
  (23 shorter events, 0.3 us)
Async XLA Ops:
  0.6 20.5 %copy-start = (bf16[1792,4096]{1,0:T(8,128)(2,1)S(1)}, bf16[1792,4096]{1,0:T(8,128)(2,1)}, u32[]{:S(2)}) copy-start(bf16[1792,4096]{1,0:T(8,128)(2,1)} %weight.1) | copy-start | bytes 44040196
  0.6 20.5 %copy-start.1 = (bf16[4096,1792]{1,0:T(8,128)(2,1)S(1)}, bf16[4096,1792]{1,0:T(8,128)(2,1)}, u32[]{:S(2)}) copy-start(bf16[4096,1792]{1,0:T(8,128)(2,1)} %gate_weight.1) | copy-start | bytes 44040196
  0.7 20.5 %copy-start.2 = (bf16[4096,1792]{1,0:T(8,128)(2,1)S(1)}, bf16[4096,1792]{1,0:T(8,128)(2,1)}, u32[]{:S(2)}) copy-start(bf16[4096,1792]{1,0:T(8,128)(2,1)} %up_weight.1) | copy-start | bytes 44040196
  3.3 5.7 %collective-permute-start = (bf16[8,3072]{1,0:T(8,128)(2,1)S(1)}, bf16[8,3072]{1,0:T(8,128)(2,1)S(1)}, u32[]{:S(2)}, u32[]{:S(2)}) collective-permute-start(bf16[8,3072]{1,0:T(8,128)(2,1)S(1)} %get-tuple-element.25), channel_id=1, source_target_pairs={{0,4},{1,5},{2,6},{3,7},{4,0},{5,1},{6,2},{7,3},{8,12},{9,13},{10,... | collective-permute-start | bytes 147464 | tf_op jit(solution)/shard_map/ppermute | solution.py:427
  6.4 5.9 %collective-permute-start.3 = (bf16[8,3072]{1,0:T(8,128)(2,1)S(1)}, bf16[8,3072]{1,0:T(8,128)(2,1)S(1)}, u32[]{:S(2)}, u32[]{:S(2)}) collective-permute-start(bf16[8,3072]{1,0:T(8,128)(2,1)S(1)} %get-tuple-element.26), channel_id=1, source_target_pairs={{0,8},{1,9},{2,10},{3,11},{4,12},{5,13},{6,14},{7,15},{8,0},{9,1},... | collective-permute-start | bytes 147464 | tf_op jit(solution)/shard_map/ppermute | solution.py:427
  9.0 5.9 %collective-permute-start.4 = (bf16[8,3072]{1,0:T(8,128)(2,1)S(1)}, bf16[8,3072]{1,0:T(8,128)(2,1)S(1)}, u32[]{:S(2)}, u32[]{:S(2)}) collective-permute-start(bf16[8,3072]{1,0:T(8,128)(2,1)S(1)} %get-tuple-element.27), channel_id=1, source_target_pairs={{0,12},{1,13},{2,14},{3,15},{4,8},{5,9},{6,10},{7,11},{8,4},{9,5},... | collective-permute-start | bytes 147464 | tf_op jit(solution)/shard_map/ppermute | solution.py:427
  9.0 7.5 %collective-permute-start.1 = (bf16[16,3072]{1,0:T(8,128)(2,1)S(1)}, bf16[16,3072]{1,0:T(8,128)(2,1)S(1)}, u32[]{:S(2)}, u32[]{:S(2)}) collective-permute-start(bf16[16,3072]{1,0:T(8,128)(2,1)S(1)} %join.6.refs_1_), channel_id=1, source_target_pairs={{0,2},{1,3},{2,0},{3,1},{4,6},{5,7},{6,4},{7,5},{8,10},{9,11},{10,... | collective-permute-start | bytes 294920 | tf_op jit(solution)/shard_map/ppermute | solution.py:427
  14.9 4.7 %collective-permute-start.5 = (bf16[16,3072]{1,0:T(8,128)(2,1)S(1)}, bf16[16,3072]{1,0:T(8,128)(2,1)S(1)}, u32[]{:S(2)}, u32[]{:S(2)}) collective-permute-start(bf16[16,3072]{1,0:T(8,128)(2,1)S(1)} %join.9.refs_1_), channel_id=1, source_target_pairs={{0,2},{1,3},{2,0},{3,1},{4,6},{5,7},{6,4},{7,5},{8,10},{9,11},{10,... | collective-permute-start | bytes 294920 | tf_op jit(solution)/shard_map/ppermute | solution.py:427
  16.5 3.2 %collective-permute-start.2 = (bf16[32,3072]{1,0:T(8,128)(2,1)S(1)}, bf16[32,3072]{1,0:T(8,128)(2,1)S(1)}, u32[]{:S(2)}, u32[]{:S(2)}) collective-permute-start(bf16[32,3072]{1,0:T(8,128)(2,1)S(1)} %join.7.refs_1_), channel_id=1, source_target_pairs={{0,1},{1,0},{2,3},{3,2},{4,5},{5,4},{6,7},{7,6},{8,9},{9,8},{10,11... | collective-permute-start | bytes 589832 | tf_op jit(solution)/shard_map/ppermute | solution.py:427
  19.6 1.5 %collective-permute-start.6 = (bf16[32,3072]{1,0:T(8,128)(2,1)S(1)}, bf16[32,3072]{1,0:T(8,128)(2,1)S(1)}, u32[]{:S(2)}, u32[]{:S(2)}) collective-permute-start(bf16[32,3072]{1,0:T(8,128)(2,1)S(1)} %join.10.refs_1_), channel_id=1, source_target_pairs={{0,1},{1,0},{2,3},{3,2},{4,5},{5,4},{6,7},{7,6},{8,9},{9,8},{10,11... | collective-permute-start | bytes 589832 | tf_op jit(solution)/shard_map/ppermute | solution.py:427
  27.6 1.5 %collective-permute-start.8 = (bf16[32,3072]{1,0:T(8,128)(2,1)S(1)}, bf16[32,3072]{1,0:T(8,128)(2,1)S(1)}, u32[]{:S(2)}, u32[]{:S(2)}) collective-permute-start(bf16[32,3072]{1,0:T(8,128)(2,1)S(1)} %get-tuple-element.31), channel_id=1, source_target_pairs={{0,1},{1,0},{2,3},{3,2},{4,5},{5,4},{6,7},{7,6},{8,9},{9,8},{10,11... | collective-permute-start | bytes 589832 | tf_op jit(solution)/shard_map/ppermute | solution.py:427
  27.8 3.4 %collective-permute-start.7 = (bf16[32,3072]{1,0:T(8,128)(2,1)S(1)}, bf16[32,3072]{1,0:T(8,128)(2,1)S(1)}, u32[]{:S(2)}, u32[]{:S(2)}) collective-permute-start(bf16[32,3072]{1,0:T(8,128)(2,1)S(1)} %get-tuple-element.29), channel_id=1, source_target_pairs={{0,1},{1,0},{2,3},{3,2},{4,5},{5,4},{6,7},{7,6},{8,9},{9,8},{10,11... | collective-permute-start | bytes 589832 | tf_op jit(solution)/shard_map/ppermute | solution.py:427
  29.2 4.3 %collective-permute-start.12 = (bf16[8,3072]{1,0:T(8,128)(2,1)S(1)}, bf16[8,3072]{1,0:T(8,128)(2,1)S(1)}, u32[]{:S(2)}, u32[]{:S(2)}) collective-permute-start(bf16[8,3072]{1,0:T(8,128)(2,1)S(1)} %get-tuple-element.39), channel_id=1, source_target_pairs={{0,2},{1,3},{2,0},{3,1},{4,6},{5,7},{6,4},{7,5},{8,10},{9,11},{10,... | collective-permute-start | bytes 147464 | tf_op jit(solution)/shard_map/ppermute | solution.py:427
  30.8 4.3 %collective-permute-start.11 = (bf16[8,3072]{1,0:T(8,128)(2,1)S(1)}, bf16[8,3072]{1,0:T(8,128)(2,1)S(1)}, u32[]{:S(2)}, u32[]{:S(2)}) collective-permute-start(bf16[8,3072]{1,0:T(8,128)(2,1)S(1)} %get-tuple-element.38), channel_id=1, source_target_pairs={{0,2},{1,3},{2,0},{3,1},{4,6},{5,7},{6,4},{7,5},{8,10},{9,11},{10,... | collective-permute-start | bytes 147464 | tf_op jit(solution)/shard_map/ppermute | solution.py:427
  31.3 4.6 %collective-permute-start.10 = (bf16[8,3072]{1,0:T(8,128)(2,1)S(1)}, bf16[8,3072]{1,0:T(8,128)(2,1)S(1)}, u32[]{:S(2)}, u32[]{:S(2)}) collective-permute-start(bf16[8,3072]{1,0:T(8,128)(2,1)S(1)} %get-tuple-element.36), channel_id=1, source_target_pairs={{0,2},{1,3},{2,0},{3,1},{4,6},{5,7},{6,4},{7,5},{8,10},{9,11},{10,... | collective-permute-start | bytes 147464 | tf_op jit(solution)/shard_map/ppermute | solution.py:427
  32.9 4.3 %collective-permute-start.9 = (bf16[8,3072]{1,0:T(8,128)(2,1)S(1)}, bf16[8,3072]{1,0:T(8,128)(2,1)S(1)}, u32[]{:S(2)}, u32[]{:S(2)}) collective-permute-start(bf16[8,3072]{1,0:T(8,128)(2,1)S(1)} %get-tuple-element.34), channel_id=1, source_target_pairs={{0,2},{1,3},{2,0},{3,1},{4,6},{5,7},{6,4},{7,5},{8,10},{9,11},{10,... | collective-permute-start | bytes 147464 | tf_op jit(solution)/shard_map/ppermute | solution.py:427
  33.5 7.5 %collective-permute-start.14 = (bf16[8,3072]{1,0:T(8,128)(2,1)S(1)}, bf16[8,3072]{1,0:T(8,128)(2,1)S(1)}, u32[]{:S(2)}, u32[]{:S(2)}) collective-permute-start(bf16[8,3072]{1,0:T(8,128)(2,1)S(1)} %fold.8.after), channel_id=1, source_target_pairs={{0,8},{1,9},{2,10},{3,11},{4,12},{5,13},{6,14},{7,15},{8,0},{9,1},... | collective-permute-start | bytes 147464 | tf_op jit(solution)/shard_map/ppermute | solution.py:427
  35.1 6.0 %collective-permute-start.15 = (bf16[8,3072]{1,0:T(8,128)(2,1)S(1)}, bf16[8,3072]{1,0:T(8,128)(2,1)S(1)}, u32[]{:S(2)}, u32[]{:S(2)}) collective-permute-start(bf16[8,3072]{1,0:T(8,128)(2,1)S(1)} %fold.9.after), channel_id=1, source_target_pairs={{0,12},{1,13},{2,14},{3,15},{4,8},{5,9},{6,10},{7,11},{8,4},{9,5},... | collective-permute-start | bytes 147464 | tf_op jit(solution)/shard_map/ppermute | solution.py:427
  36.0 5.3 %collective-permute-start.13 = (bf16[8,3072]{1,0:T(8,128)(2,1)S(1)}, bf16[8,3072]{1,0:T(8,128)(2,1)S(1)}, u32[]{:S(2)}, u32[]{:S(2)}) collective-permute-start(bf16[8,3072]{1,0:T(8,128)(2,1)S(1)} %fold.10.after), channel_id=1, source_target_pairs={{0,4},{1,5},{2,6},{3,7},{4,0},{5,1},{6,2},{7,3},{8,12},{9,13},{10,... | collective-permute-start | bytes 147464 | tf_op jit(solution)/shard_map/ppermute | solution.py:427

commit v18 on v17

--- a/solution.py
+++ b/solution.py
@@ -330,17 +330,18 @@
     return outs[0:2], outs[2:4]
 
 
-def join_kernel(*refs):
+def join_kernel(backwards, *refs):
     out, row = refs[-1], 0
-    for piece in refs[1:-1]:
+    pieces = refs[1:-1][::-1] if backwards else refs[1:-1]
+    for piece in pieces:
         out[row : row + piece.shape[0]] = piece[...]
         row += piece.shape[0]
 
 
-def join(after, *pieces):
+def join(after, *pieces, backwards=False):
     rows = sum(piece.shape[0] for piece in pieces)
     return pl.pallas_call(
-        join_kernel,
+        functools.partial(join_kernel, backwards),
         out_shape=jax.ShapeDtypeStruct((rows, pieces[0].shape[1]), BF16),
         in_specs=[ANY] + [VMEM] * len(pieces),
         out_specs=VMEM,
@@ -450,8 +451,9 @@
         router_weight, routes, down_weight,
     )
 
-    packed = [packed[0]] + [swap(packed[k], count, k * plane) for k in range(1, EXPERTS)]
-    waves = [join(share, *packed[:2]), join(share, *packed[2:])]
+    for k in (1, 3, 2):
+        packed[k] = swap(packed[k], count, k * plane)
+    waves = [join(share, *packed[:2]), join(share, packed[3], packed[2], backwards=True)]
     for bit in bits:
         waves = [join(share, wave, swap(wave, count, bit)) for wave in waves]
 

time: 42.3 us -> 42.1 us (level)
  waiting for transfers between devices: 14.4 us -> 13.9 us
    ppermute x16, waiting for transfers between devices: 14.4 us -> 13.9 us  [swap(): return lax.ppermute(value, 'dp', [(i, i ^ bit) for i in range(count)])]
  transfers between devices with their start and end apart: 16 -> 16, of which waited for: 8 -> 9; matrix products, arithmetic and copies ran while one was open for 0% -> 0% of each run, Pallas kernels for 1% -> 1%
where the time goes in v18:
time: 42.1 us; the launch traced here: 41.9 us
  starting transfers between devices  16.8 us (40%)
  waiting for transfers between devices  13.9 us (33%)
  Pallas kernels  10.4 us (25%)
  between operations  0.81 us (2%)
    ppermute x16, starting transfers between devices, swap(): return lax.ppermute(value, 'dp', [(i, i ^ bit) for i in range(count)])  16.8 us
    ppermute x16, waiting for transfers between devices, swap(): return lax.ppermute(value, 'dp', [(i, i ^ bit) for i in range(count)])  13.9 us
    pallas_call x1, Pallas kernels, hidden_rows(): pl.pallas_call(hidden_kernel, out_shape=jax.ShapeDtypeStruct((rows, colum...  4.12 us
    pallas_call x1, Pallas kernels, attend(): pl.pallas_call(functools.partial(attend_kernel, plane), out_shape=(jax.Sh...  2.66 us
    pallas_call x1, Pallas kernels, down_rows(): pl.pallas_call(down_kernel, out_shape=[jax.ShapeDtypeStruct((size, width...  2.3 us
  transfers between devices with their start and end apart: 16, of which 9 were waited for; matrix products, arithmetic and copies ran while one was open for 0% of the time, Pallas kernels for 1%

profile of v18, /device:TPU:0, one launch (start us, length us, event | category | flops | bytes accessed | tf_op | source)
XLA Modules:
  0.0 41.9 jit_solution(11597600886752211736)
XLA Ops:
  0.7 2.7 %attend.1 = (bf16[8,4096]{1,0:T(8,128)(2,1)}, bf16[8,3072]{1,0:T(8,128)(2,1)S(1)}, bf16[8,3072]{1,0:T(8,128)(2,1)S(1)}, bf16[8,3072]{1,0:T(8,128)(2,1)S(1)}, bf1...) custom-call(bf16[8,4096]{1,0:T(8,128)(2,1)} %refs_0_.1, ...), custom_call_target="tpu_custom_call" | custom-call | tf_op jit(solution)/shard_map/attend/pallas_call | solution.py:212
  3.3 3.1 %collective-permute-start = (bf16[8,3072]{1,0:T(8,128)(2,1)S(1)}, bf16[8,3072]{1,0:T(8,128)(2,1)S(1)}, u32[]{:S(2)}, u32[]{:S(2)}) collective-permute-start(bf16[8,3072]{1,0:T(8,128)(2,1)S(1)} %get-tuple-element.25), channel_id=1, source_target_pairs={{0,4},{1,5},{2,6},{3,7},{4,0},{5,1},{6,2},{7,3},{8,12},{9,13},{10,... | collective-permute-start | bytes 147464 | tf_op jit(solution)/shard_map/ppermute | solution.py:428
  6.4 2.5 %collective-permute-start.3 = (bf16[8,3072]{1,0:T(8,128)(2,1)S(1)}, bf16[8,3072]{1,0:T(8,128)(2,1)S(1)}, u32[]{:S(2)}, u32[]{:S(2)}) collective-permute-start(bf16[8,3072]{1,0:T(8,128)(2,1)S(1)} %get-tuple-element.26), channel_id=1, source_target_pairs={{0,12},{1,13},{2,14},{3,15},{4,8},{5,9},{6,10},{7,11},{8,4},{9,5},... | collective-permute-start | bytes 147464 | tf_op jit(solution)/shard_map/ppermute | solution.py:428
  8.9 0.1 collective-permute-start.4
  9.0 0.0 collective-permute-done.refs_2_
  9.0 1.6 %collective-permute-start.1 = (bf16[16,3072]{1,0:T(8,128)(2,1)S(1)}, bf16[16,3072]{1,0:T(8,128)(2,1)S(1)}, u32[]{:S(2)}, u32[]{:S(2)}) collective-permute-start(bf16[16,3072]{1,0:T(8,128)(2,1)S(1)} %join.6.refs_1_), channel_id=1, source_target_pairs={{0,2},{1,3},{2,0},{3,1},{4,6},{5,7},{6,4},{7,5},{8,10},{9,11},{10,... | collective-permute-start | bytes 294920 | tf_op jit(solution)/shard_map/ppermute | solution.py:428
  10.6 2.3 %collective-permute-done.3.refs_1_ = bf16[8,3072]{1,0:T(8,128)(2,1)S(1)} collective-permute-done((bf16[8,3072]{1,0:T(8,128)(2,1)S(1)}, bf16[8,3072]{1,0:T(8,128)(2,1)S(1)}, u32[]{:S(2)}, u32[]{:S(2)}) %collective-permute-start.3) | collective-permute-done | bytes 49184 | tf_op jit(solution)/shard_map/ppermute | solution.py:428
  12.9 1.5 %collective-permute-done.4.refs_2_ = bf16[8,3072]{1,0:T(8,128)(2,1)S(1)} collective-permute-done((bf16[8,3072]{1,0:T(8,128)(2,1)S(1)}, bf16[8,3072]{1,0:T(8,128)(2,1)S(1)}, u32[]{:S(2)}, u32[]{:S(2)}) %collective-permute-start.4) | collective-permute-done | bytes 49184 | tf_op jit(solution)/shard_map/ppermute | solution.py:428
  14.4 1.6 %collective-permute-start.5 = (bf16[16,3072]{1,0:T(8,128)(2,1)S(1)}, bf16[16,3072]{1,0:T(8,128)(2,1)S(1)}, u32[]{:S(2)}, u32[]{:S(2)}) collective-permute-start(bf16[16,3072]{1,0:T(8,128)(2,1)S(1)} %join.9.refs_1_), channel_id=1, source_target_pairs={{0,2},{1,3},{2,0},{3,1},{4,6},{5,7},{6,4},{7,5},{8,10},{9,11},{10,... | collective-permute-start | bytes 294920 | tf_op jit(solution)/shard_map/ppermute | solution.py:428
  16.0 0.1 collective-permute-start.2
  16.1 3.0 %collective-permute-done.5.refs_2_ = bf16[16,3072]{1,0:T(8,128)(2,1)S(1)} collective-permute-done((bf16[16,3072]{1,0:T(8,128)(2,1)S(1)}, bf16[16,3072]{1,0:T(8,128)(2,1)S(1)}, u32[]{:S(2)}, u32[]{:S(2)}) %collective-permute-start.5) | collective-permute-done | bytes 98336 | tf_op jit(solution)/shard_map/ppermute | solution.py:428
  19.1 0.1 collective-permute-start.6
  19.2 1.4 %collective-permute-done.6.refs_2_ = bf16[32,3072]{1,0:T(8,128)(2,1)S(1)} collective-permute-done((bf16[32,3072]{1,0:T(8,128)(2,1)S(1)}, bf16[32,3072]{1,0:T(8,128)(2,1)S(1)}, u32[]{:S(2)}, u32[]{:S(2)}) %collective-permute-start.6) | collective-permute-done | bytes 196640 | tf_op jit(solution)/shard_map/ppermute | solution.py:428
  20.7 4.1 %hidden.1 = bf16[128,1792]{1,0:T(8,128)(2,1)S(1)} custom-call(bf16[4096,1792]{1,0:T(8,128)(2,1)S(1)} %copy-done.1, bf16[4096,1792]{1,0:T(8,128)(2,1)S(1)} %copy-done.2, bf16[1792,4096]{1,0:T(8,128)(2,1)S(1)} %copy-done, bf16[64,3072]{1,0:T(8,128)(2,1)S(1)} %join.8.refs_0_, bf16[64,3072]{1,0:T(8,128)(2,1)S(1)} %join.11.refs_1_), custom_call_target="tpu_custom_call" | custom-call | flops 3758096384 | tf_op jit(solution)/shard_map/hidden/pallas_call | solution.py:262
  24.8 2.3 %down.1 = (bf16[32,3072]{1,0:T(8,128)(2,1)S(1)}, bf16[32,3072]{1,0:T(8,128)(2,1)S(1)}, bf16[32,3072]{1,0:T(8,128)(2,1)S(1)}, bf16[32,3072]{1,0:T(8,128)(2,1)S(1)}) custom-call(bf16[128,1792]{1,0:T(8,128)(2,1)S(1)} %hidden.1, bf16[1792,4096]{1,0:T(8,128)(2,1)S(1)} %copy-done), custom_call_target="tpu_custom_call" | custom-call | flops 1879048192 | tf_op jit(solution)/shard_map/down/pallas_call | solution.py:319
  27.1 0.2 collective-permute-start.8
  27.3 0.4 collective-permute-start.7
  27.7 0.9 %collective-permute-done.8.arrived = bf16[32,3072]{1,0:T(8,128)(2,1)S(1)} collective-permute-done((bf16[32,3072]{1,0:T(8,128)(2,1)S(1)}, bf16[32,3072]{1,0:T(8,128)(2,1)S(1)}, u32[]{:S(2)}, u32[]{:S(2)}) %collective-permute-start.8) | collective-permute-done | bytes 196640 | tf_op jit(solution)/shard_map/ppermute | solution.py:428
  28.7 1.6 %collective-permute-start.12 = (bf16[8,3072]{1,0:T(8,128)(2,1)S(1)}, bf16[8,3072]{1,0:T(8,128)(2,1)S(1)}, u32[]{:S(2)}, u32[]{:S(2)}) collective-permute-start(bf16[8,3072]{1,0:T(8,128)(2,1)S(1)} %get-tuple-element.39), channel_id=1, source_target_pairs={{0,2},{1,3},{2,0},{3,1},{4,6},{5,7},{6,4},{7,5},{8,10},{9,11},{10,... | collective-permute-start | bytes 147464 | tf_op jit(solution)/shard_map/ppermute | solution.py:428
  30.3 0.5 %collective-permute-start.11 = (bf16[8,3072]{1,0:T(8,128)(2,1)S(1)}, bf16[8,3072]{1,0:T(8,128)(2,1)S(1)}, u32[]{:S(2)}, u32[]{:S(2)}) collective-permute-start(bf16[8,3072]{1,0:T(8,128)(2,1)S(1)} %get-tuple-element.38), channel_id=1, source_target_pairs={{0,2},{1,3},{2,0},{3,1},{4,6},{5,7},{6,4},{7,5},{8,10},{9,11},{10,... | collective-permute-start | bytes 147464 | tf_op jit(solution)/shard_map/ppermute | solution.py:428
  30.8 0.0 collective-permute-done.7.arrived
  30.8 1.6 %collective-permute-start.10 = (bf16[8,3072]{1,0:T(8,128)(2,1)S(1)}, bf16[8,3072]{1,0:T(8,128)(2,1)S(1)}, u32[]{:S(2)}, u32[]{:S(2)}) collective-permute-start(bf16[8,3072]{1,0:T(8,128)(2,1)S(1)} %get-tuple-element.36), channel_id=1, source_target_pairs={{0,2},{1,3},{2,0},{3,1},{4,6},{5,7},{6,4},{7,5},{8,10},{9,11},{10,... | collective-permute-start | bytes 147464 | tf_op jit(solution)/shard_map/ppermute | solution.py:428
  32.4 0.5 %collective-permute-start.9 = (bf16[8,3072]{1,0:T(8,128)(2,1)S(1)}, bf16[8,3072]{1,0:T(8,128)(2,1)S(1)}, u32[]{:S(2)}, u32[]{:S(2)}) collective-permute-start(bf16[8,3072]{1,0:T(8,128)(2,1)S(1)} %get-tuple-element.34), channel_id=1, source_target_pairs={{0,2},{1,3},{2,0},{3,1},{4,6},{5,7},{6,4},{7,5},{8,10},{9,11},{10,... | collective-permute-start | bytes 147464 | tf_op jit(solution)/shard_map/ppermute | solution.py:428
  32.9 0.1 collective-permute-done.12.arrived
  33.0 0.8 %collective-permute-start.14 = (bf16[8,3072]{1,0:T(8,128)(2,1)S(1)}, bf16[8,3072]{1,0:T(8,128)(2,1)S(1)}, u32[]{:S(2)}, u32[]{:S(2)}) collective-permute-start(bf16[8,3072]{1,0:T(8,128)(2,1)S(1)} %fold.8.after), channel_id=1, source_target_pairs={{0,8},{1,9},{2,10},{3,11},{4,12},{5,13},{6,14},{7,15},{8,0},{9,1},... | collective-permute-start | bytes 147464 | tf_op jit(solution)/shard_map/ppermute | solution.py:428
  33.8 0.8 %collective-permute-done.11.arrived = bf16[8,3072]{1,0:T(8,128)(2,1)S(1)} collective-permute-done((bf16[8,3072]{1,0:T(8,128)(2,1)S(1)}, bf16[8,3072]{1,0:T(8,128)(2,1)S(1)}, u32[]{:S(2)}, u32[]{:S(2)}) %collective-permute-start.11) | collective-permute-done | bytes 49184 | tf_op jit(solution)/shard_map/ppermute | solution.py:428
  34.6 2.2 %collective-permute-start.15 = (bf16[8,3072]{1,0:T(8,128)(2,1)S(1)}, bf16[8,3072]{1,0:T(8,128)(2,1)S(1)}, u32[]{:S(2)}, u32[]{:S(2)}) collective-permute-start(bf16[8,3072]{1,0:T(8,128)(2,1)S(1)} %fold.9.after), channel_id=1, source_target_pairs={{0,12},{1,13},{2,14},{3,15},{4,8},{5,9},{6,10},{7,11},{8,4},{9,5},... | collective-permute-start | bytes 147464 | tf_op jit(solution)/shard_map/ppermute | solution.py:428
  36.8 0.1 collective-permute-start.13
  36.9 3.6 %collective-permute-done.15.three = bf16[8,3072]{1,0:T(8,128)(2,1)S(1)} collective-permute-done((bf16[8,3072]{1,0:T(8,128)(2,1)S(1)}, bf16[8,3072]{1,0:T(8,128)(2,1)S(1)}, u32[]{:S(2)}, u32[]{:S(2)}) %collective-permute-start.15) | collective-permute-done | bytes 49184 | tf_op jit(solution)/shard_map/ppermute | solution.py:428
  40.6 0.2 combine_far.1.total
  40.8 0.3 collective-permute-done.13.one
  41.1 0.8 %combine.1 = bf16[8,4096]{1,0:T(8,128)(2,1)} custom-call(f32[16,128]{1,0:T(8,128)S(1)} %get-tuple-element.22.refs_0_.after.share, bf16[4,16,128]{2,1,0:T(8,128)(2,1)S(1)} %get-tuple-element.23.take, bf16[8,3072]{1,0:T(8,128)(2,1)S(1)} %fold.11.zero, bf16[8,3072]{1,0:T(8,128)(2,1)S(1)} %collective-permute-done.13.one, f32[8,4096]{1,0:T(8,128)S(1)} %combine_far.1.total), custom_call_target="tpu_custom_call" | custom-call | bytes 16777216 | tf_op jit(solution)/shard_map/combine/pallas_call | solution.py:415
  (23 shorter events, 0.3 us)
Async XLA Ops:
  0.6 20.0 %copy-start = (bf16[1792,4096]{1,0:T(8,128)(2,1)S(1)}, bf16[1792,4096]{1,0:T(8,128)(2,1)}, u32[]{:S(2)}) copy-start(bf16[1792,4096]{1,0:T(8,128)(2,1)} %weight.1) | copy-start | bytes 44040196
  0.6 20.0 %copy-start.1 = (bf16[4096,1792]{1,0:T(8,128)(2,1)S(1)}, bf16[4096,1792]{1,0:T(8,128)(2,1)}, u32[]{:S(2)}) copy-start(bf16[4096,1792]{1,0:T(8,128)(2,1)} %gate_weight.1) | copy-start | bytes 44040196
  0.7 20.0 %copy-start.2 = (bf16[4096,1792]{1,0:T(8,128)(2,1)S(1)}, bf16[4096,1792]{1,0:T(8,128)(2,1)}, u32[]{:S(2)}) copy-start(bf16[4096,1792]{1,0:T(8,128)(2,1)} %up_weight.1) | copy-start | bytes 44040196
  3.3 5.7 %collective-permute-start = (bf16[8,3072]{1,0:T(8,128)(2,1)S(1)}, bf16[8,3072]{1,0:T(8,128)(2,1)S(1)}, u32[]{:S(2)}, u32[]{:S(2)}) collective-permute-start(bf16[8,3072]{1,0:T(8,128)(2,1)S(1)} %get-tuple-element.25), channel_id=1, source_target_pairs={{0,4},{1,5},{2,6},{3,7},{4,0},{5,1},{6,2},{7,3},{8,12},{9,13},{10,... | collective-permute-start | bytes 147464 | tf_op jit(solution)/shard_map/ppermute | solution.py:428
  6.4 6.5 %collective-permute-start.3 = (bf16[8,3072]{1,0:T(8,128)(2,1)S(1)}, bf16[8,3072]{1,0:T(8,128)(2,1)S(1)}, u32[]{:S(2)}, u32[]{:S(2)}) collective-permute-start(bf16[8,3072]{1,0:T(8,128)(2,1)S(1)} %get-tuple-element.26), channel_id=1, source_target_pairs={{0,12},{1,13},{2,14},{3,15},{4,8},{5,9},{6,10},{7,11},{8,4},{9,5},... | collective-permute-start | bytes 147464 | tf_op jit(solution)/shard_map/ppermute | solution.py:428
  8.9 5.5 %collective-permute-start.4 = (bf16[8,3072]{1,0:T(8,128)(2,1)S(1)}, bf16[8,3072]{1,0:T(8,128)(2,1)S(1)}, u32[]{:S(2)}, u32[]{:S(2)}) collective-permute-start(bf16[8,3072]{1,0:T(8,128)(2,1)S(1)} %get-tuple-element.27), channel_id=1, source_target_pairs={{0,8},{1,9},{2,10},{3,11},{4,12},{5,13},{6,14},{7,15},{8,0},{9,1},... | collective-permute-start | bytes 147464 | tf_op jit(solution)/shard_map/ppermute | solution.py:428
  9.0 7.0 %collective-permute-start.1 = (bf16[16,3072]{1,0:T(8,128)(2,1)S(1)}, bf16[16,3072]{1,0:T(8,128)(2,1)S(1)}, u32[]{:S(2)}, u32[]{:S(2)}) collective-permute-start(bf16[16,3072]{1,0:T(8,128)(2,1)S(1)} %join.6.refs_1_), channel_id=1, source_target_pairs={{0,2},{1,3},{2,0},{3,1},{4,6},{5,7},{6,4},{7,5},{8,10},{9,11},{10,... | collective-permute-start | bytes 294920 | tf_op jit(solution)/shard_map/ppermute | solution.py:428
  14.4 4.7 %collective-permute-start.5 = (bf16[16,3072]{1,0:T(8,128)(2,1)S(1)}, bf16[16,3072]{1,0:T(8,128)(2,1)S(1)}, u32[]{:S(2)}, u32[]{:S(2)}) collective-permute-start(bf16[16,3072]{1,0:T(8,128)(2,1)S(1)} %join.9.refs_1_), channel_id=1, source_target_pairs={{0,2},{1,3},{2,0},{3,1},{4,6},{5,7},{6,4},{7,5},{8,10},{9,11},{10,... | collective-permute-start | bytes 294920 | tf_op jit(solution)/shard_map/ppermute | solution.py:428
  16.0 3.2 %collective-permute-start.2 = (bf16[32,3072]{1,0:T(8,128)(2,1)S(1)}, bf16[32,3072]{1,0:T(8,128)(2,1)S(1)}, u32[]{:S(2)}, u32[]{:S(2)}) collective-permute-start(bf16[32,3072]{1,0:T(8,128)(2,1)S(1)} %join.7.refs_1_), channel_id=1, source_target_pairs={{0,1},{1,0},{2,3},{3,2},{4,5},{5,4},{6,7},{7,6},{8,9},{9,8},{10,11... | collective-permute-start | bytes 589832 | tf_op jit(solution)/shard_map/ppermute | solution.py:428
  19.1 1.5 %collective-permute-start.6 = (bf16[32,3072]{1,0:T(8,128)(2,1)S(1)}, bf16[32,3072]{1,0:T(8,128)(2,1)S(1)}, u32[]{:S(2)}, u32[]{:S(2)}) collective-permute-start(bf16[32,3072]{1,0:T(8,128)(2,1)S(1)} %join.10.refs_1_), channel_id=1, source_target_pairs={{0,1},{1,0},{2,3},{3,2},{4,5},{5,4},{6,7},{7,6},{8,9},{9,8},{10,11... | collective-permute-start | bytes 589832 | tf_op jit(solution)/shard_map/ppermute | solution.py:428
  27.1 1.5 %collective-permute-start.8 = (bf16[32,3072]{1,0:T(8,128)(2,1)S(1)}, bf16[32,3072]{1,0:T(8,128)(2,1)S(1)}, u32[]{:S(2)}, u32[]{:S(2)}) collective-permute-start(bf16[32,3072]{1,0:T(8,128)(2,1)S(1)} %get-tuple-element.31), channel_id=1, source_target_pairs={{0,1},{1,0},{2,3},{3,2},{4,5},{5,4},{6,7},{7,6},{8,9},{9,8},{10,11... | collective-permute-start | bytes 589832 | tf_op jit(solution)/shard_map/ppermute | solution.py:428
  27.3 3.4 %collective-permute-start.7 = (bf16[32,3072]{1,0:T(8,128)(2,1)S(1)}, bf16[32,3072]{1,0:T(8,128)(2,1)S(1)}, u32[]{:S(2)}, u32[]{:S(2)}) collective-permute-start(bf16[32,3072]{1,0:T(8,128)(2,1)S(1)} %get-tuple-element.29), channel_id=1, source_target_pairs={{0,1},{1,0},{2,3},{3,2},{4,5},{5,4},{6,7},{7,6},{8,9},{9,8},{10,11... | collective-permute-start | bytes 589832 | tf_op jit(solution)/shard_map/ppermute | solution.py:428
  28.7 4.3 %collective-permute-start.12 = (bf16[8,3072]{1,0:T(8,128)(2,1)S(1)}, bf16[8,3072]{1,0:T(8,128)(2,1)S(1)}, u32[]{:S(2)}, u32[]{:S(2)}) collective-permute-start(bf16[8,3072]{1,0:T(8,128)(2,1)S(1)} %get-tuple-element.39), channel_id=1, source_target_pairs={{0,2},{1,3},{2,0},{3,1},{4,6},{5,7},{6,4},{7,5},{8,10},{9,11},{10,... | collective-permute-start | bytes 147464 | tf_op jit(solution)/shard_map/ppermute | solution.py:428
  30.3 4.3 %collective-permute-start.11 = (bf16[8,3072]{1,0:T(8,128)(2,1)S(1)}, bf16[8,3072]{1,0:T(8,128)(2,1)S(1)}, u32[]{:S(2)}, u32[]{:S(2)}) collective-permute-start(bf16[8,3072]{1,0:T(8,128)(2,1)S(1)} %get-tuple-element.38), channel_id=1, source_target_pairs={{0,2},{1,3},{2,0},{3,1},{4,6},{5,7},{6,4},{7,5},{8,10},{9,11},{10,... | collective-permute-start | bytes 147464 | tf_op jit(solution)/shard_map/ppermute | solution.py:428
  30.8 6.0 %collective-permute-start.10 = (bf16[8,3072]{1,0:T(8,128)(2,1)S(1)}, bf16[8,3072]{1,0:T(8,128)(2,1)S(1)}, u32[]{:S(2)}, u32[]{:S(2)}) collective-permute-start(bf16[8,3072]{1,0:T(8,128)(2,1)S(1)} %get-tuple-element.36), channel_id=1, source_target_pairs={{0,2},{1,3},{2,0},{3,1},{4,6},{5,7},{6,4},{7,5},{8,10},{9,11},{10,... | collective-permute-start | bytes 147464 | tf_op jit(solution)/shard_map/ppermute | solution.py:428
  32.4 4.5 %collective-permute-start.9 = (bf16[8,3072]{1,0:T(8,128)(2,1)S(1)}, bf16[8,3072]{1,0:T(8,128)(2,1)S(1)}, u32[]{:S(2)}, u32[]{:S(2)}) collective-permute-start(bf16[8,3072]{1,0:T(8,128)(2,1)S(1)} %get-tuple-element.34), channel_id=1, source_target_pairs={{0,2},{1,3},{2,0},{3,1},{4,6},{5,7},{6,4},{7,5},{8,10},{9,11},{10,... | collective-permute-start | bytes 147464 | tf_op jit(solution)/shard_map/ppermute | solution.py:428
  33.0 7.5 %collective-permute-start.14 = (bf16[8,3072]{1,0:T(8,128)(2,1)S(1)}, bf16[8,3072]{1,0:T(8,128)(2,1)S(1)}, u32[]{:S(2)}, u32[]{:S(2)}) collective-permute-start(bf16[8,3072]{1,0:T(8,128)(2,1)S(1)} %fold.8.after), channel_id=1, source_target_pairs={{0,8},{1,9},{2,10},{3,11},{4,12},{5,13},{6,14},{7,15},{8,0},{9,1},... | collective-permute-start | bytes 147464 | tf_op jit(solution)/shard_map/ppermute | solution.py:428
  34.6 6.0 %collective-permute-start.15 = (bf16[8,3072]{1,0:T(8,128)(2,1)S(1)}, bf16[8,3072]{1,0:T(8,128)(2,1)S(1)}, u32[]{:S(2)}, u32[]{:S(2)}) collective-permute-start(bf16[8,3072]{1,0:T(8,128)(2,1)S(1)} %fold.9.after), channel_id=1, source_target_pairs={{0,12},{1,13},{2,14},{3,15},{4,8},{5,9},{6,10},{7,11},{8,4},{9,5},... | collective-permute-start | bytes 147464 | tf_op jit(solution)/shard_map/ppermute | solution.py:428
  36.8 4.3 %collective-permute-start.13 = (bf16[8,3072]{1,0:T(8,128)(2,1)S(1)}, bf16[8,3072]{1,0:T(8,128)(2,1)S(1)}, u32[]{:S(2)}, u32[]{:S(2)}) collective-permute-start(bf16[8,3072]{1,0:T(8,128)(2,1)S(1)} %fold.10.after), channel_id=1, source_target_pairs={{0,4},{1,5},{2,6},{3,7},{4,0},{5,1},{6,2},{7,3},{8,12},{9,13},{10,... | collective-permute-start | bytes 147464 | tf_op jit(solution)/shard_map/ppermute | solution.py:428

commit v19 on v18

--- a/solution.py
+++ b/solution.py
@@ -36,9 +36,7 @@
 def pack(picks, block):
     quarter = block.shape[1] // 4
     parts = [block[:, m * quarter : (m + 1) * quarter] for m in range(4)]
-    return [
-        (dot(picks[0], parts[m]) + dot(picks[1 + m], parts[3])).astype(BF16) for m in range(3)
-    ]
+    return [dot(picks[0], parts[m]) + dot(picks[1 + m], parts[3]) for m in range(3)]
 
 
 def unpack(picks, block):
@@ -51,9 +49,8 @@
 def attend_kernel(plane, *refs):
     refs = refs[:10] + refs[10 + HINTS :]
     sources, attended, packed, (share, take), held, semaphores = (
-        refs[:10], refs[10], refs[11:15], refs[15:17], refs[17:27], refs[28]
-    )
-    kept = refs[27]
+        refs[:10], refs[10], refs[11:15], refs[15:17], refs[17:27], refs[27]
+    )
     copies = [
         pltpu.make_async_copy(source, target, semaphores.at[i])
         for i, (source, target) in enumerate(zip(sources, held))
@@ -161,9 +158,7 @@
     pieces = [value[j * rows : (j + 1) * rows] for value in mixed for j in range(groups)]
 
     states = (residual[...].astype(F32) + jnp.concatenate(pieces, axis=1)).astype(BF16)
-    attended_copy = pltpu.make_async_copy(kept, attended, semaphores.at[len(copies)])
-    kept[...] = states
-    attended_copy.start()
+    attended[...] = states
     states = states.astype(F32)
     norm = lax.rsqrt(jnp.mean(states * states, axis=1, keepdims=True) + 1e-05)
     gains = gain[...].astype(F32)
@@ -182,7 +177,7 @@
     quarter = width // 4
     for m, value in enumerate(pack([pick[:, : 2 * rows] for pick in picks], normed)):
         for k, target in enumerate(packed):
-            target[:, m * quarter : (m + 1) * quarter] = value[8 * k : 8 * k + 8]
+            target[:, m * quarter : (m + 1) * quarter] = value[8 * k : 8 * k + 8].astype(BF16)
 
     chosen_logits = jnp.zeros((2 * rows, 1), F32)
     for e in range(EXPERTS):
@@ -190,7 +185,6 @@
         chosen_logits = jnp.where(expert_down[:, :1] == (own ^ e), both, chosen_logits)
     other = jnp.concatenate([chosen_logits[rows:], chosen_logits[:rows]], axis=0)
     share[...] = jnp.broadcast_to(1.0 / (1.0 + jnp.exp(other - chosen_logits)), share.shape)
-    attended_copy.wait()
 
 
 def attend(plane, queries, new_keys, new_values, cache_keys, cache_values, lengths, residual,
@@ -218,12 +212,12 @@
             jax.ShapeDtypeStruct((4, 2 * rows, 128), BF16),
         ),
         in_specs=[ANY] * (len(operands) + HINTS),
-        out_specs=(ANY,) + (VMEM,) * (2 + EXPERTS),
+        out_specs=(VMEM,) * (3 + EXPERTS),
         scratch_shapes=[
             (pltpu.SMEM if i in in_smem else pltpu.VMEM)(operand.shape, operand.dtype)
             for i, operand in enumerate(operands)
         ]
-        + [pltpu.VMEM((rows, width), BF16), pltpu.SemaphoreType.DMA((len(operands) + 1,))],
+        + [pltpu.SemaphoreType.DMA((len(operands),))],
         compiler_params=pltpu.CompilerParams(vmem_limit_bytes=5 * MIB),
         name="attend",
     )(*[pltpu.with_memory_space_constraint(x, pltpu.HBM) for x in operands + (weight,) * HINTS])
@@ -292,11 +286,11 @@
         tails = [dot(picks, tail[i : i + size]) for i in range(0, rows, size)]
         for m in range(3):
             moved = jnp.concatenate([x[m * size : (m + 1) * size] for x in tails], axis=0)
-            value = jnp.where(is_row, terms(m * quarter + n, step), moved).astype(BF16)
+            value = jnp.where(is_row, terms(m * quarter + n, step), moved)
             lanes = slice(m * quarter + n, m * quarter + n + step)
             for out, blocks in zip(outs, ways_back(rows // 32)):
-                for i, b in enumerate(blocks):
-                    out[8 * i : 8 * i + 8, lanes] = value[8 * b : 8 * b + 8]
+                chosen = [value[8 * b : 8 * b + 8] for b in blocks]
+                out[:, lanes] = jnp.concatenate(chosen, axis=0).astype(BF16)
 
 
 def ways_back(places):
@@ -331,11 +325,9 @@
 
 
 def join_kernel(backwards, *refs):
-    out, row = refs[-1], 0
     pieces = refs[1:-1][::-1] if backwards else refs[1:-1]
-    for piece in pieces:
-        out[row : row + piece.shape[0]] = piece[...]
-        row += piece.shape[0]
+    rows = [piece[...].astype(F32) for piece in pieces]
+    refs[-1][...] = jnp.concatenate(rows, axis=0).astype(BF16)
 
 
 def join(after, *pieces, backwards=False):
@@ -353,9 +345,9 @@
 
 def fold_kernel(held, arrived, after, *outs):
     each = outs[0].shape[0]
+    total = held[...].astype(F32) + arrived[...].astype(F32)
     for k, out in enumerate(outs):
-        block = slice(k * each, (k + 1) * each)
-        out[...] = (held[block].astype(F32) + arrived[block].astype(F32)).astype(BF16)
+        out[...] = total[k * each : (k + 1) * each].astype(BF16)
 
 
 def fold(held, arrived, after, parts):
@@ -374,7 +366,7 @@
 def combined(first, share, take, results):
     picks = [take[i][:, 8 * first : 8 * first + 16] for i in range(4)]
     rows = share.shape[0] // 2
-    block = jnp.concatenate([x[...] for x in results], axis=0)
+    block = jnp.concatenate([x[...].astype(F32) for x in results], axis=0).astype(BF16)
     values = [value * share[:, :1] for value in unpack(picks, block)]
     return [value[:rows] + value[rows:] for value in values]
 
@@ -385,18 +377,11 @@
         total[:, m * quarter : (m + 1) * quarter] = value
 
 
-def combine_kernel(share, take, zero, one, total, out, held, semaphores):
+def combine_kernel(share, take, zero, one, total, out):
     quarter = zero.shape[1] // 3
-    copies = []
     for m, value in enumerate(combined(0, share, take, (zero, one))):
-        lanes = pl.ds(m * quarter, quarter)
-        held[:, lanes] = (value + total[:, lanes]).astype(BF16)
-        copies.append(
-            pltpu.make_async_copy(held.at[:, lanes], out.at[:, lanes], semaphores.at[m])
-        )
-        copies[m].start()
-    for copy in copies:
-        copy.wait()
+        lanes = slice(m * quarter, (m + 1) * quarter)
+        out[:, lanes] = (value + total[:, lanes]).astype(BF16)
 
 
 def combine(share, take, results):
@@ -416,8 +401,7 @@
         combine_kernel,
         out_shape=jax.ShapeDtypeStruct((rows, width), BF16),
         in_specs=[VMEM] * 5,
-        out_specs=ANY,
-        scratch_shapes=[pltpu.VMEM((rows, width), BF16), pltpu.SemaphoreType.DMA((4,))],
+        out_specs=VMEM,
         compiler_params=params,
         cost_estimate=cost,
         name="combine",

time: 42.1 us -> 42.1 us (level)
  no operation moved by 1% of the time
where the time goes in v19:
time: 42.1 us; the launch traced here: 41.9 us
  starting transfers between devices  16.8 us (40%)
  waiting for transfers between devices  13.9 us (33%)
  Pallas kernels  10.4 us (25%)
  between operations  0.81 us (2%)
    ppermute x16, starting transfers between devices, swap(): return lax.ppermute(value, 'dp', [(i, i ^ bit) for i in range(count)])  16.8 us
    ppermute x16, waiting for transfers between devices, swap(): return lax.ppermute(value, 'dp', [(i, i ^ bit) for i in range(count)])  13.9 us
    pallas_call x1, Pallas kernels, hidden_rows(): pl.pallas_call(hidden_kernel, out_shape=jax.ShapeDtypeStruct((rows, colum...  4.12 us
    pallas_call x1, Pallas kernels, attend(): pl.pallas_call(functools.partial(attend_kernel, plane), out_shape=(jax.Sh...  2.65 us
    pallas_call x1, Pallas kernels, down_rows(): pl.pallas_call(down_kernel, out_shape=[jax.ShapeDtypeStruct((size, width...  2.31 us
  transfers between devices with their start and end apart: 16, of which 9 were waited for; matrix products, arithmetic and copies ran while one was open for 0% of the time, Pallas kernels for 1%

profile of v19, /device:TPU:0, one launch (start us, length us, event | category | flops | bytes accessed | tf_op | source)
XLA Modules:
  0.0 41.9 jit_solution(8679163820305067163)
XLA Ops:
  0.7 2.7 %attend.1 = (bf16[8,4096]{1,0:T(8,128)(2,1)}, bf16[8,3072]{1,0:T(8,128)(2,1)S(1)}, bf16[8,3072]{1,0:T(8,128)(2,1)S(1)}, bf16[8,3072]{1,0:T(8,128)(2,1)S(1)}, bf1...) custom-call(bf16[8,4096]{1,0:T(8,128)(2,1)} %refs_0_.1, ...), custom_call_target="tpu_custom_call" | custom-call | tf_op jit(solution)/shard_map/attend/pallas_call | solution.py:206
  3.3 3.1 %collective-permute-start = (bf16[8,3072]{1,0:T(8,128)(2,1)S(1)}, bf16[8,3072]{1,0:T(8,128)(2,1)S(1)}, u32[]{:S(2)}, u32[]{:S(2)}) collective-permute-start(bf16[8,3072]{1,0:T(8,128)(2,1)S(1)} %get-tuple-element.25), channel_id=1, source_target_pairs={{0,4},{1,5},{2,6},{3,7},{4,0},{5,1},{6,2},{7,3},{8,12},{9,13},{10,... | collective-permute-start | bytes 147464 | tf_op jit(solution)/shard_map/ppermute | solution.py:412
  6.4 2.5 %collective-permute-start.3 = (bf16[8,3072]{1,0:T(8,128)(2,1)S(1)}, bf16[8,3072]{1,0:T(8,128)(2,1)S(1)}, u32[]{:S(2)}, u32[]{:S(2)}) collective-permute-start(bf16[8,3072]{1,0:T(8,128)(2,1)S(1)} %get-tuple-element.26), channel_id=1, source_target_pairs={{0,12},{1,13},{2,14},{3,15},{4,8},{5,9},{6,10},{7,11},{8,4},{9,5},... | collective-permute-start | bytes 147464 | tf_op jit(solution)/shard_map/ppermute | solution.py:412
  8.9 0.1 collective-permute-start.4
  9.0 1.6 %collective-permute-start.1 = (bf16[16,3072]{1,0:T(8,128)(2,1)S(1)}, bf16[16,3072]{1,0:T(8,128)(2,1)S(1)}, u32[]{:S(2)}, u32[]{:S(2)}) collective-permute-start(bf16[16,3072]{1,0:T(8,128)(2,1)S(1)} %join.6.refs_1_), channel_id=1, source_target_pairs={{0,2},{1,3},{2,0},{3,1},{4,6},{5,7},{6,4},{7,5},{8,10},{9,11},{10,... | collective-permute-start | bytes 294920 | tf_op jit(solution)/shard_map/ppermute | solution.py:412
  10.6 2.3 %collective-permute-done.3.refs_1_ = bf16[8,3072]{1,0:T(8,128)(2,1)S(1)} collective-permute-done((bf16[8,3072]{1,0:T(8,128)(2,1)S(1)}, bf16[8,3072]{1,0:T(8,128)(2,1)S(1)}, u32[]{:S(2)}, u32[]{:S(2)}) %collective-permute-start.3) | collective-permute-done | bytes 49184 | tf_op jit(solution)/shard_map/ppermute | solution.py:412
  12.9 1.5 %collective-permute-done.4.refs_2_ = bf16[8,3072]{1,0:T(8,128)(2,1)S(1)} collective-permute-done((bf16[8,3072]{1,0:T(8,128)(2,1)S(1)}, bf16[8,3072]{1,0:T(8,128)(2,1)S(1)}, u32[]{:S(2)}, u32[]{:S(2)}) %collective-permute-start.4) | collective-permute-done | bytes 49184 | tf_op jit(solution)/shard_map/ppermute | solution.py:412
  14.4 1.6 %collective-permute-start.5 = (bf16[16,3072]{1,0:T(8,128)(2,1)S(1)}, bf16[16,3072]{1,0:T(8,128)(2,1)S(1)}, u32[]{:S(2)}, u32[]{:S(2)}) collective-permute-start(bf16[16,3072]{1,0:T(8,128)(2,1)S(1)} %join.9.refs_1_), channel_id=1, source_target_pairs={{0,2},{1,3},{2,0},{3,1},{4,6},{5,7},{6,4},{7,5},{8,10},{9,11},{10,... | collective-permute-start | bytes 294920 | tf_op jit(solution)/shard_map/ppermute | solution.py:412
  16.0 0.1 collective-permute-start.2
  16.1 3.0 %collective-permute-done.5.refs_2_ = bf16[16,3072]{1,0:T(8,128)(2,1)S(1)} collective-permute-done((bf16[16,3072]{1,0:T(8,128)(2,1)S(1)}, bf16[16,3072]{1,0:T(8,128)(2,1)S(1)}, u32[]{:S(2)}, u32[]{:S(2)}) %collective-permute-start.5) | collective-permute-done | bytes 98336 | tf_op jit(solution)/shard_map/ppermute | solution.py:412
  19.1 0.1 collective-permute-start.6
  19.2 0.0 collective-permute-done.2.refs_2_
  19.2 1.4 %collective-permute-done.6.refs_2_ = bf16[32,3072]{1,0:T(8,128)(2,1)S(1)} collective-permute-done((bf16[32,3072]{1,0:T(8,128)(2,1)S(1)}, bf16[32,3072]{1,0:T(8,128)(2,1)S(1)}, u32[]{:S(2)}, u32[]{:S(2)}) %collective-permute-start.6) | collective-permute-done | bytes 196640 | tf_op jit(solution)/shard_map/ppermute | solution.py:412
  20.7 4.1 %hidden.1 = bf16[128,1792]{1,0:T(8,128)(2,1)S(1)} custom-call(bf16[4096,1792]{1,0:T(8,128)(2,1)S(1)} %copy-done.1, bf16[4096,1792]{1,0:T(8,128)(2,1)S(1)} %copy-done.2, bf16[1792,4096]{1,0:T(8,128)(2,1)S(1)} %copy-done, bf16[64,3072]{1,0:T(8,128)(2,1)S(1)} %join.8.refs_0_, bf16[64,3072]{1,0:T(8,128)(2,1)S(1)} %join.11.refs_1_), custom_call_target="tpu_custom_call" | custom-call | flops 3758096384 | tf_op jit(solution)/shard_map/hidden/pallas_call | solution.py:256
  24.8 2.3 %down.1 = (bf16[32,3072]{1,0:T(8,128)(2,1)S(1)}, bf16[32,3072]{1,0:T(8,128)(2,1)S(1)}, bf16[32,3072]{1,0:T(8,128)(2,1)S(1)}, bf16[32,3072]{1,0:T(8,128)(2,1)S(1)}) custom-call(bf16[128,1792]{1,0:T(8,128)(2,1)S(1)} %hidden.1, bf16[1792,4096]{1,0:T(8,128)(2,1)S(1)} %copy-done), custom_call_target="tpu_custom_call" | custom-call | flops 1879048192 | tf_op jit(solution)/shard_map/down/pallas_call | solution.py:313
  27.1 0.2 collective-permute-start.8
  27.3 0.4 collective-permute-start.7
  27.7 0.9 %collective-permute-done.8.arrived = bf16[32,3072]{1,0:T(8,128)(2,1)S(1)} collective-permute-done((bf16[32,3072]{1,0:T(8,128)(2,1)S(1)}, bf16[32,3072]{1,0:T(8,128)(2,1)S(1)}, u32[]{:S(2)}, u32[]{:S(2)}) %collective-permute-start.8) | collective-permute-done | bytes 196640 | tf_op jit(solution)/shard_map/ppermute | solution.py:412
  28.7 1.6 %collective-permute-start.12 = (bf16[8,3072]{1,0:T(8,128)(2,1)S(1)}, bf16[8,3072]{1,0:T(8,128)(2,1)S(1)}, u32[]{:S(2)}, u32[]{:S(2)}) collective-permute-start(bf16[8,3072]{1,0:T(8,128)(2,1)S(1)} %get-tuple-element.39), channel_id=1, source_target_pairs={{0,2},{1,3},{2,0},{3,1},{4,6},{5,7},{6,4},{7,5},{8,10},{9,11},{10,... | collective-permute-start | bytes 147464 | tf_op jit(solution)/shard_map/ppermute | solution.py:412
  30.3 0.5 %collective-permute-start.11 = (bf16[8,3072]{1,0:T(8,128)(2,1)S(1)}, bf16[8,3072]{1,0:T(8,128)(2,1)S(1)}, u32[]{:S(2)}, u32[]{:S(2)}) collective-permute-start(bf16[8,3072]{1,0:T(8,128)(2,1)S(1)} %get-tuple-element.38), channel_id=1, source_target_pairs={{0,2},{1,3},{2,0},{3,1},{4,6},{5,7},{6,4},{7,5},{8,10},{9,11},{10,... | collective-permute-start | bytes 147464 | tf_op jit(solution)/shard_map/ppermute | solution.py:412
  30.8 1.6 %collective-permute-start.10 = (bf16[8,3072]{1,0:T(8,128)(2,1)S(1)}, bf16[8,3072]{1,0:T(8,128)(2,1)S(1)}, u32[]{:S(2)}, u32[]{:S(2)}) collective-permute-start(bf16[8,3072]{1,0:T(8,128)(2,1)S(1)} %get-tuple-element.36), channel_id=1, source_target_pairs={{0,2},{1,3},{2,0},{3,1},{4,6},{5,7},{6,4},{7,5},{8,10},{9,11},{10,... | collective-permute-start | bytes 147464 | tf_op jit(solution)/shard_map/ppermute | solution.py:412
  32.4 0.5 %collective-permute-start.9 = (bf16[8,3072]{1,0:T(8,128)(2,1)S(1)}, bf16[8,3072]{1,0:T(8,128)(2,1)S(1)}, u32[]{:S(2)}, u32[]{:S(2)}) collective-permute-start(bf16[8,3072]{1,0:T(8,128)(2,1)S(1)} %get-tuple-element.34), channel_id=1, source_target_pairs={{0,2},{1,3},{2,0},{3,1},{4,6},{5,7},{6,4},{7,5},{8,10},{9,11},{10,... | collective-permute-start | bytes 147464 | tf_op jit(solution)/shard_map/ppermute | solution.py:412
  32.9 0.1 collective-permute-done.12.arrived
  33.1 0.8 %collective-permute-start.14 = (bf16[8,3072]{1,0:T(8,128)(2,1)S(1)}, bf16[8,3072]{1,0:T(8,128)(2,1)S(1)}, u32[]{:S(2)}, u32[]{:S(2)}) collective-permute-start(bf16[8,3072]{1,0:T(8,128)(2,1)S(1)} %fold.8.after), channel_id=1, source_target_pairs={{0,8},{1,9},{2,10},{3,11},{4,12},{5,13},{6,14},{7,15},{8,0},{9,1},... | collective-permute-start | bytes 147464 | tf_op jit(solution)/shard_map/ppermute | solution.py:412
  33.8 0.8 %collective-permute-done.11.arrived = bf16[8,3072]{1,0:T(8,128)(2,1)S(1)} collective-permute-done((bf16[8,3072]{1,0:T(8,128)(2,1)S(1)}, bf16[8,3072]{1,0:T(8,128)(2,1)S(1)}, u32[]{:S(2)}, u32[]{:S(2)}) %collective-permute-start.11) | collective-permute-done | bytes 49184 | tf_op jit(solution)/shard_map/ppermute | solution.py:412
  34.6 2.2 %collective-permute-start.15 = (bf16[8,3072]{1,0:T(8,128)(2,1)S(1)}, bf16[8,3072]{1,0:T(8,128)(2,1)S(1)}, u32[]{:S(2)}, u32[]{:S(2)}) collective-permute-start(bf16[8,3072]{1,0:T(8,128)(2,1)S(1)} %fold.9.after), channel_id=1, source_target_pairs={{0,12},{1,13},{2,14},{3,15},{4,8},{5,9},{6,10},{7,11},{8,4},{9,5},... | collective-permute-start | bytes 147464 | tf_op jit(solution)/shard_map/ppermute | solution.py:412
  36.8 0.0 collective-permute-done.10.arrived
  36.8 0.1 collective-permute-start.13
  36.9 3.6 %collective-permute-done.15.three = bf16[8,3072]{1,0:T(8,128)(2,1)S(1)} collective-permute-done((bf16[8,3072]{1,0:T(8,128)(2,1)S(1)}, bf16[8,3072]{1,0:T(8,128)(2,1)S(1)}, u32[]{:S(2)}, u32[]{:S(2)}) %collective-permute-start.15) | collective-permute-done | bytes 49184 | tf_op jit(solution)/shard_map/ppermute | solution.py:412
  40.6 0.2 combine_far.1.total
  40.8 0.3 collective-permute-done.13.one
  41.1 0.8 %combine.1 = bf16[8,4096]{1,0:T(8,128)(2,1)} custom-call(f32[16,128]{1,0:T(8,128)S(1)} %get-tuple-element.22.refs_0_.after.share, bf16[4,16,128]{2,1,0:T(8,128)(2,1)S(1)} %get-tuple-element.23.take, bf16[8,3072]{1,0:T(8,128)(2,1)S(1)} %fold.11.zero, bf16[8,3072]{1,0:T(8,128)(2,1)S(1)} %collective-permute-done.13.one, f32[8,4096]{1,0:T(8,128)S(1)} %combine_far.1.total), custom_call_target="tpu_custom_call" | custom-call | bytes 16777216 | tf_op jit(solution)/shard_map/combine/pallas_call | solution.py:400
  (23 shorter events, 0.3 us)
Async XLA Ops:
  0.6 20.0 %copy-start = (bf16[1792,4096]{1,0:T(8,128)(2,1)S(1)}, bf16[1792,4096]{1,0:T(8,128)(2,1)}, u32[]{:S(2)}) copy-start(bf16[1792,4096]{1,0:T(8,128)(2,1)} %weight.1) | copy-start | bytes 44040196
  0.6 20.0 %copy-start.1 = (bf16[4096,1792]{1,0:T(8,128)(2,1)S(1)}, bf16[4096,1792]{1,0:T(8,128)(2,1)}, u32[]{:S(2)}) copy-start(bf16[4096,1792]{1,0:T(8,128)(2,1)} %gate_weight.1) | copy-start | bytes 44040196
  0.7 20.0 %copy-start.2 = (bf16[4096,1792]{1,0:T(8,128)(2,1)S(1)}, bf16[4096,1792]{1,0:T(8,128)(2,1)}, u32[]{:S(2)}) copy-start(bf16[4096,1792]{1,0:T(8,128)(2,1)} %up_weight.1) | copy-start | bytes 44040196
  3.3 5.7 %collective-permute-start = (bf16[8,3072]{1,0:T(8,128)(2,1)S(1)}, bf16[8,3072]{1,0:T(8,128)(2,1)S(1)}, u32[]{:S(2)}, u32[]{:S(2)}) collective-permute-start(bf16[8,3072]{1,0:T(8,128)(2,1)S(1)} %get-tuple-element.25), channel_id=1, source_target_pairs={{0,4},{1,5},{2,6},{3,7},{4,0},{5,1},{6,2},{7,3},{8,12},{9,13},{10,... | collective-permute-start | bytes 147464 | tf_op jit(solution)/shard_map/ppermute | solution.py:412
  6.4 6.5 %collective-permute-start.3 = (bf16[8,3072]{1,0:T(8,128)(2,1)S(1)}, bf16[8,3072]{1,0:T(8,128)(2,1)S(1)}, u32[]{:S(2)}, u32[]{:S(2)}) collective-permute-start(bf16[8,3072]{1,0:T(8,128)(2,1)S(1)} %get-tuple-element.26), channel_id=1, source_target_pairs={{0,12},{1,13},{2,14},{3,15},{4,8},{5,9},{6,10},{7,11},{8,4},{9,5},... | collective-permute-start | bytes 147464 | tf_op jit(solution)/shard_map/ppermute | solution.py:412
  8.9 5.5 %collective-permute-start.4 = (bf16[8,3072]{1,0:T(8,128)(2,1)S(1)}, bf16[8,3072]{1,0:T(8,128)(2,1)S(1)}, u32[]{:S(2)}, u32[]{:S(2)}) collective-permute-start(bf16[8,3072]{1,0:T(8,128)(2,1)S(1)} %get-tuple-element.27), channel_id=1, source_target_pairs={{0,8},{1,9},{2,10},{3,11},{4,12},{5,13},{6,14},{7,15},{8,0},{9,1},... | collective-permute-start | bytes 147464 | tf_op jit(solution)/shard_map/ppermute | solution.py:412
  9.0 7.0 %collective-permute-start.1 = (bf16[16,3072]{1,0:T(8,128)(2,1)S(1)}, bf16[16,3072]{1,0:T(8,128)(2,1)S(1)}, u32[]{:S(2)}, u32[]{:S(2)}) collective-permute-start(bf16[16,3072]{1,0:T(8,128)(2,1)S(1)} %join.6.refs_1_), channel_id=1, source_target_pairs={{0,2},{1,3},{2,0},{3,1},{4,6},{5,7},{6,4},{7,5},{8,10},{9,11},{10,... | collective-permute-start | bytes 294920 | tf_op jit(solution)/shard_map/ppermute | solution.py:412
  14.4 4.7 %collective-permute-start.5 = (bf16[16,3072]{1,0:T(8,128)(2,1)S(1)}, bf16[16,3072]{1,0:T(8,128)(2,1)S(1)}, u32[]{:S(2)}, u32[]{:S(2)}) collective-permute-start(bf16[16,3072]{1,0:T(8,128)(2,1)S(1)} %join.9.refs_1_), channel_id=1, source_target_pairs={{0,2},{1,3},{2,0},{3,1},{4,6},{5,7},{6,4},{7,5},{8,10},{9,11},{10,... | collective-permute-start | bytes 294920 | tf_op jit(solution)/shard_map/ppermute | solution.py:412
  16.0 3.2 %collective-permute-start.2 = (bf16[32,3072]{1,0:T(8,128)(2,1)S(1)}, bf16[32,3072]{1,0:T(8,128)(2,1)S(1)}, u32[]{:S(2)}, u32[]{:S(2)}) collective-permute-start(bf16[32,3072]{1,0:T(8,128)(2,1)S(1)} %join.7.refs_1_), channel_id=1, source_target_pairs={{0,1},{1,0},{2,3},{3,2},{4,5},{5,4},{6,7},{7,6},{8,9},{9,8},{10,11... | collective-permute-start | bytes 589832 | tf_op jit(solution)/shard_map/ppermute | solution.py:412
  19.1 1.5 %collective-permute-start.6 = (bf16[32,3072]{1,0:T(8,128)(2,1)S(1)}, bf16[32,3072]{1,0:T(8,128)(2,1)S(1)}, u32[]{:S(2)}, u32[]{:S(2)}) collective-permute-start(bf16[32,3072]{1,0:T(8,128)(2,1)S(1)} %join.10.refs_1_), channel_id=1, source_target_pairs={{0,1},{1,0},{2,3},{3,2},{4,5},{5,4},{6,7},{7,6},{8,9},{9,8},{10,11... | collective-permute-start | bytes 589832 | tf_op jit(solution)/shard_map/ppermute | solution.py:412
  27.1 1.5 %collective-permute-start.8 = (bf16[32,3072]{1,0:T(8,128)(2,1)S(1)}, bf16[32,3072]{1,0:T(8,128)(2,1)S(1)}, u32[]{:S(2)}, u32[]{:S(2)}) collective-permute-start(bf16[32,3072]{1,0:T(8,128)(2,1)S(1)} %get-tuple-element.31), channel_id=1, source_target_pairs={{0,1},{1,0},{2,3},{3,2},{4,5},{5,4},{6,7},{7,6},{8,9},{9,8},{10,11... | collective-permute-start | bytes 589832 | tf_op jit(solution)/shard_map/ppermute | solution.py:412
  27.3 3.4 %collective-permute-start.7 = (bf16[32,3072]{1,0:T(8,128)(2,1)S(1)}, bf16[32,3072]{1,0:T(8,128)(2,1)S(1)}, u32[]{:S(2)}, u32[]{:S(2)}) collective-permute-start(bf16[32,3072]{1,0:T(8,128)(2,1)S(1)} %get-tuple-element.29), channel_id=1, source_target_pairs={{0,1},{1,0},{2,3},{3,2},{4,5},{5,4},{6,7},{7,6},{8,9},{9,8},{10,11... | collective-permute-start | bytes 589832 | tf_op jit(solution)/shard_map/ppermute | solution.py:412
  28.7 4.4 %collective-permute-start.12 = (bf16[8,3072]{1,0:T(8,128)(2,1)S(1)}, bf16[8,3072]{1,0:T(8,128)(2,1)S(1)}, u32[]{:S(2)}, u32[]{:S(2)}) collective-permute-start(bf16[8,3072]{1,0:T(8,128)(2,1)S(1)} %get-tuple-element.39), channel_id=1, source_target_pairs={{0,2},{1,3},{2,0},{3,1},{4,6},{5,7},{6,4},{7,5},{8,10},{9,11},{10,... | collective-permute-start | bytes 147464 | tf_op jit(solution)/shard_map/ppermute | solution.py:412
  30.3 4.3 %collective-permute-start.11 = (bf16[8,3072]{1,0:T(8,128)(2,1)S(1)}, bf16[8,3072]{1,0:T(8,128)(2,1)S(1)}, u32[]{:S(2)}, u32[]{:S(2)}) collective-permute-start(bf16[8,3072]{1,0:T(8,128)(2,1)S(1)} %get-tuple-element.38), channel_id=1, source_target_pairs={{0,2},{1,3},{2,0},{3,1},{4,6},{5,7},{6,4},{7,5},{8,10},{9,11},{10,... | collective-permute-start | bytes 147464 | tf_op jit(solution)/shard_map/ppermute | solution.py:412
  30.8 6.0 %collective-permute-start.10 = (bf16[8,3072]{1,0:T(8,128)(2,1)S(1)}, bf16[8,3072]{1,0:T(8,128)(2,1)S(1)}, u32[]{:S(2)}, u32[]{:S(2)}) collective-permute-start(bf16[8,3072]{1,0:T(8,128)(2,1)S(1)} %get-tuple-element.36), channel_id=1, source_target_pairs={{0,2},{1,3},{2,0},{3,1},{4,6},{5,7},{6,4},{7,5},{8,10},{9,11},{10,... | collective-permute-start | bytes 147464 | tf_op jit(solution)/shard_map/ppermute | solution.py:412
  32.4 4.5 %collective-permute-start.9 = (bf16[8,3072]{1,0:T(8,128)(2,1)S(1)}, bf16[8,3072]{1,0:T(8,128)(2,1)S(1)}, u32[]{:S(2)}, u32[]{:S(2)}) collective-permute-start(bf16[8,3072]{1,0:T(8,128)(2,1)S(1)} %get-tuple-element.34), channel_id=1, source_target_pairs={{0,2},{1,3},{2,0},{3,1},{4,6},{5,7},{6,4},{7,5},{8,10},{9,11},{10,... | collective-permute-start | bytes 147464 | tf_op jit(solution)/shard_map/ppermute | solution.py:412
  33.1 7.5 %collective-permute-start.14 = (bf16[8,3072]{1,0:T(8,128)(2,1)S(1)}, bf16[8,3072]{1,0:T(8,128)(2,1)S(1)}, u32[]{:S(2)}, u32[]{:S(2)}) collective-permute-start(bf16[8,3072]{1,0:T(8,128)(2,1)S(1)} %fold.8.after), channel_id=1, source_target_pairs={{0,8},{1,9},{2,10},{3,11},{4,12},{5,13},{6,14},{7,15},{8,0},{9,1},... | collective-permute-start | bytes 147464 | tf_op jit(solution)/shard_map/ppermute | solution.py:412
  34.6 6.0 %collective-permute-start.15 = (bf16[8,3072]{1,0:T(8,128)(2,1)S(1)}, bf16[8,3072]{1,0:T(8,128)(2,1)S(1)}, u32[]{:S(2)}, u32[]{:S(2)}) collective-permute-start(bf16[8,3072]{1,0:T(8,128)(2,1)S(1)} %fold.9.after), channel_id=1, source_target_pairs={{0,12},{1,13},{2,14},{3,15},{4,8},{5,9},{6,10},{7,11},{8,4},{9,5},... | collective-permute-start | bytes 147464 | tf_op jit(solution)/shard_map/ppermute | solution.py:412
  36.8 4.3 %collective-permute-start.13 = (bf16[8,3072]{1,0:T(8,128)(2,1)S(1)}, bf16[8,3072]{1,0:T(8,128)(2,1)S(1)}, u32[]{:S(2)}, u32[]{:S(2)}) collective-permute-start(bf16[8,3072]{1,0:T(8,128)(2,1)S(1)} %fold.10.after), channel_id=1, source_target_pairs={{0,4},{1,5},{2,6},{3,7},{4,0},{5,1},{6,2},{7,3},{8,12},{9,13},{10,... | collective-permute-start | bytes 147464 | tf_op jit(solution)/shard_map/ppermute | solution.py:412

commit v20 on v19

--- a/solution.py
+++ b/solution.py
@@ -438,8 +438,9 @@
     for k in (1, 3, 2):
         packed[k] = swap(packed[k], count, k * plane)
     waves = [join(share, *packed[:2]), join(share, packed[3], packed[2], backwards=True)]
-    for bit in bits:
+    for bit in bits[:-1]:
         waves = [join(share, wave, swap(wave, count, bit)) for wave in waves]
+    waves = [piece for wave in waves for piece in (wave, swap(wave, count, bits[-1]))]
 
     hidden = hidden_rows(waves, gate_weight, up_weight, down_weight)
 

time: 42.1 us -> 42 us (level)
  no operation moved by 1% of the time
where the time goes in v20:
time: 42 us; the launch traced here: 41.9 us
  starting transfers between devices  16.8 us (40%)
  waiting for transfers between devices  14 us (33%)
  Pallas kernels  10.3 us (25%)
  between operations  0.78 us (2%)
    ppermute x16, starting transfers between devices, swap(): return lax.ppermute(value, 'dp', [(i, i ^ bit) for i in range(count)])  16.8 us
    ppermute x16, waiting for transfers between devices, swap(): return lax.ppermute(value, 'dp', [(i, i ^ bit) for i in range(count)])  14 us
    pallas_call x1, Pallas kernels, hidden_rows(): pl.pallas_call(hidden_kernel, out_shape=jax.ShapeDtypeStruct((rows, colum...  4.12 us
    pallas_call x1, Pallas kernels, attend(): pl.pallas_call(functools.partial(attend_kernel, plane), out_shape=(jax.Sh...  2.65 us
    pallas_call x1, Pallas kernels, down_rows(): pl.pallas_call(down_kernel, out_shape=[jax.ShapeDtypeStruct((size, width...  2.3 us
  transfers between devices with their start and end apart: 16, of which 9 were waited for; matrix products, arithmetic and copies ran while one was open for 0% of the time, Pallas kernels for 1%

profile of v20, /device:TPU:0, one launch (start us, length us, event | category | flops | bytes accessed | tf_op | source)
XLA Modules:
  0.0 41.9 jit_solution(9234931030964752375)
XLA Ops:
  0.7 2.7 %attend.1 = (bf16[8,4096]{1,0:T(8,128)(2,1)}, bf16[8,3072]{1,0:T(8,128)(2,1)S(1)}, bf16[8,3072]{1,0:T(8,128)(2,1)S(1)}, bf16[8,3072]{1,0:T(8,128)(2,1)S(1)}, bf1...) custom-call(bf16[8,4096]{1,0:T(8,128)(2,1)} %refs_0_.1, ...), custom_call_target="tpu_custom_call" | custom-call | tf_op jit(solution)/shard_map/attend/pallas_call | solution.py:206
  3.3 3.1 %collective-permute-start = (bf16[8,3072]{1,0:T(8,128)(2,1)S(1)}, bf16[8,3072]{1,0:T(8,128)(2,1)S(1)}, u32[]{:S(2)}, u32[]{:S(2)}) collective-permute-start(bf16[8,3072]{1,0:T(8,128)(2,1)S(1)} %get-tuple-element.25), channel_id=1, source_target_pairs={{0,4},{1,5},{2,6},{3,7},{4,0},{5,1},{6,2},{7,3},{8,12},{9,13},{10,... | collective-permute-start | bytes 147464 | tf_op jit(solution)/shard_map/ppermute | solution.py:412
  6.4 2.5 %collective-permute-start.3 = (bf16[8,3072]{1,0:T(8,128)(2,1)S(1)}, bf16[8,3072]{1,0:T(8,128)(2,1)S(1)}, u32[]{:S(2)}, u32[]{:S(2)}) collective-permute-start(bf16[8,3072]{1,0:T(8,128)(2,1)S(1)} %get-tuple-element.26), channel_id=1, source_target_pairs={{0,12},{1,13},{2,14},{3,15},{4,8},{5,9},{6,10},{7,11},{8,4},{9,5},... | collective-permute-start | bytes 147464 | tf_op jit(solution)/shard_map/ppermute | solution.py:412
  8.9 0.1 collective-permute-start.4
  9.0 1.6 %collective-permute-start.1 = (bf16[16,3072]{1,0:T(8,128)(2,1)S(1)}, bf16[16,3072]{1,0:T(8,128)(2,1)S(1)}, u32[]{:S(2)}, u32[]{:S(2)}) collective-permute-start(bf16[16,3072]{1,0:T(8,128)(2,1)S(1)} %join.4.refs_1_), channel_id=1, source_target_pairs={{0,2},{1,3},{2,0},{3,1},{4,6},{5,7},{6,4},{7,5},{8,10},{9,11},{10,... | collective-permute-start | bytes 294920 | tf_op jit(solution)/shard_map/ppermute | solution.py:412
  10.6 2.3 %collective-permute-done.3.refs_1_ = bf16[8,3072]{1,0:T(8,128)(2,1)S(1)} collective-permute-done((bf16[8,3072]{1,0:T(8,128)(2,1)S(1)}, bf16[8,3072]{1,0:T(8,128)(2,1)S(1)}, u32[]{:S(2)}, u32[]{:S(2)}) %collective-permute-start.3) | collective-permute-done | bytes 49184 | tf_op jit(solution)/shard_map/ppermute | solution.py:412
  12.9 1.5 %collective-permute-done.4.refs_2_ = bf16[8,3072]{1,0:T(8,128)(2,1)S(1)} collective-permute-done((bf16[8,3072]{1,0:T(8,128)(2,1)S(1)}, bf16[8,3072]{1,0:T(8,128)(2,1)S(1)}, u32[]{:S(2)}, u32[]{:S(2)}) %collective-permute-start.4) | collective-permute-done | bytes 49184 | tf_op jit(solution)/shard_map/ppermute | solution.py:412
  14.4 1.6 %collective-permute-start.5 = (bf16[16,3072]{1,0:T(8,128)(2,1)S(1)}, bf16[16,3072]{1,0:T(8,128)(2,1)S(1)}, u32[]{:S(2)}, u32[]{:S(2)}) collective-permute-start(bf16[16,3072]{1,0:T(8,128)(2,1)S(1)} %join.6.refs_1_), channel_id=1, source_target_pairs={{0,2},{1,3},{2,0},{3,1},{4,6},{5,7},{6,4},{7,5},{8,10},{9,11},{10,... | collective-permute-start | bytes 294920 | tf_op jit(solution)/shard_map/ppermute | solution.py:412
  16.0 0.0 collective-permute-done.1.refs_2_
  16.0 0.1 collective-permute-start.2
  16.1 3.0 %collective-permute-done.5.refs_2_ = bf16[16,3072]{1,0:T(8,128)(2,1)S(1)} collective-permute-done((bf16[16,3072]{1,0:T(8,128)(2,1)S(1)}, bf16[16,3072]{1,0:T(8,128)(2,1)S(1)}, u32[]{:S(2)}, u32[]{:S(2)}) %collective-permute-start.5) | collective-permute-done | bytes 98336 | tf_op jit(solution)/shard_map/ppermute | solution.py:412
  19.1 0.1 collective-permute-start.6
  19.2 0.0 collective-permute-done.2.refs_1_
  19.2 1.4 %collective-permute-done.6.refs_3_ = bf16[32,3072]{1,0:T(8,128)(2,1)S(1)} collective-permute-done((bf16[32,3072]{1,0:T(8,128)(2,1)S(1)}, bf16[32,3072]{1,0:T(8,128)(2,1)S(1)}, u32[]{:S(2)}, u32[]{:S(2)}) %collective-permute-start.6) | collective-permute-done | bytes 196640 | tf_op jit(solution)/shard_map/ppermute | solution.py:412
  20.6 4.1 %hidden.1 = bf16[128,1792]{1,0:T(8,128)(2,1)S(1)} custom-call(bf16[4096,1792]{1,0:T(8,128)(2,1)S(1)} %copy-done.1, bf16[4096,1792]{1,0:T(8,128)(2,1)S(1)} %copy-done.2, bf16[1792,4096]{1,0:T(8,128)(2,1)S(1)} %copy-done, bf16[32,3072]{1,0:T(8,128)(2,1)S(1)} %join.5.refs_0_, bf16[32,3072]{1,0:T(8,128)(2,1)S(1)} %collective-permute-done.2.refs_1_, ...), custom_call_target="tpu_custom_call" | custom-call | flops 3758096384 | tf_op jit(solution)/shard_map/hidden/pallas_call | solution.py:256
  24.8 2.3 %down.1 = (bf16[32,3072]{1,0:T(8,128)(2,1)S(1)}, bf16[32,3072]{1,0:T(8,128)(2,1)S(1)}, bf16[32,3072]{1,0:T(8,128)(2,1)S(1)}, bf16[32,3072]{1,0:T(8,128)(2,1)S(1)}) custom-call(bf16[128,1792]{1,0:T(8,128)(2,1)S(1)} %hidden.1, bf16[1792,4096]{1,0:T(8,128)(2,1)S(1)} %copy-done), custom_call_target="tpu_custom_call" | custom-call | flops 1879048192 | tf_op jit(solution)/shard_map/down/pallas_call | solution.py:313
  27.1 0.2 collective-permute-start.8
  27.3 0.4 collective-permute-start.7
  27.7 0.9 %collective-permute-done.8.arrived = bf16[32,3072]{1,0:T(8,128)(2,1)S(1)} collective-permute-done((bf16[32,3072]{1,0:T(8,128)(2,1)S(1)}, bf16[32,3072]{1,0:T(8,128)(2,1)S(1)}, u32[]{:S(2)}, u32[]{:S(2)}) %collective-permute-start.8) | collective-permute-done | bytes 196640 | tf_op jit(solution)/shard_map/ppermute | solution.py:412
  28.6 1.6 %collective-permute-start.12 = (bf16[8,3072]{1,0:T(8,128)(2,1)S(1)}, bf16[8,3072]{1,0:T(8,128)(2,1)S(1)}, u32[]{:S(2)}, u32[]{:S(2)}) collective-permute-start(bf16[8,3072]{1,0:T(8,128)(2,1)S(1)} %get-tuple-element.39), channel_id=1, source_target_pairs={{0,2},{1,3},{2,0},{3,1},{4,6},{5,7},{6,4},{7,5},{8,10},{9,11},{10,... | collective-permute-start | bytes 147464 | tf_op jit(solution)/shard_map/ppermute | solution.py:412
  30.2 0.5 %collective-permute-start.11 = (bf16[8,3072]{1,0:T(8,128)(2,1)S(1)}, bf16[8,3072]{1,0:T(8,128)(2,1)S(1)}, u32[]{:S(2)}, u32[]{:S(2)}) collective-permute-start(bf16[8,3072]{1,0:T(8,128)(2,1)S(1)} %get-tuple-element.38), channel_id=1, source_target_pairs={{0,2},{1,3},{2,0},{3,1},{4,6},{5,7},{6,4},{7,5},{8,10},{9,11},{10,... | collective-permute-start | bytes 147464 | tf_op jit(solution)/shard_map/ppermute | solution.py:412
  30.8 1.6 %collective-permute-start.10 = (bf16[8,3072]{1,0:T(8,128)(2,1)S(1)}, bf16[8,3072]{1,0:T(8,128)(2,1)S(1)}, u32[]{:S(2)}, u32[]{:S(2)}) collective-permute-start(bf16[8,3072]{1,0:T(8,128)(2,1)S(1)} %get-tuple-element.36), channel_id=1, source_target_pairs={{0,2},{1,3},{2,0},{3,1},{4,6},{5,7},{6,4},{7,5},{8,10},{9,11},{10,... | collective-permute-start | bytes 147464 | tf_op jit(solution)/shard_map/ppermute | solution.py:412
  32.4 0.5 %collective-permute-start.9 = (bf16[8,3072]{1,0:T(8,128)(2,1)S(1)}, bf16[8,3072]{1,0:T(8,128)(2,1)S(1)}, u32[]{:S(2)}, u32[]{:S(2)}) collective-permute-start(bf16[8,3072]{1,0:T(8,128)(2,1)S(1)} %get-tuple-element.34), channel_id=1, source_target_pairs={{0,2},{1,3},{2,0},{3,1},{4,6},{5,7},{6,4},{7,5},{8,10},{9,11},{10,... | collective-permute-start | bytes 147464 | tf_op jit(solution)/shard_map/ppermute | solution.py:412
  32.9 0.1 collective-permute-done.12.arrived
  33.0 0.8 %collective-permute-start.14 = (bf16[8,3072]{1,0:T(8,128)(2,1)S(1)}, bf16[8,3072]{1,0:T(8,128)(2,1)S(1)}, u32[]{:S(2)}, u32[]{:S(2)}) collective-permute-start(bf16[8,3072]{1,0:T(8,128)(2,1)S(1)} %fold.8.after), channel_id=1, source_target_pairs={{0,8},{1,9},{2,10},{3,11},{4,12},{5,13},{6,14},{7,15},{8,0},{9,1},... | collective-permute-start | bytes 147464 | tf_op jit(solution)/shard_map/ppermute | solution.py:412
  33.8 0.8 %collective-permute-done.11.arrived = bf16[8,3072]{1,0:T(8,128)(2,1)S(1)} collective-permute-done((bf16[8,3072]{1,0:T(8,128)(2,1)S(1)}, bf16[8,3072]{1,0:T(8,128)(2,1)S(1)}, u32[]{:S(2)}, u32[]{:S(2)}) %collective-permute-start.11) | collective-permute-done | bytes 49184 | tf_op jit(solution)/shard_map/ppermute | solution.py:412
  34.6 2.2 %collective-permute-start.15 = (bf16[8,3072]{1,0:T(8,128)(2,1)S(1)}, bf16[8,3072]{1,0:T(8,128)(2,1)S(1)}, u32[]{:S(2)}, u32[]{:S(2)}) collective-permute-start(bf16[8,3072]{1,0:T(8,128)(2,1)S(1)} %fold.9.after), channel_id=1, source_target_pairs={{0,12},{1,13},{2,14},{3,15},{4,8},{5,9},{6,10},{7,11},{8,4},{9,5},... | collective-permute-start | bytes 147464 | tf_op jit(solution)/shard_map/ppermute | solution.py:412
  36.8 0.1 collective-permute-start.13
  36.9 3.6 %collective-permute-done.15.three = bf16[8,3072]{1,0:T(8,128)(2,1)S(1)} collective-permute-done((bf16[8,3072]{1,0:T(8,128)(2,1)S(1)}, bf16[8,3072]{1,0:T(8,128)(2,1)S(1)}, u32[]{:S(2)}, u32[]{:S(2)}) %collective-permute-start.15) | collective-permute-done | bytes 49184 | tf_op jit(solution)/shard_map/ppermute | solution.py:412
  40.5 0.2 combine_far.1.total
  40.8 0.3 collective-permute-done.13.one
  41.1 0.8 %combine.1 = bf16[8,4096]{1,0:T(8,128)(2,1)} custom-call(f32[16,128]{1,0:T(8,128)S(1)} %get-tuple-element.22.refs_0_.after.share, bf16[4,16,128]{2,1,0:T(8,128)(2,1)S(1)} %get-tuple-element.23.take, bf16[8,3072]{1,0:T(8,128)(2,1)S(1)} %fold.11.zero, bf16[8,3072]{1,0:T(8,128)(2,1)S(1)} %collective-permute-done.13.one, f32[8,4096]{1,0:T(8,128)S(1)} %combine_far.1.total), custom_call_target="tpu_custom_call" | custom-call | bytes 16777216 | tf_op jit(solution)/shard_map/combine/pallas_call | solution.py:400
  (21 shorter events, 0.2 us)
Async XLA Ops:
  0.6 20.0 %copy-start = (bf16[1792,4096]{1,0:T(8,128)(2,1)S(1)}, bf16[1792,4096]{1,0:T(8,128)(2,1)}, u32[]{:S(2)}) copy-start(bf16[1792,4096]{1,0:T(8,128)(2,1)} %weight.1) | copy-start | bytes 44040196
  0.6 20.0 %copy-start.1 = (bf16[4096,1792]{1,0:T(8,128)(2,1)S(1)}, bf16[4096,1792]{1,0:T(8,128)(2,1)}, u32[]{:S(2)}) copy-start(bf16[4096,1792]{1,0:T(8,128)(2,1)} %gate_weight.1) | copy-start | bytes 44040196
  0.7 20.0 %copy-start.2 = (bf16[4096,1792]{1,0:T(8,128)(2,1)S(1)}, bf16[4096,1792]{1,0:T(8,128)(2,1)}, u32[]{:S(2)}) copy-start(bf16[4096,1792]{1,0:T(8,128)(2,1)} %up_weight.1) | copy-start | bytes 44040196
  3.3 5.7 %collective-permute-start = (bf16[8,3072]{1,0:T(8,128)(2,1)S(1)}, bf16[8,3072]{1,0:T(8,128)(2,1)S(1)}, u32[]{:S(2)}, u32[]{:S(2)}) collective-permute-start(bf16[8,3072]{1,0:T(8,128)(2,1)S(1)} %get-tuple-element.25), channel_id=1, source_target_pairs={{0,4},{1,5},{2,6},{3,7},{4,0},{5,1},{6,2},{7,3},{8,12},{9,13},{10,... | collective-permute-start | bytes 147464 | tf_op jit(solution)/shard_map/ppermute | solution.py:412
  6.4 6.5 %collective-permute-start.3 = (bf16[8,3072]{1,0:T(8,128)(2,1)S(1)}, bf16[8,3072]{1,0:T(8,128)(2,1)S(1)}, u32[]{:S(2)}, u32[]{:S(2)}) collective-permute-start(bf16[8,3072]{1,0:T(8,128)(2,1)S(1)} %get-tuple-element.26), channel_id=1, source_target_pairs={{0,12},{1,13},{2,14},{3,15},{4,8},{5,9},{6,10},{7,11},{8,4},{9,5},... | collective-permute-start | bytes 147464 | tf_op jit(solution)/shard_map/ppermute | solution.py:412
  8.9 5.5 %collective-permute-start.4 = (bf16[8,3072]{1,0:T(8,128)(2,1)S(1)}, bf16[8,3072]{1,0:T(8,128)(2,1)S(1)}, u32[]{:S(2)}, u32[]{:S(2)}) collective-permute-start(bf16[8,3072]{1,0:T(8,128)(2,1)S(1)} %get-tuple-element.27), channel_id=1, source_target_pairs={{0,8},{1,9},{2,10},{3,11},{4,12},{5,13},{6,14},{7,15},{8,0},{9,1},... | collective-permute-start | bytes 147464 | tf_op jit(solution)/shard_map/ppermute | solution.py:412
  9.0 7.0 %collective-permute-start.1 = (bf16[16,3072]{1,0:T(8,128)(2,1)S(1)}, bf16[16,3072]{1,0:T(8,128)(2,1)S(1)}, u32[]{:S(2)}, u32[]{:S(2)}) collective-permute-start(bf16[16,3072]{1,0:T(8,128)(2,1)S(1)} %join.4.refs_1_), channel_id=1, source_target_pairs={{0,2},{1,3},{2,0},{3,1},{4,6},{5,7},{6,4},{7,5},{8,10},{9,11},{10,... | collective-permute-start | bytes 294920 | tf_op jit(solution)/shard_map/ppermute | solution.py:412
  14.4 4.7 %collective-permute-start.5 = (bf16[16,3072]{1,0:T(8,128)(2,1)S(1)}, bf16[16,3072]{1,0:T(8,128)(2,1)S(1)}, u32[]{:S(2)}, u32[]{:S(2)}) collective-permute-start(bf16[16,3072]{1,0:T(8,128)(2,1)S(1)} %join.6.refs_1_), channel_id=1, source_target_pairs={{0,2},{1,3},{2,0},{3,1},{4,6},{5,7},{6,4},{7,5},{8,10},{9,11},{10,... | collective-permute-start | bytes 294920 | tf_op jit(solution)/shard_map/ppermute | solution.py:412
  16.0 3.2 %collective-permute-start.2 = (bf16[32,3072]{1,0:T(8,128)(2,1)S(1)}, bf16[32,3072]{1,0:T(8,128)(2,1)S(1)}, u32[]{:S(2)}, u32[]{:S(2)}) collective-permute-start(bf16[32,3072]{1,0:T(8,128)(2,1)S(1)} %join.5.refs_0_), channel_id=1, source_target_pairs={{0,1},{1,0},{2,3},{3,2},{4,5},{5,4},{6,7},{7,6},{8,9},{9,8},{10,11... | collective-permute-start | bytes 589832 | tf_op jit(solution)/shard_map/ppermute | solution.py:412
  19.1 1.5 %collective-permute-start.6 = (bf16[32,3072]{1,0:T(8,128)(2,1)S(1)}, bf16[32,3072]{1,0:T(8,128)(2,1)S(1)}, u32[]{:S(2)}, u32[]{:S(2)}) collective-permute-start(bf16[32,3072]{1,0:T(8,128)(2,1)S(1)} %join.7.refs_2_), channel_id=1, source_target_pairs={{0,1},{1,0},{2,3},{3,2},{4,5},{5,4},{6,7},{7,6},{8,9},{9,8},{10,11... | collective-permute-start | bytes 589832 | tf_op jit(solution)/shard_map/ppermute | solution.py:412
  27.1 1.5 %collective-permute-start.8 = (bf16[32,3072]{1,0:T(8,128)(2,1)S(1)}, bf16[32,3072]{1,0:T(8,128)(2,1)S(1)}, u32[]{:S(2)}, u32[]{:S(2)}) collective-permute-start(bf16[32,3072]{1,0:T(8,128)(2,1)S(1)} %get-tuple-element.31), channel_id=1, source_target_pairs={{0,1},{1,0},{2,3},{3,2},{4,5},{5,4},{6,7},{7,6},{8,9},{9,8},{10,11... | collective-permute-start | bytes 589832 | tf_op jit(solution)/shard_map/ppermute | solution.py:412
  27.3 3.5 %collective-permute-start.7 = (bf16[32,3072]{1,0:T(8,128)(2,1)S(1)}, bf16[32,3072]{1,0:T(8,128)(2,1)S(1)}, u32[]{:S(2)}, u32[]{:S(2)}) collective-permute-start(bf16[32,3072]{1,0:T(8,128)(2,1)S(1)} %get-tuple-element.29), channel_id=1, source_target_pairs={{0,1},{1,0},{2,3},{3,2},{4,5},{5,4},{6,7},{7,6},{8,9},{9,8},{10,11... | collective-permute-start | bytes 589832 | tf_op jit(solution)/shard_map/ppermute | solution.py:412
  28.6 4.4 %collective-permute-start.12 = (bf16[8,3072]{1,0:T(8,128)(2,1)S(1)}, bf16[8,3072]{1,0:T(8,128)(2,1)S(1)}, u32[]{:S(2)}, u32[]{:S(2)}) collective-permute-start(bf16[8,3072]{1,0:T(8,128)(2,1)S(1)} %get-tuple-element.39), channel_id=1, source_target_pairs={{0,2},{1,3},{2,0},{3,1},{4,6},{5,7},{6,4},{7,5},{8,10},{9,11},{10,... | collective-permute-start | bytes 147464 | tf_op jit(solution)/shard_map/ppermute | solution.py:412
  30.2 4.3 %collective-permute-start.11 = (bf16[8,3072]{1,0:T(8,128)(2,1)S(1)}, bf16[8,3072]{1,0:T(8,128)(2,1)S(1)}, u32[]{:S(2)}, u32[]{:S(2)}) collective-permute-start(bf16[8,3072]{1,0:T(8,128)(2,1)S(1)} %get-tuple-element.38), channel_id=1, source_target_pairs={{0,2},{1,3},{2,0},{3,1},{4,6},{5,7},{6,4},{7,5},{8,10},{9,11},{10,... | collective-permute-start | bytes 147464 | tf_op jit(solution)/shard_map/ppermute | solution.py:412
  30.8 6.0 %collective-permute-start.10 = (bf16[8,3072]{1,0:T(8,128)(2,1)S(1)}, bf16[8,3072]{1,0:T(8,128)(2,1)S(1)}, u32[]{:S(2)}, u32[]{:S(2)}) collective-permute-start(bf16[8,3072]{1,0:T(8,128)(2,1)S(1)} %get-tuple-element.36), channel_id=1, source_target_pairs={{0,2},{1,3},{2,0},{3,1},{4,6},{5,7},{6,4},{7,5},{8,10},{9,11},{10,... | collective-permute-start | bytes 147464 | tf_op jit(solution)/shard_map/ppermute | solution.py:412
  32.4 4.5 %collective-permute-start.9 = (bf16[8,3072]{1,0:T(8,128)(2,1)S(1)}, bf16[8,3072]{1,0:T(8,128)(2,1)S(1)}, u32[]{:S(2)}, u32[]{:S(2)}) collective-permute-start(bf16[8,3072]{1,0:T(8,128)(2,1)S(1)} %get-tuple-element.34), channel_id=1, source_target_pairs={{0,2},{1,3},{2,0},{3,1},{4,6},{5,7},{6,4},{7,5},{8,10},{9,11},{10,... | collective-permute-start | bytes 147464 | tf_op jit(solution)/shard_map/ppermute | solution.py:412
  33.0 7.5 %collective-permute-start.14 = (bf16[8,3072]{1,0:T(8,128)(2,1)S(1)}, bf16[8,3072]{1,0:T(8,128)(2,1)S(1)}, u32[]{:S(2)}, u32[]{:S(2)}) collective-permute-start(bf16[8,3072]{1,0:T(8,128)(2,1)S(1)} %fold.8.after), channel_id=1, source_target_pairs={{0,8},{1,9},{2,10},{3,11},{4,12},{5,13},{6,14},{7,15},{8,0},{9,1},... | collective-permute-start | bytes 147464 | tf_op jit(solution)/shard_map/ppermute | solution.py:412
  34.6 6.0 %collective-permute-start.15 = (bf16[8,3072]{1,0:T(8,128)(2,1)S(1)}, bf16[8,3072]{1,0:T(8,128)(2,1)S(1)}, u32[]{:S(2)}, u32[]{:S(2)}) collective-permute-start(bf16[8,3072]{1,0:T(8,128)(2,1)S(1)} %fold.9.after), channel_id=1, source_target_pairs={{0,12},{1,13},{2,14},{3,15},{4,8},{5,9},{6,10},{7,11},{8,4},{9,5},... | collective-permute-start | bytes 147464 | tf_op jit(solution)/shard_map/ppermute | solution.py:412
  36.8 4.3 %collective-permute-start.13 = (bf16[8,3072]{1,0:T(8,128)(2,1)S(1)}, bf16[8,3072]{1,0:T(8,128)(2,1)S(1)}, u32[]{:S(2)}, u32[]{:S(2)}) collective-permute-start(bf16[8,3072]{1,0:T(8,128)(2,1)S(1)} %fold.10.after), channel_id=1, source_target_pairs={{0,4},{1,5},{2,6},{3,7},{4,0},{5,1},{6,2},{7,3},{8,12},{9,13},{10,... | collective-permute-start | bytes 147464 | tf_op jit(solution)/shard_map/ppermute | solution.py:412

commit v21 on v20

--- a/solution.py
+++ b/solution.py
@@ -226,7 +226,7 @@
 def hidden_kernel(gate_weight, up_weight, down_weight, *refs):
     waves, hidden = refs[:-1], refs[-1]
     columns = gate_weight.shape[1]
-    step = 512
+    step = 896
     quarter = waves[0].shape[1] // 3
     blocks = jnp.concatenate([wave[...] for wave in waves], axis=0)
     size = 128

time: 42 us -> 42.6 us (1.014)
  Pallas kernels: 10.3 us -> 10.9 us
    pallas_call x1, Pallas kernels: 4.12 us -> 4.67 us  [hidden_rows(): pl.pallas_call(hidden_kernel, out_shape=jax.ShapeDtypeStruct((rows, colum...]
where the time goes in v21:
time: 42.6 us; the launch traced here: 42.4 us
  starting transfers between devices  16.8 us (39%)
  waiting for transfers between devices  14 us (33%)
  Pallas kernels  10.9 us (26%)
  between operations  0.78 us (2%)
    ppermute x16, starting transfers between devices, swap(): return lax.ppermute(value, 'dp', [(i, i ^ bit) for i in range(count)])  16.8 us
    ppermute x16, waiting for transfers between devices, swap(): return lax.ppermute(value, 'dp', [(i, i ^ bit) for i in range(count)])  14 us
    pallas_call x1, Pallas kernels, hidden_rows(): pl.pallas_call(hidden_kernel, out_shape=jax.ShapeDtypeStruct((rows, colum...  4.67 us
    pallas_call x1, Pallas kernels, attend(): pl.pallas_call(functools.partial(attend_kernel, plane), out_shape=(jax.Sh...  2.65 us
    pallas_call x1, Pallas kernels, down_rows(): pl.pallas_call(down_kernel, out_shape=[jax.ShapeDtypeStruct((size, width...  2.3 us
  transfers between devices with their start and end apart: 16, of which 9 were waited for; matrix products, arithmetic and copies ran while one was open for 0% of the time, Pallas kernels for 1%

profile of v21, /device:TPU:0, one launch (start us, length us, event | category | flops | bytes accessed | tf_op | source)
XLA Modules:
  0.0 42.4 jit_solution(7555141443325284144)
XLA Ops:
  0.7 2.7 %attend.1 = (bf16[8,4096]{1,0:T(8,128)(2,1)}, bf16[8,3072]{1,0:T(8,128)(2,1)S(1)}, bf16[8,3072]{1,0:T(8,128)(2,1)S(1)}, bf16[8,3072]{1,0:T(8,128)(2,1)S(1)}, bf1...) custom-call(bf16[8,4096]{1,0:T(8,128)(2,1)} %refs_0_.1, ...), custom_call_target="tpu_custom_call" | custom-call | tf_op jit(solution)/shard_map/attend/pallas_call | solution.py:206
  3.3 3.1 %collective-permute-start = (bf16[8,3072]{1,0:T(8,128)(2,1)S(1)}, bf16[8,3072]{1,0:T(8,128)(2,1)S(1)}, u32[]{:S(2)}, u32[]{:S(2)}) collective-permute-start(bf16[8,3072]{1,0:T(8,128)(2,1)S(1)} %get-tuple-element.25), channel_id=1, source_target_pairs={{0,4},{1,5},{2,6},{3,7},{4,0},{5,1},{6,2},{7,3},{8,12},{9,13},{10,... | collective-permute-start | bytes 147464 | tf_op jit(solution)/shard_map/ppermute | solution.py:412
  6.4 2.5 %collective-permute-start.3 = (bf16[8,3072]{1,0:T(8,128)(2,1)S(1)}, bf16[8,3072]{1,0:T(8,128)(2,1)S(1)}, u32[]{:S(2)}, u32[]{:S(2)}) collective-permute-start(bf16[8,3072]{1,0:T(8,128)(2,1)S(1)} %get-tuple-element.26), channel_id=1, source_target_pairs={{0,12},{1,13},{2,14},{3,15},{4,8},{5,9},{6,10},{7,11},{8,4},{9,5},... | collective-permute-start | bytes 147464 | tf_op jit(solution)/shard_map/ppermute | solution.py:412
  8.9 0.1 collective-permute-start.4
  9.0 0.0 collective-permute-done.refs_2_
  9.0 1.6 %collective-permute-start.1 = (bf16[16,3072]{1,0:T(8,128)(2,1)S(1)}, bf16[16,3072]{1,0:T(8,128)(2,1)S(1)}, u32[]{:S(2)}, u32[]{:S(2)}) collective-permute-start(bf16[16,3072]{1,0:T(8,128)(2,1)S(1)} %join.4.refs_1_), channel_id=1, source_target_pairs={{0,2},{1,3},{2,0},{3,1},{4,6},{5,7},{6,4},{7,5},{8,10},{9,11},{10,... | collective-permute-start | bytes 294920 | tf_op jit(solution)/shard_map/ppermute | solution.py:412
  10.6 2.3 %collective-permute-done.3.refs_1_ = bf16[8,3072]{1,0:T(8,128)(2,1)S(1)} collective-permute-done((bf16[8,3072]{1,0:T(8,128)(2,1)S(1)}, bf16[8,3072]{1,0:T(8,128)(2,1)S(1)}, u32[]{:S(2)}, u32[]{:S(2)}) %collective-permute-start.3) | collective-permute-done | bytes 49184 | tf_op jit(solution)/shard_map/ppermute | solution.py:412
  12.9 1.5 %collective-permute-done.4.refs_2_ = bf16[8,3072]{1,0:T(8,128)(2,1)S(1)} collective-permute-done((bf16[8,3072]{1,0:T(8,128)(2,1)S(1)}, bf16[8,3072]{1,0:T(8,128)(2,1)S(1)}, u32[]{:S(2)}, u32[]{:S(2)}) %collective-permute-start.4) | collective-permute-done | bytes 49184 | tf_op jit(solution)/shard_map/ppermute | solution.py:412
  14.4 1.6 %collective-permute-start.5 = (bf16[16,3072]{1,0:T(8,128)(2,1)S(1)}, bf16[16,3072]{1,0:T(8,128)(2,1)S(1)}, u32[]{:S(2)}, u32[]{:S(2)}) collective-permute-start(bf16[16,3072]{1,0:T(8,128)(2,1)S(1)} %join.6.refs_1_), channel_id=1, source_target_pairs={{0,2},{1,3},{2,0},{3,1},{4,6},{5,7},{6,4},{7,5},{8,10},{9,11},{10,... | collective-permute-start | bytes 294920 | tf_op jit(solution)/shard_map/ppermute | solution.py:412
  16.0 0.0 collective-permute-done.1.refs_2_
  16.0 0.1 collective-permute-start.2
  16.1 3.0 %collective-permute-done.5.refs_2_ = bf16[16,3072]{1,0:T(8,128)(2,1)S(1)} collective-permute-done((bf16[16,3072]{1,0:T(8,128)(2,1)S(1)}, bf16[16,3072]{1,0:T(8,128)(2,1)S(1)}, u32[]{:S(2)}, u32[]{:S(2)}) %collective-permute-start.5) | collective-permute-done | bytes 98336 | tf_op jit(solution)/shard_map/ppermute | solution.py:412
  19.1 0.1 collective-permute-start.6
  19.2 1.4 %collective-permute-done.6.refs_3_ = bf16[32,3072]{1,0:T(8,128)(2,1)S(1)} collective-permute-done((bf16[32,3072]{1,0:T(8,128)(2,1)S(1)}, bf16[32,3072]{1,0:T(8,128)(2,1)S(1)}, u32[]{:S(2)}, u32[]{:S(2)}) %collective-permute-start.6) | collective-permute-done | bytes 196640 | tf_op jit(solution)/shard_map/ppermute | solution.py:412
  20.6 4.7 %hidden.1 = bf16[128,1792]{1,0:T(8,128)(2,1)S(1)} custom-call(bf16[4096,1792]{1,0:T(8,128)(2,1)S(1)} %copy-done.1, bf16[4096,1792]{1,0:T(8,128)(2,1)S(1)} %copy-done.2, bf16[1792,4096]{1,0:T(8,128)(2,1)S(1)} %copy-done, bf16[32,3072]{1,0:T(8,128)(2,1)S(1)} %join.5.refs_0_, bf16[32,3072]{1,0:T(8,128)(2,1)S(1)} %collective-permute-done.2.refs_1_, ...), custom_call_target="tpu_custom_call" | custom-call | flops 3758096384 | tf_op jit(solution)/shard_map/hidden/pallas_call | solution.py:256
  25.3 2.3 %down.1 = (bf16[32,3072]{1,0:T(8,128)(2,1)S(1)}, bf16[32,3072]{1,0:T(8,128)(2,1)S(1)}, bf16[32,3072]{1,0:T(8,128)(2,1)S(1)}, bf16[32,3072]{1,0:T(8,128)(2,1)S(1)}) custom-call(bf16[128,1792]{1,0:T(8,128)(2,1)S(1)} %hidden.1, bf16[1792,4096]{1,0:T(8,128)(2,1)S(1)} %copy-done), custom_call_target="tpu_custom_call" | custom-call | flops 1879048192 | tf_op jit(solution)/shard_map/down/pallas_call | solution.py:313
  27.6 0.2 collective-permute-start.8
  27.8 0.4 collective-permute-start.7
  28.2 0.9 %collective-permute-done.8.arrived = bf16[32,3072]{1,0:T(8,128)(2,1)S(1)} collective-permute-done((bf16[32,3072]{1,0:T(8,128)(2,1)S(1)}, bf16[32,3072]{1,0:T(8,128)(2,1)S(1)}, u32[]{:S(2)}, u32[]{:S(2)}) %collective-permute-start.8) | collective-permute-done | bytes 196640 | tf_op jit(solution)/shard_map/ppermute | solution.py:412
  29.2 1.6 %collective-permute-start.12 = (bf16[8,3072]{1,0:T(8,128)(2,1)S(1)}, bf16[8,3072]{1,0:T(8,128)(2,1)S(1)}, u32[]{:S(2)}, u32[]{:S(2)}) collective-permute-start(bf16[8,3072]{1,0:T(8,128)(2,1)S(1)} %get-tuple-element.39), channel_id=1, source_target_pairs={{0,2},{1,3},{2,0},{3,1},{4,6},{5,7},{6,4},{7,5},{8,10},{9,11},{10,... | collective-permute-start | bytes 147464 | tf_op jit(solution)/shard_map/ppermute | solution.py:412
  30.8 0.5 %collective-permute-start.11 = (bf16[8,3072]{1,0:T(8,128)(2,1)S(1)}, bf16[8,3072]{1,0:T(8,128)(2,1)S(1)}, u32[]{:S(2)}, u32[]{:S(2)}) collective-permute-start(bf16[8,3072]{1,0:T(8,128)(2,1)S(1)} %get-tuple-element.38), channel_id=1, source_target_pairs={{0,2},{1,3},{2,0},{3,1},{4,6},{5,7},{6,4},{7,5},{8,10},{9,11},{10,... | collective-permute-start | bytes 147464 | tf_op jit(solution)/shard_map/ppermute | solution.py:412
  31.3 1.6 %collective-permute-start.10 = (bf16[8,3072]{1,0:T(8,128)(2,1)S(1)}, bf16[8,3072]{1,0:T(8,128)(2,1)S(1)}, u32[]{:S(2)}, u32[]{:S(2)}) collective-permute-start(bf16[8,3072]{1,0:T(8,128)(2,1)S(1)} %get-tuple-element.36), channel_id=1, source_target_pairs={{0,2},{1,3},{2,0},{3,1},{4,6},{5,7},{6,4},{7,5},{8,10},{9,11},{10,... | collective-permute-start | bytes 147464 | tf_op jit(solution)/shard_map/ppermute | solution.py:412
  32.9 0.5 %collective-permute-start.9 = (bf16[8,3072]{1,0:T(8,128)(2,1)S(1)}, bf16[8,3072]{1,0:T(8,128)(2,1)S(1)}, u32[]{:S(2)}, u32[]{:S(2)}) collective-permute-start(bf16[8,3072]{1,0:T(8,128)(2,1)S(1)} %get-tuple-element.34), channel_id=1, source_target_pairs={{0,2},{1,3},{2,0},{3,1},{4,6},{5,7},{6,4},{7,5},{8,10},{9,11},{10,... | collective-permute-start | bytes 147464 | tf_op jit(solution)/shard_map/ppermute | solution.py:412
  33.4 0.1 collective-permute-done.12.arrived
  33.6 0.8 %collective-permute-start.14 = (bf16[8,3072]{1,0:T(8,128)(2,1)S(1)}, bf16[8,3072]{1,0:T(8,128)(2,1)S(1)}, u32[]{:S(2)}, u32[]{:S(2)}) collective-permute-start(bf16[8,3072]{1,0:T(8,128)(2,1)S(1)} %fold.8.after), channel_id=1, source_target_pairs={{0,8},{1,9},{2,10},{3,11},{4,12},{5,13},{6,14},{7,15},{8,0},{9,1},... | collective-permute-start | bytes 147464 | tf_op jit(solution)/shard_map/ppermute | solution.py:412
  34.3 0.8 %collective-permute-done.11.arrived = bf16[8,3072]{1,0:T(8,128)(2,1)S(1)} collective-permute-done((bf16[8,3072]{1,0:T(8,128)(2,1)S(1)}, bf16[8,3072]{1,0:T(8,128)(2,1)S(1)}, u32[]{:S(2)}, u32[]{:S(2)}) %collective-permute-start.11) | collective-permute-done | bytes 49184 | tf_op jit(solution)/shard_map/ppermute | solution.py:412
  35.1 2.2 %collective-permute-start.15 = (bf16[8,3072]{1,0:T(8,128)(2,1)S(1)}, bf16[8,3072]{1,0:T(8,128)(2,1)S(1)}, u32[]{:S(2)}, u32[]{:S(2)}) collective-permute-start(bf16[8,3072]{1,0:T(8,128)(2,1)S(1)} %fold.9.after), channel_id=1, source_target_pairs={{0,12},{1,13},{2,14},{3,15},{4,8},{5,9},{6,10},{7,11},{8,4},{9,5},... | collective-permute-start | bytes 147464 | tf_op jit(solution)/shard_map/ppermute | solution.py:412
  37.3 0.1 collective-permute-start.13
  37.4 3.7 %collective-permute-done.15.three = bf16[8,3072]{1,0:T(8,128)(2,1)S(1)} collective-permute-done((bf16[8,3072]{1,0:T(8,128)(2,1)S(1)}, bf16[8,3072]{1,0:T(8,128)(2,1)S(1)}, u32[]{:S(2)}, u32[]{:S(2)}) %collective-permute-start.15) | collective-permute-done | bytes 49184 | tf_op jit(solution)/shard_map/ppermute | solution.py:412
  41.1 0.2 combine_far.1.total
  41.3 0.3 collective-permute-done.13.one
  41.6 0.8 %combine.1 = bf16[8,4096]{1,0:T(8,128)(2,1)} custom-call(f32[16,128]{1,0:T(8,128)S(1)} %get-tuple-element.22.refs_0_.after.share, bf16[4,16,128]{2,1,0:T(8,128)(2,1)S(1)} %get-tuple-element.23.take, bf16[8,3072]{1,0:T(8,128)(2,1)S(1)} %fold.11.zero, bf16[8,3072]{1,0:T(8,128)(2,1)S(1)} %collective-permute-done.13.one, f32[8,4096]{1,0:T(8,128)S(1)} %combine_far.1.total), custom_call_target="tpu_custom_call" | custom-call | bytes 16777216 | tf_op jit(solution)/shard_map/combine/pallas_call | solution.py:400
  (21 shorter events, 0.2 us)
Async XLA Ops:
  0.6 20.0 %copy-start = (bf16[1792,4096]{1,0:T(8,128)(2,1)S(1)}, bf16[1792,4096]{1,0:T(8,128)(2,1)}, u32[]{:S(2)}) copy-start(bf16[1792,4096]{1,0:T(8,128)(2,1)} %weight.1) | copy-start | bytes 44040196
  0.6 20.0 %copy-start.1 = (bf16[4096,1792]{1,0:T(8,128)(2,1)S(1)}, bf16[4096,1792]{1,0:T(8,128)(2,1)}, u32[]{:S(2)}) copy-start(bf16[4096,1792]{1,0:T(8,128)(2,1)} %gate_weight.1) | copy-start | bytes 44040196
  0.7 20.0 %copy-start.2 = (bf16[4096,1792]{1,0:T(8,128)(2,1)S(1)}, bf16[4096,1792]{1,0:T(8,128)(2,1)}, u32[]{:S(2)}) copy-start(bf16[4096,1792]{1,0:T(8,128)(2,1)} %up_weight.1) | copy-start | bytes 44040196
  3.3 5.7 %collective-permute-start = (bf16[8,3072]{1,0:T(8,128)(2,1)S(1)}, bf16[8,3072]{1,0:T(8,128)(2,1)S(1)}, u32[]{:S(2)}, u32[]{:S(2)}) collective-permute-start(bf16[8,3072]{1,0:T(8,128)(2,1)S(1)} %get-tuple-element.25), channel_id=1, source_target_pairs={{0,4},{1,5},{2,6},{3,7},{4,0},{5,1},{6,2},{7,3},{8,12},{9,13},{10,... | collective-permute-start | bytes 147464 | tf_op jit(solution)/shard_map/ppermute | solution.py:412
  6.4 6.5 %collective-permute-start.3 = (bf16[8,3072]{1,0:T(8,128)(2,1)S(1)}, bf16[8,3072]{1,0:T(8,128)(2,1)S(1)}, u32[]{:S(2)}, u32[]{:S(2)}) collective-permute-start(bf16[8,3072]{1,0:T(8,128)(2,1)S(1)} %get-tuple-element.26), channel_id=1, source_target_pairs={{0,12},{1,13},{2,14},{3,15},{4,8},{5,9},{6,10},{7,11},{8,4},{9,5},... | collective-permute-start | bytes 147464 | tf_op jit(solution)/shard_map/ppermute | solution.py:412
  8.9 5.5 %collective-permute-start.4 = (bf16[8,3072]{1,0:T(8,128)(2,1)S(1)}, bf16[8,3072]{1,0:T(8,128)(2,1)S(1)}, u32[]{:S(2)}, u32[]{:S(2)}) collective-permute-start(bf16[8,3072]{1,0:T(8,128)(2,1)S(1)} %get-tuple-element.27), channel_id=1, source_target_pairs={{0,8},{1,9},{2,10},{3,11},{4,12},{5,13},{6,14},{7,15},{8,0},{9,1},... | collective-permute-start | bytes 147464 | tf_op jit(solution)/shard_map/ppermute | solution.py:412
  9.0 7.0 %collective-permute-start.1 = (bf16[16,3072]{1,0:T(8,128)(2,1)S(1)}, bf16[16,3072]{1,0:T(8,128)(2,1)S(1)}, u32[]{:S(2)}, u32[]{:S(2)}) collective-permute-start(bf16[16,3072]{1,0:T(8,128)(2,1)S(1)} %join.4.refs_1_), channel_id=1, source_target_pairs={{0,2},{1,3},{2,0},{3,1},{4,6},{5,7},{6,4},{7,5},{8,10},{9,11},{10,... | collective-permute-start | bytes 294920 | tf_op jit(solution)/shard_map/ppermute | solution.py:412
  14.4 4.7 %collective-permute-start.5 = (bf16[16,3072]{1,0:T(8,128)(2,1)S(1)}, bf16[16,3072]{1,0:T(8,128)(2,1)S(1)}, u32[]{:S(2)}, u32[]{:S(2)}) collective-permute-start(bf16[16,3072]{1,0:T(8,128)(2,1)S(1)} %join.6.refs_1_), channel_id=1, source_target_pairs={{0,2},{1,3},{2,0},{3,1},{4,6},{5,7},{6,4},{7,5},{8,10},{9,11},{10,... | collective-permute-start | bytes 294920 | tf_op jit(solution)/shard_map/ppermute | solution.py:412
  16.0 3.2 %collective-permute-start.2 = (bf16[32,3072]{1,0:T(8,128)(2,1)S(1)}, bf16[32,3072]{1,0:T(8,128)(2,1)S(1)}, u32[]{:S(2)}, u32[]{:S(2)}) collective-permute-start(bf16[32,3072]{1,0:T(8,128)(2,1)S(1)} %join.5.refs_0_), channel_id=1, source_target_pairs={{0,1},{1,0},{2,3},{3,2},{4,5},{5,4},{6,7},{7,6},{8,9},{9,8},{10,11... | collective-permute-start | bytes 589832 | tf_op jit(solution)/shard_map/ppermute | solution.py:412
  19.1 1.5 %collective-permute-start.6 = (bf16[32,3072]{1,0:T(8,128)(2,1)S(1)}, bf16[32,3072]{1,0:T(8,128)(2,1)S(1)}, u32[]{:S(2)}, u32[]{:S(2)}) collective-permute-start(bf16[32,3072]{1,0:T(8,128)(2,1)S(1)} %join.7.refs_2_), channel_id=1, source_target_pairs={{0,1},{1,0},{2,3},{3,2},{4,5},{5,4},{6,7},{7,6},{8,9},{9,8},{10,11... | collective-permute-start | bytes 589832 | tf_op jit(solution)/shard_map/ppermute | solution.py:412
  27.6 1.5 %collective-permute-start.8 = (bf16[32,3072]{1,0:T(8,128)(2,1)S(1)}, bf16[32,3072]{1,0:T(8,128)(2,1)S(1)}, u32[]{:S(2)}, u32[]{:S(2)}) collective-permute-start(bf16[32,3072]{1,0:T(8,128)(2,1)S(1)} %get-tuple-element.31), channel_id=1, source_target_pairs={{0,1},{1,0},{2,3},{3,2},{4,5},{5,4},{6,7},{7,6},{8,9},{9,8},{10,11... | collective-permute-start | bytes 589832 | tf_op jit(solution)/shard_map/ppermute | solution.py:412
  27.8 3.4 %collective-permute-start.7 = (bf16[32,3072]{1,0:T(8,128)(2,1)S(1)}, bf16[32,3072]{1,0:T(8,128)(2,1)S(1)}, u32[]{:S(2)}, u32[]{:S(2)}) collective-permute-start(bf16[32,3072]{1,0:T(8,128)(2,1)S(1)} %get-tuple-element.29), channel_id=1, source_target_pairs={{0,1},{1,0},{2,3},{3,2},{4,5},{5,4},{6,7},{7,6},{8,9},{9,8},{10,11... | collective-permute-start | bytes 589832 | tf_op jit(solution)/shard_map/ppermute | solution.py:412
  29.2 4.4 %collective-permute-start.12 = (bf16[8,3072]{1,0:T(8,128)(2,1)S(1)}, bf16[8,3072]{1,0:T(8,128)(2,1)S(1)}, u32[]{:S(2)}, u32[]{:S(2)}) collective-permute-start(bf16[8,3072]{1,0:T(8,128)(2,1)S(1)} %get-tuple-element.39), channel_id=1, source_target_pairs={{0,2},{1,3},{2,0},{3,1},{4,6},{5,7},{6,4},{7,5},{8,10},{9,11},{10,... | collective-permute-start | bytes 147464 | tf_op jit(solution)/shard_map/ppermute | solution.py:412
  30.8 4.3 %collective-permute-start.11 = (bf16[8,3072]{1,0:T(8,128)(2,1)S(1)}, bf16[8,3072]{1,0:T(8,128)(2,1)S(1)}, u32[]{:S(2)}, u32[]{:S(2)}) collective-permute-start(bf16[8,3072]{1,0:T(8,128)(2,1)S(1)} %get-tuple-element.38), channel_id=1, source_target_pairs={{0,2},{1,3},{2,0},{3,1},{4,6},{5,7},{6,4},{7,5},{8,10},{9,11},{10,... | collective-permute-start | bytes 147464 | tf_op jit(solution)/shard_map/ppermute | solution.py:412
  31.3 6.0 %collective-permute-start.10 = (bf16[8,3072]{1,0:T(8,128)(2,1)S(1)}, bf16[8,3072]{1,0:T(8,128)(2,1)S(1)}, u32[]{:S(2)}, u32[]{:S(2)}) collective-permute-start(bf16[8,3072]{1,0:T(8,128)(2,1)S(1)} %get-tuple-element.36), channel_id=1, source_target_pairs={{0,2},{1,3},{2,0},{3,1},{4,6},{5,7},{6,4},{7,5},{8,10},{9,11},{10,... | collective-permute-start | bytes 147464 | tf_op jit(solution)/shard_map/ppermute | solution.py:412
  32.9 4.5 %collective-permute-start.9 = (bf16[8,3072]{1,0:T(8,128)(2,1)S(1)}, bf16[8,3072]{1,0:T(8,128)(2,1)S(1)}, u32[]{:S(2)}, u32[]{:S(2)}) collective-permute-start(bf16[8,3072]{1,0:T(8,128)(2,1)S(1)} %get-tuple-element.34), channel_id=1, source_target_pairs={{0,2},{1,3},{2,0},{3,1},{4,6},{5,7},{6,4},{7,5},{8,10},{9,11},{10,... | collective-permute-start | bytes 147464 | tf_op jit(solution)/shard_map/ppermute | solution.py:412
  33.6 7.5 %collective-permute-start.14 = (bf16[8,3072]{1,0:T(8,128)(2,1)S(1)}, bf16[8,3072]{1,0:T(8,128)(2,1)S(1)}, u32[]{:S(2)}, u32[]{:S(2)}) collective-permute-start(bf16[8,3072]{1,0:T(8,128)(2,1)S(1)} %fold.8.after), channel_id=1, source_target_pairs={{0,8},{1,9},{2,10},{3,11},{4,12},{5,13},{6,14},{7,15},{8,0},{9,1},... | collective-permute-start | bytes 147464 | tf_op jit(solution)/shard_map/ppermute | solution.py:412
  35.1 6.0 %collective-permute-start.15 = (bf16[8,3072]{1,0:T(8,128)(2,1)S(1)}, bf16[8,3072]{1,0:T(8,128)(2,1)S(1)}, u32[]{:S(2)}, u32[]{:S(2)}) collective-permute-start(bf16[8,3072]{1,0:T(8,128)(2,1)S(1)} %fold.9.after), channel_id=1, source_target_pairs={{0,12},{1,13},{2,14},{3,15},{4,8},{5,9},{6,10},{7,11},{8,4},{9,5},... | collective-permute-start | bytes 147464 | tf_op jit(solution)/shard_map/ppermute | solution.py:412
  37.3 4.3 %collective-permute-start.13 = (bf16[8,3072]{1,0:T(8,128)(2,1)S(1)}, bf16[8,3072]{1,0:T(8,128)(2,1)S(1)}, u32[]{:S(2)}, u32[]{:S(2)}) collective-permute-start(bf16[8,3072]{1,0:T(8,128)(2,1)S(1)} %fold.10.after), channel_id=1, source_target_pairs={{0,4},{1,5},{2,6},{3,7},{4,0},{5,1},{6,2},{7,3},{8,12},{9,13},{10,... | collective-permute-start | bytes 147464 | tf_op jit(solution)/shard_map/ppermute | solution.py:412
